TPU v7x, 32 devices: a whole 2x2x4 slice. The times are simulated.
32 devices in a mesh: batch: 8 (over z, x), rows: 4 (over y, core).
Axes of the slice: x: 2, y: 2, z: 4, core: 2. Of those that a mesh axis runs over, the one named last changes fastest.
Arguments:
- features: float32 [8, 16, 40, 2048], P('batch', 'rows'), may hold values from -25 to 25
- reduce_weight: float32 [2048, 512], P('batch'), may hold values from -0.125 to 0.125
- reduce_norm: float32 [2, 512], P(None, 'batch'), may hold values from -1.5 to 1.5
- dilate_weight: float32 [4608, 512], P('batch'), may hold values from -0.09375 to 0.09375
- dilate_norm: float32 [2, 512], P(None, 'batch'), may hold values from -1.5 to 1.5
- expand_weight: float32 [512, 2048], P('batch'), may hold values from -0.25 to 0.25
- expand_norm: float32 [2, 2048], P(None, 'batch'), may hold values from -1.5 to 1.5
- depth_head: float32 [4608, 512], P('batch'), may hold values from -0.09375 to 0.09375
- segment_head: float32 [4608, 512], P('batch'), may hold values from -0.09375 to 0.09375
- normal_head: float32 [4608, 512], P('batch'), may hold values from -0.09375 to 0.09375
- contour_head: float32 [4608, 512], P('batch'), may hold values from -0.09375 to 0.09375
- depth_message: float32 [4608, 512], P('batch'), may hold values from -0.0625 to 0.0625
- segment_message: float32 [4608, 512], P('batch'), may hold values from -0.0625 to 0.0625
- normal_message: float32 [4608, 512], P('batch'), may hold values from -0.0625 to 0.0625
- contour_message: float32 [4608, 512], P('batch'), may hold values from -0.0625 to 0.0625
- depth_gate: float32 [512, 512], P('batch'), may hold values from -0.25 to 0.25
- segment_gate: float32 [512, 512], P('batch'), may hold values from -0.25 to 0.25
- classifier: float32 [512, 40], P('batch'), may hold values from -0.5 to 0.5
- depth_valid: int32 [8, 16, 40], P('batch', 'rows'), may hold values from 0 to 1, as said below
- labels: int32 [8, 16, 40], P('batch', 'rows'), may hold values from 0 to 39
- block_cotangent: float32 [8, 16, 40, 2048], P('batch', 'rows'), may hold values from -6 to 6
- depth_cotangent: float32 [8, 16, 40, 512], P('batch', 'rows'), may hold values from -1.75 to 1.75
Outputs:
- block_out: float32 [8, 16, 40, 2048], P('batch', 'rows')
- depth_stream: float32 [8, 16, 40, 512], P('batch', 'rows')
- segment_stream: float32 [8, 16, 40, 512], P('batch', 'rows')
- features_grad: float32 [8, 16, 40, 2048], P('batch', 'rows')
- reduce_weight_grad: float32 [2048, 512], P('batch')
- reduce_norm_grad: float32 [2, 512], P(None, 'batch')
- dilate_weight_grad: float32 [4608, 512], P('batch')
- dilate_norm_grad: float32 [2, 512], P(None, 'batch')
- expand_weight_grad: float32 [512, 2048], P('batch')
- expand_norm_grad: float32 [2, 2048], P(None, 'batch')
- depth_head_grad: float32 [4608, 512], P('batch')
- segment_head_grad: float32 [4608, 512], P('batch')
- normal_head_grad: float32 [4608, 512], P('batch')
- contour_head_grad: float32 [4608, 512], P('batch')
- depth_message_grad: float32 [4608, 512], P('batch')
- segment_message_grad: float32 [4608, 512], P('batch')
- normal_message_grad: float32 [4608, 512], P('batch')
- contour_message_grad: float32 [4608, 512], P('batch')
- depth_gate_grad: float32 [512, 512], P('batch')
- segment_gate_grad: float32 [512, 512], P('batch')
- classifier_grad: float32 [512, 40], P('batch')
Inputs may be any that keep to these rules, and one draw needn't show every extreme that they name: `depth_valid`: every image has a valid pixel at its first row and first column.
All inputs are finite; a program needn't handle non-finite values.
Results may differ from a plain program's by a relative error of at most 0.0003.
Values sent between devices are 32-bit elements; how exact they have to be, the bound alone decides.
No kernel may reach another device: no remote copies, remote signals or barrier semaphores. Data moves between devices by JAX's collectives and lax.ppermute only.
A program may use at most 384 MiB of HBM per device.

v0:
```python
import jax
import jax.numpy as jnp
from jax import lax
from jax.sharding import PartitionSpec as P

EPSILON = 1e-05
PRECISE = lax.Precision.HIGHEST


def extended(array, sides, width):
    for axis, dim in sides:
        size, length = (lax.axis_size(axis), array.shape[dim])
        up = [(i, (i + 1) % size) for i in range(size - 1)]
        down = [(j, i) for i, j in up]
        last = lax.slice_in_dim(array, length - width, length, axis=dim)
        leading = lax.slice_in_dim(array, 0, width, axis=dim)
        before = lax.ppermute(last, axis, up)
        after = lax.ppermute(leading, axis, down)
        array = jnp.concatenate([before, array, after], axis=dim)
    return array


def matmul(values, weight):
    return jnp.dot(values, weight, precision=PRECISE)


def matmul_back(values, weight):
    return lax.dot_general(
        values, weight, (((values.ndim - 1,), (1,)), ((), ())), precision=PRECISE
    )


def weight_grad(inputs, grads):
    flat_in = inputs.reshape(-1, inputs.shape[-1])
    flat_grad = grads.reshape(-1, grads.shape[-1])
    return lax.dot_general(flat_in, flat_grad, (((0,), (0,)), ((), ())), precision=PRECISE)


def columns(padded, dilation):
    height = padded.shape[-3] - 2 * dilation
    breadth = padded.shape[-2]
    widths = [(0, 0)] * (padded.ndim - 2) + [(dilation, dilation), (0, 0)]
    framed = jnp.pad(padded, widths)
    pieces = []
    for vertical in range(3):
        for across in range(3):
            pieces.append(
                framed[
                    ...,
                    vertical * dilation : vertical * dilation + height,
                    across * dilation : across * dilation + breadth,
                    :,
                ]
            )
    return jnp.concatenate(pieces, axis=-1)


def flipped(weight):
    taps_in = weight.shape[0] // 9
    blocks = weight.reshape(9, taps_in, weight.shape[1])[::-1]
    return jnp.transpose(blocks, (0, 2, 1)).reshape(9 * weight.shape[1], taps_in)


def silu_grad(values):
    gate_val = jax.nn.sigmoid(values)
    return gate_val * (1.0 + values * (1.0 - gate_val))


def statistics(total, squares, count):
    center = total / count
    inverse = lax.rsqrt(squares / count - center * center + EPSILON)
    return (center, inverse)


def normalize(values, center, inverse, params):
    centered = (values - center) * inverse
    return (centered, centered * params[0] + params[1])


def moments(values):
    return lax.psum(
        (jnp.sum(values, axis=(0, 1, 2)), jnp.sum(values * values, axis=(0, 1, 2))),
        ("batch", "rows"),
    )


def norm_back(d_out, centered, inverse, params, count):
    total, along = lax.psum(
        (jnp.sum(d_out, axis=(0, 1, 2)), jnp.sum(d_out * centered, axis=(0, 1, 2))),
        ("batch", "rows"),
    )
    d_values = inverse * (
        d_out * params[0] - params[0] * total / count - centered * (params[0] * along / count)
    )
    return (d_values, jnp.stack([along, total]))


def shards(
    features,
    reduce_weight,
    reduce_norm,
    dilate_weight,
    dilate_norm,
    expand_weight,
    expand_norm,
    depth_head,
    segment_head,
    normal_head,
    contour_head,
    depth_message,
    segment_message,
    normal_message,
    contour_message,
    depth_gate,
    segment_gate,
    classifier,
    depth_valid,
    labels,
    block_cotangent,
    depth_cotangent,
):
    gathered = (
        lax.all_gather(reduce_weight, "batch", axis=0, tiled=True),
        lax.all_gather(reduce_norm, "batch", axis=1, tiled=True),
        lax.all_gather(dilate_weight, "batch", axis=0, tiled=True),
        lax.all_gather(dilate_norm, "batch", axis=1, tiled=True),
        lax.all_gather(expand_weight, "batch", axis=0, tiled=True),
        lax.all_gather(expand_norm, "batch", axis=1, tiled=True),
        lax.all_gather(depth_head, "batch", axis=0, tiled=True),
        lax.all_gather(segment_head, "batch", axis=0, tiled=True),
        lax.all_gather(normal_head, "batch", axis=0, tiled=True),
        lax.all_gather(contour_head, "batch", axis=0, tiled=True),
        lax.all_gather(depth_message, "batch", axis=0, tiled=True),
        lax.all_gather(segment_message, "batch", axis=0, tiled=True),
        lax.all_gather(normal_message, "batch", axis=0, tiled=True),
        lax.all_gather(contour_message, "batch", axis=0, tiled=True),
        lax.all_gather(depth_gate, "batch", axis=0, tiled=True),
        lax.all_gather(segment_gate, "batch", axis=0, tiled=True),
        lax.all_gather(classifier, "batch", axis=0, tiled=True),
    )
    reduce_full, reduce_scale, dilate_full, dilate_scale, expand_full, expand_scale = gathered[:6]
    heads_full = jnp.concatenate([gathered[6], gathered[7], gathered[8], gathered[9]], axis=1)
    depth_message_full, segment_message_full, normal_message_full, contour_message_full = gathered[
        10:14
    ]
    depth_gate_full, segment_gate_full, classifier_full = gathered[14:]
    chan_mid = reduce_weight.shape[1]
    nine = 9 * chan_mid
    classes = classifier.shape[1]
    count_all = float(
        features.shape[0]
        * features.shape[1]
        * features.shape[2]
        * lax.axis_size("batch")
        * lax.axis_size("rows")
    )
    pre_reduce = matmul(features, reduce_full)
    total_one, square_one, valid_total = lax.psum(
        (
            jnp.sum(pre_reduce, axis=(0, 1, 2)),
            jnp.sum(pre_reduce * pre_reduce, axis=(0, 1, 2)),
            jnp.sum(depth_valid.astype(jnp.float32)),
        ),
        ("batch", "rows"),
    )
    center_one, inverse_one = statistics(total_one, square_one, count_all)
    hat_one, normed_one = normalize(pre_reduce, center_one, inverse_one, reduce_scale)
    mid_pad = extended(jax.nn.silu(normed_one), (("rows", 1),), 2)
    mid_cols = columns(mid_pad, 2)
    pre_dilate = matmul(mid_cols, dilate_full)
    total_two, square_two = moments(pre_dilate)
    center_two, inverse_two = statistics(total_two, square_two, count_all)
    hat_two, normed_two = normalize(pre_dilate, center_two, inverse_two, dilate_scale)
    mid_out = jax.nn.silu(normed_two)
    pre_expand = matmul(mid_out, expand_full)
    total_three, square_three = moments(pre_expand)
    center_three, inverse_three = statistics(total_three, square_three, count_all)
    hat_three, normed_three = normalize(pre_expand, center_three, inverse_three, expand_scale)
    summed = normed_three + features
    block_out = jax.nn.silu(summed)
    head_pad = extended(mid_out, (("rows", 1),), 1)
    head_cols = columns(head_pad, 1)
    all_heads = matmul(head_cols, heads_full)
    depth_feat = all_heads[..., :chan_mid]
    segment_feat = all_heads[..., chan_mid : 2 * chan_mid]
    normal_feat = all_heads[..., 2 * chan_mid : 3 * chan_mid]
    contour_feat = all_heads[..., 3 * chan_mid :]
    stream_pad = extended(
        jnp.stack([depth_feat, segment_feat, normal_feat, contour_feat]), (("rows", 2),), 1
    )
    depth_msg_cols = jnp.concatenate(
        [columns(stream_pad[1], 1), columns(stream_pad[2], 1)], axis=-1
    )
    segment_msg_cols = jnp.concatenate(
        [columns(stream_pad[0], 1), columns(stream_pad[3], 1)], axis=-1
    )
    depth_note = matmul(
        depth_msg_cols, jnp.concatenate([depth_message_full, normal_message_full], axis=0)
    )
    segment_note = matmul(
        segment_msg_cols, jnp.concatenate([segment_message_full, contour_message_full], axis=0)
    )
    depth_open = jax.nn.sigmoid(matmul(depth_feat, depth_gate_full))
    segment_open = jax.nn.sigmoid(matmul(segment_feat, segment_gate_full))
    depth_stream = depth_feat + depth_open * depth_note
    segment_stream = segment_feat + segment_open * segment_note
    logits = matmul(segment_stream, classifier_full)
    shifted = jnp.exp(logits - jnp.max(logits, axis=-1, keepdims=True))
    onehot = (labels[..., None] == jnp.arange(classes, dtype=jnp.int32)).astype(jnp.float32)
    d_logits = shifted / jnp.sum(shifted, axis=-1, keepdims=True) - onehot
    reduce_back, reduce_scale_b, dilate_back, dilate_scale_b, expand_back, expand_scale_b = (
        gathered[:6]
    )
    depth_head_back, segment_head_back, normal_head_back, contour_head_back = gathered[6:10]
    depth_message_back, segment_message_back, normal_message_back, contour_message_back = gathered[
        10:14
    ]
    depth_gate_back, segment_gate_back, classifier_back = gathered[14:]
    classifier_grad = weight_grad(segment_stream, d_logits)
    d_segment = matmul_back(d_logits, classifier_back)
    d_depth = (
        depth_valid.astype(jnp.float32)[..., None] * depth_cotangent * (count_all / valid_total)
    )
    d_depth_note = d_depth * depth_open
    d_depth_pre = d_depth * depth_note * depth_open * (1.0 - depth_open)
    depth_gate_grad = weight_grad(depth_feat, d_depth_pre)
    d_depth_feat = d_depth + matmul_back(d_depth_pre, depth_gate_back)
    d_segment_note = d_segment * segment_open
    d_segment_pre = d_segment * segment_note * segment_open * (1.0 - segment_open)
    segment_gate_grad = weight_grad(segment_feat, d_segment_pre)
    d_segment_feat = d_segment + matmul_back(d_segment_pre, segment_gate_back)
    depth_pair_grad = weight_grad(depth_msg_cols, d_depth_note)
    segment_pair_grad = weight_grad(segment_msg_cols, d_segment_note)
    note_pad = extended(jnp.stack([d_depth_note, d_segment_note]), (("rows", 2),), 1)
    from_depth = matmul(
        columns(note_pad[0], 1),
        jnp.concatenate([flipped(depth_message_back), flipped(normal_message_back)], axis=1),
    )
    from_segment = matmul(
        columns(note_pad[1], 1),
        jnp.concatenate([flipped(segment_message_back), flipped(contour_message_back)], axis=1),
    )
    d_segment_feat = d_segment_feat + from_depth[..., :chan_mid]
    d_normal_feat = from_depth[..., chan_mid:]
    d_depth_feat = d_depth_feat + from_segment[..., :chan_mid]
    d_contour_feat = from_segment[..., chan_mid:]
    heads_grad = weight_grad(
        head_cols,
        jnp.concatenate([d_depth_feat, d_segment_feat, d_normal_feat, d_contour_feat], axis=-1),
    )
    feat_pad = extended(
        jnp.stack([d_depth_feat, d_segment_feat, d_normal_feat, d_contour_feat]), (("rows", 2),), 1
    )
    back_cols = jnp.concatenate(
        [
            columns(feat_pad[0], 1),
            columns(feat_pad[1], 1),
            columns(feat_pad[2], 1),
            columns(feat_pad[3], 1),
        ],
        axis=-1,
    )
    d_mid_out = matmul(
        back_cols,
        jnp.concatenate(
            [
                flipped(depth_head_back),
                flipped(segment_head_back),
                flipped(normal_head_back),
                flipped(contour_head_back),
            ],
            axis=0,
        ),
    )
    again_in, again_reduce, again_dilate, again_expand, again_scales = lax.optimization_barrier(
        (
            features,
            reduce_back,
            dilate_back,
            expand_back,
            (reduce_scale_b, dilate_scale_b, expand_scale_b),
        )
    )
    hat_one_b, normed_one_b = normalize(
        matmul(again_in, again_reduce), center_one, inverse_one, again_scales[0]
    )
    mid_pad_b = extended(jax.nn.silu(normed_one_b), (("rows", 1),), 2)
    mid_cols_b = columns(mid_pad_b, 2)
    hat_two_b, normed_two_b = normalize(
        matmul(mid_cols_b, again_dilate), center_two, inverse_two, again_scales[1]
    )
    mid_out_b = jax.nn.silu(normed_two_b)
    hat_three_b, normed_three_b = normalize(
        matmul(mid_out_b, again_expand), center_three, inverse_three, again_scales[2]
    )
    summed_b = normed_three_b + again_in
    d_summed = block_cotangent * silu_grad(summed_b)
    d_pre_expand, expand_norm_full = norm_back(
        d_summed, hat_three_b, inverse_three, expand_scale_b, count_all
    )
    expand_grad = weight_grad(mid_out_b, d_pre_expand)
    d_mid_out = d_mid_out + matmul_back(d_pre_expand, expand_back)
    d_pre_dilate, dilate_norm_full = norm_back(
        d_mid_out * silu_grad(normed_two_b), hat_two_b, inverse_two, dilate_scale_b, count_all
    )
    dilate_grad = weight_grad(mid_cols_b, d_pre_dilate)
    dilate_pad = extended(d_pre_dilate, (("rows", 1),), 2)
    d_mid_in = matmul(columns(dilate_pad, 2), flipped(dilate_back))
    d_pre_reduce, reduce_norm_full = norm_back(
        d_mid_in * silu_grad(normed_one_b), hat_one_b, inverse_one, reduce_scale_b, count_all
    )
    reduce_grad = weight_grad(features, d_pre_reduce)
    features_grad = d_summed + matmul_back(d_pre_reduce, reduce_back)
    part_grads = (
        lax.psum_scatter(reduce_grad, "batch", scatter_dimension=0, tiled=True),
        lax.psum_scatter(dilate_grad, "batch", scatter_dimension=0, tiled=True),
        lax.psum_scatter(expand_grad, "batch", scatter_dimension=0, tiled=True),
        lax.psum_scatter(heads_grad[:, :chan_mid], "batch", scatter_dimension=0, tiled=True),
        lax.psum_scatter(
            heads_grad[:, chan_mid : 2 * chan_mid], "batch", scatter_dimension=0, tiled=True
        ),
        lax.psum_scatter(
            heads_grad[:, 2 * chan_mid : 3 * chan_mid], "batch", scatter_dimension=0, tiled=True
        ),
        lax.psum_scatter(heads_grad[:, 3 * chan_mid :], "batch", scatter_dimension=0, tiled=True),
        lax.psum_scatter(depth_pair_grad[:nine], "batch", scatter_dimension=0, tiled=True),
        lax.psum_scatter(segment_pair_grad[:nine], "batch", scatter_dimension=0, tiled=True),
        lax.psum_scatter(depth_pair_grad[nine:], "batch", scatter_dimension=0, tiled=True),
        lax.psum_scatter(segment_pair_grad[nine:], "batch", scatter_dimension=0, tiled=True),
        lax.psum_scatter(depth_gate_grad, "batch", scatter_dimension=0, tiled=True),
        lax.psum_scatter(segment_gate_grad, "batch", scatter_dimension=0, tiled=True),
        lax.psum_scatter(classifier_grad, "batch", scatter_dimension=0, tiled=True),
    )
    summed_grads = lax.psum(
        (
            part_grads[0],
            part_grads[1],
            part_grads[2],
            part_grads[3],
            part_grads[4],
            part_grads[5],
            part_grads[6],
            part_grads[7],
            part_grads[8],
            part_grads[9],
            part_grads[10],
            part_grads[11],
            part_grads[12],
            part_grads[13],
        ),
        "rows",
    )
    factor = count_all ** (-0.5)
    batch_index = lax.axis_index("batch")
    batch_count = lax.axis_size("batch")

    def local_cols(stats):
        share_len = stats.shape[1] // batch_count
        return lax.dynamic_slice_in_dim(stats, batch_index * share_len, share_len, 1) * factor

    return (
        block_out,
        depth_stream,
        segment_stream,
        features_grad,
        summed_grads[0] * factor,
        local_cols(reduce_norm_full),
        summed_grads[1] * factor,
        local_cols(dilate_norm_full),
        summed_grads[2] * factor,
        local_cols(expand_norm_full),
        summed_grads[3] * factor,
        summed_grads[4] * factor,
        summed_grads[5] * factor,
        summed_grads[6] * factor,
        summed_grads[7] * factor,
        summed_grads[8] * factor,
        summed_grads[9] * factor,
        summed_grads[10] * factor,
        summed_grads[11] * factor,
        summed_grads[12] * factor,
        summed_grads[13] * factor,
    )


def solution(mesh):
    in_specs = (
        P("batch", "rows", None, None),
        P("batch", None),
        P(None, "batch"),
        P("batch", None),
        P(None, "batch"),
        P("batch", None),
        P(None, "batch"),
        P("batch", None),
        P("batch", None),
        P("batch", None),
        P("batch", None),
        P("batch", None),
        P("batch", None),
        P("batch", None),
        P("batch", None),
        P("batch", None),
        P("batch", None),
        P("batch", None),
        P("batch", "rows", None),
        P("batch", "rows", None),
        P("batch", "rows", None, None),
        P("batch", "rows", None, None),
    )
    out_specs = (
        P("batch", "rows", None, None),
        P("batch", "rows", None, None),
        P("batch", "rows", None, None),
        P("batch", "rows", None, None),
        P("batch", None),
        P(None, "batch"),
        P("batch", None),
        P(None, "batch"),
        P("batch", None),
        P(None, "batch"),
        P("batch", None),
        P("batch", None),
        P("batch", None),
        P("batch", None),
        P("batch", None),
        P("batch", None),
        P("batch", None),
        P("batch", None),
        P("batch", None),
        P("batch", None),
        P("batch", None),
    )
    return jax.shard_map(shards, mesh=mesh, in_specs=in_specs, out_specs=out_specs, check_vma=False)
```

profile of v0, /device:TPU:1, one launch (start us, length us, event | category | flops | bytes accessed | tf_op | source)
XLA Modules:
  0.0 3821.2 jit_solution(4888787662983932364)
XLA Ops:
  47.4 22.7 all_gather.56
  89.7 43.1 %all-reduce.19 = (f32[512]{0:T(512)S(1)}, f32[512]{0:T(512)S(1)}) all-reduce(f32[512]{0:T(512)S(1)} %get-tuple-element.109, f32[512]{0:T(512)S(1)} %get-tuple-element.108), channel_id=1, replica_groups=mesh['batch'=8,'rows'=4] {'batch','rows'}, use_global_device_ids=true, to_apply=%region_3.0 | all-reduce | flops 1024 | bytes 8192 | tf_op jit(solution)/shard_map/psum | solution.py:158
  140.0 25.7 all-gather.2
  174.3 53.7 %all-gather.19.cloned.1.call-done = f32[4608,512]{1,0:T(8,128)} async-done(((f32[576,512]{1,0:T(8,128)}), f32[4608,512]{1,0:T(8,128)}) %all-gather.19.cloned.1.call-update) | async-done | bytes 9437200 | tf_op jit(solution)/shard_map/all_gather | solution.py:125
  237.1 40.1 %all-reduce.18 = (f32[512]{0:T(512)S(1)}, f32[512]{0:T(512)S(1)}) all-reduce(f32[512]{0:T(512)S(1)} %get-tuple-element.107, f32[512]{0:T(512)S(1)} %get-tuple-element.106), channel_id=1, replica_groups=mesh['batch'=8,'rows'=4] {'batch','rows'}, use_global_device_ids=true, to_apply=%region_7.8 | all-reduce | flops 1024 | bytes 8192 | tf_op jit(solution)/shard_map/psum | solution.py:81
  314.5 126.6 %all-gather.29.cloned.1.call-done = f32[4608,512]{1,0:T(8,128)} async-done(((f32[576,512]{1,0:T(8,128)}), f32[4608,512]{1,0:T(8,128)}) %all-gather.29.cloned.1.call-update) | async-done | bytes 9437200 | tf_op jit(solution)/shard_map/all_gather | solution.py:132
  449.4 130.0 %all-gather.27.cloned.1.call-done = f32[4608,512]{1,0:T(8,128)} async-done(((f32[576,512]{1,0:T(8,128)}), f32[4608,512]{1,0:T(8,128)}) %all-gather.27.cloned.1.call-update) | async-done | bytes 9437200 | tf_op jit(solution)/shard_map/all_gather | solution.py:131
  587.7 130.0 %all-gather.25.cloned.1.call-done = f32[4608,512]{1,0:T(8,128)} async-done(((f32[576,512]{1,0:T(8,128)}), f32[4608,512]{1,0:T(8,128)}) %all-gather.25.cloned.1.call-update) | async-done | bytes 9437200 | tf_op jit(solution)/shard_map/all_gather | solution.py:130
  726.1 130.0 %all-gather.23.cloned.1.call-done = f32[4608,512]{1,0:T(8,128)} async-done(((f32[576,512]{1,0:T(8,128)}), f32[4608,512]{1,0:T(8,128)}) %all-gather.23.cloned.1.call-update) | async-done | bytes 9437200 | tf_op jit(solution)/shard_map/all_gather | solution.py:129
  864.6 130.0 %all-gather.41.cloned.1.call-done = f32[4608,512]{1,0:T(8,128)} async-done(((f32[576,512]{1,0:T(8,128)}), f32[4608,512]{1,0:T(8,128)}) %all-gather.41.cloned.1.call-update) | async-done | bytes 9437200 | tf_op jit(solution)/shard_map/all_gather | solution.py:136
  1002.9 130.2 %all-gather.39.cloned.1.call-done = f32[4608,512]{1,0:T(8,128)} async-done(((f32[576,512]{1,0:T(8,128)}), f32[4608,512]{1,0:T(8,128)}) %all-gather.39.cloned.1.call-update) | async-done | bytes 9437200 | tf_op jit(solution)/shard_map/all_gather | solution.py:134
  1141.4 129.9 %all-gather.35.cloned.1.call-done = f32[4608,512]{1,0:T(8,128)} async-done(((f32[576,512]{1,0:T(8,128)}), f32[4608,512]{1,0:T(8,128)}) %all-gather.35.cloned.1.call-update) | async-done | bytes 9437200 | tf_op jit(solution)/shard_map/all_gather | solution.py:135
  1279.8 130.0 %all-gather.33.cloned.1.call-done = f32[4608,512]{1,0:T(8,128)} async-done(((f32[576,512]{1,0:T(8,128)}), f32[4608,512]{1,0:T(8,128)}) %all-gather.33.cloned.1.call-update) | async-done | bytes 9437200 | tf_op jit(solution)/shard_map/all_gather | solution.py:133
  1422.6 38.5 %all-reduce.17 = (f32[2048]{0:T(1024)S(1)}, f32[2048]{0:T(1024)S(1)}) all-reduce(f32[2048]{0:T(1024)S(1)} %get-tuple-element.101, f32[2048]{0:T(1024)S(1)} %get-tuple-element.100), channel_id=1, replica_groups=mesh['batch'=8,'rows'=4] {'batch','rows'}, use_global_device_ids=true, to_apply=%region_11.12 | all-reduce | flops 4096 | bytes 32768 | tf_op jit(solution)/shard_map/psum | solution.py:81
  1538.6 27.1 fusion.57
  1597.1 39.3 %all-reduce.16 = (f32[]{:T(128)}, f32[2048]{0:T(1024)S(1)}, f32[2048]{0:T(1024)S(1)}) all-reduce(f32[]{:T(128)} %convert_reduce_fusion, f32[2048]{0:T(1024)S(1)} %get-tuple-element.99, f32[2048]{0:T(1024)S(1)} %get-tuple-element.98), channel_id=1, replica_groups=mesh['batch'=8,'rows'=4] {'batch','rows'}, use_global_device_ids=true, to_apply=%region_13.14 | all-reduce | flops 4097 | bytes 32776 | tf_op jit(solution)/shard_map/psum | solution.py:158
  1766.5 40.3 %fusion.8 = f32[4,40,512]{2,1,0:T(8,128)} fusion(f32[4608,512]{1,0:T(8,128)} %bitcast.439, f32[4608,512]{1,0:T(8,128)} %bitcast.440, f32[4608,512]{1,0:T(8,128)} %bitcast.441, f32[4608,512]{1,0:T(8,128)} %bitcast.442, f32[1,4,40,18432]{3,2,1,0:T(8,128)} %copy-done.81), kind=kOutput, calls=%fused_computation.10 | convolution fusion | flops 18147704832 | bytes 49872896 | tf_op jit(solution)/shard_map/dot_general | solution.py:24
  1814.8 40.4 %all-reduce.15 = (f32[512]{0:T(512)S(1)}, f32[512]{0:T(512)S(1)}) all-reduce(f32[512]{0:T(512)S(1)} %get-tuple-element.105, f32[512]{0:T(512)S(1)} %get-tuple-element.104), channel_id=1, replica_groups=mesh['batch'=8,'rows'=4] {'batch','rows'}, use_global_device_ids=true, to_apply=%region_23.24 | all-reduce | flops 1024 | bytes 8192 | tf_op jit(solution)/shard_map/psum | solution.py:88
  1890.0 37.4 all-reduce.14
  1986.2 35.3 convolution_bitcast_fusion
  2021.5 26.1 fusion.259
  2072.9 115.3 %reduce-scatter.31.cloned.1.call-done = f32[576,512]{1,0:T(8,128)} async-done(((f32[4608,512]{1,0:T(8,128)}), f32[576,512]{1,0:T(8,128)}) %reduce-scatter.31.cloned.1.call-update) | async-done | bytes 1179664 | tf_op jit(solution)/shard_map/reduce_scatter | solution.py:326
  2188.3 166.0 %reduce-scatter.33.cloned.1.call-done = f32[576,512]{1,0:T(8,128)} async-done(((f32[4608,512]{1,0:T(8,128)}), f32[576,512]{1,0:T(8,128)}) %reduce-scatter.33.cloned.1.call-update) | async-done | bytes 1179664 | tf_op jit(solution)/shard_map/reduce_scatter | solution.py:327
  2354.3 165.8 %reduce-scatter.35.cloned.1.call-done = f32[576,512]{1,0:T(8,128)} async-done(((f32[4608,512]{1,0:T(8,128)}), f32[576,512]{1,0:T(8,128)}) %reduce-scatter.35.cloned.1.call-update) | async-done | bytes 1179664 | tf_op jit(solution)/shard_map/reduce_scatter | solution.py:328
  2520.1 166.2 %reduce-scatter.37.cloned.1.call-done = f32[576,512]{1,0:T(8,128)} async-done(((f32[4608,512]{1,0:T(8,128)}), f32[576,512]{1,0:T(8,128)}) %reduce-scatter.37.cloned.1.call-update) | async-done | bytes 1179664 | tf_op jit(solution)/shard_map/reduce_scatter | solution.py:329
  2686.3 166.0 %reduce-scatter.23.cloned.1.call-done = f32[576,512]{1,0:T(8,128)} async-done(((f32[4608,512]{1,0:T(8,128)}), f32[576,512]{1,0:T(8,128)}) %reduce-scatter.23.cloned.1.call-update) | async-done | bytes 1179664 | tf_op jit(solution)/shard_map/reduce_scatter | solution.py:318
  2852.4 166.2 %reduce-scatter.25.cloned.1.call-done = f32[576,512]{1,0:T(8,128)} async-done(((f32[4608,512]{1,0:T(8,128)}), f32[576,512]{1,0:T(8,128)}) %reduce-scatter.25.cloned.1.call-update) | async-done | bytes 1179664 | tf_op jit(solution)/shard_map/reduce_scatter | solution.py:319
  3018.6 166.0 %reduce-scatter.27.cloned.1.call-done = f32[576,512]{1,0:T(8,128)} async-done(((f32[4608,512]{1,0:T(8,128)}), f32[576,512]{1,0:T(8,128)}) %reduce-scatter.27.cloned.1.call-update) | async-done | bytes 1179664 | tf_op jit(solution)/shard_map/reduce_scatter | solution.py:322
  3184.6 166.0 %reduce-scatter.29.cloned.1.call-done = f32[576,512]{1,0:T(8,128)} async-done(((f32[4608,512]{1,0:T(8,128)}), f32[576,512]{1,0:T(8,128)}) %reduce-scatter.29.cloned.1.call-update) | async-done | bytes 1179664 | tf_op jit(solution)/shard_map/reduce_scatter | solution.py:325
  3350.6 166.0 %reduce-scatter.19.cloned.1.call-done = f32[576,512]{1,0:T(8,128)} async-done(((f32[4608,512]{1,0:T(8,128)}), f32[576,512]{1,0:T(8,128)}) %reduce-scatter.19.cloned.1.call-update) | async-done | bytes 1179664 | tf_op jit(solution)/shard_map/reduce_scatter | solution.py:316
  3520.6 58.2 %reduce-scatter.43.cloned.1.call-done = f32[64,40]{1,0:T(8,128)} async-done(((f32[512,40]{1,0:T(8,128)}), f32[64,40]{1,0:T(8,128)}) %reduce-scatter.43.cloned.1.call-update) | async-done | bytes 10256
  3602.8 194.9 %all-reduce.23.cloned.1.call-done = (f32[256,512]{0,1:T(8,128)}, f32[576,512]{1,0:T(8,128)}, f32[64,2048]{1,0:T(8,128)}, f32[576,512]{1,0:T(8,128)}, f32[576,512...) async-done(((f32[256,512]{0,1:T(8,128)}, ...) | async-done | bytes 11927568 | tf_op jit(solution)/shard_map/psum | solution.py:334
  (525 shorter events, 600.2 us)
Async XLA Ops:
  7.2 77.6 %all-gather.17.cloned.1.call-start = ((), (), s32[]{:S(2)}) async-start(), calls=%async_computation.14 | async-start | bytes 4718592 | tf_op jit(solution)/shard_map/all_gather | solution.py:123
  7.9 220.1 %all-gather.19.cloned.1.call-start = ((), (), s32[]{:S(2)}) async-start(), calls=%async_computation.15 | async-start | bytes 10616832 | tf_op jit(solution)/shard_map/all_gather | solution.py:125
  8.7 293.2 %all-gather.21.cloned.1.call-start = ((), (), s32[]{:S(2)}) async-start(), calls=%async_computation.16 | async-start | bytes 4718592 | tf_op jit(solution)/shard_map/all_gather | solution.py:127
  9.4 431.6 %all-gather.29.cloned.1.call-start = ((), (), s32[]{:S(2)}) async-start(), calls=%async_computation.20 | async-start | bytes 10616832 | tf_op jit(solution)/shard_map/all_gather | solution.py:132
  10.0 569.3 %all-gather.27.cloned.1.call-start = ((), (), s32[]{:S(2)}) async-start(), calls=%async_computation.19 | async-start | bytes 10616832 | tf_op jit(solution)/shard_map/all_gather | solution.py:131
  10.6 707.0 %all-gather.25.cloned.1.call-start = ((), (), s32[]{:S(2)}) async-start(), calls=%async_computation.18 | async-start | bytes 10616832 | tf_op jit(solution)/shard_map/all_gather | solution.py:130
  11.2 844.9 %all-gather.23.cloned.1.call-start = ((), (), s32[]{:S(2)}) async-start(), calls=%async_computation.17 | async-start | bytes 10616832 | tf_op jit(solution)/shard_map/all_gather | solution.py:129
  11.9 982.6 %all-gather.41.cloned.1.call-start = ((), (), s32[]{:S(2)}) async-start(), calls=%async_computation.26 | async-start | bytes 10616832 | tf_op jit(solution)/shard_map/all_gather | solution.py:136
  12.7 1120.3 %all-gather.39.cloned.1.call-start = ((), (), s32[]{:S(2)}) async-start(), calls=%async_computation.25 | async-start | bytes 10616832 | tf_op jit(solution)/shard_map/all_gather | solution.py:134
  13.4 1257.9 %all-gather.35.cloned.1.call-start = ((), (), s32[]{:S(2)}) async-start(), calls=%async_computation.23 | async-start | bytes 10616832 | tf_op jit(solution)/shard_map/all_gather | solution.py:135
  14.0 1395.8 %all-gather.33.cloned.1.call-start = ((), (), s32[]{:S(2)}) async-start(), calls=%async_computation.22 | async-start | bytes 10616832 | tf_op jit(solution)/shard_map/all_gather | solution.py:133
  14.8 1560.2 %all-gather.37.cloned.1.call-start = ((), (), s32[]{:S(2)}) async-start(), calls=%async_computation.24 | async-start | bytes 1179648 | tf_op jit(solution)/shard_map/all_gather | solution.py:138
  15.3 1562.4 %all-gather.31.cloned.1.call-start = ((), (), s32[]{:S(2)}) async-start(), calls=%async_computation.21 | async-start | bytes 1179648 | tf_op jit(solution)/shard_map/all_gather | solution.py:137
  16.1 2056.8 %reduce-scatter.39.cloned.1.call-start = ((), (), s32[]{:S(2)}) async-start(), calls=%async_computation.38 | async-start | bytes 1179648 | tf_op jit(solution)/shard_map/reduce_scatter | solution.py:330
  277.3 1260.8 %collective-permute-start.3 = (f32[1,1,40,512]{3,2,1,0:T(8,128)S(1)}, f32[1,1,40,512]{3,2,1,0:T(8,128)S(1)}, u32[]{:S(2)}, u32[]{:S(2)}) collective-permute-start(f32[1,1,40,512]{3,2,1,0:T(8,128)S(1)} %get-tuple-element.177), channel_id=1, source_target_pairs={{1,0},{2,1},{3,2},{5,4},{6,5},{7,6},{9,8},{10,9},{11,10},{13,12},{... | collective-permute-start | bytes 245768 | tf_op jit(solution)/shard_map/ppermute | solution.py:18
  279.9 1258.3 %collective-permute-start.2 = (f32[1,1,40,512]{3,2,1,0:T(8,128)S(1)}, f32[1,1,40,512]{3,2,1,0:T(8,128)S(1)}, u32[]{:S(2)}, u32[]{:S(2)}) collective-permute-start(f32[1,1,40,512]{3,2,1,0:T(8,128)S(1)} %get-tuple-element.176), channel_id=1, source_target_pairs={{0,1},{1,2},{2,3},{4,5},{5,6},{6,7},{8,9},{9,10},{10,11},{12,13},{... | collective-permute-start | bytes 245768 | tf_op jit(solution)/shard_map/ppermute | solution.py:17
  307.7 1272.9 %collective-permute-start.7 = (f32[1,2,40,512]{3,2,1,0:T(8,128)}, f32[1,2,40,512]{3,2,1,0:T(8,128)S(1)}, u32[]{:S(2)}, u32[]{:S(2)}) collective-permute-start(f32[1,2,40,512]{3,2,1,0:T(8,128)} %get-tuple-element.175), channel_id=1, source_target_pairs={{1,0},{2,1},{3,2},{5,4},{6,5},{7,6},{9,8},{10,9},{11,10},{13,12},{... | collective-permute-start | bytes 491528 | tf_op jit(solution)/shard_map/ppermute | solution.py:18
  311.5 1269.1 %collective-permute-start.6 = (f32[1,2,40,512]{3,2,1,0:T(8,128)}, f32[1,2,40,512]{3,2,1,0:T(8,128)}, u32[]{:S(2)}, u32[]{:S(2)}) collective-permute-start(f32[1,2,40,512]{3,2,1,0:T(8,128)} %get-tuple-element.174), channel_id=1, source_target_pairs={{0,1},{1,2},{2,3},{4,5},{5,6},{6,7},{8,9},{9,10},{10,11},{12,13},{... | collective-permute-start | bytes 491528 | tf_op jit(solution)/shard_map/ppermute | solution.py:17
  1673.7 399.2 %reduce-scatter.41.cloned.1.call-start = ((), (), s32[]{:S(2)}) async-start(), calls=%async_computation.39 | async-start | bytes 1179648 | tf_op jit(solution)/shard_map/reduce_scatter | solution.py:331
  1703.3 369.6 %reduce-scatter.21.cloned.1.call-start = ((), (), s32[]{:S(2)}) async-start(), calls=%async_computation.29 | async-start | bytes 4718592 | tf_op jit(solution)/shard_map/reduce_scatter | solution.py:317
  1758.7 314.2 %reduce-scatter.17.cloned.1.call-start = ((), (), s32[]{:S(2)}) async-start(), calls=%async_computation.27 | async-start | bytes 4718592 | tf_op jit(solution)/shard_map/reduce_scatter | solution.py:315
  1932.6 255.6 %reduce-scatter.31.cloned.1.call-start = ((), (), s32[]{:S(2)}) async-start(), calls=%async_computation.34 | async-start | bytes 10616832 | tf_op jit(solution)/shard_map/reduce_scatter | solution.py:326
  1958.9 395.4 %reduce-scatter.33.cloned.1.call-start = ((), (), s32[]{:S(2)}) async-start(), calls=%async_computation.35 | async-start | bytes 10616832 | tf_op jit(solution)/shard_map/reduce_scatter | solution.py:327
  1984.3 535.9 %reduce-scatter.35.cloned.1.call-start = ((), (), s32[]{:S(2)}) async-start(), calls=%async_computation.36 | async-start | bytes 10616832 | tf_op jit(solution)/shard_map/reduce_scatter | solution.py:328
  1984.9 701.5 %reduce-scatter.37.cloned.1.call-start = ((), (), s32[]{:S(2)}) async-start(), calls=%async_computation.37 | async-start | bytes 10616832 | tf_op jit(solution)/shard_map/reduce_scatter | solution.py:329
  1985.6 866.8 %reduce-scatter.23.cloned.1.call-start = ((), (), s32[]{:S(2)}) async-start(), calls=%async_computation.30 | async-start | bytes 10616832 | tf_op jit(solution)/shard_map/reduce_scatter | solution.py:318
  2047.6 970.9 %reduce-scatter.25.cloned.1.call-start = ((), (), s32[]{:S(2)}) async-start(), calls=%async_computation.31 | async-start | bytes 10616832 | tf_op jit(solution)/shard_map/reduce_scatter | solution.py:319
  2048.4 1136.2 %reduce-scatter.27.cloned.1.call-start = ((), (), s32[]{:S(2)}) async-start(), calls=%async_computation.32 | async-start | bytes 10616832 | tf_op jit(solution)/shard_map/reduce_scatter | solution.py:322
  2049.0 1301.7 %reduce-scatter.29.cloned.1.call-start = ((), (), s32[]{:S(2)}) async-start(), calls=%async_computation.33 | async-start | bytes 10616832 | tf_op jit(solution)/shard_map/reduce_scatter | solution.py:325
  2049.7 1467.0 %reduce-scatter.19.cloned.1.call-start = ((), (), s32[]{:S(2)}) async-start(), calls=%async_computation.28 | async-start | bytes 10616832 | tf_op jit(solution)/shard_map/reduce_scatter | solution.py:316
  2069.3 1509.5 %reduce-scatter.43.cloned.1.call-start = ((), (), s32[]{:S(2)}) async-start(), calls=%async_computation.40 | async-start | bytes 294912
  2072.8 1724.9 %all-reduce.23.cloned.1.call-start = ((), (), s32[]{:S(2)}) async-start(), calls=%async_computation.41 | async-start | bytes 23855104 | tf_op jit(solution)/shard_map/psum | solution.py:334
  (105 other events, 2111.9 us)
Sparse Core Ops, SparseCore 0:
  10.2 74.5 all-gather.16
  86.9 141.0 all-gather.18
  230.1 71.6 all-gather.20
  303.9 137.1 all-gather.28
  443.1 136.2 all-gather.26
  581.4 136.2 all-gather.24
  719.8 136.2 all-gather.22
  858.3 136.2 all-gather.40
  996.8 136.2 all-gather.38
  1135.1 136.2 all-gather.34
  1273.5 136.2 all-gather.32
  1411.8 37.7 all-gather.36
  1451.8 38.9 all-gather.30
  1673.7 61.6 reduce-scatter.38
  1739.7 62.5 reduce-scatter.40
  1805.8 90.3 reduce-scatter.20
  1932.8 88.9 reduce-scatter.16
  2025.2 163.0 reduce-scatter.30
  2191.9 162.3 reduce-scatter.32
  2357.7 162.3 reduce-scatter.34
  2523.7 162.5 reduce-scatter.36
  2689.9 162.4 reduce-scatter.22
  2856.0 162.5 reduce-scatter.24
  3022.0 162.5 reduce-scatter.26
  3188.2 162.3 reduce-scatter.28
  3354.1 162.5 reduce-scatter.18
  3520.4 58.3 reduce-scatter.42
  3582.7 214.9 all-reduce.22
where the time goes:
time: 3830 us; the launch traced here: 3820 us
  waiting for transfers between devices  2830 us (74%)
  blocking collectives  331 us (9%)
  matrix products  311 us (8%)
  local copies, waits for them, and re-layouts  245 us (6%)
  starting transfers between devices  49.9 us (1%)
    psum x1, waiting for transfers between devices, shards(): lax.psum((part_grads[0], part_grads[1], part_grads[2], part_grads[3], par...  195 us
    dot_general x16, matrix products, matmul(): return jnp.dot(values, weight, precision=PRECISE)  184 us
    reduce_scatter x1, waiting for transfers between devices, shards(): lax.psum_scatter(segment_pair_grad[nine:], 'batch', scatter_dimension=0,...  166 us
    reduce_scatter x1, waiting for transfers between devices, shards(): lax.psum_scatter(heads_grad[:, chan_mid:2 * chan_mid], 'batch', scatter_d...  166 us
    reduce_scatter x1, waiting for transfers between devices, shards(): lax.psum_scatter(dilate_grad, 'batch', scatter_dimension=0, tiled=True)  166 us
    reduce_scatter x1, waiting for transfers between devices, shards(): lax.psum_scatter(heads_grad[:, :chan_mid], 'batch', scatter_dimension=0,...  166 us
    reduce_scatter x1, waiting for transfers between devices, shards(): lax.psum_scatter(heads_grad[:, 2 * chan_mid:3 * chan_mid], 'batch', scatt...  166 us
    reduce_scatter x1, waiting for transfers between devices, shards(): lax.psum_scatter(segment_pair_grad[:nine], 'batch', scatter_dimension=0,...  166 us
  transfers between devices with their start and end apart: 42, of which 23 were waited for; matrix products, arithmetic and copies ran while one was open for 14% of the time, Pallas kernels for 0%

commit v1 on v0

v1 whole, which is shorter than its diff:
```python
import math

import jax
import jax.numpy as jnp
from jax import lax
from jax.experimental import pallas as pl
from jax.experimental.pallas import tpu as pltpu
from jax.sharding import PartitionSpec as P

EPSILON = 1e-05
EXACT = lax.Precision.HIGHEST
FINE = lax.Precision.HIGH
LONGEST_RING = 8
LANES = 128


def product(left, right, left_dim, right_dim, precision=FINE):
    return lax.dot_general(
        left,
        right,
        (((left_dim,), (right_dim,)), ((), ())),
        precision=precision,
        preferred_element_type=jnp.float32,
    )


def halves(values):
    high = values.astype(jnp.bfloat16)
    return high, (values - high.astype(jnp.float32)).astype(jnp.bfloat16)


def three_pass(left, right, left_dim, right_dim):
    dims = (((left_dim,), (right_dim,)), ((), ()))

    def one(a, b):
        return lax.dot_general(a, b, dims, preferred_element_type=jnp.float32)

    return one(left[0], right[0]) + (one(left[0], right[1]) + one(left[1], right[0]))


def frame(image_ref, framed, dilation):
    height, breadth, depth = image_ref.shape
    edge = jnp.zeros((3, dilation, breadth, depth), jnp.float32)
    framed[:, :dilation] = edge
    framed[:, dilation + height :] = edge
    image = image_ref[...]
    side = jnp.zeros((height, dilation, depth), jnp.float32)
    inner = slice(dilation, dilation + height)
    framed[1, inner] = image
    framed[0, inner, dilation:, :] = image[:, : breadth - dilation]
    framed[0, inner, :dilation, :] = side
    framed[2, inner, : breadth - dilation, :] = image[:, dilation:]
    framed[2, inner, breadth - dilation :, :] = side


def shifted(framed, tap, height, dilation):
    block = framed[tap % 3, pl.ds((tap // 3) * dilation, height)]
    return block.reshape(height * block.shape[1], block.shape[2])


def conv_kernel(dilation, image_ref, weight_ref, out_ref, framed):
    tap = pl.program_id(0)

    @pl.when(tap == 0)
    def _():
        frame(image_ref, framed, dilation)
        out_ref[...] = jnp.zeros_like(out_ref)

    moved = halves(shifted(framed, tap, image_ref.shape[0], dilation))
    out_ref[...] += three_pass(moved, halves(weight_ref[...]), 1, 0)


def conv_back_kernel(dilation, image_ref, weight_ref, out_ref, framed):
    tap = pl.program_id(0)

    @pl.when(tap == 0)
    def _():
        frame(image_ref, framed, dilation)
        out_ref[...] = jnp.zeros_like(out_ref)

    moved = halves(shifted(framed, 8 - tap, image_ref.shape[0], dilation))
    out_ref[...] += three_pass(moved, halves(weight_ref[...]), 1, 1)


def conv_grad_kernel(dilation, input_ref, grad_ref, out_ref, framed, high, low):
    tap = pl.program_id(0)

    @pl.when(tap == 0)
    def _():
        frame(grad_ref, framed, dilation)
        high[...], low[...] = halves(jnp.transpose(input_ref[...]))

    moved = halves(shifted(framed, 8 - tap, grad_ref.shape[0], dilation))
    out_ref[...] = three_pass((high[...], low[...]), moved, 1, 0)


def source_rows(weight, start, count):
    return jnp.concatenate(
        [weight[:, k].reshape(-1, weight.shape[-1]) for k in range(start, start + count)], axis=0
    )


def notes_kernel(image_ref, weight_ref, out_ref, framed, total):
    tap = pl.program_id(0)

    @pl.when(tap == 0)
    def _():
        frame(image_ref, framed, 1)
        total[...] = jnp.zeros_like(total)

    moved = shifted(framed, tap, image_ref.shape[0], 1)
    weight = weight_ref[...]
    lanes = moved.shape[1] // 2
    for note in range(2):
        total[note] += three_pass(
            halves(moved[:, note * lanes : (note + 1) * lanes]),
            halves(source_rows(weight, 2 * note, 2)),
            1,
            0,
        )

    @pl.when(tap == 8)
    def _():
        nrows, _, quarter, mid = out_ref.shape
        for note in range(2):
            out_ref[:, note] = total[note].reshape(nrows, quarter, mid)


def notes_back_kernel(notes_ref, weight_ref, direct_ref, out_ref, framed):
    note, tap = pl.program_id(0), pl.program_id(1)

    @pl.when(tap == 0)
    def _():
        frame(notes_ref.at[0], framed, 1)
        part = direct_ref.shape[-1]
        out_ref[:, :part] = direct_ref[0]
        out_ref[:, part:] = jnp.zeros_like(direct_ref[0])

    moved = halves(shifted(framed, 8 - tap, notes_ref.shape[1], 1))
    out_ref[...] += three_pass(moved, halves(source_rows(weight_ref[...], 0, 2)), 1, 1)


def notes_grad_kernel(input_ref, notes_ref, out_ref, framed, high, low):
    note, tap = pl.program_id(0), pl.program_id(1)

    @pl.when(tap == 0)
    def _():
        frame(notes_ref.at[0], framed, 1)
        high[...], low[...] = halves(jnp.transpose(input_ref[...]))

    moved = halves(shifted(framed, 8 - tap, notes_ref.shape[1], 1))
    grad = three_pass((high[...], low[...]), moved, 1, 0)
    runs, _, grain, mid = out_ref.shape
    part = grad.shape[0] // 2
    for k in range(2):
        out_ref[:, k] = grad[k * part : (k + 1) * part].reshape(runs, grain, mid)


def regroup(array, run):
    runs, sources, grain, mid = array.shape
    if grain == run:
        return array
    if run > grain:
        lists = array.reshape(-1, run // grain, sources, grain, mid)
        return jnp.transpose(lists, (0, 2, 1, 3, 4)).reshape(-1, sources, run, mid)
    parts = array.reshape(runs, sources, grain // run, run, mid)
    return jnp.transpose(parts, (0, 2, 1, 3, 4)).reshape(-1, sources, run, mid)


VMEM_LIMIT = 40 * 2**20


def kernel_call(body, grid, in_specs, out_specs, out_shape, scratch, flops):
    return pl.pallas_call(
        body,
        grid=grid,
        in_specs=in_specs,
        out_specs=out_specs,
        out_shape=out_shape,
        scratch_shapes=scratch,
        compiler_params=pltpu.CompilerParams(
            dimension_semantics=("arbitrary",) * len(grid), vmem_limit_bytes=VMEM_LIMIT
        ),
        cost_estimate=pl.CostEstimate(flops=3 * flops, bytes_accessed=12 * 2**20, transcendentals=0),
    )


def framed_scratch(image, dilation):
    height, breadth, depth = image
    return pltpu.VMEM((3, height + 2 * dilation, breadth, depth), jnp.float32)


def whole_spec(shape):
    return pl.BlockSpec(shape, lambda *_: (0,) * len(shape))


def conv(image, weight, dilation, backward=False):
    height, breadth, depth = image.shape
    rows, cols = weight.shape[0] // 9, weight.shape[1]
    wide = rows if backward else cols
    body = conv_back_kernel if backward else conv_kernel

    def run(image_ref, weight_ref, out_ref, framed):
        body(dilation, image_ref, weight_ref, out_ref, framed)

    shape = (height * breadth, wide)
    return kernel_call(
        run,
        (9,),
        [whole_spec(image.shape), pl.BlockSpec((rows, cols), lambda tap: (tap, 0))],
        whole_spec(shape),
        jax.ShapeDtypeStruct(shape, jnp.float32),
        [framed_scratch(image.shape, dilation)],
        2 * 9 * height * breadth * rows * cols,
    )(image, weight)


def conv_grad(flat_input, image_grad, dilation):
    pixels, depth = flat_input.shape
    cols = image_grad.shape[2]

    def run(*refs):
        conv_grad_kernel(dilation, *refs)

    return kernel_call(
        run,
        (9,),
        [whole_spec(flat_input.shape), whole_spec(image_grad.shape)],
        pl.BlockSpec((depth, cols), lambda tap: (tap, 0)),
        jax.ShapeDtypeStruct((9 * depth, cols), jnp.float32),
        [framed_scratch(image_grad.shape, dilation)]
        + [pltpu.VMEM((depth, pixels), jnp.bfloat16)] * 2,
        2 * 9 * pixels * depth * cols,
    )(flat_input, image_grad)


def notes_forward(image, weight, nrows):
    height, breadth, depth = image.shape
    runs, mid = weight.shape[0] // 9, weight.shape[3]
    pixels = height * breadth
    shape = (nrows, 2, pixels // nrows, mid)
    return kernel_call(
        notes_kernel,
        (9,),
        [
            whole_spec(image.shape),
            pl.BlockSpec((runs,) + weight.shape[1:], lambda tap: (tap, 0, 0, 0)),
        ],
        whole_spec(shape),
        jax.ShapeDtypeStruct(shape, jnp.float32),
        [framed_scratch(image.shape, 1), pltpu.VMEM((2, pixels, mid), jnp.float32)],
        2 * 9 * pixels * depth * mid,
    )(image, weight)


def notes_back(notes, weight, direct):
    _, height, breadth, mid = notes.shape
    _, pixels, part = direct.shape
    runs, _, grain, _ = weight.shape
    runs = runs // 9
    return kernel_call(
        notes_back_kernel,
        (2, 9),
        [
            pl.BlockSpec((1, height, breadth, mid), lambda note, tap: (note, 0, 0, 0)),
            pl.BlockSpec((runs, 2, grain, mid), lambda note, tap: (tap, note, 0, 0)),
            pl.BlockSpec((1, pixels, part), lambda note, tap: (note, 0, 0)),
        ],
        pl.BlockSpec((pixels, 2 * part), lambda note, tap: (0, note)),
        jax.ShapeDtypeStruct((pixels, 4 * part), jnp.float32),
        [framed_scratch((height, breadth, mid), 1)],
        2 * 9 * pixels * 4 * part * mid,
    )(notes, weight, direct)


def notes_grad(flat_input, notes, grain):
    pixels, depth = flat_input.shape
    _, height, breadth, mid = notes.shape
    part = depth // 4
    runs = part // grain
    return kernel_call(
        notes_grad_kernel,
        (2, 9),
        [
            pl.BlockSpec((pixels, 2 * part), lambda note, tap: (0, note)),
            pl.BlockSpec((1, height, breadth, mid), lambda note, tap: (note, 0, 0, 0)),
        ],
        pl.BlockSpec((runs, 2, grain, mid), lambda note, tap: (tap, note, 0, 0)),
        jax.ShapeDtypeStruct((9 * runs, 4, grain, mid), jnp.float32),
        [framed_scratch((height, breadth, mid), 1)]
        + [pltpu.VMEM((2 * part, pixels), jnp.bfloat16)] * 2,
        2 * 9 * pixels * depth * mid,
    )(flat_input, notes)


def silu_grad(values):
    gate_val = jax.nn.sigmoid(values)
    return gate_val * (1.0 + values * (1.0 - gate_val))


def swap_rows(block, mask):
    size = lax.axis_size("rows")
    return lax.ppermute(block, "rows", [(i, i ^ mask) for i in range(size)])


def in_order(blocks, row):
    count = len(blocks)
    if count == 1:
        return blocks
    half = count // 2
    near = in_order(blocks[:half], row)
    far = in_order(blocks[half:], row)
    upper = (row & half) != 0
    first = [jnp.where(upper, f, n) for n, f in zip(near, far)]
    second = [jnp.where(upper, n, f) for n, f in zip(near, far)]
    return first + second


def gather_rows(block, row):
    size = lax.axis_size("rows")
    blocks = {0: block}
    mask = size // 2
    while mask:
        for key in sorted(blocks):
            blocks[key | mask] = swap_rows(blocks[key], mask)
        mask //= 2
    return in_order([blocks[key] for key in range(size)], row)


def scatter_rows(blocks, row):
    size = lax.axis_size("rows")
    mask = 1
    rest = blocks
    tail = blocks.shape[1:]
    while mask < size:
        pairs = rest.reshape((-1, 2) + tail)
        bit = (row // mask) % 2
        keep = lax.dynamic_index_in_dim(pairs, bit, 1, keepdims=False)
        give = lax.dynamic_index_in_dim(pairs, 1 - bit, 1, keepdims=False)
        rest = keep + swap_rows(give, mask)
        mask *= 2
    return rest.reshape(tail)


def exchange_rows(blocks, row):
    size = lax.axis_size("rows")
    got = []
    for mask in range(size):
        block = lax.dynamic_index_in_dim(blocks, row ^ mask, 0, keepdims=False)
        got.append(swap_rows(block, mask) if mask else block)
    return in_order(got, row)


def sum_batch(values):
    size = lax.axis_size("batch")
    if size & (size - 1):
        return lax.psum(values, "batch")
    mask = 1
    while mask < size:
        values = values + lax.ppermute(values, "batch", [(i, i ^ mask) for i in range(size)])
        mask *= 2
    return values


class Ring:
    def __init__(self, batch):
        size = lax.axis_size("batch")
        self.batch, self.size = batch, size
        self.order = list(range(0, size, 2)) + [i for i in reversed(range(size)) if i % 2]
        self.place = {b: p for p, b in enumerate(self.order)}
        self.up = [(self.order[p], self.order[(p + 1) % size]) for p in range(size)]
        self.down = [(b, a) for a, b in self.up]
        table = [[self.order[(self.place[b] + k) % size] for k in range(size)] for b in range(size)]
        self.row = jnp.array(table, jnp.int32)[batch]

    def at(self, offset):
        return self.row[offset % self.size]

    def steps(self, longer_up):
        more = self.size // 2
        less = self.size - 1 - more
        return (more, less) if longer_up else (less, more)

    def gather(self, block, longer_up):
        if self.size > LONGEST_RING:
            return lax.all_gather(block, "batch", axis=0, tiled=False)
        whole = jnp.zeros((self.size,) + block.shape, block.dtype)
        whole = lax.dynamic_update_index_in_dim(whole, block, self.batch, 0)
        ups, downs = self.steps(longer_up)
        rising = falling = block
        for k in range(1, max(ups, downs) + 1):
            if k <= ups:
                rising = lax.ppermute(rising, "batch", self.up)
                whole = lax.dynamic_update_index_in_dim(whole, rising, self.at(-k), 0)
            if k <= downs:
                falling = lax.ppermute(falling, "batch", self.down)
                whole = lax.dynamic_update_index_in_dim(whole, falling, self.at(k), 0)
        return whole

    def scatter(self, blocks, longer_up):
        if self.size > LONGEST_RING:
            return lax.psum_scatter(blocks, "batch", scatter_dimension=0, tiled=False)

        def own(offset):
            return lax.dynamic_index_in_dim(blocks, self.at(offset), 0, keepdims=False)

        ups, downs = self.steps(longer_up)
        rising, falling = own(ups), own(-downs)
        for k in range(max(ups, downs)):
            if k < ups:
                rising = lax.ppermute(rising, "batch", self.up)
                if k < ups - 1:
                    rising = rising + own(ups - 1 - k)
            if k < downs:
                falling = lax.ppermute(falling, "batch", self.down)
                if k < downs - 1:
                    falling = falling + own(-(downs - 1 - k))
        return own(0) + rising + falling


def norm_forward(values, gain, bias, ring_sum, count):
    total = ring_sum(jnp.stack([jnp.sum(values, axis=0), jnp.sum(values * values, axis=0)]))
    center = total[0] / count
    inverse = lax.rsqrt(total[1] / count - center * center + EPSILON)
    hat = (values - center) * inverse
    return hat, hat * gain + bias, inverse


def norm_backward(d_out, hat, inverse, gain, count):
    sums = sum_batch(jnp.stack([jnp.sum(d_out * hat, axis=0), jnp.sum(d_out, axis=0)]))
    d_values = inverse * gain * (d_out - sums[1] / count - hat * (sums[0] / count))
    return d_values, sums


def shards(
    features,
    reduce_weight,
    reduce_norm,
    dilate_weight,
    dilate_norm,
    expand_weight,
    expand_norm,
    depth_head,
    segment_head,
    normal_head,
    contour_head,
    depth_message,
    segment_message,
    normal_message,
    contour_message,
    depth_gate,
    segment_gate,
    classifier,
    depth_valid,
    labels,
    block_cotangent,
    depth_cotangent,
):
    row, batch = lax.axis_index("rows"), lax.axis_index("batch")
    nrows, nbatch = lax.axis_size("rows"), lax.axis_size("batch")
    ring = Ring(batch)
    _, local_height, breadth, wide = features.shape
    mid = reduce_weight.shape[1]
    part = mid // nrows
    quarter = local_height * breadth
    height = local_height * nrows
    pixels = quarter * nrows
    count = float(pixels * nbatch)
    factor = count ** (-0.5)
    classes = classifier.shape[1]
    held = dilate_weight.shape[0]
    grain = math.gcd(held, mid) // nrows
    groups = held // (nrows * grain)
    wide_held = wide // nbatch
    wide_part = wide_held // nrows
    mid_held = mid // nbatch

    def row_slice(array, dim):
        size = array.shape[dim] // nrows
        return lax.dynamic_slice_in_dim(array, row * size, size, dim)

    channel = jnp.arange(mid)
    slot = jnp.arange(part)
    mine = (slot // grain) * (nrows * grain) + row * grain + slot % grain
    pick = (channel[:, None] == mine[None, :]).astype(jnp.float32)
    split = jnp.arange(mid)
    natural = ((split % part) // grain) * (nrows * grain) + (split // part) * grain + split % grain
    mix = (natural[:, None] == channel[None, :]).astype(jnp.float32)

    def to_narrow(array):
        return jnp.concatenate(
            [array[:, i * part : (i + 1) * part] for i in range(nrows)], axis=0
        )

    def from_narrow(array):
        size = array.shape[1] // nrows
        return jnp.concatenate([array[:, i * size : (i + 1) * size] for i in range(nrows)], axis=2)

    tiny_width = max(mid_held, wide_part)

    def tiny(array):
        return jnp.pad(array, ((0, 0), (0, tiny_width - array.shape[1])))

    heads_mine = jnp.concatenate(
        [
            product(head, pick, 1, 0, EXACT)
            for head in (segment_head, normal_head, depth_head, contour_head)
        ],
        axis=1,
    )
    heads_full = lax.all_gather(heads_mine, "batch", axis=0, tiled=True)

    def message_runs(array):
        runs = array.reshape(groups, nrows, grain, mid)
        return lax.dynamic_index_in_dim(runs, row, 1, keepdims=True)

    messages_mine = jnp.concatenate(
        [
            message_runs(array)
            for array in (depth_message, normal_message, segment_message, contour_message)
        ],
        axis=1,
    )
    messages_full = lax.all_gather(
        messages_mine.reshape(held, mid), "batch", axis=0, tiled=True
    ).reshape(nbatch * groups, 4, grain, mid)
    run = grain if grain % 8 == 0 else part
    messages_full = regroup(messages_full, run)

    expand_norm_mine = lax.dynamic_index_in_dim(
        expand_norm.reshape(2, nrows, wide_part), row, 1, keepdims=False
    )
    params = jnp.concatenate([tiny(reduce_norm), tiny(dilate_norm), tiny(expand_norm_mine)], axis=0)
    params = jnp.pad(params, ((0, 2), (0, part - tiny_width)))
    expand_mine = lax.dynamic_index_in_dim(
        expand_weight.reshape(mid_held, nbatch, nrows, wide_part), row, 2, keepdims=False
    ).reshape(mid_held, nbatch * wide_part)
    class_lanes = -(-classes // part) * part
    pieces = {
        "reduce": to_narrow(row_slice(reduce_weight, 0)),
        "params": params,
        "dilate": row_slice(dilate_weight, 1),
        "expand": to_narrow(expand_mine),
        "depth_gate": to_narrow(depth_gate),
        "segment_gate": to_narrow(segment_gate),
        "classifier": jnp.concatenate(
            [
                jnp.pad(classifier, ((0, 0), (0, class_lanes - classes)))[:, i : i + part]
                for i in range(0, class_lanes, part)
            ],
            axis=0,
        ),
    }
    first_all = ring.gather(jnp.concatenate(list(pieces.values()), axis=0), True)
    starts, start = {}, 0
    for name, piece in pieces.items():
        starts[name] = (start, start + piece.shape[0])
        start += piece.shape[0]

    def piece_of(name):
        return first_all[:, starts[name][0] : starts[name][1]]

    reduce_full = from_narrow(piece_of("reduce")).reshape(nbatch * wide_part, mid)
    params_all = piece_of("params")
    dilate_full = piece_of("dilate").reshape(nbatch * held, part)

    def all_params(pair, size):
        return jnp.transpose(params_all[:, pair : pair + 2, :size], (1, 0, 2)).reshape(2, nbatch * size)

    reduce_gain, reduce_bias = row_slice(all_params(0, mid_held), 1)
    dilate_gain, dilate_bias = row_slice(all_params(2, mid_held), 1)
    expand_gain, expand_bias = all_params(4, wide_part)
    expand_w, depth_gate_w, segment_gate_w = [
        from_narrow(piece_of(name)).reshape(mid, mid)
        for name in ("expand", "depth_gate", "segment_gate")
    ]
    classifier_w = jnp.concatenate(
        [
            piece_of("classifier")[:, i * mid_held : (i + 1) * mid_held]
            for i in range(class_lanes // part)
        ],
        axis=2,
    ).reshape(mid, class_lanes)

    def spread_wide(array):
        blocks = jnp.transpose(array.reshape(quarter, nbatch, nrows, wide_part), (2, 0, 1, 3))
        return jnp.concatenate(
            exchange_rows(blocks.reshape(nrows, quarter, nbatch * wide_part), row), axis=0
        )

    def collect_wide(array):
        blocks = array.reshape(nrows, quarter, nbatch * wide_part)
        got = jnp.stack(exchange_rows(blocks, row))
        got = got.reshape(nrows, quarter, nbatch, wide_part)
        return jnp.transpose(got, (1, 2, 0, 3)).reshape(1, local_height, breadth, wide)

    valid = depth_valid.astype(jnp.float32).reshape(quarter)
    valid_row = jnp.full((1, LANES), jnp.sum(valid))
    mask = 1
    while mask < nrows:
        valid_row = valid_row + swap_rows(valid_row, mask)
        mask *= 2
    valid_total = sum_batch(valid_row)[0, 0]

    features, block_cotangent, _ = lax.optimization_barrier(
        (features, block_cotangent, (heads_mine, messages_mine))
    )
    inputs = spread_wide(features.reshape(quarter, wide))
    cotangent = spread_wide(block_cotangent.reshape(quarter, wide))

    def by_slices(array):
        return jnp.stack([array[:, i * part : (i + 1) * part] for i in range(nrows)])

    pre_reduce = scatter_rows(by_slices(product(inputs, reduce_full, 1, 0)), row)
    hat_one, normed_one, inverse_one = norm_forward(
        pre_reduce, reduce_gain, reduce_bias, sum_batch, count
    )
    mid_in = jnp.concatenate(gather_rows(jax.nn.silu(normed_one), row), axis=1)
    mid_in_image = mid_in.reshape(height, breadth, mid)
    pre_dilate = conv(mid_in_image, dilate_full, 2)
    hat_two, normed_two, inverse_two = norm_forward(
        pre_dilate, dilate_gain, dilate_bias, sum_batch, count
    )
    mid_out = jnp.concatenate(gather_rows(jax.nn.silu(normed_two), row), axis=1)
    feats = conv(mid_out.reshape(height, breadth, mid), heads_full, 1)
    notes = scatter_rows(
        notes_forward(feats.reshape(height, breadth, nrows * part), messages_full, nrows).reshape(
            nrows, 2 * quarter, mid
        ),
        row,
    )
    depth_note, segment_note = notes[:quarter], notes[quarter:]

    pair = jnp.concatenate(
        [
            feats[:, 2 * part : 3 * part].reshape(nrows, quarter, part),
            feats[:, :part].reshape(nrows, quarter, part),
        ],
        axis=1,
    )
    pair_got = jnp.concatenate(exchange_rows(pair, row), axis=1)
    pair_natural = product(pair_got, mix, 1, 0, EXACT)
    depth_feat, segment_feat = pair_natural[:quarter], pair_natural[quarter:]

    depth_open = jax.nn.sigmoid(product(depth_feat, depth_gate_w, 1, 0))
    segment_open = jax.nn.sigmoid(product(segment_feat, segment_gate_w, 1, 0))
    depth_stream = depth_feat + depth_open * depth_note
    segment_stream = segment_feat + segment_open * segment_note
    logits = product(segment_stream, classifier_w, 1, 0)
    lane = jnp.arange(class_lanes, dtype=jnp.int32)
    real = lane < classes
    top = jnp.max(jnp.where(real, logits, -jnp.inf), axis=-1, keepdims=True)
    shifted = jnp.where(real, jnp.exp(logits - top), 0.0)
    onehot = (labels.reshape(quarter, 1) == lane).astype(jnp.float32)
    d_logits = shifted / jnp.sum(shifted, axis=-1, keepdims=True) - onehot

    classifier_grad = product(segment_stream, d_logits, 0, 0)
    d_segment = product(d_logits, classifier_w, 1, 1)
    d_depth = valid[:, None] * depth_cotangent.reshape(quarter, mid) * (count / valid_total)
    d_depth_note = d_depth * depth_open
    d_depth_pre = d_depth_note * depth_note * (1.0 - depth_open)
    d_segment_note = d_segment * segment_open
    d_segment_pre = d_segment_note * segment_note * (1.0 - segment_open)

    d_notes = gather_rows(jnp.stack([d_depth_note, d_segment_note]), row)
    notes_image = jnp.concatenate(d_notes, axis=1).reshape(2, height, breadth, mid)
    message_grads = regroup(notes_grad(feats, notes_image, run), grain).reshape(
        nbatch * held, mid
    )
    message_grads, notes_image = lax.optimization_barrier((message_grads, notes_image))
    message_sums = lax.psum_scatter(message_grads, "batch", scatter_dimension=0, tiled=True)

    depth_gate_grad = product(depth_feat, d_depth_pre, 0, 0)
    segment_gate_grad = product(segment_feat, d_segment_pre, 0, 0)
    classifier_grad = jnp.pad(classifier_grad, ((0, 0), (0, mid - class_lanes)))

    direct = jnp.concatenate(
        [
            d_depth + product(d_depth_pre, depth_gate_w, 1, 1),
            d_segment + product(d_segment_pre, segment_gate_w, 1, 1),
        ],
        axis=0,
    )
    direct_split = product(direct, mix, 1, 1, EXACT)
    direct_got = exchange_rows(by_slices(direct_split), row)
    direct_both = jnp.stack(
        [
            jnp.concatenate([block[quarter:] for block in direct_got], axis=0),
            jnp.concatenate([block[:quarter] for block in direct_got], axis=0),
        ]
    )
    d_feats = notes_back(notes_image, messages_full, direct_both)
    d_feats_image = d_feats.reshape(height, breadth, nrows * part)
    heads_grad = conv_grad(mid_out, d_feats_image, 1).reshape(nbatch, held, nrows * part)

    hat_three, normed_three, inverse_three = norm_forward(
        product(mid_out, expand_w, 1, 0), expand_gain, expand_bias, sum_batch, count
    )
    summed = normed_three + inputs
    block_out = collect_wide(jax.nn.silu(summed))
    d_summed = cotangent * silu_grad(summed)
    d_pre_expand, expand_sums = norm_backward(d_summed, hat_three, inverse_three, expand_gain, count)
    expand_grad = product(mid_out, d_pre_expand, 0, 0).reshape(nbatch, mid_held, mid)

    gate_terms = jnp.stack([depth_gate_grad, segment_gate_grad, classifier_grad])
    gate_terms = jnp.transpose(
        gate_terms.reshape(3, nbatch, nrows, mid_held // nrows, mid), (2, 1, 0, 3, 4)
    )
    gate_sums = scatter_rows(gate_terms, row).reshape(nbatch, 3 * (mid_held // nrows), mid)

    d_mid_part = conv(d_feats_image, heads_full, 1, True) + product(d_pre_expand, expand_w, 1, 1)
    d_mid_out = scatter_rows(by_slices(d_mid_part), row)
    d_pre_dilate, dilate_sums = norm_backward(
        d_mid_out * silu_grad(normed_two), hat_two, inverse_two, dilate_gain, count
    )
    d_dilate_image = d_pre_dilate.reshape(height, breadth, part)
    d_mid_in = scatter_rows(by_slices(conv(d_dilate_image, dilate_full, 2, True)), row)
    d_pre_reduce, reduce_sums = norm_backward(
        d_mid_in * silu_grad(normed_one), hat_one, inverse_one, reduce_gain, count
    )
    dilate_grad = conv_grad(mid_in, d_dilate_image, 2).reshape(nbatch, held, part)
    square_grad = jnp.concatenate([expand_grad, gate_sums], axis=1)
    heads_grad, dilate_grad, square_grad, reduce_sums = lax.optimization_barrier(
        (heads_grad, dilate_grad, square_grad, reduce_sums)
    )
    heads_sums = ring.scatter(heads_grad, False)
    square_sums = ring.scatter(square_grad, True)
    dilate_out = ring.scatter(dilate_grad, True)
    d_pre_reduce_all = jnp.concatenate(gather_rows(d_pre_reduce, row), axis=1)
    reduce_grad = product(inputs, d_pre_reduce_all, 0, 0).reshape(nbatch, wide_part, mid)
    reduce_out = ring.scatter(reduce_grad, False)
    features_grad = collect_wide(d_summed + product(d_pre_reduce_all, reduce_full, 1, 1))

    messages_got = jnp.stack(gather_rows(message_sums * factor, row)).reshape(
        nrows, groups, 4, grain, mid
    )

    def message_out(index):
        return jnp.transpose(messages_got[:, :, index], (1, 0, 2, 3)).reshape(held, mid)

    heads_got = gather_rows(heads_sums * factor, row)

    def head_out(index):
        lanes = [block[:, index * part : (index + 1) * part] for block in heads_got]
        return product(jnp.concatenate(lanes, axis=1), mix, 1, 0, EXACT)

    squares_got = jnp.stack(gather_rows(square_sums * factor, row))
    expand_out = jnp.transpose(
        squares_got[:, :mid_held].reshape(nrows, mid_held, nbatch, wide_part), (1, 2, 0, 3)
    ).reshape(mid_held, wide)
    gate_rows = mid_held // nrows

    def gate_out(index):
        start = mid_held + index * gate_rows
        return squares_got[:, start : start + gate_rows].reshape(mid_held, mid)

    dilate_got = jnp.concatenate(gather_rows(dilate_out * factor, row), axis=1)
    reduce_got = jnp.concatenate(gather_rows(reduce_out * factor, row), axis=0)

    expand_mine_sums = lax.dynamic_slice_in_dim(expand_sums, batch * wide_part, wide_part, 1)
    pad_to = max(part, wide_part)
    norm_sums = jnp.concatenate(
        [
            jnp.pad(sums, ((0, 0), (0, pad_to - sums.shape[1])))
            for sums in (reduce_sums, dilate_sums, expand_mine_sums)
        ],
        axis=0,
    )
    norms_got = gather_rows(jnp.pad(norm_sums, ((0, 2), (0, 0))) * factor, row)

    def norm_out(start):
        full = jnp.concatenate([block[start : start + 2, :part] for block in norms_got], axis=1)
        return lax.dynamic_slice_in_dim(full, batch * mid_held, mid_held, 1)

    expand_norm_out = jnp.concatenate([block[4:6, :wide_part] for block in norms_got], axis=1)

    return (
        block_out,
        depth_stream.reshape(1, local_height, breadth, mid),
        segment_stream.reshape(1, local_height, breadth, mid),
        features_grad,
        reduce_got,
        norm_out(0),
        dilate_got,
        norm_out(2),
        expand_out,
        expand_norm_out,
        head_out(2),
        head_out(0),
        head_out(1),
        head_out(3),
        message_out(0),
        message_out(2),
        message_out(1),
        message_out(3),
        gate_out(0),
        gate_out(1),
        gate_out(2)[:, :classes],
    )


def solution(mesh):
    pixels = P("batch", "rows", None, None)
    plane = P("batch", "rows", None)
    weight = P("batch", None)
    norm = P(None, "batch")
    in_specs = (
        (pixels, weight, norm, weight, norm, weight, norm) + (weight,) * 11 + (plane, plane, pixels, pixels)
    )
    out_specs = (pixels,) * 4 + (weight, norm) * 3 + (weight,) * 11
    return jax.shard_map(shards, mesh=mesh, in_specs=in_specs, out_specs=out_specs, check_vma=False)
```

time: 3830 us -> 910 us (0.24)
  waiting for transfers between devices: 2830 us -> 396 us
  blocking collectives: 331 us -> 0 us
  matrix products: 311 us -> 28.9 us
  local copies, waits for them, and re-layouts: 245 us -> 112 us
  starting transfers between devices: 49.9 us -> 166 us
  Pallas kernels: 0 us -> 108 us
    reduce_scatter x13 -> x1, waiting for transfers between devices: 1440 us -> 0.01 us  [shards(): lax.psum_scatter(message_grads, 'batch', scatter_dimension=0, tiled=True)]
    all_gather x13 -> x2, waiting for transfers between devices: 1120 us -> 2.62 us  [the longest x1 2.6 us: shards(): lax.all_gather(messages_mine.reshape(held, mid), 'batch', axis=0, tiled=T...]
    ppermute x14 -> x116, waiting for transfers between devices: 0.23 us -> 393 us  [the longest x60 130 us: swap_rows(): return lax.ppermute(block, 'rows', [(i, i ^ mask) for i in range(size)])]
    dot_general x30 -> x25, matrix products: 311 us -> 28.9 us  [product(): lax.dot_general(left, right, (((left_dim,), (right_dim,)), ((), ())), pre...]
    psum x7 -> x0, blocking collectives: 252 us -> none  [the longest x2 82.4 us: shards(): lax.psum((jnp.sum(pre_reduce, axis=(0, 1, 2)), jnp.sum(pre_reduce * pre_r...]
    psum x1 -> x0, waiting for transfers between devices: 195 us -> none  [shards(): lax.psum((part_grads[0], part_grads[1], part_grads[2], part_grads[3], par...]
    transpose x18 -> x8, local copies, waits for them, and re-layouts: 162 us -> 14.9 us  [the longest x2 6.89 us: spread_wide(): jnp.transpose(array.reshape(quarter, nbatch, nrows, wide_part), (2, 0, 1,...]
    ppermute x14 -> x116, starting transfers between devices: 47 us -> 166 us  [the longest x60 79.9 us: swap_rows(): return lax.ppermute(block, 'rows', [(i, i ^ mask) for i in range(size)])]
  transfers between devices with their start and end apart: 42 -> 119, of which waited for: 23 -> 44; matrix products, arithmetic and copies ran while one was open for 14% -> 18% of each run, Pallas kernels for 0% -> 12%
where the time goes in v1:
time: 910 us; the launch traced here: 904 us
  waiting for transfers between devices  396 us (44%)
  starting transfers between devices  166 us (18%)
  local copies, waits for them, and re-layouts  112 us (12%)
  Pallas kernels  108 us (12%)
  other arithmetic  61 us (7%)
  between operations  32.3 us (4%)
  matrix products  28.9 us (3%)
    ppermute x60, waiting for transfers between devices, swap_rows(): return lax.ppermute(block, 'rows', [(i, i ^ mask) for i in range(size)])  130 us
    ppermute x14, waiting for transfers between devices, scatter(): falling = lax.ppermute(falling, 'batch', self.down)  103 us
    ppermute x60, starting transfers between devices, swap_rows(): return lax.ppermute(block, 'rows', [(i, i ^ mask) for i in range(size)])  79.9 us
    ppermute x4, waiting for transfers between devices, gather(): rising = lax.ppermute(rising, 'batch', self.up)  69.9 us
    unnamed x257, local copies, waits for them, and re-layouts  40.3 us
    ppermute x21, starting transfers between devices, sum_batch(): lax.ppermute(values, 'batch', [(i, i ^ mask) for i in range(size)])  38.8 us
    ppermute x3, waiting for transfers between devices, gather(): falling = lax.ppermute(falling, 'batch', self.down)  38.1 us
    pallas_call x4, Pallas kernels, conv(): kernel_call(run, (9,), [whole_spec(image.shape), pl.BlockSpec((rows, cols...  36.3 us
  transfers between devices with their start and end apart: 119, of which 44 were waited for; matrix products, arithmetic and copies ran while one was open for 18% of the time, Pallas kernels for 12%

profile of v1, /device:TPU:1, one launch (start us, length us, event | category | flops | bytes accessed | tf_op | source)
XLA Modules:
  0.0 904.3 jit_solution(2825554300617895634)
XLA Ops:
  53.6 12.1 %collective-permute-done.4 = f32[1672,128]{1,0:T(8,128)} collective-permute-done((f32[1672,128]{1,0:T(8,128)S(1)}, f32[1672,128]{1,0:T(8,128)}, u32[]{:S(2)}, u32[]{:S(2)}) %collective-permute-start.4) | collective-permute-done | bytes 856096 | tf_op jit(solution)/shard_map/ppermute | solution.py:396
  69.6 26.0 %collective-permute-done.6 = f32[1672,128]{1,0:T(8,128)S(1)} collective-permute-done((f32[1672,128]{1,0:T(8,128)}, f32[1672,128]{1,0:T(8,128)S(1)}, u32[]{:S(2)}, u32[]{:S(2)}) %collective-permute-start.6) | collective-permute-done | bytes 856096 | tf_op jit(solution)/shard_map/ppermute | solution.py:396
  97.3 36.3 %collective-permute-done.7 = f32[1672,128]{1,0:T(8,128)S(1)} collective-permute-done((f32[1672,128]{1,0:T(8,128)S(1)}, f32[1672,128]{1,0:T(8,128)S(1)}, u32[]{:S(2)}, u32[]{:S(2)}) %collective-permute-start.7) | collective-permute-done | bytes 856096 | tf_op jit(solution)/shard_map/ppermute | solution.py:393
  133.6 20.4 %collective-permute-start.9 = (f32[1672,128]{1,0:T(8,128)S(1)}, f32[1672,128]{1,0:T(8,128)S(1)}, u32[]{:S(2)}, u32[]{:S(2)}) collective-permute-start(f32[1672,128]{1,0:T(8,128)S(1)} %collective-permute-done.7), channel_id=1, source_target_pairs={{0,8},{8,16},{16,24},{24,28},{28,20},{20,12},{12,4},{4,0},{1,9},{9... | collective-permute-start | bytes 2568200 | tf_op jit(solution)/shard_map/ppermute | solution.py:393
  154.2 33.6 %collective-permute-done.9 = f32[1672,128]{1,0:T(8,128)S(1)} collective-permute-done((f32[1672,128]{1,0:T(8,128)S(1)}, f32[1672,128]{1,0:T(8,128)S(1)}, u32[]{:S(2)}, u32[]{:S(2)}) %collective-permute-start.9) | collective-permute-done | bytes 856096 | tf_op jit(solution)/shard_map/ppermute | solution.py:393
  199.0 7.5 collective-permute-done.11
  206.7 23.4 %collective-permute-start.12 = (f32[2,128]{1,0:T(2,128)S(1)}, f32[2,128]{1,0:T(2,128)S(1)}, u32[]{:S(2)}, u32[]{:S(2)}) collective-permute-start(f32[2,128]{1,0:T(2,128)S(1)} %pad_maximum_fusion.31), channel_id=1, source_target_pairs={{0,4},{4,0},{8,12},{12,8},{16,20},{20,16},{24,28},{28,24},{1,5},{5... | collective-permute-start | bytes 3080 | tf_op jit(solution)/shard_map/ppermute | solution.py:360
  251.4 6.8 shard_map.382
  285.6 4.8 collective-permute-start.37
  301.4 5.5 collective-permute-start.35
  338.2 11.3 %shard_map.383.input_ref = f32[640,512]{1,0:T(8,128)S(1)} custom-call(f32[16,40,512]{2,1,0:T(8,128)S(1)} %bitcast.503, f32[4608,512]{1,0:T(8,128)S(1)} %copy-done.12), custom_call_target="tpu_custom_call" | custom-call | flops 9059696640 | bytes 12582912 | tf_op jit(solution)/shard_map/pallas_call | solution.py:207
  358.2 20.0 %shard_map.384 = f32[4,2,160,512]{3,2,1,0:T(8,128)S(1)} custom-call(f32[16,40,512]{2,1,0:T(8,128)S(1)} %bitcast.506, f32[72,4,16,512]{3,2,1,0:T(8,128)S(1)} %bitcast.507), custom_call_target="tpu_custom_call" | custom-call | flops 9059696640 | bytes 12582912 | tf_op jit(solution)/shard_map/pallas_call | solution.py:242
  397.0 17.4 %collective-permute-done.34 = f32[1,320,512]{2,1,0:T(8,128)S(1)} collective-permute-done((f32[1,320,512]{2,1,0:T(8,128)S(1)}, f32[1,320,512]{2,1,0:T(8,128)S(1)}, u32[]{:S(2)}, u32[]{:S(2)}) %collective-permute-start.34) | collective-permute-done | bytes 655392 | tf_op jit(solution)/shard_map/ppermute | solution.py:303
  431.9 18.8 %collective-permute-done.43 = f32[2,160,512]{2,1,0:T(8,128)S(1)} collective-permute-done((f32[2,160,512]{2,1,0:T(8,128)S(1)}, f32[2,160,512]{2,1,0:T(8,128)S(1)}, u32[]{:S(2)}, u32[]{:S(2)}) %collective-permute-start.43) | collective-permute-done | bytes 655392 | tf_op jit(solution)/shard_map/ppermute | solution.py:303
  454.1 16.4 %shard_map.385 = f32[72,4,16,512]{3,2,1,0:T(8,128)S(1)} custom-call(f32[640,512]{1,0:T(8,128)S(1)} %copy-done.11, f32[2,16,40,512]{3,2,1,0:T(8,128)S(1)} %bitcast.493), custom_call_target="tpu_custom_call" | custom-call | flops 9059696640 | bytes 12582912 | tf_op jit(solution)/shard_map/pallas_call | solution.py:281
  479.6 15.1 %shard_map.386 = f32[640,512]{1,0:T(8,128)S(1)} custom-call(f32[2,16,40,512]{3,2,1,0:T(8,128)S(1)} %bitcast.494, f32[72,4,16,512]{3,2,1,0:T(8,128)S(1)} %bitcast.508, f32[2,640,128]{2,1,0:T(8,128)S(1)} %pad_maximum_fusion.23.direct_ref), custom_call_target="tpu_custom_call" | custom-call | flops 9059696640 | bytes 12582912 | tf_op jit(solution)/shard_map/pallas_call | solution.py:261
  498.9 11.8 %shard_map.387 = f32[640,512]{1,0:T(8,128)S(1)} custom-call(f32[16,40,512]{2,1,0:T(8,128)S(1)} %bitcast.509, f32[4608,512]{1,0:T(8,128)S(1)} %copy-done.13), custom_call_target="tpu_custom_call" | custom-call | flops 9059696640 | bytes 12582912 | tf_op jit(solution)/shard_map/pallas_call | solution.py:207
  540.0 6.3 collective-permute-done.53
  557.5 6.4 shard_map.388
  566.7 13.4 %shard_map.389 = f32[4608,512]{1,0:T(8,128)S(1)} custom-call(f32[640,512]{1,0:T(8,128)S(1)} %copy-done.9, f32[16,40,512]{2,1,0:T(8,128)S(1)} %bitcast.510), custom_call_target="tpu_custom_call" | custom-call | flops 9059696640 | bytes 12582912 | tf_op jit(solution)/shard_map/pallas_call | solution.py:225
  582.4 5.6 collective-permute-done.58
  589.3 6.6 shard_map.390
  596.4 8.5 collective-permute-done.79
  620.2 38.3 %collective-permute-done.106 = f32[576,512]{1,0:T(8,128)S(1)} collective-permute-done((f32[576,512]{1,0:T(8,128)S(1)}, f32[576,512]{1,0:T(8,128)S(1)}, u32[]{:S(2)}, u32[]{:S(2)}) %collective-permute-start.106) | collective-permute-done | bytes 1179680 | tf_op jit(solution)/shard_map/ppermute | solution.py:415
  661.1 29.8 %collective-permute-done.97 = f32[112,512]{1,0:T(8,128)S(1)} collective-permute-done((f32[112,512]{1,0:T(8,128)S(1)}, f32[112,512]{1,0:T(8,128)S(1)}, u32[]{:S(2)}, u32[]{:S(2)}) %collective-permute-start.97) | collective-permute-done | bytes 229408 | tf_op jit(solution)/shard_map/ppermute | solution.py:415
  693.1 5.1 collective-permute-done.87
  711.0 27.7 %collective-permute-done.104 = f32[576,512]{1,0:T(8,128)S(1)} collective-permute-done((f32[576,512]{1,0:T(8,128)S(1)}, f32[576,512]{1,0:T(8,128)S(1)}, u32[]{:S(2)}, u32[]{:S(2)}) %collective-permute-start.104) | collective-permute-done | bytes 1179680 | tf_op jit(solution)/shard_map/ppermute | solution.py:411
  745.9 28.8 %collective-permute-done.72 = f32[64,512]{1,0:T(8,128)S(1)} collective-permute-done((f32[64,512]{1,0:T(8,128)S(1)}, f32[64,512]{1,0:T(8,128)S(1)}, u32[]{:S(2)}, u32[]{:S(2)}) %collective-permute-start.72) | collective-permute-done | bytes 131104 | tf_op jit(solution)/shard_map/ppermute | solution.py:415
  783.3 5.1 collective-permute-done.66
  789.2 6.6 collective-permute-done.65
  827.3 11.0 %collective-permute-done.75 = f32[64,512]{1,0:T(8,128)} collective-permute-done((f32[64,512]{1,0:T(8,128)}, f32[64,512]{1,0:T(8,128)}, u32[]{:S(2)}, u32[]{:S(2)}) %collective-permute-start.75) | collective-permute-done | bytes 131104 | tf_op jit(solution)/shard_map/ppermute | solution.py:303
  857.0 22.9 %collective-permute-done.113 = f32[576,512]{1,0:T(8,128)S(1)} collective-permute-done((f32[576,512]{1,0:T(8,128)S(1)}, f32[576,512]{1,0:T(8,128)S(1)}, u32[]{:S(2)}, u32[]{:S(2)}) %collective-permute-start.113) | collective-permute-done | bytes 1179680 | tf_op jit(solution)/shard_map/ppermute | solution.py:303
  (728 shorter events, 362.4 us)
Async XLA Ops:
  7.2 325.9 %all-gather.3.cloned.1.call-start = ((), (), s32[]{:S(2)}) async-start(), calls=%async_computation.1 | async-start | bytes 10616832 | tf_op jit(solution)/shard_map/all_gather | solution.py:511
  12.4 340.7 %all-gather.5.cloned.1.call-start = ((), (), s32[]{:S(2)}) async-start(), calls=%async_computation.2 | async-start | bytes 10616832 | tf_op jit(solution)/shard_map/all_gather | solution.py:524
  18.6 47.1 %collective-permute-start.4 = (f32[1672,128]{1,0:T(8,128)S(1)}, f32[1672,128]{1,0:T(8,128)}, u32[]{:S(2)}, u32[]{:S(2)}) collective-permute-start(f32[1672,128]{1,0:T(8,128)S(1)} %constant_dynamic-update-slice_fusion), channel_id=1, source_target_pairs={{8,0},{16,8},{24,16},{28,24},{20,28},{12,20},{4,12},{0,4},{9,1},{1... | collective-permute-start | bytes 2568200 | tf_op jit(solution)/shard_map/ppermute | solution.py:396
  20.7 45.0 %collective-permute-start.3 = (f32[1672,128]{1,0:T(8,128)S(1)}, f32[1672,128]{1,0:T(8,128)}, u32[]{:S(2)}, u32[]{:S(2)}) collective-permute-start(f32[1672,128]{1,0:T(8,128)S(1)} %constant_dynamic-update-slice_fusion), channel_id=1, source_target_pairs={{0,8},{8,16},{16,24},{24,28},{28,20},{20,12},{12,4},{4,0},{1,9},{9... | collective-permute-start | bytes 2568200 | tf_op jit(solution)/shard_map/ppermute | solution.py:393
  24.3 826.6 %reduce-scatter.2.cloned.1.call-start = ((), (), s32[]{:S(2)}) async-start(), calls=%async_computation.3 | async-start | bytes 10616832 | tf_op jit(solution)/shard_map/reduce_scatter | solution.py:671
  95.7 58.4 %collective-permute-start.8 = (f32[1672,128]{1,0:T(8,128)S(1)}, f32[1672,128]{1,0:T(8,128)S(1)}, u32[]{:S(2)}, u32[]{:S(2)}) collective-permute-start(f32[1672,128]{1,0:T(8,128)S(1)} %collective-permute-done.6), channel_id=1, source_target_pairs={{8,0},{16,8},{24,16},{28,24},{20,28},{12,20},{4,12},{0,4},{9,1},{1... | collective-permute-start | bytes 2568200 | tf_op jit(solution)/shard_map/ppermute | solution.py:396
  95.7 37.9 %collective-permute-start.7 = (f32[1672,128]{1,0:T(8,128)S(1)}, f32[1672,128]{1,0:T(8,128)S(1)}, u32[]{:S(2)}, u32[]{:S(2)}) collective-permute-start(f32[1672,128]{1,0:T(8,128)S(1)} %collective-permute-done.5), channel_id=1, source_target_pairs={{0,8},{8,16},{16,24},{24,28},{28,20},{20,12},{12,4},{4,0},{1,9},{9... | collective-permute-start | bytes 2568200 | tf_op jit(solution)/shard_map/ppermute | solution.py:393
  133.6 54.2 %collective-permute-start.9 = (f32[1672,128]{1,0:T(8,128)S(1)}, f32[1672,128]{1,0:T(8,128)S(1)}, u32[]{:S(2)}, u32[]{:S(2)}) collective-permute-start(f32[1672,128]{1,0:T(8,128)S(1)} %collective-permute-done.7), channel_id=1, source_target_pairs={{0,8},{8,16},{16,24},{24,28},{28,20},{20,12},{12,4},{4,0},{1,9},{9... | collective-permute-start | bytes 2568200 | tf_op jit(solution)/shard_map/ppermute | solution.py:393
  333.1 46.4 %collective-permute-start.50 = (f32[2,512]{1,0:T(2,128)S(1)}, f32[2,512]{1,0:T(2,128)S(1)}, u32[]{:S(2)}, u32[]{:S(2)}) collective-permute-start(f32[2,512]{1,0:T(2,128)S(1)} %fusion.137), channel_id=1, source_target_pairs={{0,8},{4,12},{8,0},{12,4},{16,24},{20,28},{24,16},{28,20},{1,9},{5... | collective-permute-start | bytes 12296 | tf_op jit(solution)/shard_map/ppermute | solution.py:360
  381.8 135.1 %collective-permute-start.29 = (f32[160,512]{1,0:T(8,128)}, f32[160,512]{1,0:T(8,128)}, u32[]{:S(2)}, u32[]{:S(2)}) collective-permute-start(f32[160,512]{1,0:T(8,128)} %get-tuple-element.180), channel_id=1, source_target_pairs={{0,1},{1,0},{2,3},{3,2},{4,5},{5,4},{6,7},{7,6},{8,9},{9,8},{10,11... | collective-permute-start | bytes 983048 | tf_op jit(solution)/shard_map/ppermute | solution.py:303
  386.3 130.7 %collective-permute-start.28 = (f32[160,512]{1,0:T(8,128)}, f32[160,512]{1,0:T(8,128)}, u32[]{:S(2)}, u32[]{:S(2)}) collective-permute-start(f32[160,512]{1,0:T(8,128)} %get-tuple-element.181), channel_id=1, source_target_pairs={{0,2},{1,3},{2,0},{3,1},{4,6},{5,7},{6,4},{7,5},{8,10},{9,11},{10,... | collective-permute-start | bytes 983048 | tf_op jit(solution)/shard_map/ppermute | solution.py:303
  422.2 94.7 %collective-permute-start.27 = (f32[160,512]{1,0:T(8,128)}, f32[160,512]{1,0:T(8,128)}, u32[]{:S(2)}, u32[]{:S(2)}) collective-permute-start(f32[160,512]{1,0:T(8,128)} %get-tuple-element.182), channel_id=1, source_target_pairs={{0,3},{1,2},{2,1},{3,0},{4,7},{5,6},{6,5},{7,4},{8,11},{9,10},{10,... | collective-permute-start | bytes 983048 | tf_op jit(solution)/shard_map/ppermute | solution.py:303
  613.8 86.6 %collective-permute-start.62 = (f32[640,128]{1,0:T(8,128)S(1)}, f32[640,128]{1,0:T(8,128)S(1)}, u32[]{:S(2)}, u32[]{:S(2)}) collective-permute-start(f32[640,128]{1,0:T(8,128)S(1)} %subtract_multiply_fusion.2), channel_id=1, source_target_pairs={{0,2},{1,3},{2,0},{3,1},{4,6},{5,7},{6,4},{7,5},{8,10},{9,11},{10,... | collective-permute-start | bytes 983048 | tf_op jit(solution)/shard_map/ppermute | solution.py:303
  614.2 45.4 %collective-permute-start.93 = (f32[112,512]{1,0:T(8,128)S(1)}, f32[112,512]{1,0:T(8,128)S(1)}, u32[]{:S(2)}, u32[]{:S(2)}) collective-permute-start(f32[112,512]{1,0:T(8,128)S(1)} %get-tuple-element.156), channel_id=1, source_target_pairs={{0,8},{8,16},{16,24},{24,28},{28,20},{20,12},{12,4},{4,0},{1,9},{9... | collective-permute-start | bytes 688136 | tf_op jit(solution)/shard_map/ppermute | solution.py:411
  615.0 46.0 %collective-permute-start.83 = (f32[576,128]{1,0:T(8,128)S(1)}, f32[576,128]{1,0:T(8,128)S(1)}, u32[]{:S(2)}, u32[]{:S(2)}) collective-permute-start(f32[576,128]{1,0:T(8,128)S(1)} %get-tuple-element.134), channel_id=1, source_target_pairs={{0,8},{8,16},{16,24},{24,28},{28,20},{20,12},{12,4},{4,0},{1,9},{9... | collective-permute-start | bytes 884744 | tf_op jit(solution)/shard_map/ppermute | solution.py:411
  617.1 84.6 %collective-permute-start.103 = (f32[576,512]{1,0:T(8,128)S(1)}, f32[576,512]{1,0:T(8,128)S(1)}, u32[]{:S(2)}, u32[]{:S(2)}) collective-permute-start(f32[576,512]{1,0:T(8,128)S(1)} %get-tuple-element.89), channel_id=1, source_target_pairs={{0,8},{8,16},{16,24},{24,28},{28,20},{20,12},{12,4},{4,0},{1,9},{9... | collective-permute-start | bytes 3538952 | tf_op jit(solution)/shard_map/ppermute | solution.py:411
  619.5 39.1 %collective-permute-start.106 = (f32[576,512]{1,0:T(8,128)S(1)}, f32[576,512]{1,0:T(8,128)S(1)}, u32[]{:S(2)}, u32[]{:S(2)}) collective-permute-start(f32[576,512]{1,0:T(8,128)S(1)} %get-tuple-element.90), channel_id=1, source_target_pairs={{8,0},{16,8},{24,16},{28,24},{20,28},{12,20},{4,12},{0,4},{9,1},{1... | collective-permute-start | bytes 3538952 | tf_op jit(solution)/shard_map/ppermute | solution.py:415
  658.8 43.2 %collective-permute-start.107 = (f32[576,512]{1,0:T(8,128)S(1)}, f32[576,512]{1,0:T(8,128)S(1)}, u32[]{:S(2)}, u32[]{:S(2)}) collective-permute-start(f32[576,512]{1,0:T(8,128)S(1)} %bitcast_add_fusion.4), channel_id=1, source_target_pairs={{8,0},{16,8},{24,16},{28,24},{20,28},{12,20},{4,12},{0,4},{9,1},{1... | collective-permute-start | bytes 3538952 | tf_op jit(solution)/shard_map/ppermute | solution.py:415
  659.5 31.4 %collective-permute-start.97 = (f32[112,512]{1,0:T(8,128)S(1)}, f32[112,512]{1,0:T(8,128)S(1)}, u32[]{:S(2)}, u32[]{:S(2)}) collective-permute-start(f32[112,512]{1,0:T(8,128)S(1)} %get-tuple-element.157), channel_id=1, source_target_pairs={{8,0},{16,8},{24,16},{28,24},{20,28},{12,20},{4,12},{0,4},{9,1},{1... | collective-permute-start | bytes 688136 | tf_op jit(solution)/shard_map/ppermute | solution.py:415
  702.0 42.1 %collective-permute-start.85 = (f32[576,128]{1,0:T(8,128)S(1)}, f32[576,128]{1,0:T(8,128)S(1)}, u32[]{:S(2)}, u32[]{:S(2)}) collective-permute-start(f32[576,128]{1,0:T(8,128)S(1)} %get-tuple-element.132), channel_id=1, source_target_pairs={{0,8},{8,16},{16,24},{24,28},{28,20},{20,12},{12,4},{4,0},{1,9},{9... | collective-permute-start | bytes 884744 | tf_op jit(solution)/shard_map/ppermute | solution.py:411
  703.9 34.9 %collective-permute-start.104 = (f32[576,512]{1,0:T(8,128)S(1)}, f32[576,512]{1,0:T(8,128)S(1)}, u32[]{:S(2)}, u32[]{:S(2)}) collective-permute-start(f32[576,512]{1,0:T(8,128)S(1)} %get-tuple-element.87), channel_id=1, source_target_pairs={{0,8},{8,16},{16,24},{24,28},{28,20},{20,12},{12,4},{4,0},{1,9},{9... | collective-permute-start | bytes 3538952 | tf_op jit(solution)/shard_map/ppermute | solution.py:411
  705.2 33.6 %collective-permute-start.108 = (f32[576,512]{1,0:T(8,128)S(1)}, f32[576,512]{1,0:T(8,128)S(1)}, u32[]{:S(2)}, u32[]{:S(2)}) collective-permute-start(f32[576,512]{1,0:T(8,128)S(1)} %get-tuple-element.88), channel_id=1, source_target_pairs={{8,0},{16,8},{24,16},{28,24},{20,28},{12,20},{4,12},{0,4},{9,1},{1... | collective-permute-start | bytes 3538952 | tf_op jit(solution)/shard_map/ppermute | solution.py:415
  709.4 34.9 %collective-permute-start.88 = (f32[576,128]{1,0:T(8,128)S(1)}, f32[576,128]{1,0:T(8,128)S(1)}, u32[]{:S(2)}, u32[]{:S(2)}) collective-permute-start(f32[576,128]{1,0:T(8,128)S(1)} %get-tuple-element.133), channel_id=1, source_target_pairs={{8,0},{16,8},{24,16},{28,24},{20,28},{12,20},{4,12},{0,4},{9,1},{1... | collective-permute-start | bytes 884744 | tf_op jit(solution)/shard_map/ppermute | solution.py:415
  709.9 32.9 %collective-permute-start.68 = (f32[64,512]{1,0:T(8,128)S(1)}, f32[64,512]{1,0:T(8,128)S(1)}, u32[]{:S(2)}, u32[]{:S(2)}) collective-permute-start(f32[64,512]{1,0:T(8,128)S(1)} %get-tuple-element.226), channel_id=1, source_target_pairs={{0,8},{8,16},{16,24},{24,28},{28,20},{20,12},{12,4},{4,0},{1,9},{9... | collective-permute-start | bytes 393224 | tf_op jit(solution)/shard_map/ppermute | solution.py:411
  740.7 62.2 %collective-permute-start.105 = (f32[576,512]{1,0:T(8,128)}, f32[576,512]{1,0:T(8,128)}, u32[]{:S(2)}, u32[]{:S(2)}) collective-permute-start(f32[576,512]{1,0:T(8,128)} %get-tuple-element.85), channel_id=1, source_target_pairs={{0,8},{8,16},{16,24},{24,28},{28,20},{20,12},{12,4},{4,0},{1,9},{9... | collective-permute-start | bytes 3538952 | tf_op jit(solution)/shard_map/ppermute | solution.py:411
  742.6 60.6 %collective-permute-start.109 = (f32[576,512]{1,0:T(8,128)}, f32[576,512]{1,0:T(8,128)}, u32[]{:S(2)}, u32[]{:S(2)}) collective-permute-start(f32[576,512]{1,0:T(8,128)} %get-tuple-element.86), channel_id=1, source_target_pairs={{8,0},{16,8},{24,16},{28,24},{20,28},{12,20},{4,12},{0,4},{9,1},{1... | collective-permute-start | bytes 3538952 | tf_op jit(solution)/shard_map/ppermute | solution.py:415
  742.8 36.1 %collective-permute-start.96 = (f32[112,512]{1,0:T(8,128)S(1)}, f32[112,512]{1,0:T(8,128)S(1)}, u32[]{:S(2)}, u32[]{:S(2)}) collective-permute-start(f32[112,512]{1,0:T(8,128)S(1)} %get-tuple-element.152), channel_id=1, source_target_pairs={{0,8},{8,16},{16,24},{24,28},{28,20},{20,12},{12,4},{4,0},{1,9},{9... | collective-permute-start | bytes 688136 | tf_op jit(solution)/shard_map/ppermute | solution.py:411
  744.1 35.9 %collective-permute-start.99 = (f32[112,512]{1,0:T(8,128)S(1)}, f32[112,512]{1,0:T(8,128)S(1)}, u32[]{:S(2)}, u32[]{:S(2)}) collective-permute-start(f32[112,512]{1,0:T(8,128)S(1)} %get-tuple-element.153), channel_id=1, source_target_pairs={{8,0},{16,8},{24,16},{28,24},{20,28},{12,20},{4,12},{0,4},{9,1},{1... | collective-permute-start | bytes 688136 | tf_op jit(solution)/shard_map/ppermute | solution.py:415
  782.0 41.5 %collective-permute-start.86 = (f32[576,128]{1,0:T(8,128)}, f32[576,128]{1,0:T(8,128)}, u32[]{:S(2)}, u32[]{:S(2)}) collective-permute-start(f32[576,128]{1,0:T(8,128)} %get-tuple-element.130), channel_id=1, source_target_pairs={{0,8},{8,16},{16,24},{24,28},{28,20},{20,12},{12,4},{4,0},{1,9},{9... | collective-permute-start | bytes 884744 | tf_op jit(solution)/shard_map/ppermute | solution.py:411
  788.4 35.6 %collective-permute-start.89 = (f32[576,128]{1,0:T(8,128)}, f32[576,128]{1,0:T(8,128)}, u32[]{:S(2)}, u32[]{:S(2)}) collective-permute-start(f32[576,128]{1,0:T(8,128)} %get-tuple-element.131), channel_id=1, source_target_pairs={{8,0},{16,8},{24,16},{28,24},{20,28},{12,20},{4,12},{0,4},{9,1},{1... | collective-permute-start | bytes 884744 | tf_op jit(solution)/shard_map/ppermute | solution.py:415
  806.7 35.1 %collective-permute-start.110 = (f32[576,512]{1,0:T(8,128)S(1)}, f32[576,512]{1,0:T(8,128)}, u32[]{:S(2)}, u32[]{:S(2)}) collective-permute-start(f32[576,512]{1,0:T(8,128)S(1)} %fusion.40), channel_id=1, source_target_pairs={{0,2},{1,3},{2,0},{3,1},{4,6},{5,7},{6,4},{7,5},{8,10},{9,11},{10,... | collective-permute-start | bytes 3538952 | tf_op jit(solution)/shard_map/ppermute | solution.py:303
  856.6 33.4 %collective-permute-start.115 = (f32[576,512]{1,0:T(8,128)S(1)}, f32[576,512]{1,0:T(8,128)S(1)}, u32[]{:S(2)}, u32[]{:S(2)}) collective-permute-start(f32[576,512]{1,0:T(8,128)S(1)} %broadcast_multiply_fusion), channel_id=1, source_target_pairs={{0,1},{1,0},{2,3},{3,2},{4,5},{5,4},{6,7},{7,6},{8,9},{9,8},{10,11... | collective-permute-start | bytes 3538952 | tf_op jit(solution)/shard_map/ppermute | solution.py:303
  (204 other events, 2559.5 us)
Sparse Core Ops, SparseCore 0:
  12.5 197.8 all-gather.2
  213.2 139.9 all-gather.4
  474.3 173.8 reduce-scatter.1

commit v2 on v1

v2 whole, which is shorter than its diff:
```python
import math

import jax
import jax.numpy as jnp
from jax import lax
from jax.experimental import pallas as pl
from jax.experimental.pallas import tpu as pltpu
from jax.sharding import PartitionSpec as P

EPSILON = 1e-05
EXACT = lax.Precision.HIGHEST
FINE = lax.Precision.HIGH
LONGEST_RING = 8
LANES = 128


def product(left, right, left_dim, right_dim, precision=FINE):
    return lax.dot_general(
        left,
        right,
        (((left_dim,), (right_dim,)), ((), ())),
        precision=precision,
        preferred_element_type=jnp.float32,
    )


def halves(values):
    high = values.astype(jnp.bfloat16)
    return high, (values - high.astype(jnp.float32)).astype(jnp.bfloat16)


def three_pass(left, right, left_dim, right_dim):
    dims = (((left_dim,), (right_dim,)), ((), ()))

    def one(a, b):
        return lax.dot_general(a, b, dims, preferred_element_type=jnp.float32)

    return one(left[0], right[0]) + (one(left[0], right[1]) + one(left[1], right[0]))


def frame(image_ref, framed, dilation):
    height, breadth, depth = image_ref.shape
    edge = jnp.zeros((3, dilation, breadth, depth), jnp.float32)
    framed[:, :dilation] = edge
    framed[:, dilation + height :] = edge
    image = image_ref[...]
    side = jnp.zeros((height, dilation, depth), jnp.float32)
    inner = slice(dilation, dilation + height)
    framed[1, inner] = image
    framed[0, inner, dilation:, :] = image[:, : breadth - dilation]
    framed[0, inner, :dilation, :] = side
    framed[2, inner, : breadth - dilation, :] = image[:, dilation:]
    framed[2, inner, breadth - dilation :, :] = side


def shifted(framed, tap, height, dilation):
    block = framed[tap % 3, pl.ds((tap // 3) * dilation, height)]
    return block.reshape(height * block.shape[1], block.shape[2])


def exact_pick(values, choice, choice_dim):
    high = values.astype(jnp.bfloat16)
    rest = values - high.astype(jnp.float32)
    middle = rest.astype(jnp.bfloat16)
    low = (rest - middle.astype(jnp.float32)).astype(jnp.bfloat16)
    dims = (((1,), (choice_dim,)), ((), ()))

    def one(part):
        return lax.dot_general(part, choice, dims, preferred_element_type=jnp.float32)

    return one(high) + (one(middle) + one(low))


def at_lanes(index, size):
    return pl.ds(pl.multiple_of(index * size, size), size)


def keep_and_give(row, load, keep_ref, give_ref):
    core, side = row & 1, row >> 1
    for k in range(2):
        base = (side ^ k) * 2
        keep_ref[k] = load(base + core)
        give_ref[k] = load(base + 1 - core)


def joined_conv_kernel(dilation, row_ref, one, two, three, four, weight_ref, out_ref, image_ref, framed):
    tap = pl.program_id(0)

    @pl.when(tap == 0)
    def _():
        part = one.shape[2]
        for key, block in enumerate((one, two, three, four)):
            image_ref[:, :, at_lanes(row_ref[0] ^ key, part)] = block[...]
        frame(image_ref, framed, dilation)
        out_ref[...] = jnp.zeros_like(out_ref)

    moved = halves(shifted(framed, tap, image_ref.shape[0], dilation))
    out_ref[...] += three_pass(moved, halves(weight_ref[...]), 1, 0)


def heads_kernel(
    row_ref, one, two, three, four, weight_ref, out_ref, image_ref, pairs_ref, framed
):
    joined_conv_kernel(1, row_ref, one, two, three, four, weight_ref, out_ref, image_ref, framed)

    @pl.when(pl.program_id(0) == 8)
    def _():
        _, double, part = pairs_ref.shape
        quarter = double // 2
        for key in range(4):
            rows = pl.ds((row_ref[0] ^ key) * quarter, quarter)
            pairs_ref[key, :quarter] = out_ref[rows, 2 * part : 3 * part]
            pairs_ref[key, quarter:] = out_ref[rows, :part]


def split_product_kernel(row_ref, left_ref, right_ref, extra_ref, keep_ref, give_ref, total):
    total[...] = three_pass(halves(left_ref[...]), halves(right_ref[...]), 1, 0)
    pixels, part = left_ref.shape[0], keep_ref.shape[2]
    keep_and_give(
        row_ref[0],
        lambda j: total[:, at_lanes(j, part)],
        keep_ref.at[:, :pixels],
        give_ref.at[:, :pixels],
    )
    for ref in (keep_ref, give_ref):
        ref[:, pixels:] = jnp.broadcast_to(extra_ref[...], (2, 8, part))


def conv_back_kernel(dilation, row_ref, image_ref, weight_ref, *rest):
    extra_ref = rest[0] if len(rest) == 5 else None
    keep_ref, give_ref, framed, total = rest[-4:]
    tap = pl.program_id(0)

    @pl.when(tap == 0)
    def _():
        frame(image_ref, framed, dilation)
        total[...] = jnp.zeros_like(total) if extra_ref is None else extra_ref[...]

    moved = halves(shifted(framed, 8 - tap, image_ref.shape[0], dilation))
    total[...] += three_pass(moved, halves(weight_ref[...]), 1, 1)

    @pl.when(tap == 8)
    def _():
        part = keep_ref.shape[2]
        keep_and_give(row_ref[0], lambda j: total[:, at_lanes(j, part)], keep_ref, give_ref)


def conv_grad_kernel(dilation, input_ref, grad_ref, out_ref, framed, high, low):
    tap = pl.program_id(0)

    @pl.when(tap == 0)
    def _():
        frame(grad_ref, framed, dilation)
        high[...], low[...] = halves(jnp.transpose(input_ref[...]))

    moved = halves(shifted(framed, 8 - tap, grad_ref.shape[0], dilation))
    out_ref[...] = three_pass((high[...], low[...]), moved, 1, 0)


def heads_grad_kernel(
    row_ref, input_ref, first_ref, second_ref, direct_ref, out_ref, image_ref, framed, high, low
):
    tap = pl.program_id(0)

    @pl.when(tap == 0)
    def _():
        lanes = first_ref.shape[2]
        _, double, breadth, part = direct_ref.shape
        lines = double // 2
        image_ref[:, :, :lanes] = first_ref[...]
        image_ref[:, :, lanes:] = second_ref[...]
        for key in range(4):
            rows = pl.ds((row_ref[0] ^ key) * lines, lines)
            image_ref[rows, :, :part] += direct_ref[key, :lines]
            image_ref[rows, :, lanes : lanes + part] += direct_ref[key, lines:]

    conv_grad_kernel(1, input_ref, image_ref, out_ref, framed, high, low)


def source_rows(weight):
    return jnp.concatenate(
        [weight[:, k].reshape(-1, weight.shape[-1]) for k in range(weight.shape[1])], axis=0
    )


def note_kernel(row_ref, image_ref, weight_ref, keep_ref, give_ref, framed, total):
    tap = pl.program_id(0)

    @pl.when(tap == 0)
    def _():
        frame(image_ref, framed, 1)
        total[...] = jnp.zeros_like(total)

    moved = shifted(framed, tap, image_ref.shape[0], 1)
    total[...] += three_pass(halves(moved), halves(source_rows(weight_ref[...])), 1, 0)

    @pl.when(tap == 8)
    def _():
        quarter = keep_ref.shape[1]
        keep_and_give(
            row_ref[0], lambda j: total[pl.ds(j * quarter, quarter), :], keep_ref, give_ref
        )


def note_back_kernel(note_ref, weight_ref, out_ref, framed):
    tap = pl.program_id(0)

    @pl.when(tap == 0)
    def _():
        frame(note_ref, framed, 1)
        out_ref[...] = jnp.zeros_like(out_ref)

    moved = halves(shifted(framed, 8 - tap, note_ref.shape[0], 1))
    out_ref[...] += three_pass(moved, halves(source_rows(weight_ref[...])), 1, 1)


def note_grad_kernel(
    row_ref, input_ref, one, two, three, four, out_ref, image_ref, framed, high, low
):
    tap = pl.program_id(0)

    @pl.when(tap == 0)
    def _():
        lines = one.shape[0]
        for key, block in enumerate((one, two, three, four)):
            image_ref[pl.ds((row_ref[0] ^ key) * lines, lines)] = block[...]
        frame(image_ref, framed, 1)
        high[...], low[...] = halves(jnp.transpose(input_ref[...]))

    moved = halves(shifted(framed, 8 - tap, image_ref.shape[0], 1))
    grad = three_pass((high[...], low[...]), moved, 1, 0)
    runs, _, grain, mid = out_ref.shape
    part = grad.shape[0] // 2
    for k in range(2):
        out_ref[:, k] = grad[k * part : (k + 1) * part].reshape(runs, grain, mid)


def gates_kernel(
    row_ref, pairs_ref, mix_ref, depth_gate_ref, segment_gate_ref, cotangent_ref, scale_ref,
    feat_ref, open_ref, d_note_ref, joined,
):
    _, double, part = pairs_ref.shape
    quarter = double // 2
    for key in range(4):
        joined[:, at_lanes(row_ref[0] ^ key, part)] = pairs_ref[key]
    feat = exact_pick(joined[...], mix_ref[...], 0)
    feat_ref[...] = feat
    for index, gate_ref in enumerate((depth_gate_ref, segment_gate_ref)):
        rows = slice(index * quarter, (index + 1) * quarter)
        gate = three_pass(halves(feat[rows]), halves(gate_ref[...]), 1, 0)
        open_ref[rows] = jax.nn.sigmoid(gate)
    d_note_ref[...] = cotangent_ref[...] * scale_ref[...] * open_ref[:quarter]


def gate_back(row_ref, feat, opened, note, d_stream, d_note, gate_ref, mix_ref, gate_grad_ref, joined):
    d_pre = halves(d_note * note * (1.0 - opened))
    gate_grad_ref[...] = three_pass(halves(jnp.transpose(feat)), d_pre, 1, 0)
    direct = d_stream + three_pass(d_pre, halves(gate_ref[...]), 1, 1)
    joined[...] = exact_pick(direct, mix_ref[...], 1)


def segment_kernel(
    classes, row_ref, mine_ref, got_ref, feat_ref, open_ref, labels_ref, classifier_ref, gate_ref, mix_ref,
    stream_ref, d_note_ref, direct_ref, gate_grad_ref, classifier_grad_ref, joined,
):
    note = mine_ref[...] + got_ref[...]
    feat, opened = feat_ref[...], open_ref[...]
    stream = feat + opened * note
    stream_ref[...] = stream
    weight = halves(classifier_ref[...])
    logits = three_pass(halves(stream), weight, 1, 0)
    lane = lax.broadcasted_iota(jnp.int32, logits.shape, 1)
    real = lane < classes
    top = jnp.max(jnp.where(real, logits, -3e38), axis=1, keepdims=True)
    powers = jnp.where(real, jnp.exp(jnp.where(real, logits - top, 0.0)), 0.0)
    onehot = jnp.where(lane == labels_ref[...], 1.0, 0.0)
    d_logits = powers / jnp.sum(powers, axis=1, keepdims=True) - onehot
    d_stream = three_pass(halves(d_logits), weight, 1, 1)
    d_note = d_stream * opened
    d_note_ref[...] = d_note
    classifier_grad_ref[...] = three_pass(halves(jnp.transpose(stream)), halves(d_logits), 1, 0)
    gate_back(row_ref, feat, opened, note, d_stream, d_note, gate_ref, mix_ref, gate_grad_ref, joined)
    part = direct_ref.shape[2]
    for key in range(4):
        direct_ref[key] = joined[:, at_lanes(row_ref[0] ^ key, part)]


def depth_kernel(
    row_ref, mine_ref, got_ref, feat_ref, open_ref, cotangent_ref, scale_ref, gate_ref, mix_ref, other_ref,
    stream_ref, direct_ref, gate_grad_ref, joined,
):
    note = mine_ref[...] + got_ref[...]
    feat, opened = feat_ref[...], open_ref[...]
    stream_ref[...] = feat + opened * note
    d_stream = cotangent_ref[...] * scale_ref[...]
    gate_back(
        row_ref, feat, opened, note, d_stream, d_stream * opened, gate_ref, mix_ref, gate_grad_ref, joined
    )
    _, double, part = direct_ref.shape
    quarter = double // 2
    for key in range(4):
        direct_ref[key, :quarter] = other_ref[key]
        direct_ref[key, quarter:] = joined[:, at_lanes(row_ref[0] ^ key, part)]


def reduce_back_kernel(
    row_ref, one, two, three, four, input_ref, weight_ref, d_summed_ref, grad_ref, out_ref, joined
):
    part = one.shape[1]
    for key, block in enumerate((one, two, three, four)):
        joined[:, at_lanes(row_ref[0] ^ key, part)] = block[...]
    d_pre = halves(joined[...])
    grad_ref[...] = three_pass(halves(jnp.transpose(input_ref[...])), d_pre, 1, 0)
    out_ref[...] = d_summed_ref[...] + three_pass(d_pre, halves(weight_ref[...]), 1, 1)


def heads_out_kernel(row_ref, one, two, three, four, mix_ref, *rest):
    outs, joined = rest[:-1], rest[-1]
    part = joined.shape[1] // 4
    for index, out_ref in enumerate(outs):
        lanes = slice(index * part, (index + 1) * part)
        for key, block in enumerate((one, two, three, four)):
            joined[:, at_lanes(row_ref[0] ^ key, part)] = block[:, lanes]
        out_ref[...] = exact_pick(joined[...], mix_ref[...], 0)


def spread_kernel(row_ref, array_ref, out_ref):
    low = lax.broadcasted_iota(jnp.int32, (array_ref.shape[0], 128), 1) < 64
    for device in range(4):
        key = row_ref[0] ^ device
        for k in range(out_ref.shape[2] // 128):
            start = 512 * k + 128 * (device // 2)
            even = array_ref[:, start : start + 128]
            odd = array_ref[:, start + 256 : start + 384]
            if device % 2:
                block = jnp.where(low, pltpu.roll(even, 64, 1), odd)
            else:
                block = jnp.where(low, even, pltpu.roll(odd, 64, 1))
            out_ref[key, :, 128 * k : 128 * (k + 1)] = block


def collect_kernel(row_ref, one, two, three, four, out_ref, ordered):
    for key, block in enumerate((one, two, three, four)):
        ordered[row_ref[0] ^ key] = block[...]
    low = lax.broadcasted_iota(jnp.int32, (one.shape[0], 128), 1) < 64
    for k in range(one.shape[1] // 128):
        for pair in range(2):
            first = ordered[2 * pair, :, 128 * k : 128 * (k + 1)]
            second = ordered[2 * pair + 1, :, 128 * k : 128 * (k + 1)]
            start = 512 * k + 128 * pair
            out_ref[:, start : start + 128] = jnp.where(low, first, pltpu.roll(second, 64, 1))
            out_ref[:, start + 256 : start + 384] = jnp.where(low, pltpu.roll(first, 64, 1), second)


def regroup(array, run):
    runs, sources, grain, mid = array.shape
    if grain == run:
        return array
    if run > grain:
        lists = array.reshape(-1, run // grain, sources, grain, mid)
        return jnp.transpose(lists, (0, 2, 1, 3, 4)).reshape(-1, sources, run, mid)
    parts = array.reshape(runs, sources, grain // run, run, mid)
    return jnp.transpose(parts, (0, 2, 1, 3, 4)).reshape(-1, sources, run, mid)


VMEM_LIMIT = 56 * 2**20
SCALAR = pl.BlockSpec(memory_space=pltpu.SMEM)


def kernel_call(body, grid, in_specs, out_specs, out_shape, scratch, flops):
    return pl.pallas_call(
        body,
        grid=grid,
        in_specs=in_specs,
        out_specs=out_specs,
        out_shape=out_shape,
        scratch_shapes=scratch,
        compiler_params=pltpu.CompilerParams(
            dimension_semantics=("arbitrary",) * len(grid), vmem_limit_bytes=VMEM_LIMIT
        ),
        cost_estimate=pl.CostEstimate(flops=3 * flops, bytes_accessed=12 * 2**20, transcendentals=0),
    )


def single_call(body, args, outs, scratch, flops):
    return kernel_call(
        body,
        (1,),
        [SCALAR] + [whole_spec(arg.shape) for arg in args[1:]],
        [whole_spec(out) for out in outs],
        [jax.ShapeDtypeStruct(out, jnp.float32) for out in outs],
        [pltpu.VMEM(shape, jnp.float32) for shape in scratch],
        flops,
    )(*args)


def framed_scratch(image, dilation):
    height, breadth, depth = image
    return pltpu.VMEM((3, height + 2 * dilation, breadth, depth), jnp.float32)


def whole_spec(shape):
    return pl.BlockSpec(shape, lambda *_: (0,) * len(shape))


def struct(shape):
    return jax.ShapeDtypeStruct(shape, jnp.float32)


def tap_rows(rows, cols):
    return pl.BlockSpec((rows, cols), lambda tap: (tap, 0))


def tap_runs(weight_shape):
    return pl.BlockSpec((weight_shape[0] // 9,) + weight_shape[1:], lambda tap: (tap, 0, 0, 0))


def joined_conv(row, blocks, weight, dilation, with_pairs=False):
    height, breadth, part = blocks[0].shape
    image = (height, breadth, 4 * part)
    rows, cols = weight.shape[0] // 9, weight.shape[1]
    shapes = [(height * breadth, cols), image]
    if with_pairs:
        body = heads_kernel
        shapes.append((4, height * breadth // 2, part))
    else:

        def body(*refs):
            joined_conv_kernel(dilation, *refs)

    return kernel_call(
        body,
        (9,),
        [SCALAR] + [whole_spec(blocks[0].shape)] * 4 + [tap_rows(rows, cols)],
        [whole_spec(shape) for shape in shapes],
        [struct(shape) for shape in shapes],
        [framed_scratch(image, dilation)],
        2 * 9 * height * breadth * rows * cols,
    )(row, *blocks, weight)


def conv_back(row, image, weight, dilation, extra=None):
    height, breadth, _ = image.shape
    rows, cols = weight.shape[0] // 9, weight.shape[1]
    pixels = height * breadth
    shape = (2, pixels, rows // 4)

    def body(*refs):
        conv_back_kernel(dilation, *refs)

    extras = [] if extra is None else [extra]
    return kernel_call(
        body,
        (9,),
        [SCALAR, whole_spec(image.shape), tap_rows(rows, cols)]
        + [whole_spec(array.shape) for array in extras],
        [whole_spec(shape)] * 2,
        [struct(shape)] * 2,
        [framed_scratch(image.shape, dilation), pltpu.VMEM((pixels, rows), jnp.float32)],
        2 * 9 * pixels * rows * cols,
    )(row, image, weight, *extras)


def conv_grad(flat_input, image_grad, dilation):
    pixels, depth = flat_input.shape
    cols = image_grad.shape[2]

    def body(*refs):
        conv_grad_kernel(dilation, *refs)

    return kernel_call(
        body,
        (9,),
        [whole_spec(flat_input.shape), whole_spec(image_grad.shape)],
        tap_rows(depth, cols),
        struct((9 * depth, cols)),
        [framed_scratch(image_grad.shape, dilation)]
        + [pltpu.VMEM((depth, pixels), jnp.bfloat16)] * 2,
        2 * 9 * pixels * depth * cols,
    )(flat_input, image_grad)


def heads_grad_of(row, flat_input, first, second, direct):
    pixels, depth = flat_input.shape
    height, breadth, lanes = first.shape
    image = (height, breadth, 2 * lanes)
    return kernel_call(
        heads_grad_kernel,
        (9,),
        [SCALAR] + [whole_spec(array.shape) for array in (flat_input, first, second, direct)],
        [tap_rows(depth, 2 * lanes), whole_spec(image)],
        [struct((9 * depth, 2 * lanes)), struct(image)],
        [framed_scratch(image, 1)] + [pltpu.VMEM((depth, pixels), jnp.bfloat16)] * 2,
        2 * 9 * pixels * depth * 2 * lanes,
    )(row, flat_input, first, second, direct)


def note_forward(row, image, pair, weight):
    height, breadth, depth = image.shape
    depth = depth // 2
    mid = weight.shape[3]
    pixels = height * breadth
    shape = (2, pixels // 4, mid)
    return kernel_call(
        note_kernel,
        (9,),
        [
            SCALAR,
            pl.BlockSpec((height, breadth, depth), lambda tap: (0, 0, pair)),
            tap_runs(weight.shape),
        ],
        [whole_spec(shape)] * 2,
        [struct(shape)] * 2,
        [framed_scratch((height, breadth, depth), 1), pltpu.VMEM((pixels, mid), jnp.float32)],
        2 * 9 * pixels * depth * mid,
    )(row, image, weight)


def note_back(note, weight):
    height, breadth, mid = note.shape
    shape = (height * breadth, weight.shape[0] // 9 * weight.shape[1] * weight.shape[2])
    return kernel_call(
        note_back_kernel,
        (9,),
        [whole_spec(note.shape), tap_runs(weight.shape)],
        whole_spec(shape),
        struct(shape),
        [framed_scratch(note.shape, 1)],
        2 * 9 * shape[0] * shape[1] * mid,
    )(note, weight)


def note_grad(row, flat_input, pair, blocks, grain):
    pixels, depth = flat_input.shape
    depth = depth // 2
    lines, breadth, mid = blocks[0].shape
    image = (4 * lines, breadth, mid)
    runs = depth // 2 // grain
    grad = (9 * runs, 2, grain, mid)
    return kernel_call(
        note_grad_kernel,
        (9,),
        [SCALAR, pl.BlockSpec((pixels, depth), lambda tap: (0, pair))]
        + [whole_spec(blocks[0].shape)] * 4,
        [tap_runs(grad), whole_spec(image)],
        [struct(grad), struct(image)],
        [framed_scratch(image, 1)] + [pltpu.VMEM((depth, pixels), jnp.bfloat16)] * 2,
        2 * 9 * pixels * depth * mid,
    )(row, flat_input, *blocks)


def silu_grad(values):
    gate_val = jax.nn.sigmoid(values)
    return gate_val * (1.0 + values * (1.0 - gate_val))


def swap_rows(block, mask):
    size = lax.axis_size("rows")
    return lax.ppermute(block, "rows", [(i, i ^ mask) for i in range(size)])


def in_order(blocks, row):
    count = len(blocks)
    if count == 1:
        return blocks
    half = count // 2
    near = in_order(blocks[:half], row)
    far = in_order(blocks[half:], row)
    upper = (row & half) != 0
    first = [jnp.where(upper, f, n) for n, f in zip(near, far)]
    second = [jnp.where(upper, n, f) for n, f in zip(near, far)]
    return first + second


def gather_keyed(block):
    far = swap_rows(block, 2)
    return [block, swap_rows(block, 1), far, swap_rows(far, 1)]


def gather_rows(block, row):
    return in_order(gather_keyed(block), row)


def scatter_end(keep, give):
    got = swap_rows(give, 1)
    other = keep[1] + got[1]
    return keep[0] + got[0], swap_rows(other, 2)


def scatter_rows(blocks, row):
    core, side = row & 1, row >> 1
    pairs = blocks.reshape((2, 2) + blocks.shape[1:])
    keep = lax.dynamic_index_in_dim(pairs, core, 1, keepdims=False)
    got = keep + swap_rows(lax.dynamic_index_in_dim(pairs, 1 - core, 1, keepdims=False), 1)
    mine = lax.dynamic_index_in_dim(got, side, 0, keepdims=False)
    return mine + swap_rows(lax.dynamic_index_in_dim(got, 1 - side, 0, keepdims=False), 2)


def exchange_keyed(blocks):
    return [blocks[0]] + [swap_rows(blocks[mask], mask) for mask in range(1, 4)]


def sum_batch(values, direct=False):
    size = lax.axis_size("batch")
    if size & (size - 1):
        return lax.psum(values, "batch")

    def swap(block, mask):
        return lax.ppermute(block, "batch", [(i, i ^ mask) for i in range(size)])

    if direct and size <= LONGEST_RING:
        return values + sum(swap(values, mask) for mask in range(1, size))
    mask = 1
    while mask < size:
        values = values + swap(values, mask)
        mask *= 2
    return values


class Ring:
    def __init__(self, batch):
        size = lax.axis_size("batch")
        self.batch, self.size = batch, size
        self.order = list(range(0, size, 2)) + [i for i in reversed(range(size)) if i % 2]
        self.place = {b: p for p, b in enumerate(self.order)}
        self.up = [(self.order[p], self.order[(p + 1) % size]) for p in range(size)]
        self.down = [(b, a) for a, b in self.up]
        table = [[self.order[(self.place[b] + k) % size] for k in range(size)] for b in range(size)]
        self.row = jnp.array(table, jnp.int32)[batch]

    def at(self, offset):
        return self.row[offset % self.size]

    def steps(self, longer_up):
        more = self.size // 2
        less = self.size - 1 - more
        return (more, less) if longer_up else (less, more)

    def gather(self, block, longer_up, beside=None, beside_step=0):
        if self.size > LONGEST_RING:
            return lax.all_gather(block, "batch", axis=0, tiled=False), beside
        whole = jnp.zeros((self.size,) + block.shape, block.dtype)
        whole = lax.dynamic_update_index_in_dim(whole, block, self.batch, 0)
        ups, downs = self.steps(longer_up)
        rising = falling = block
        for k in range(1, max(ups, downs) + 1):
            if k == beside_step and beside is not None:
                rising, falling, beside = lax.optimization_barrier((rising, falling, beside))
            if k <= ups:
                rising = lax.ppermute(rising, "batch", self.up)
                whole = lax.dynamic_update_index_in_dim(whole, rising, self.at(-k), 0)
            if k <= downs:
                falling = lax.ppermute(falling, "batch", self.down)
                whole = lax.dynamic_update_index_in_dim(whole, falling, self.at(k), 0)
        return whole, beside

    def scatter(self, blocks, longer_up, beside=None, beside_step=0):
        if self.size > LONGEST_RING:
            return lax.psum_scatter(blocks, "batch", scatter_dimension=0, tiled=False), beside

        def own(offset):
            return lax.dynamic_index_in_dim(blocks, self.at(offset), 0, keepdims=False)

        ups, downs = self.steps(longer_up)
        rising, falling = own(ups), own(-downs)
        for k in range(max(ups, downs)):
            if k + 1 == beside_step and beside is not None:
                rising, falling, beside = lax.optimization_barrier((rising, falling, beside))
            if k < ups:
                rising = lax.ppermute(rising, "batch", self.up)
                if k < ups - 1:
                    rising = rising + own(ups - 1 - k)
            if k < downs:
                falling = lax.ppermute(falling, "batch", self.down)
                if k < downs - 1:
                    falling = falling + own(-(downs - 1 - k))
        return own(0) + rising + falling, beside


def sums_of(values, others):
    return jnp.stack([jnp.sum(values, axis=0), jnp.sum(values * others, axis=0)])


def norm_forward(values, total, gain, bias, count):
    center = total[0] / count
    inverse = lax.rsqrt(total[1] / count - center * center + EPSILON)
    hat = (values - center) * inverse
    return hat, hat * gain + bias, inverse


def norm_backward(d_out, hat, inverse, gain, count, direct):
    sums = sum_batch(jnp.stack([jnp.sum(d_out * hat, axis=0), jnp.sum(d_out, axis=0)]), direct)
    d_values = inverse * gain * (d_out - sums[1] / count - hat * (sums[0] / count))
    return d_values, sums


def shards(
    features,
    reduce_weight,
    reduce_norm,
    dilate_weight,
    dilate_norm,
    expand_weight,
    expand_norm,
    depth_head,
    segment_head,
    normal_head,
    contour_head,
    depth_message,
    segment_message,
    normal_message,
    contour_message,
    depth_gate,
    segment_gate,
    classifier,
    depth_valid,
    labels,
    block_cotangent,
    depth_cotangent,
):
    row, batch = lax.axis_index("rows"), lax.axis_index("batch")
    nrows, nbatch = lax.axis_size("rows"), lax.axis_size("batch")
    ring = Ring(batch)
    _, local_height, breadth, wide = features.shape
    mid = reduce_weight.shape[1]
    part = mid // nrows
    quarter = local_height * breadth
    height = local_height * nrows
    pixels = quarter * nrows
    count = float(pixels * nbatch)
    factor = count ** (-0.5)
    classes = classifier.shape[1]
    held = dilate_weight.shape[0]
    grain = math.gcd(held, mid) // nrows
    groups = held // (nrows * grain)
    wide_held = wide // nbatch
    wide_part = wide_held // nrows
    mid_held = mid // nbatch

    def row_slice(array, dim):
        size = array.shape[dim] // nrows
        return lax.dynamic_slice_in_dim(array, row * size, size, dim)

    channel = jnp.arange(mid)
    slot = jnp.arange(part)
    mine = (slot // grain) * (nrows * grain) + row * grain + slot % grain
    pick = (channel[:, None] == mine[None, :]).astype(jnp.float32)
    split = jnp.arange(mid)
    natural = ((split % part) // grain) * (nrows * grain) + (split // part) * grain + split % grain
    mix = (natural[:, None] == channel[None, :]).astype(jnp.bfloat16)
    here = row.astype(jnp.int32).reshape(1)

    def to_narrow(array):
        return jnp.concatenate(
            [array[:, i * part : (i + 1) * part] for i in range(nrows)], axis=0
        )

    def from_narrow(array):
        size = array.shape[1] // nrows
        return jnp.concatenate([array[:, i * size : (i + 1) * size] for i in range(nrows)], axis=2)

    tiny_width = max(mid_held, wide_part)

    def tiny(array):
        return jnp.pad(array, ((0, 0), (0, tiny_width - array.shape[1])))

    heads_mine = jnp.concatenate(
        [
            product(head, pick, 1, 0, EXACT)
            for head in (segment_head, normal_head, depth_head, contour_head)
        ],
        axis=1,
    )
    heads_full = lax.all_gather(heads_mine, "batch", axis=0, tiled=True)

    def message_runs(array):
        runs = array.reshape(groups, nrows, grain, mid)
        return lax.dynamic_index_in_dim(runs, row, 1, keepdims=True)

    def message_pair(first, second):
        return jnp.concatenate([message_runs(first), message_runs(second)], axis=1)

    run = grain if grain % 8 == 0 else part
    segment_pair_mine = message_pair(segment_message, contour_message).reshape(held // 2, mid)
    depth_pair_mine = message_pair(depth_message, normal_message).reshape(held // 2, mid)
    segment_pair_w, depth_pair_w = [
        regroup(
            lax.all_gather(mine, "batch", axis=0, tiled=True).reshape(
                nbatch * groups, 2, grain, mid
            ),
            run,
        )
        for mine in (segment_pair_mine, depth_pair_mine)
    ]

    expand_norm_mine = lax.dynamic_index_in_dim(
        expand_norm.reshape(2, nrows, wide_part), row, 1, keepdims=False
    )
    params = jnp.concatenate([tiny(reduce_norm), tiny(dilate_norm), tiny(expand_norm_mine)], axis=0)
    params = jnp.pad(params, ((0, 2), (0, part - tiny_width)))
    expand_mine = lax.dynamic_index_in_dim(
        expand_weight.reshape(mid_held, nbatch, nrows, wide_part), row, 2, keepdims=False
    ).reshape(mid_held, nbatch * wide_part)
    class_lanes = -(-classes // part) * part

    def packed(pieces):
        spans, start = {}, 0
        for name, piece in pieces.items():
            spans[name] = slice(start, start + piece.shape[0])
            start += piece.shape[0]
        return jnp.concatenate(list(pieces.values()), axis=0), spans

    first_mine, first_spans = packed(
        {
            "reduce": to_narrow(row_slice(reduce_weight, 0)),
            "params": params,
            "dilate": row_slice(dilate_weight, 1),
        }
    )
    first_all, _ = ring.gather(first_mine, True)
    reduce_full = from_narrow(first_all[:, first_spans["reduce"]]).reshape(nbatch * wide_part, mid)
    params_all = first_all[:, first_spans["params"]]
    dilate_full = first_all[:, first_spans["dilate"]].reshape(nbatch * held, part)

    def all_params(pair, size):
        return jnp.transpose(params_all[:, pair : pair + 2, :size], (1, 0, 2)).reshape(2, nbatch * size)

    reduce_gain, reduce_bias = row_slice(all_params(0, mid_held), 1)
    dilate_gain, dilate_bias = row_slice(all_params(2, mid_held), 1)
    expand_gain, expand_bias = all_params(4, wide_part)

    spread_by_kernel = wide_part == 64 and part % 128 == 0

    def spread_wide(array):
        if spread_by_kernel:
            (blocks,) = single_call(
                spread_kernel, (here, array), [(nrows, quarter, wide // nrows)], [], 1
            )
            blocks = [blocks[key] for key in range(4)]
        else:
            split_blocks = jnp.transpose(array.reshape(quarter, nbatch, nrows, wide_part), (2, 0, 1, 3))
            split_blocks = split_blocks.reshape(nrows, quarter, nbatch * wide_part)
            blocks = [
                lax.dynamic_index_in_dim(split_blocks, row ^ key, 0, keepdims=False)
                for key in range(4)
            ]
        return jnp.concatenate(in_order(exchange_keyed(blocks), row), axis=0)

    def collect_wide(array):
        blocks = array.reshape(nrows, quarter, nbatch * wide_part)
        got = exchange_keyed(
            [lax.dynamic_index_in_dim(blocks, row ^ key, 0, keepdims=False) for key in range(4)]
        )
        if spread_by_kernel:
            (out,) = single_call(
                collect_kernel,
                (here, *got),
                [(quarter, wide)],
                [(nrows, quarter, wide // nrows)],
                1,
            )
        else:
            out = jnp.stack(in_order(got, row)).reshape(nrows, quarter, nbatch, wide_part)
            out = jnp.transpose(out, (1, 2, 0, 3))
        return out.reshape(1, local_height, breadth, wide)

    def image_of(array):
        return array.reshape(height, breadth, array.shape[-1])

    features, _ = lax.optimization_barrier((features, (heads_mine, segment_pair_mine, first_mine)))
    inputs = spread_wide(features.reshape(quarter, wide))

    valid = depth_valid.astype(jnp.float32).reshape(quarter, 1)
    keep, give = single_call(
        split_product_kernel,
        (here, inputs, reduce_full, jnp.full((1, part), jnp.sum(valid))),
        [(2, pixels + 8, part)] * 2,
        [(pixels, mid)],
        2 * pixels * mid * mid,
    )
    mine_terms, got_terms = scatter_end(keep, give)
    pre_reduce = mine_terms + got_terms
    valid_row = pre_reduce[pixels]
    pre_reduce = pre_reduce[:pixels]
    total_one = sum_batch(jnp.concatenate([sums_of(pre_reduce, pre_reduce), valid_row[None]]))
    scale = valid * (count / total_one[2, 0])
    hat_one, normed_one, inverse_one = norm_forward(
        pre_reduce, total_one, reduce_gain, reduce_bias, count
    )
    pre_dilate, mid_in = joined_conv(
        here, gather_keyed(image_of(jax.nn.silu(normed_one))), dilate_full, 2
    )
    hat_two, normed_two, inverse_two = norm_forward(
        pre_dilate, sum_batch(sums_of(pre_dilate, pre_dilate)), dilate_gain, dilate_bias, count
    )

    beside = mid // class_lanes
    square_mine, square_spans = packed(
        {
            "depth_gate": depth_gate,
            "segment_gate": segment_gate,
            "expand": expand_mine,
            "classifier": jnp.pad(classifier, ((0, 0), (0, class_lanes - classes)))
            .reshape(beside, mid_held // beside, class_lanes)
            .transpose(1, 0, 2)
            .reshape(mid_held // beside, mid),
        }
    )
    square_mine, inverse_two = lax.optimization_barrier((square_mine, inverse_two))
    feats, mid_out, pairs = joined_conv(
        here, gather_keyed(image_of(jax.nn.silu(normed_two))), heads_full, 1, True
    )
    square_all, feats = ring.gather(square_mine, False, feats, 2)
    depth_gate_w, segment_gate_w, expand_w = [
        square_all[:, square_spans[name]].reshape(mid, mid)
        for name in ("depth_gate", "segment_gate", "expand")
    ]
    classifier_w = (
        square_all[:, square_spans["classifier"]]
        .reshape(nbatch, mid_held // beside, beside, class_lanes)
        .transpose(0, 2, 1, 3)
        .reshape(mid, class_lanes)
    )
    feats_image = image_of(feats)

    segment_mine, segment_got = scatter_end(*note_forward(here, feats_image, 1, segment_pair_w))
    pairs_got = jnp.stack(exchange_keyed([pairs[key] for key in range(4)]))
    depth_cotangent = depth_cotangent.reshape(quarter, mid)
    both, one_map = (2 * quarter, mid), (quarter, mid)
    feat_pair, open_pair, d_depth_note = single_call(
        gates_kernel,
        (here, pairs_got, mix, depth_gate_w, segment_gate_w, depth_cotangent, scale),
        [both, both, one_map],
        [both],
        8 * quarter * mid * mid,
    )
    feat_pair, open_pair, segment_mine = lax.optimization_barrier((feat_pair, open_pair, segment_mine))

    def segment_body(*refs):
        segment_kernel(classes, *refs)

    segment_stream, d_segment_note, direct_segment, segment_gate_grad, classifier_grad = single_call(
        segment_body,
        (
            here,
            segment_mine,
            segment_got,
            feat_pair[quarter:],
            open_pair[quarter:],
            labels.reshape(quarter, 1),
            classifier_w,
            segment_gate_w,
            mix,
        ),
        [one_map, one_map, (4, quarter, part), (mid, mid), (mid, class_lanes)],
        [one_map],
        8 * quarter * mid * mid,
    )

    def lines(array):
        return array.reshape(local_height, breadth, mid)

    depth_pair_grad, d_depth_image = note_grad(here, feats, 0, gather_keyed(lines(d_depth_note)), run)
    depth_pair_sums = lax.psum_scatter(
        regroup(depth_pair_grad, grain).reshape(-1, mid), "batch", scatter_dimension=0, tiled=True
    )
    segment_pair_grad, d_segment_image = note_grad(
        here, feats, 1, gather_keyed(lines(d_segment_note)), run
    )
    segment_pair_sums = lax.psum_scatter(
        regroup(segment_pair_grad, grain).reshape(-1, mid), "batch", scatter_dimension=0, tiled=True
    )
    feats_late, d_segment_image, depth_pair_grad = lax.optimization_barrier(
        (feats_image, d_segment_image, depth_pair_grad)
    )
    depth_mine, depth_got = scatter_end(*note_forward(here, feats_late, 0, depth_pair_w))
    depth_stream, direct_both, depth_gate_grad = single_call(
        depth_kernel,
        (
            here,
            depth_mine,
            depth_got,
            feat_pair[:quarter],
            open_pair[:quarter],
            depth_cotangent,
            scale,
            depth_gate_w,
            mix,
            direct_segment,
        ),
        [one_map, (4, 2 * quarter, part), (mid, mid)],
        [one_map],
        8 * quarter * mid * mid,
    )
    direct_got = jnp.stack(exchange_keyed([direct_both[key] for key in range(4)]))
    flat_mid_out = mid_out.reshape(pixels, mid)
    heads_grad, d_feats = heads_grad_of(
        here,
        flat_mid_out,
        image_of(note_back(d_depth_image, depth_pair_w)),
        image_of(note_back(d_segment_image, segment_pair_w)),
        direct_got.reshape(4, 2 * local_height, breadth, part),
    )
    heads_sums, _ = ring.scatter(heads_grad.reshape(nbatch, held, nrows * part), True)

    expand_input, _ = lax.optimization_barrier((flat_mid_out, segment_pair_grad))
    block_cotangent, _ = lax.optimization_barrier((block_cotangent, feats))
    cotangent = spread_wide(block_cotangent.reshape(quarter, wide))
    pre_expand = product(expand_input, expand_w, 1, 0)
    hat_three, normed_three, inverse_three = norm_forward(
        pre_expand, sum_batch(sums_of(pre_expand, pre_expand)), expand_gain, expand_bias, count
    )
    summed = normed_three + inputs
    block_out = collect_wide(jax.nn.silu(summed))
    d_summed = cotangent * silu_grad(summed)
    d_pre_expand, expand_sums = norm_backward(
        d_summed, hat_three, inverse_three, expand_gain, count, False
    )
    expand_grad = product(flat_mid_out, d_pre_expand, 0, 0).reshape(nbatch, mid_held, mid)

    gate_terms = jnp.stack(
        [
            depth_gate_grad,
            segment_gate_grad,
            jnp.pad(classifier_grad, ((0, 0), (0, mid - class_lanes))),
        ]
    )
    gate_rows = mid_held // nrows
    gate_terms = jnp.transpose(gate_terms.reshape(3, nbatch, nrows, gate_rows, mid), (2, 1, 0, 3, 4))
    gate_sums = scatter_rows(gate_terms, row).reshape(nbatch, 3 * gate_rows, mid)

    mine_terms, got_terms = scatter_end(
        *conv_back(here, d_feats, heads_full, 1, product(d_pre_expand, expand_w, 1, 1))
    )
    d_pre_dilate, dilate_sums = norm_backward(
        (mine_terms + got_terms) * silu_grad(normed_two), hat_two, inverse_two, dilate_gain, count, True
    )
    d_dilate_image = image_of(d_pre_dilate)
    mine_terms, got_terms = scatter_end(*conv_back(here, d_dilate_image, dilate_full, 2))
    d_pre_reduce, reduce_sums = norm_backward(
        (mine_terms + got_terms) * silu_grad(normed_one), hat_one, inverse_one, reduce_gain, count, True
    )
    reduce_grad, features_back = single_call(
        reduce_back_kernel,
        (here, *gather_keyed(d_pre_reduce), inputs, reduce_full, d_summed),
        [(mid, mid), (pixels, mid)],
        [(pixels, mid)],
        4 * pixels * mid * mid,
    )
    dilate_grad = conv_grad(mid_in.reshape(pixels, mid), d_dilate_image, 2).reshape(
        nbatch, held, part
    )
    narrow = held // nrows
    square_grad = jnp.concatenate(
        [
            jnp.concatenate(
                [dilate_grad[:, i * narrow : (i + 1) * narrow] for i in range(nrows)], axis=2
            ),
            expand_grad,
            gate_sums,
        ],
        axis=1,
    )
    square_grad, reduce_sums, depth_pair_sums = lax.optimization_barrier(
        (square_grad, reduce_sums, depth_pair_sums)
    )
    square_sums, _ = ring.scatter(square_grad, False)
    reduce_out, segment_pair_sums = ring.scatter(
        reduce_grad.reshape(nbatch, wide_part, mid), True, segment_pair_sums, 2
    )
    features_grad = collect_wide(features_back)

    depth_pair_out, segment_pair_out = [
        jnp.stack(gather_rows(sums * factor, row)).reshape(nrows, groups, 2, grain, mid)
        for sums in (depth_pair_sums, segment_pair_sums)
    ]

    def message_out(pair_got, index):
        return jnp.transpose(pair_got[:, :, index], (1, 0, 2, 3)).reshape(held, mid)

    segment_out, normal_out, depth_out, contour_out = single_call(
        heads_out_kernel,
        (here, *gather_keyed(heads_sums * factor), mix),
        [(held, mid)] * 4,
        [(held, mid)],
        8 * held * mid * mid,
    )

    expand_mine_sums = lax.dynamic_slice_in_dim(expand_sums, batch * wide_part, wide_part, 1)
    norm_sums = jnp.concatenate(
        [
            jnp.pad(sums, ((0, 0), (0, mid - sums.shape[1])))
            for sums in (reduce_sums, dilate_sums, expand_mine_sums)
        ],
        axis=0,
    )
    small = jnp.concatenate([square_sums, jnp.pad(norm_sums, ((0, 2), (0, 0)))], axis=0) * factor
    small_got = gather_rows(small, row)
    squares_got = jnp.stack([block[narrow : narrow + mid_held + 3 * gate_rows] for block in small_got])
    dilate_out = jnp.concatenate(
        [
            jnp.concatenate(
                [block[:narrow, i * part : (i + 1) * part] for i in range(nrows)], axis=0
            )
            for block in small_got
        ],
        axis=1,
    )
    expand_out = jnp.transpose(
        squares_got[:, :mid_held].reshape(nrows, mid_held, nbatch, wide_part), (1, 2, 0, 3)
    ).reshape(mid_held, wide)

    def gate_out(index):
        start = mid_held + index * gate_rows
        return squares_got[:, start : start + gate_rows].reshape(mid_held, mid)

    norms_got = [block[-8:] for block in small_got]

    def norm_out(start):
        full = jnp.concatenate([block[start : start + 2, :part] for block in norms_got], axis=1)
        return lax.dynamic_slice_in_dim(full, batch * mid_held, mid_held, 1)

    expand_norm_out = jnp.concatenate([block[4:6, :wide_part] for block in norms_got], axis=1)
    reduce_got = jnp.concatenate(gather_rows(reduce_out * factor, row), axis=0)

    return (
        block_out,
        depth_stream.reshape(1, local_height, breadth, mid),
        segment_stream.reshape(1, local_height, breadth, mid),
        features_grad,
        reduce_got,
        norm_out(0),
        dilate_out,
        norm_out(2),
        expand_out,
        expand_norm_out,
        depth_out,
        segment_out,
        normal_out,
        contour_out,
        message_out(depth_pair_out, 0),
        message_out(segment_pair_out, 0),
        message_out(depth_pair_out, 1),
        message_out(segment_pair_out, 1),
        gate_out(0),
        gate_out(1),
        gate_out(2)[:, :classes],
    )


def solution(mesh):
    pixels = P("batch", "rows", None, None)
    plane = P("batch", "rows", None)
    weight = P("batch", None)
    norm = P(None, "batch")
    in_specs = (
        (pixels, weight, norm, weight, norm, weight, norm) + (weight,) * 11 + (plane, plane, pixels, pixels)
    )
    out_specs = (pixels,) * 4 + (weight, norm) * 3 + (weight,) * 11
    return jax.shard_map(shards, mesh=mesh, in_specs=in_specs, out_specs=out_specs, check_vma=False)
```

time: 910 us -> 847 us (0.931)
  Pallas kernels: 108 us -> 183 us
  waiting for transfers between devices: 396 us -> 324 us
  local copies, waits for them, and re-layouts: 112 us -> 73 us
  matrix products: 28.9 us -> 7.94 us
    pallas_call x9 -> x22, Pallas kernels: 108 us -> 183 us  [the longest x10 44.4 us: single_call(): kernel_call(body, (1,), [SCALAR] + [whole_spec(arg.shape) for arg in args...]
    ppermute x14 -> x10, waiting for transfers between devices: 103 us -> 47.6 us  [scatter(): falling = lax.ppermute(falling, 'batch', self.down)]
    ppermute x21 -> x26, waiting for transfers between devices: 24.1 us -> 65.9 us  [swap(): return lax.ppermute(block, 'batch', [(i, i ^ mask) for i in range(size)])]
    ppermute x4 -> x7, waiting for transfers between devices: 69.9 us -> 38.2 us  [gather(): rising = lax.ppermute(rising, 'batch', self.up)]
    ppermute x14 -> x11, waiting for transfers between devices: 27.8 us -> 4.08 us  [scatter(): rising = lax.ppermute(rising, 'batch', self.up)]
    unnamed x257 -> x180, local copies, waits for them, and re-layouts: 40.3 us -> 17.8 us
    dot_general x25 -> x7, matrix products: 28.9 us -> 7.94 us  [product(): lax.dot_general(left, right, (((left_dim,), (right_dim,)), ((), ())), pre...]
    another operation x14 -> x5, local copies, waits for them, and re-layouts: 19.7 us -> 0.63 us  [the longest x1 0.57 us: shards(): jnp.stack([depth_gate_grad, segment_gate_grad, jnp.pad(classifier_grad, (...]
  transfers between devices with their start and end apart: 119 -> 126, of which waited for: 44 -> 50; matrix products, arithmetic and copies ran while one was open for 18% -> 14% of each run, Pallas kernels for 12% -> 22%
where the time goes in v2:
time: 847 us; the launch traced here: 835 us
  waiting for transfers between devices  324 us (38%)
  Pallas kernels  183 us (22%)
  starting transfers between devices  161 us (19%)
  local copies, waits for them, and re-layouts  73 us (9%)
  other arithmetic  53.9 us (6%)
  between operations  32 us (4%)
    ppermute x60, waiting for transfers between devices, swap_rows(): return lax.ppermute(block, 'rows', [(i, i ^ mask) for i in range(size)])  112 us
    ppermute x60, starting transfers between devices, swap_rows(): return lax.ppermute(block, 'rows', [(i, i ^ mask) for i in range(size)])  80 us
    ppermute x26, waiting for transfers between devices, swap(): return lax.ppermute(block, 'batch', [(i, i ^ mask) for i in range(size)])  65.9 us
    ppermute x7, waiting for transfers between devices, gather(): falling = lax.ppermute(falling, 'batch', self.down)  55.7 us
    ppermute x10, waiting for transfers between devices, scatter(): falling = lax.ppermute(falling, 'batch', self.down)  47.6 us
    ppermute x26, starting transfers between devices, swap(): return lax.ppermute(block, 'batch', [(i, i ^ mask) for i in range(size)])  45.7 us
    pallas_call x10, Pallas kernels, single_call(): kernel_call(body, (1,), [SCALAR] + [whole_spec(arg.shape) for arg in args...  44.4 us
    ppermute x7, waiting for transfers between devices, gather(): rising = lax.ppermute(rising, 'batch', self.up)  38.2 us
  transfers between devices with their start and end apart: 126, of which 50 were waited for; matrix products, arithmetic and copies ran while one was open for 14% of the time, Pallas kernels for 22%

profile of v2, /device:TPU:1, one launch (start us, length us, event | category | flops | bytes accessed | tf_op | source)
XLA Modules:
  0.0 835.2 jit_solution(3814268094619564301)
XLA Ops:
  48.2 28.6 %collective-permute-done.6 = f32[840,128]{1,0:T(8,128)S(1)} collective-permute-done((f32[840,128]{1,0:T(8,128)S(1)}, f32[840,128]{1,0:T(8,128)S(1)}, u32[]{:S(2)}, u32[]{:S(2)}) %collective-permute-start.6) | collective-permute-done | bytes 430112 | tf_op jit(solution)/shard_map/ppermute | solution.py:653
  78.4 8.9 %collective-permute-done.7 = f32[840,128]{1,0:T(8,128)S(1)} collective-permute-done((f32[840,128]{1,0:T(8,128)S(1)}, f32[840,128]{1,0:T(8,128)S(1)}, u32[]{:S(2)}, u32[]{:S(2)}) %collective-permute-start.7) | collective-permute-done | bytes 430112 | tf_op jit(solution)/shard_map/ppermute | solution.py:650
  88.7 17.4 %collective-permute-done.9 = f32[840,128]{1,0:T(8,128)S(1)} collective-permute-done((f32[840,128]{1,0:T(8,128)S(1)}, f32[840,128]{1,0:T(8,128)S(1)}, u32[]{:S(2)}, u32[]{:S(2)}) %collective-permute-start.9) | collective-permute-done | bytes 430112 | tf_op jit(solution)/shard_map/ppermute | solution.py:650
  113.4 10.3 %collective-permute-start.10 = (f32[2,648,128]{2,1,0:T(8,128)}, f32[2,648,128]{2,1,0:T(8,128)S(1)}, u32[]{:S(2)}, u32[]{:S(2)}) collective-permute-start(f32[2,648,128]{2,1,0:T(8,128)} %get-tuple-element.80), channel_id=1, source_target_pairs={{0,1},{1,0},{2,3},{3,2},{4,5},{5,4},{6,7},{7,6},{8,9},{9,8},{10,11... | collective-permute-start | bytes 1990664 | tf_op jit(solution)/shard_map/ppermute | solution.py:559
  129.5 6.8 collective-permute-done.11
  136.4 12.4 %collective-permute-start.12 = (f32[3,128]{1,0:T(4,128)S(1)}, f32[3,128]{1,0:T(4,128)S(1)}, u32[]{:S(2)}, u32[]{:S(2)}) collective-permute-start(f32[3,128]{1,0:T(4,128)S(1)} %pad_maximum_fusion.19), channel_id=1, source_target_pairs={{0,4},{4,0},{8,12},{12,8},{16,20},{20,16},{24,28},{28,24},{1,5},{5... | collective-permute-start | bytes 4616 | tf_op jit(solution)/shard_map/ppermute | solution.py:609
  176.8 10.0 %shard_map.384 = (f32[640,128]{1,0:T(8,128)}, f32[16,40,512]{2,1,0:T(8,128)}) custom-call(s32[1]{0:T(128)} %bitcast.row_ref.refs_0_, f32[16,40,128]{2,1,0:T(8,128)} %bitcast.458, f32[16,40,128]{2,1,0:T(8,128)} %copy-done.77, f32[16,40,128]{2,1,0:T(8,128)} %copy-done.75, f32[16,40,128]{2,1,0:T(8,128)} %copy-done.82, f32[4608,128]{1,0:T(8,128)} %bitcast.422), custom_call_target="tpu_custom_call" | custom-call | flops 2264924160 | bytes 12582912 | tf_op jit(solution)/shard_map/pallas_call | solution.py:431
  218.6 15.1 %shard_map.385 = (f32[640,512]{1,0:T(8,128)}, f32[16,40,512]{2,1,0:T(8,128)}, f32[4,320,128]{2,1,0:T(8,128)}) custom-call(s32[1]{0:T(128)} %bitcast.row_ref.refs_0_, f32[16,40,128]{2,1,0:T(8,128)} %bitcast.455, f32[16,40,128]{2,1,0:T(8,128)} %copy-done.73, f32[16,40,128]{2,1,0:T(8,128)} %copy-done.72, f32[16,40,128]{2,1,0:T(8,128)} %collective-permute-done.23.four, ...), custom_call_target="tpu_custom_call" | custom-call | flops 9059696640 | bytes 12582912 | tf_op jit(solution)/shard_map/pallas_call | solution.py:431
  270.1 13.5 %collective-permute-done.32 = f32[208,512]{1,0:T(8,128)S(1)} collective-permute-done((f32[208,512]{1,0:T(8,128)S(1)}, f32[208,512]{1,0:T(8,128)S(1)}, u32[]{:S(2)}, u32[]{:S(2)}) %collective-permute-start.32) | collective-permute-done | bytes 426016 | tf_op jit(solution)/shard_map/ppermute | solution.py:653
  285.8 8.1 collective-permute-done.33
  315.1 10.4 %shard_map.391 = (f32[72,2,16,512]{3,2,1,0:T(8,128)}, f32[16,40,512]{2,1,0:T(8,128)}) custom-call(s32[1]{0:T(128)} %bitcast.row_ref.refs_0_, f32[640,512]{1,0:T(8,128)} %get-tuple-element.85.input_ref, f32[4,40,512]{2,1,0:T(8,128)} %bitcast.535, f32[4,40,512]{2,1,0:T(8,128)} %copy-done.81, f32[4,40,512]{2,1,0:T(8,128)} %copy-done.79, f32[4,40,512]{2,1,0:T(8,128)} %copy-done.84), custom_call_target="tpu_custom_call" | custom-call | flops 4529848320 | bytes 12582912 | tf_op jit(solution)/shard_map/pallas_call | solution.py:540
  325.6 10.5 %shard_map.387 = (f32[2,160,512]{2,1,0:T(8,128)}, f32[2,160,512]{2,1,0:T(8,128)}) custom-call(s32[1]{0:T(128)} %bitcast.row_ref.refs_0_, f32[16,40,512]{2,1,0:T(8,128)} %bitcast.537, f32[72,2,16,512]{3,2,1,0:T(8,128)} %bitcast.524), custom_call_target="tpu_custom_call" | custom-call | flops 4529848320 | bytes 12582912 | tf_op jit(solution)/shard_map/pallas_call | solution.py:504
  370.5 10.4 %shard_map.389 = (f32[72,2,16,512]{3,2,1,0:T(8,128)}, f32[16,40,512]{2,1,0:T(8,128)}) custom-call(s32[1]{0:T(128)} %bitcast.row_ref.refs_0_, f32[640,512]{1,0:T(8,128)} %get-tuple-element.85.input_ref, f32[4,40,512]{2,1,0:T(8,128)} %bitcast.532, f32[4,40,512]{2,1,0:T(8,128)} %copy-done.80, f32[4,40,512]{2,1,0:T(8,128)} %copy-done.78, f32[4,40,512]{2,1,0:T(8,128)} %copy-done.83), custom_call_target="tpu_custom_call" | custom-call | flops 4529848320 | bytes 12582912 | tf_op jit(solution)/shard_map/pallas_call | solution.py:540
  394.0 7.5 collective-permute-done.53
  406.0 10.5 %shard_map.392 = (f32[2,160,512]{2,1,0:T(8,128)}, f32[2,160,512]{2,1,0:T(8,128)}) custom-call(s32[1]{0:T(128)} %bitcast.row_ref.refs_0_, f32[16,40,512]{2,1,0:T(8,128)} %bitcast.538, f32[72,2,16,512]{3,2,1,0:T(8,128)} %bitcast.526), custom_call_target="tpu_custom_call" | custom-call | flops 4529848320 | bytes 12582912 | tf_op jit(solution)/shard_map/pallas_call | solution.py:504
  420.7 10.8 %shard_map.394 = f32[640,256]{1,0:T(8,128)} custom-call(f32[16,40,512]{2,1,0:T(8,128)} %get-tuple-element.109.note_ref, f32[72,2,16,512]{3,2,1,0:T(8,128)} %bitcast.527), custom_call_target="tpu_custom_call" | custom-call | flops 4529848320 | bytes 12582912 | tf_op jit(solution)/shard_map/pallas_call | solution.py:522
  434.4 10.8 %shard_map.395 = f32[640,256]{1,0:T(8,128)} custom-call(f32[16,40,512]{2,1,0:T(8,128)} %get-tuple-element.110.note_ref, f32[72,2,16,512]{3,2,1,0:T(8,128)} %bitcast.525), custom_call_target="tpu_custom_call" | custom-call | flops 4529848320 | bytes 12582912 | tf_op jit(solution)/shard_map/pallas_call | solution.py:522
  463.0 16.6 %shard_map.396 = (f32[4608,512]{1,0:T(8,128)}, f32[16,40,512]{2,1,0:T(8,128)}) custom-call(s32[1]{0:T(128)} %bitcast.row_ref.refs_0_, f32[640,512]{1,0:T(8,128)} %bitcast.404, f32[16,40,256]{2,1,0:T(8,128)} %bitcast.539, f32[16,40,256]{2,1,0:T(8,128)} %bitcast.540, f32[4,8,40,128]{3,2,1,0:T(8,128)} %pad_maximum_fusion.9.direct_ref), custom_call_target="tpu_custom_call" | custom-call | flops 9059696640 | bytes 12582912 | tf_op jit(solution)/shard_map/pallas_call | solution.py:487
  479.7 14.9 %shard_map.398 = (f32[2,640,128]{2,1,0:T(8,128)}, f32[2,640,128]{2,1,0:T(8,128)}) custom-call(s32[1]{0:T(128)} %bitcast.row_ref.refs_0_, f32[16,40,512]{2,1,0:T(8,128)} %get-tuple-element.112.refs_1_, f32[4608,512]{1,0:T(8,128)} %all-gather.4.cloned.1.call-done.weight_ref.refs_2_, f32[640,512]{1,0:T(8,128)} %fusion.29.refs_3_), custom_call_target="tpu_custom_call" | custom-call | flops 9059696640 | bytes 12582912 | tf_op jit(solution)/shard_map/pallas_call | solution.py:452
  514.1 29.8 %collective-permute-done.67 = f32[2,128]{1,0:T(2,128)S(1)} collective-permute-done((f32[2,128]{1,0:T(2,128)S(1)}, f32[2,128]{1,0:T(2,128)S(1)}, u32[]{:S(2)}, u32[]{:S(2)}) %collective-permute-start.67) | collective-permute-done | bytes 1056 | tf_op jit(solution)/shard_map/ppermute | solution.py:609
  549.0 9.8 %shard_map.399 = (f32[2,640,128]{2,1,0:T(8,128)}, f32[2,640,128]{2,1,0:T(8,128)}) custom-call(s32[1]{0:T(128)} %bitcast.row_ref.refs_0_, f32[16,40,128]{2,1,0:T(8,128)} %bitcast.451, f32[4608,128]{1,0:T(8,128)} %bitcast.423), custom_call_target="tpu_custom_call" | custom-call | flops 2264924160 | bytes 12582912 | tf_op jit(solution)/shard_map/pallas_call | solution.py:452
  580.6 20.6 %collective-permute-done.109 = f32[576,512]{1,0:T(8,128)} collective-permute-done((f32[576,512]{1,0:T(8,128)}, f32[576,512]{1,0:T(8,128)}, u32[]{:S(2)}, u32[]{:S(2)}) %collective-permute-start.109) | collective-permute-done | bytes 1179680 | tf_op jit(solution)/shard_map/ppermute | solution.py:674
  614.5 18.1 %collective-permute-done.75 = f32[2,128]{1,0:T(2,128)S(1)} collective-permute-done((f32[2,128]{1,0:T(2,128)S(1)}, f32[2,128]{1,0:T(2,128)S(1)}, u32[]{:S(2)}, u32[]{:S(2)}) %collective-permute-start.75) | collective-permute-done | bytes 1056 | tf_op jit(solution)/shard_map/ppermute | solution.py:609
  646.9 8.8 %shard_map.402 = f32[4608,128]{1,0:T(8,128)} custom-call(f32[640,512]{1,0:T(8,128)} %bitcast.536, f32[16,40,128]{2,1,0:T(8,128)} %bitcast.452), custom_call_target="tpu_custom_call" | custom-call | flops 2264924160 | bytes 12582912 | tf_op jit(solution)/shard_map/pallas_call | solution.py:471
  657.5 8.3 collective-permute-done.94
  666.2 6.6 collective-permute-done.78.three
  690.3 13.5 %collective-permute-done.84 = f32[64,512]{1,0:T(8,128)S(1)} collective-permute-done((f32[64,512]{1,0:T(8,128)S(1)}, f32[64,512]{1,0:T(8,128)S(1)}, u32[]{:S(2)}, u32[]{:S(2)}) %collective-permute-start.84) | collective-permute-done | bytes 131104 | tf_op jit(solution)/shard_map/ppermute | solution.py:674
  710.6 8.7 %collective-permute-done.43.three = f32[160,512]{1,0:T(8,128)} collective-permute-done((f32[160,512]{1,0:T(8,128)}, f32[160,512]{1,0:T(8,128)}, u32[]{:S(2)}, u32[]{:S(2)}) %collective-permute-start.43) | collective-permute-done | bytes 327712 | tf_op jit(solution)/shard_map/ppermute | solution.py:559
  752.5 11.3 %collective-permute-done.89 = f32[64,512]{1,0:T(8,128)S(1)} collective-permute-done((f32[64,512]{1,0:T(8,128)S(1)}, f32[64,512]{1,0:T(8,128)S(1)}, u32[]{:S(2)}, u32[]{:S(2)}) %collective-permute-start.89) | collective-permute-done | bytes 131104 | tf_op jit(solution)/shard_map/ppermute | solution.py:674
  769.0 11.2 %collective-permute-done.90 = f32[64,512]{1,0:T(8,128)} collective-permute-done((f32[64,512]{1,0:T(8,128)S(1)}, f32[64,512]{1,0:T(8,128)}, u32[]{:S(2)}, u32[]{:S(2)}) %collective-permute-start.90) | collective-permute-done | bytes 131104 | tf_op jit(solution)/shard_map/ppermute | solution.py:559
  786.7 7.8 shard_map.403
  803.6 9.4 %collective-permute-done.102 = f32[264,512]{1,0:T(8,128)S(1)} collective-permute-done((f32[264,512]{1,0:T(8,128)S(1)}, f32[264,512]{1,0:T(8,128)S(1)}, u32[]{:S(2)}, u32[]{:S(2)}) %collective-permute-start.102) | collective-permute-done | bytes 540704 | tf_op jit(solution)/shard_map/ppermute | solution.py:559
  (617 shorter events, 405.8 us)
Async XLA Ops:
  7.2 211.4 %all-gather.4.cloned.1.call-start = ((), (), s32[]{:S(2)}) async-start(), calls=%async_computation.2 | async-start | bytes 10616832 | tf_op jit(solution)/shard_map/all_gather | solution.py:774
  12.4 313.2 %all-gather.6.cloned.1.call-start = ((), (), s32[]{:S(2)}) async-start(), calls=%async_computation.3 | async-start | bytes 5308416 | tf_op jit(solution)/shard_map/all_gather | solution.py:788
  14.5 391.5 %all-gather.8.cloned.1.call-start = ((), (), s32[]{:S(2)}) async-start(), calls=%async_computation.4 | async-start | bytes 5308416 | tf_op jit(solution)/shard_map/all_gather | solution.py:788
  18.7 27.7 %collective-permute-start.4 = (f32[840,128]{1,0:T(8,128)S(1)}, f32[840,128]{1,0:T(8,128)S(1)}, u32[]{:S(2)}, u32[]{:S(2)}) collective-permute-start(f32[840,128]{1,0:T(8,128)S(1)} %dynamic-slice_dynamic-update-slice_fusion), channel_id=1, source_target_pairs={{8,0},{16,8},{24,16},{28,24},{20,28},{12,20},{4,12},{0,4},{9,1},{1... | collective-permute-start | bytes 1290248 | tf_op jit(solution)/shard_map/ppermute | solution.py:653
  46.4 30.5 %collective-permute-start.6 = (f32[840,128]{1,0:T(8,128)S(1)}, f32[840,128]{1,0:T(8,128)S(1)}, u32[]{:S(2)}, u32[]{:S(2)}) collective-permute-start(f32[840,128]{1,0:T(8,128)S(1)} %collective-permute-done.4), channel_id=1, source_target_pairs={{8,0},{16,8},{24,16},{28,24},{20,28},{12,20},{4,12},{0,4},{9,1},{1... | collective-permute-start | bytes 1290248 | tf_op jit(solution)/shard_map/ppermute | solution.py:653
  48.0 28.8 %collective-permute-start.5 = (f32[840,128]{1,0:T(8,128)S(1)}, f32[840,128]{1,0:T(8,128)S(1)}, u32[]{:S(2)}, u32[]{:S(2)}) collective-permute-start(f32[840,128]{1,0:T(8,128)S(1)} %collective-permute-done.3), channel_id=1, source_target_pairs={{0,8},{8,16},{16,24},{24,28},{28,20},{20,12},{12,4},{4,0},{1,9},{9... | collective-permute-start | bytes 1290248 | tf_op jit(solution)/shard_map/ppermute | solution.py:650
  149.7 534.9 %reduce-scatter.5.cloned.1.call-start = ((), (), s32[]{:S(2)}) async-start(), calls=%async_computation.6 | async-start | bytes 5308416 | tf_op jit(solution)/shard_map/reduce_scatter | solution.py:964
  203.7 30.0 %collective-permute-start.25 = (f32[208,512]{1,0:T(8,128)S(1)}, f32[208,512]{1,0:T(8,128)S(1)}, u32[]{:S(2)}, u32[]{:S(2)}) collective-permute-start(f32[208,512]{1,0:T(8,128)S(1)} %pad_maximum_fusion.13), channel_id=1, source_target_pairs={{8,0},{16,8},{24,16},{28,24},{20,28},{12,20},{4,12},{0,4},{9,1},{1... | collective-permute-start | bytes 1277960 | tf_op jit(solution)/shard_map/ppermute | solution.py:653
  236.0 31.9 %collective-permute-start.30 = (f32[208,512]{1,0:T(8,128)S(1)}, f32[208,512]{1,0:T(8,128)S(1)}, u32[]{:S(2)}, u32[]{:S(2)}) collective-permute-start(f32[208,512]{1,0:T(8,128)S(1)} %collective-permute-done.25), channel_id=1, source_target_pairs={{8,0},{16,8},{24,16},{28,24},{20,28},{12,20},{4,12},{0,4},{9,1},{1... | collective-permute-start | bytes 1277960 | tf_op jit(solution)/shard_map/ppermute | solution.py:653
  325.5 385.1 %reduce-scatter.3.cloned.1.call-start = ((), (), s32[]{:S(2)}) async-start(), calls=%async_computation.5 | async-start | bytes 5308416 | tf_op jit(solution)/shard_map/reduce_scatter | solution.py:970
  501.7 61.5 %collective-permute-start.105 = (f32[576,512]{1,0:T(8,128)}, f32[576,512]{1,0:T(8,128)}, u32[]{:S(2)}, u32[]{:S(2)}) collective-permute-start(f32[576,512]{1,0:T(8,128)} %get-tuple-element.202), channel_id=1, source_target_pairs={{0,8},{8,16},{16,24},{24,28},{28,20},{20,12},{12,4},{4,0},{1,9},{9... | collective-permute-start | bytes 3538952 | tf_op jit(solution)/shard_map/ppermute | solution.py:670
  507.6 36.4 %collective-permute-start.67 = (f32[2,128]{1,0:T(2,128)S(1)}, f32[2,128]{1,0:T(2,128)S(1)}, u32[]{:S(2)}, u32[]{:S(2)}) collective-permute-start(f32[2,128]{1,0:T(2,128)S(1)} %pad_maximum_fusion.22), channel_id=1, source_target_pairs={{0,28},{4,24},{8,20},{12,16},{16,12},{20,8},{24,4},{28,0},{1,29},{... | collective-permute-start | bytes 3080 | tf_op jit(solution)/shard_map/ppermute | solution.py:609
  508.6 35.4 %collective-permute-start.66 = (f32[2,128]{1,0:T(2,128)S(1)}, f32[2,128]{1,0:T(2,128)S(1)}, u32[]{:S(2)}, u32[]{:S(2)}) collective-permute-start(f32[2,128]{1,0:T(2,128)S(1)} %pad_maximum_fusion.22), channel_id=1, source_target_pairs={{0,24},{4,28},{8,16},{12,20},{16,8},{20,12},{24,0},{28,4},{1,25},{... | collective-permute-start | bytes 3080 | tf_op jit(solution)/shard_map/ppermute | solution.py:609
  510.5 33.5 %collective-permute-start.65 = (f32[2,128]{1,0:T(2,128)S(1)}, f32[2,128]{1,0:T(2,128)S(1)}, u32[]{:S(2)}, u32[]{:S(2)}) collective-permute-start(f32[2,128]{1,0:T(2,128)S(1)} %pad_maximum_fusion.22), channel_id=1, source_target_pairs={{0,20},{4,16},{8,28},{12,24},{16,4},{20,0},{24,12},{28,8},{1,21},{... | collective-permute-start | bytes 3080 | tf_op jit(solution)/shard_map/ppermute | solution.py:609
  511.4 35.2 %collective-permute-start.64 = (f32[2,128]{1,0:T(2,128)S(1)}, f32[2,128]{1,0:T(2,128)S(1)}, u32[]{:S(2)}, u32[]{:S(2)}) collective-permute-start(f32[2,128]{1,0:T(2,128)S(1)} %pad_maximum_fusion.22), channel_id=1, source_target_pairs={{0,16},{4,20},{8,24},{12,28},{16,0},{20,4},{24,8},{28,12},{1,17},{... | collective-permute-start | bytes 3080 | tf_op jit(solution)/shard_map/ppermute | solution.py:609
  561.4 39.8 %collective-permute-start.109 = (f32[576,512]{1,0:T(8,128)}, f32[576,512]{1,0:T(8,128)}, u32[]{:S(2)}, u32[]{:S(2)}) collective-permute-start(f32[576,512]{1,0:T(8,128)} %get-tuple-element.203), channel_id=1, source_target_pairs={{8,0},{16,8},{24,16},{28,24},{20,28},{12,20},{4,12},{0,4},{9,1},{1... | collective-permute-start | bytes 3538952 | tf_op jit(solution)/shard_map/ppermute | solution.py:674
  566.1 35.1 %collective-permute-start.106 = (f32[576,512]{1,0:T(8,128)}, f32[576,512]{1,0:T(8,128)}, u32[]{:S(2)}, u32[]{:S(2)}) collective-permute-start(f32[576,512]{1,0:T(8,128)} %bitcast_add_fusion.5), channel_id=1, source_target_pairs={{0,8},{8,16},{16,24},{24,28},{28,20},{20,12},{12,4},{4,0},{1,9},{9... | collective-permute-start | bytes 3538952 | tf_op jit(solution)/shard_map/ppermute | solution.py:670
  569.7 39.6 %collective-permute-start.93 = (f32[2,8,3,16,512]{4,3,2,1,0:T(8,128)}, f32[2,8,3,16,512]{4,3,2,1,0:T(8,128)}, u32[]{:S(2)}, u32[]{:S(2)}) collective-permute-start(f32[2,8,3,16,512]{4,3,2,1,0:T(8,128)} %dynamic-slice_bitcast_fusion), channel_id=1, source_target_pairs={{0,1},{1,0},{2,3},{3,2},{4,5},{5,4},{6,7},{7,6},{8,9},{9,8},{10,11... | collective-permute-start | bytes 4718600 | tf_op jit(solution)/shard_map/ppermute | solution.py:559
  580.5 30.0 %collective-permute-start.76 = (f32[2,128]{1,0:T(2,128)S(1)}, f32[2,128]{1,0:T(2,128)S(1)}, u32[]{:S(2)}, u32[]{:S(2)}) collective-permute-start(f32[2,128]{1,0:T(2,128)S(1)} %pad_maximum_fusion.23), channel_id=1, source_target_pairs={{0,28},{4,24},{8,20},{12,16},{16,12},{20,8},{24,4},{28,0},{1,29},{... | collective-permute-start | bytes 3080 | tf_op jit(solution)/shard_map/ppermute | solution.py:609
  604.1 37.8 %collective-permute-start.107 = (f32[576,512]{1,0:T(8,128)S(1)}, f32[576,512]{1,0:T(8,128)S(1)}, u32[]{:S(2)}, u32[]{:S(2)}) collective-permute-start(f32[576,512]{1,0:T(8,128)S(1)} %get-tuple-element.200), channel_id=1, source_target_pairs={{0,8},{8,16},{16,24},{24,28},{28,20},{20,12},{12,4},{4,0},{1,9},{9... | collective-permute-start | bytes 3538952 | tf_op jit(solution)/shard_map/ppermute | solution.py:670
  605.3 36.6 %collective-permute-start.110 = (f32[576,512]{1,0:T(8,128)S(1)}, f32[576,512]{1,0:T(8,128)S(1)}, u32[]{:S(2)}, u32[]{:S(2)}) collective-permute-start(f32[576,512]{1,0:T(8,128)S(1)} %get-tuple-element.201), channel_id=1, source_target_pairs={{8,0},{16,8},{24,16},{28,24},{20,28},{12,20},{4,12},{0,4},{9,1},{1... | collective-permute-start | bytes 3538952 | tf_op jit(solution)/shard_map/ppermute | solution.py:674
  636.2 53.2 %collective-permute-start.44 = (f32[160,512]{1,0:T(8,128)}, f32[160,512]{1,0:T(8,128)}, u32[]{:S(2)}, u32[]{:S(2)}) collective-permute-start(f32[160,512]{1,0:T(8,128)} %get-tuple-element.258), channel_id=1, source_target_pairs={{0,3},{1,2},{2,1},{3,0},{4,7},{5,6},{6,5},{7,4},{8,11},{9,10},{10,... | collective-permute-start | bytes 983048 | tf_op jit(solution)/shard_map/ppermute | solution.py:559
  640.6 32.3 %collective-permute-start.78 = (f32[640,128]{1,0:T(8,128)S(1)}, f32[640,128]{1,0:T(8,128)}, u32[]{:S(2)}, u32[]{:S(2)}) collective-permute-start(f32[640,128]{1,0:T(8,128)S(1)} %subtract_multiply_fusion.2.one), channel_id=1, source_target_pairs={{0,2},{1,3},{2,0},{3,1},{4,6},{5,7},{6,4},{7,5},{8,10},{9,11},{10,... | collective-permute-start | bytes 983048 | tf_op jit(solution)/shard_map/ppermute | solution.py:559
  645.4 37.0 %collective-permute-start.108 = (f32[576,512]{1,0:T(8,128)}, f32[576,512]{1,0:T(8,128)S(1)}, u32[]{:S(2)}, u32[]{:S(2)}) collective-permute-start(f32[576,512]{1,0:T(8,128)} %get-tuple-element.198), channel_id=1, source_target_pairs={{0,8},{8,16},{16,24},{24,28},{28,20},{20,12},{12,4},{4,0},{1,9},{9... | collective-permute-start | bytes 3538952 | tf_op jit(solution)/shard_map/ppermute | solution.py:670
  645.7 36.7 %collective-permute-start.111 = (f32[576,512]{1,0:T(8,128)}, f32[576,512]{1,0:T(8,128)}, u32[]{:S(2)}, u32[]{:S(2)}) collective-permute-start(f32[576,512]{1,0:T(8,128)} %get-tuple-element.199), channel_id=1, source_target_pairs={{8,0},{16,8},{24,16},{28,24},{20,28},{12,20},{4,12},{0,4},{9,1},{1... | collective-permute-start | bytes 3538952 | tf_op jit(solution)/shard_map/ppermute | solution.py:674
  684.6 56.3 %collective-permute-start.113 = (f32[576,512]{1,0:T(8,128)S(1)}, f32[576,512]{1,0:T(8,128)}, u32[]{:S(2)}, u32[]{:S(2)}) collective-permute-start(f32[576,512]{1,0:T(8,128)S(1)} %fusion.4.one), channel_id=1, source_target_pairs={{0,2},{1,3},{2,0},{3,1},{4,6},{5,7},{6,4},{7,5},{8,10},{9,11},{10,... | collective-permute-start | bytes 3538952 | tf_op jit(solution)/shard_map/ppermute | solution.py:559
  687.4 33.9 %collective-permute-start.98 = (f32[256,512]{1,0:T(8,128)}, f32[256,512]{1,0:T(8,128)}, u32[]{:S(2)}, u32[]{:S(2)}) collective-permute-start(f32[256,512]{1,0:T(8,128)} %get-tuple-element.209), channel_id=1, source_target_pairs={{8,0},{16,8},{24,16},{28,24},{20,28},{12,20},{4,12},{0,4},{9,1},{1... | collective-permute-start | bytes 1572872 | tf_op jit(solution)/shard_map/ppermute | solution.py:674
  688.4 30.9 %collective-permute-start.43 = (f32[160,512]{1,0:T(8,128)}, f32[160,512]{1,0:T(8,128)}, u32[]{:S(2)}, u32[]{:S(2)}) collective-permute-start(f32[160,512]{1,0:T(8,128)} %get-tuple-element.259), channel_id=1, source_target_pairs={{0,2},{1,3},{2,0},{3,1},{4,6},{5,7},{6,4},{7,5},{8,10},{9,11},{10,... | collective-permute-start | bytes 983048 | tf_op jit(solution)/shard_map/ppermute | solution.py:559
  689.4 29.9 %collective-permute-start.42 = (f32[160,512]{1,0:T(8,128)}, f32[160,512]{1,0:T(8,128)}, u32[]{:S(2)}, u32[]{:S(2)}) collective-permute-start(f32[160,512]{1,0:T(8,128)} %get-tuple-element.260), channel_id=1, source_target_pairs={{0,1},{1,0},{2,3},{3,2},{4,5},{5,4},{6,7},{7,6},{8,9},{9,8},{10,11... | collective-permute-start | bytes 983048 | tf_op jit(solution)/shard_map/ppermute | solution.py:559
  743.6 41.0 %collective-permute-start.114 = (f32[576,512]{1,0:T(8,128)}, f32[576,512]{1,0:T(8,128)S(1)}, u32[]{:S(2)}, u32[]{:S(2)}) collective-permute-start(f32[576,512]{1,0:T(8,128)} %collective-permute-done.113.three), channel_id=1, source_target_pairs={{0,1},{1,0},{2,3},{3,2},{4,5},{5,4},{6,7},{7,6},{8,9},{9,8},{10,11... | collective-permute-start | bytes 3538952 | tf_op jit(solution)/shard_map/ppermute | solution.py:559
  763.7 30.8 %collective-permute-start.118 = (f32[288,512]{1,0:T(8,128)}, f32[288,512]{1,0:T(8,128)S(1)}, u32[]{:S(2)}, u32[]{:S(2)}) collective-permute-start(f32[288,512]{1,0:T(8,128)} %broadcast_multiply_fusion), channel_id=1, source_target_pairs={{0,2},{1,3},{2,0},{3,1},{4,6},{5,7},{6,4},{7,5},{8,10},{9,11},{10,... | collective-permute-start | bytes 1769480 | tf_op jit(solution)/shard_map/ppermute | solution.py:559
  768.3 29.6 %collective-permute-start.115 = (f32[288,512]{1,0:T(8,128)}, f32[288,512]{1,0:T(8,128)S(1)}, u32[]{:S(2)}, u32[]{:S(2)}) collective-permute-start(f32[288,512]{1,0:T(8,128)} %broadcast_multiply_fusion.1), channel_id=1, source_target_pairs={{0,2},{1,3},{2,0},{3,1},{4,6},{5,7},{6,4},{7,5},{8,10},{9,11},{10,... | collective-permute-start | bytes 1769480 | tf_op jit(solution)/shard_map/ppermute | solution.py:559
  (179 other events, 2558.9 us)
Sparse Core Ops, SparseCore 0:
  12.5 162.9 all-gather.3
  178.2 106.2 all-gather.5
  287.2 80.6 all-gather.7
  371.5 94.3 reduce-scatter.4
  469.3 113.1 reduce-scatter.2

commit v3 on v2

--- a/solution.py
+++ b/solution.py
@@ -654,27 +654,49 @@
                 whole = lax.dynamic_update_index_in_dim(whole, falling, self.at(k), 0)
         return whole, beside
 
-    def scatter(self, blocks, longer_up, beside=None, beside_step=0):
-        if self.size > LONGEST_RING:
-            return lax.psum_scatter(blocks, "batch", scatter_dimension=0, tiled=False), beside
-
-        def own(offset):
-            return lax.dynamic_index_in_dim(blocks, self.at(offset), 0, keepdims=False)
-
-        ups, downs = self.steps(longer_up)
-        rising, falling = own(ups), own(-downs)
-        for k in range(max(ups, downs)):
-            if k + 1 == beside_step and beside is not None:
-                rising, falling, beside = lax.optimization_barrier((rising, falling, beside))
-            if k < ups:
-                rising = lax.ppermute(rising, "batch", self.up)
-                if k < ups - 1:
-                    rising = rising + own(ups - 1 - k)
-            if k < downs:
-                falling = lax.ppermute(falling, "batch", self.down)
-                if k < downs - 1:
-                    falling = falling + own(-(downs - 1 - k))
-        return own(0) + rising + falling, beside
+    def scatter(self, blocks, longer_up):
+        hops = Hops(self, blocks, longer_up)
+        while not hops.done:
+            hops.step()
+        return hops.result()
+
+
+class Hops:
+    def __init__(self, ring, blocks, longer_up):
+        self.ring, self.blocks, self.hop = ring, blocks, 0
+        if ring.size > LONGEST_RING:
+            self.sums = lax.psum_scatter(blocks, "batch", scatter_dimension=0, tiled=False)
+            self.done = True
+            return
+        self.sums, self.done = None, False
+        self.ups, self.downs = ring.steps(longer_up)
+        self.rising, self.falling = self.own(self.ups), self.own(-self.downs)
+
+    def own(self, offset):
+        return lax.dynamic_index_in_dim(self.blocks, self.ring.at(offset), 0, keepdims=False)
+
+    def step(self, later=None):
+        if self.done:
+            return later
+        k = self.hop
+        if k < self.ups:
+            self.rising = lax.ppermute(self.rising, "batch", self.ring.up)
+        if k < self.downs:
+            self.falling = lax.ppermute(self.falling, "batch", self.ring.down)
+        if later is not None:
+            self.rising, self.falling, later = lax.optimization_barrier(
+                (self.rising, self.falling, later)
+            )
+        if k < self.ups - 1:
+            self.rising = self.rising + self.own(self.ups - 1 - k)
+        if k < self.downs - 1:
+            self.falling = self.falling + self.own(-(self.downs - 1 - k))
+        self.hop += 1
+        self.done = self.hop == max(self.ups, self.downs)
+        return later
+
+    def result(self):
+        return self.sums if self.sums is not None else self.own(0) + self.rising + self.falling
 
 
 def sums_of(values, others):
@@ -846,11 +868,13 @@
             ]
         return jnp.concatenate(in_order(exchange_keyed(blocks), row), axis=0)
 
-    def collect_wide(array):
+    def exchange_wide(array):
         blocks = array.reshape(nrows, quarter, nbatch * wide_part)
-        got = exchange_keyed(
+        return exchange_keyed(
             [lax.dynamic_index_in_dim(blocks, row ^ key, 0, keepdims=False) for key in range(4)]
         )
+
+    def collect_wide(got):
         if spread_by_kernel:
             (out,) = single_call(
                 collect_kernel,
@@ -890,8 +914,10 @@
     pre_dilate, mid_in = joined_conv(
         here, gather_keyed(image_of(jax.nn.silu(normed_one))), dilate_full, 2
     )
+    total_two = sum_batch(sums_of(pre_dilate, pre_dilate))
+    total_two, heads_full = lax.optimization_barrier((total_two, heads_full))
     hat_two, normed_two, inverse_two = norm_forward(
-        pre_dilate, sum_batch(sums_of(pre_dilate, pre_dilate)), dilate_gain, dilate_bias, count
+        pre_dilate, total_two, dilate_gain, dilate_bias, count
     )
 
     beside = mid // class_lanes
@@ -911,6 +937,7 @@
         here, gather_keyed(image_of(jax.nn.silu(normed_two))), heads_full, 1, True
     )
     square_all, feats = ring.gather(square_mine, False, feats, 2)
+    square_all, segment_pair_w = lax.optimization_barrier((square_all, segment_pair_w))
     depth_gate_w, segment_gate_w, expand_w = [
         square_all[:, square_spans[name]].reshape(mid, mid)
         for name in ("depth_gate", "segment_gate", "expand")
@@ -925,6 +952,9 @@
 
     segment_mine, segment_got = scatter_end(*note_forward(here, feats_image, 1, segment_pair_w))
     pairs_got = jnp.stack(exchange_keyed([pairs[key] for key in range(4)]))
+    block_cotangent, _ = lax.optimization_barrier((block_cotangent, feats))
+    cotangent = spread_wide(block_cotangent.reshape(quarter, wide))
+    pairs_got, segment_mine, cotangent = lax.optimization_barrier((pairs_got, segment_mine, cotangent))
     depth_cotangent = depth_cotangent.reshape(quarter, mid)
     both, one_map = (2 * quarter, mid), (quarter, mid)
     feat_pair, open_pair, d_depth_note = single_call(
@@ -934,7 +964,6 @@
         [both],
         8 * quarter * mid * mid,
     )
-    feat_pair, open_pair, segment_mine = lax.optimization_barrier((feat_pair, open_pair, segment_mine))
 
     def segment_body(*refs):
         segment_kernel(classes, *refs)
@@ -960,20 +989,36 @@
     def lines(array):
         return array.reshape(local_height, breadth, mid)
 
-    depth_pair_grad, d_depth_image = note_grad(here, feats, 0, gather_keyed(lines(d_depth_note)), run)
+    d_depth_blocks, d_segment_note = lax.optimization_barrier(
+        (gather_keyed(lines(d_depth_note)), d_segment_note)
+    )
+    depth_pair_grad, d_depth_image = note_grad(here, feats, 0, d_depth_blocks, run)
     depth_pair_sums = lax.psum_scatter(
         regroup(depth_pair_grad, grain).reshape(-1, mid), "batch", scatter_dimension=0, tiled=True
     )
     segment_pair_grad, d_segment_image = note_grad(
         here, feats, 1, gather_keyed(lines(d_segment_note)), run
     )
-    segment_pair_sums = lax.psum_scatter(
-        regroup(segment_pair_grad, grain).reshape(-1, mid), "batch", scatter_dimension=0, tiled=True
-    )
-    feats_late, d_segment_image, depth_pair_grad = lax.optimization_barrier(
-        (feats_image, d_segment_image, depth_pair_grad)
-    )
+    flat_mid_out = mid_out.reshape(pixels, mid)
+    expand_input, _ = lax.optimization_barrier((flat_mid_out, d_segment_note))
+    pre_expand = product(expand_input, expand_w, 1, 0)
+    hat_three, normed_three, inverse_three = norm_forward(
+        pre_expand, sum_batch(sums_of(pre_expand, pre_expand)), expand_gain, expand_bias, count
+    )
+    summed = normed_three + inputs
+    block_blocks = exchange_wide(jax.nn.silu(summed))
+    d_summed = cotangent * silu_grad(summed)
+    d_pre_expand, expand_sums = norm_backward(
+        d_summed, hat_three, inverse_three, expand_gain, count, False
+    )
+
+    feats_late, depth_pair_w, _ = lax.optimization_barrier(
+        (feats_image, depth_pair_w, (segment_pair_grad, depth_pair_grad, expand_sums))
+    )
+    segment_pair_grad, _ = lax.optimization_barrier((segment_pair_grad, expand_sums))
+    hops = Hops(ring, regroup(segment_pair_grad, grain).reshape(nbatch, held // 2, mid), True)
     depth_mine, depth_got = scatter_end(*note_forward(here, feats_late, 0, depth_pair_w))
+    depth_back = note_back(hops.step(d_depth_image), depth_pair_w)
     depth_stream, direct_both, depth_gate_grad = single_call(
         depth_kernel,
         (
@@ -993,29 +1038,16 @@
         8 * quarter * mid * mid,
     )
     direct_got = jnp.stack(exchange_keyed([direct_both[key] for key in range(4)]))
-    flat_mid_out = mid_out.reshape(pixels, mid)
+    segment_back = note_back(hops.step(d_segment_image), segment_pair_w)
     heads_grad, d_feats = heads_grad_of(
         here,
-        flat_mid_out,
-        image_of(note_back(d_depth_image, depth_pair_w)),
-        image_of(note_back(d_segment_image, segment_pair_w)),
+        hops.step(flat_mid_out),
+        image_of(depth_back),
+        image_of(segment_back),
         direct_got.reshape(4, 2 * local_height, breadth, part),
     )
-    heads_sums, _ = ring.scatter(heads_grad.reshape(nbatch, held, nrows * part), True)
-
-    expand_input, _ = lax.optimization_barrier((flat_mid_out, segment_pair_grad))
-    block_cotangent, _ = lax.optimization_barrier((block_cotangent, feats))
-    cotangent = spread_wide(block_cotangent.reshape(quarter, wide))
-    pre_expand = product(expand_input, expand_w, 1, 0)
-    hat_three, normed_three, inverse_three = norm_forward(
-        pre_expand, sum_batch(sums_of(pre_expand, pre_expand)), expand_gain, expand_bias, count
-    )
-    summed = normed_three + inputs
-    block_out = collect_wide(jax.nn.silu(summed))
-    d_summed = cotangent * silu_grad(summed)
-    d_pre_expand, expand_sums = norm_backward(
-        d_summed, hat_three, inverse_three, expand_gain, count, False
-    )
+    heads_sums = lax.psum_scatter(heads_grad, "batch", scatter_dimension=0, tiled=True)
+
     expand_grad = product(flat_mid_out, d_pre_expand, 0, 0).reshape(nbatch, mid_held, mid)
 
     gate_terms = jnp.stack(
@@ -1029,16 +1061,19 @@
     gate_terms = jnp.transpose(gate_terms.reshape(3, nbatch, nrows, gate_rows, mid), (2, 1, 0, 3, 4))
     gate_sums = scatter_rows(gate_terms, row).reshape(nbatch, 3 * gate_rows, mid)
 
+    d_feats, block_blocks = lax.optimization_barrier((hops.step(d_feats), block_blocks))
+    block_out = collect_wide(block_blocks)
+    segment_pair_sums = hops.result()
     mine_terms, got_terms = scatter_end(
         *conv_back(here, d_feats, heads_full, 1, product(d_pre_expand, expand_w, 1, 1))
     )
     d_pre_dilate, dilate_sums = norm_backward(
-        (mine_terms + got_terms) * silu_grad(normed_two), hat_two, inverse_two, dilate_gain, count, True
+        (mine_terms + got_terms) * silu_grad(normed_two), hat_two, inverse_two, dilate_gain, count, False
     )
     d_dilate_image = image_of(d_pre_dilate)
     mine_terms, got_terms = scatter_end(*conv_back(here, d_dilate_image, dilate_full, 2))
     d_pre_reduce, reduce_sums = norm_backward(
-        (mine_terms + got_terms) * silu_grad(normed_one), hat_one, inverse_one, reduce_gain, count, True
+        (mine_terms + got_terms) * silu_grad(normed_one), hat_one, inverse_one, reduce_gain, count, False
     )
     reduce_grad, features_back = single_call(
         reduce_back_kernel,
@@ -1061,19 +1096,16 @@
         ],
         axis=1,
     )
-    square_grad, reduce_sums, depth_pair_sums = lax.optimization_barrier(
-        (square_grad, reduce_sums, depth_pair_sums)
-    )
-    square_sums, _ = ring.scatter(square_grad, False)
-    reduce_out, segment_pair_sums = ring.scatter(
-        reduce_grad.reshape(nbatch, wide_part, mid), True, segment_pair_sums, 2
-    )
-    features_grad = collect_wide(features_back)
-
-    depth_pair_out, segment_pair_out = [
-        jnp.stack(gather_rows(sums * factor, row)).reshape(nrows, groups, 2, grain, mid)
-        for sums in (depth_pair_sums, segment_pair_sums)
-    ]
+    square_grad, reduce_sums, depth_pair_sums, segment_pair_sums = lax.optimization_barrier(
+        (square_grad, reduce_sums, depth_pair_sums, segment_pair_sums)
+    )
+    square_sums = ring.scatter(square_grad, False)
+    reduce_out = ring.scatter(reduce_grad.reshape(nbatch, wide_part, mid), True)
+    features_grad = collect_wide(exchange_wide(features_back))
+
+    pair_sums = jnp.concatenate([depth_pair_sums, segment_pair_sums], axis=0) * factor
+    pairs_out = jnp.stack(gather_rows(pair_sums, row)).reshape(nrows, 2, groups, 2, grain, mid)
+    depth_pair_out, segment_pair_out = pairs_out[:, 0], pairs_out[:, 1]
 
     def message_out(pair_got, index):
         return jnp.transpose(pair_got[:, :, index], (1, 0, 2, 3)).reshape(held, mid)

time: 847 us -> 831 us (0.981)
  waiting for transfers between devices: 324 us -> 296 us
  starting transfers between devices: 161 us -> 170 us
    ppermute x26 -> x18, waiting for transfers between devices: 65.9 us -> 19 us  [swap(): return lax.ppermute(block, 'batch', [(i, i ^ mask) for i in range(size)])]
    ppermute x21, waiting for transfers between devices: 51.7 us -> 75.9 us  [the longest x10 43.2 us: step(): self.falling = lax.ppermute(self.falling, 'batch', self.ring.down)]
    ppermute x7, waiting for transfers between devices: 55.7 us -> 34.1 us  [gather(): falling = lax.ppermute(falling, 'batch', self.down)]
    ppermute x7, waiting for transfers between devices: 38.2 us -> 58.2 us  [gather(): rising = lax.ppermute(rising, 'batch', self.up)]
    ppermute x7, starting transfers between devices: 11.2 us -> 24.1 us  [gather(): rising = lax.ppermute(rising, 'batch', self.up)]
    unnamed x180 -> x166, local copies, waits for them, and re-layouts: 17.8 us -> 14.1 us
    ppermute x26 -> x18, starting transfers between devices: 45.7 us -> 49.3 us  [swap(): return lax.ppermute(block, 'batch', [(i, i ^ mask) for i in range(size)])]
    ppermute x60 -> x57, waiting for transfers between devices: 112 us -> 109 us  [swap_rows(): return lax.ppermute(block, 'rows', [(i, i ^ mask) for i in range(size)])]
  transfers between devices with their start and end apart: 126 -> 115, of which waited for: 50 -> 50; matrix products, arithmetic and copies ran while one was open for 14% -> 15% of each run, Pallas kernels for 22% -> 21%
where the time goes in v3:
time: 831 us; the launch traced here: 819 us
  waiting for transfers between devices  296 us (36%)
  Pallas kernels  183 us (22%)
  starting transfers between devices  170 us (20%)
  local copies, waits for them, and re-layouts  71.5 us (9%)
  other arithmetic  57.1 us (7%)
  between operations  31.8 us (4%)
  matrix products  9.25 us (1%)
    ppermute x57, waiting for transfers between devices, swap_rows(): return lax.ppermute(block, 'rows', [(i, i ^ mask) for i in range(size)])  109 us
    ppermute x57, starting transfers between devices, swap_rows(): return lax.ppermute(block, 'rows', [(i, i ^ mask) for i in range(size)])  77.9 us
    ppermute x7, waiting for transfers between devices, gather(): rising = lax.ppermute(rising, 'batch', self.up)  58.2 us
    ppermute x18, starting transfers between devices, swap(): return lax.ppermute(block, 'batch', [(i, i ^ mask) for i in range(size)])  49.3 us
    pallas_call x10, Pallas kernels, single_call(): kernel_call(body, (1,), [SCALAR] + [whole_spec(arg.shape) for arg in args...  44.3 us
    ppermute x10, waiting for transfers between devices, step(): self.falling = lax.ppermute(self.falling, 'batch', self.ring.down)  43.2 us
    ppermute x7, waiting for transfers between devices, gather(): falling = lax.ppermute(falling, 'batch', self.down)  34.1 us
    ppermute x11, waiting for transfers between devices, step(): self.rising = lax.ppermute(self.rising, 'batch', self.ring.up)  32.7 us
  transfers between devices with their start and end apart: 115, of which 50 were waited for; matrix products, arithmetic and copies ran while one was open for 15% of the time, Pallas kernels for 21%

profile of v3, /device:TPU:1, one launch (start us, length us, event | category | flops | bytes accessed | tf_op | source)
XLA Modules:
  0.0 819.5 jit_solution(2776828787585586594)
XLA Ops:
  48.2 18.4 %collective-permute-done.5 = f32[840,128]{1,0:T(8,128)S(1)} collective-permute-done((f32[840,128]{1,0:T(8,128)S(1)}, f32[840,128]{1,0:T(8,128)S(1)}, u32[]{:S(2)}, u32[]{:S(2)}) %collective-permute-start.5) | collective-permute-done | bytes 430112 | tf_op jit(solution)/shard_map/ppermute | solution.py:650
  66.6 9.2 %collective-permute-start.7 = (f32[840,128]{1,0:T(8,128)S(1)}, f32[840,128]{1,0:T(8,128)S(1)}, u32[]{:S(2)}, u32[]{:S(2)}) collective-permute-start(f32[840,128]{1,0:T(8,128)S(1)} %collective-permute-done.5), channel_id=1, source_target_pairs={{0,8},{8,16},{16,24},{24,28},{28,20},{20,12},{12,4},{4,0},{1,9},{9... | collective-permute-start | bytes 1290248 | tf_op jit(solution)/shard_map/ppermute | solution.py:650
  78.0 9.0 %collective-permute-done.7 = f32[840,128]{1,0:T(8,128)S(1)} collective-permute-done((f32[840,128]{1,0:T(8,128)S(1)}, f32[840,128]{1,0:T(8,128)S(1)}, u32[]{:S(2)}, u32[]{:S(2)}) %collective-permute-start.7) | collective-permute-done | bytes 430112 | tf_op jit(solution)/shard_map/ppermute | solution.py:650
  89.3 17.7 %collective-permute-done.9 = f32[840,128]{1,0:T(8,128)S(1)} collective-permute-done((f32[840,128]{1,0:T(8,128)S(1)}, f32[840,128]{1,0:T(8,128)S(1)}, u32[]{:S(2)}, u32[]{:S(2)}) %collective-permute-start.9) | collective-permute-done | bytes 430112 | tf_op jit(solution)/shard_map/ppermute | solution.py:650
  121.4 9.1 %collective-permute-done.11 = f32[648,128]{1,0:T(8,128)S(1)} collective-permute-done((f32[648,128]{1,0:T(8,128)S(1)}, f32[648,128]{1,0:T(8,128)S(1)}, u32[]{:S(2)}, u32[]{:S(2)}) %collective-permute-start.11) | collective-permute-done | bytes 331808 | tf_op jit(solution)/shard_map/ppermute | solution.py:559
  131.6 10.0 %collective-permute-start.12 = (f32[3,128]{1,0:T(4,128)S(1)}, f32[3,128]{1,0:T(4,128)S(1)}, u32[]{:S(2)}, u32[]{:S(2)}) collective-permute-start(f32[3,128]{1,0:T(4,128)S(1)} %pad_maximum_fusion.19), channel_id=1, source_target_pairs={{0,4},{4,0},{8,12},{12,8},{16,20},{20,16},{24,28},{28,24},{1,5},{5... | collective-permute-start | bytes 4616 | tf_op jit(solution)/shard_map/ppermute | solution.py:609
  170.1 10.0 %shard_map.384 = (f32[640,128]{1,0:T(8,128)}, f32[16,40,512]{2,1,0:T(8,128)}) custom-call(s32[1]{0:T(128)} %bitcast.row_ref.refs_0_, f32[16,40,128]{2,1,0:T(8,128)} %bitcast.447, f32[16,40,128]{2,1,0:T(8,128)} %copy-done.78, f32[16,40,128]{2,1,0:T(8,128)} %copy-done.65, f32[16,40,128]{2,1,0:T(8,128)} %copy-done.79, f32[4608,128]{1,0:T(8,128)} %bitcast.414), custom_call_target="tpu_custom_call" | custom-call | flops 2264924160 | bytes 12582912 | tf_op jit(solution)/shard_map/pallas_call | solution.py:431
  202.4 10.1 %collective-permute-done.21 = f32[208,512]{1,0:T(8,128)S(1)} collective-permute-done((f32[208,512]{1,0:T(8,128)S(1)}, f32[208,512]{1,0:T(8,128)S(1)}, u32[]{:S(2)}, u32[]{:S(2)}) %collective-permute-start.21) | collective-permute-done | bytes 426016 | tf_op jit(solution)/shard_map/ppermute | solution.py:650
  221.1 15.1 %shard_map.385 = (f32[640,512]{1,0:T(8,128)}, f32[16,40,512]{2,1,0:T(8,128)}, f32[4,320,128]{2,1,0:T(8,128)}) custom-call(s32[1]{0:T(128)} %bitcast.row_ref.refs_0_, f32[16,40,128]{2,1,0:T(8,128)} %bitcast.450, f32[16,40,128]{2,1,0:T(8,128)} %copy-done.72, f32[16,40,128]{2,1,0:T(8,128)} %copy-done.67, f32[16,40,128]{2,1,0:T(8,128)} %copy-done.77, ...), custom_call_target="tpu_custom_call" | custom-call | flops 9059696640 | bytes 12582912 | tf_op jit(solution)/shard_map/pallas_call | solution.py:431
  271.8 10.6 %collective-permute-done.32 = f32[208,512]{1,0:T(8,128)S(1)} collective-permute-done((f32[208,512]{1,0:T(8,128)S(1)}, f32[208,512]{1,0:T(8,128)S(1)}, u32[]{:S(2)}, u32[]{:S(2)}) %collective-permute-start.32) | collective-permute-done | bytes 426016 | tf_op jit(solution)/shard_map/ppermute | solution.py:653
  284.2 8.7 %collective-permute-done.33 = f32[208,512]{1,0:T(8,128)S(1)} collective-permute-done((f32[208,512]{1,0:T(8,128)S(1)}, f32[208,512]{1,0:T(8,128)S(1)}, u32[]{:S(2)}, u32[]{:S(2)}) %collective-permute-start.33) | collective-permute-done | bytes 426016 | tf_op jit(solution)/shard_map/ppermute | solution.py:653
  293.8 10.5 %shard_map.386 = (f32[2,160,512]{2,1,0:T(8,128)}, f32[2,160,512]{2,1,0:T(8,128)}) custom-call(s32[1]{0:T(128)} %bitcast.row_ref.refs_0_, f32[16,40,512]{2,1,0:T(8,128)} %bitcast.531, f32[72,2,16,512]{3,2,1,0:T(8,128)} %bitcast.518), custom_call_target="tpu_custom_call" | custom-call | flops 4529848320 | bytes 12582912 | tf_op jit(solution)/shard_map/pallas_call | solution.py:504
  341.3 10.3 %shard_map.391 = (f32[72,2,16,512]{3,2,1,0:T(8,128)}, f32[16,40,512]{2,1,0:T(8,128)}) custom-call(s32[1]{0:T(128)} %bitcast.row_ref.refs_0_, f32[640,512]{1,0:T(8,128)} %get-tuple-element.111.input_ref, f32[4,40,512]{2,1,0:T(8,128)} %bitcast.529, f32[4,40,512]{2,1,0:T(8,128)} %copy-done.68, f32[4,40,512]{2,1,0:T(8,128)} %copy-done.64, f32[4,40,512]{2,1,0:T(8,128)} %copy-done.73), custom_call_target="tpu_custom_call" | custom-call | flops 4529848320 | bytes 12582912 | tf_op jit(solution)/shard_map/pallas_call | solution.py:540
  383.3 10.4 %shard_map.390 = (f32[72,2,16,512]{3,2,1,0:T(8,128)}, f32[16,40,512]{2,1,0:T(8,128)}) custom-call(s32[1]{0:T(128)} %bitcast.row_ref.refs_0_, f32[640,512]{1,0:T(8,128)} %get-tuple-element.111.input_ref, f32[4,40,512]{2,1,0:T(8,128)} %bitcast.525, f32[4,40,512]{2,1,0:T(8,128)} %copy-done.69, f32[4,40,512]{2,1,0:T(8,128)} %copy-done.63, f32[4,40,512]{2,1,0:T(8,128)} %copy-done.70), custom_call_target="tpu_custom_call" | custom-call | flops 4529848320 | bytes 12582912 | tf_op jit(solution)/shard_map/pallas_call | solution.py:540
  393.7 10.7 %shard_map.394 = (f32[2,160,512]{2,1,0:T(8,128)}, f32[2,160,512]{2,1,0:T(8,128)}) custom-call(s32[1]{0:T(128)} %bitcast.row_ref.refs_0_, f32[16,40,512]{2,1,0:T(8,128)} %bitcast.532, f32[72,2,16,512]{3,2,1,0:T(8,128)} %bitcast.520), custom_call_target="tpu_custom_call" | custom-call | flops 4529848320 | bytes 12582912 | tf_op jit(solution)/shard_map/pallas_call | solution.py:504
  410.0 19.9 %collective-permute-done.51 = f32[288,512]{1,0:T(8,128)S(1)} collective-permute-done((f32[288,512]{1,0:T(8,128)S(1)}, f32[288,512]{1,0:T(8,128)S(1)}, u32[]{:S(2)}, u32[]{:S(2)}) %collective-permute-start.51) | collective-permute-done | bytes 589856 | tf_op jit(solution)/shard_map/ppermute | solution.py:683
  454.7 10.7 %shard_map.392 = f32[640,256]{1,0:T(8,128)} custom-call(f32[16,40,512]{2,1,0:T(8,128)} %get-tuple-element.145.note_ref, f32[72,2,16,512]{3,2,1,0:T(8,128)} %bitcast.521), custom_call_target="tpu_custom_call" | custom-call | flops 4529848320 | bytes 12582912 | tf_op jit(solution)/shard_map/pallas_call | solution.py:522
  467.2 10.7 %shard_map.393 = f32[640,256]{1,0:T(8,128)} custom-call(f32[16,40,512]{2,1,0:T(8,128)} %get-tuple-element.148.note_ref, f32[72,2,16,512]{3,2,1,0:T(8,128)} %bitcast.519), custom_call_target="tpu_custom_call" | custom-call | flops 4529848320 | bytes 12582912 | tf_op jit(solution)/shard_map/pallas_call | solution.py:522
  483.9 16.8 %shard_map.396 = (f32[4608,512]{1,0:T(8,128)}, f32[16,40,512]{2,1,0:T(8,128)}) custom-call(s32[1]{0:T(128)} %bitcast.row_ref.refs_0_, f32[640,512]{1,0:T(8,128)} %bitcast.397, f32[16,40,256]{2,1,0:T(8,128)} %bitcast.533, f32[16,40,256]{2,1,0:T(8,128)} %bitcast.534, f32[4,8,40,128]{3,2,1,0:T(8,128)} %pad_maximum_fusion.9.direct_ref), custom_call_target="tpu_custom_call" | custom-call | flops 9059696640 | bytes 12582912 | tf_op jit(solution)/shard_map/pallas_call | solution.py:487
  516.2 7.4 collective-permute-done.65.four
  524.3 14.9 %shard_map.398 = (f32[2,640,128]{2,1,0:T(8,128)}, f32[2,640,128]{2,1,0:T(8,128)}) custom-call(s32[1]{0:T(128)} %bitcast.row_ref.refs_0_, f32[16,40,512]{2,1,0:T(8,128)} %get-tuple-element.163.refs_1_, f32[4608,512]{1,0:T(8,128)} %all-gather.4.cloned.1.call-done.weight_ref.refs_2_, f32[640,512]{1,0:T(8,128)} %fusion.28.refs_3_), custom_call_target="tpu_custom_call" | custom-call | flops 9059696640 | bytes 12582912 | tf_op jit(solution)/shard_map/pallas_call | solution.py:452
  545.4 7.9 collective-permute-done.67
  554.5 7.3 collective-permute-start.68
  576.4 9.7 %shard_map.399 = (f32[2,640,128]{2,1,0:T(8,128)}, f32[2,640,128]{2,1,0:T(8,128)}) custom-call(s32[1]{0:T(128)} %bitcast.row_ref.refs_0_, f32[16,40,128]{2,1,0:T(8,128)} %bitcast.443, f32[4608,128]{1,0:T(8,128)} %bitcast.415), custom_call_target="tpu_custom_call" | custom-call | flops 2264924160 | bytes 12582912 | tf_op jit(solution)/shard_map/pallas_call | solution.py:452
  610.2 8.8 %collective-permute-done.93 = f32[8,3,16,512]{3,2,1,0:T(8,128)S(1)} collective-permute-done((f32[8,3,16,512]{3,2,1,0:T(8,128)S(1)}, f32[8,3,16,512]{3,2,1,0:T(8,128)S(1)}, u32[]{:S(2)}, u32[]{:S(2)}) %collective-permute-start.93) | collective-permute-done | bytes 786464 | tf_op jit(solution)/shard_map/ppermute | solution.py:559
  620.8 8.8 %shard_map.402 = f32[4608,128]{1,0:T(8,128)} custom-call(f32[640,512]{1,0:T(8,128)} %bitcast.530, f32[16,40,128]{2,1,0:T(8,128)} %bitcast.444), custom_call_target="tpu_custom_call" | custom-call | flops 2264924160 | bytes 12582912 | tf_op jit(solution)/shard_map/pallas_call | solution.py:471
  658.7 15.6 %collective-permute-done.97 = f32[256,512]{1,0:T(8,128)S(1)} collective-permute-done((f32[256,512]{1,0:T(8,128)S(1)}, f32[256,512]{1,0:T(8,128)S(1)}, u32[]{:S(2)}, u32[]{:S(2)}) %collective-permute-start.97) | collective-permute-done | bytes 524320 | tf_op jit(solution)/shard_map/ppermute | solution.py:685
  675.5 7.7 collective-permute-done.86
  690.0 10.7 %collective-permute-done.87 = f32[64,512]{1,0:T(8,128)S(1)} collective-permute-done((f32[64,512]{1,0:T(8,128)S(1)}, f32[64,512]{1,0:T(8,128)S(1)}, u32[]{:S(2)}, u32[]{:S(2)}) %collective-permute-start.87) | collective-permute-done | bytes 131104 | tf_op jit(solution)/shard_map/ppermute | solution.py:685
  711.0 8.3 %collective-permute-done.80.three = f32[160,512]{1,0:T(8,128)S(1)} collective-permute-done((f32[160,512]{1,0:T(8,128)S(1)}, f32[160,512]{1,0:T(8,128)S(1)}, u32[]{:S(2)}, u32[]{:S(2)}) %collective-permute-start.80) | collective-permute-done | bytes 327712 | tf_op jit(solution)/shard_map/ppermute | solution.py:559
  773.6 25.2 %collective-permute-done.105.three = f32[576,512]{1,0:T(8,128)} collective-permute-done((f32[576,512]{1,0:T(8,128)}, f32[576,512]{1,0:T(8,128)}, u32[]{:S(2)}, u32[]{:S(2)}) %collective-permute-start.105) | collective-permute-done | bytes 1179680 | tf_op jit(solution)/shard_map/ppermute | solution.py:559
  804.7 7.9 shard_map.403
  (589 shorter events, 419.5 us)
Async XLA Ops:
  7.2 184.6 %all-gather.4.cloned.1.call-start = ((), (), s32[]{:S(2)}) async-start(), calls=%async_computation.2 | async-start | bytes 10616832 | tf_op jit(solution)/shard_map/all_gather | solution.py:796
  12.4 281.4 %all-gather.6.cloned.1.call-start = ((), (), s32[]{:S(2)}) async-start(), calls=%async_computation.3 | async-start | bytes 5308416 | tf_op jit(solution)/shard_map/all_gather | solution.py:810
  14.5 379.2 %all-gather.8.cloned.1.call-start = ((), (), s32[]{:S(2)}) async-start(), calls=%async_computation.4 | async-start | bytes 5308416 | tf_op jit(solution)/shard_map/all_gather | solution.py:810
  18.7 27.9 %collective-permute-start.3 = (f32[840,128]{1,0:T(8,128)S(1)}, f32[840,128]{1,0:T(8,128)S(1)}, u32[]{:S(2)}, u32[]{:S(2)}) collective-permute-start(f32[840,128]{1,0:T(8,128)S(1)} %dynamic-slice_dynamic-update-slice_fusion), channel_id=1, source_target_pairs={{0,8},{8,16},{16,24},{24,28},{28,20},{20,12},{12,4},{4,0},{1,9},{9... | collective-permute-start | bytes 1290248 | tf_op jit(solution)/shard_map/ppermute | solution.py:650
  20.9 27.1 %collective-permute-start.4 = (f32[840,128]{1,0:T(8,128)S(1)}, f32[840,128]{1,0:T(8,128)S(1)}, u32[]{:S(2)}, u32[]{:S(2)}) collective-permute-start(f32[840,128]{1,0:T(8,128)S(1)} %dynamic-slice_dynamic-update-slice_fusion), channel_id=1, source_target_pairs={{8,0},{16,8},{24,16},{28,24},{20,28},{12,20},{4,12},{0,4},{9,1},{1... | collective-permute-start | bytes 1290248 | tf_op jit(solution)/shard_map/ppermute | solution.py:653
  48.0 29.9 %collective-permute-start.6 = (f32[840,128]{1,0:T(8,128)S(1)}, f32[840,128]{1,0:T(8,128)S(1)}, u32[]{:S(2)}, u32[]{:S(2)}) collective-permute-start(f32[840,128]{1,0:T(8,128)S(1)} %collective-permute-done.4), channel_id=1, source_target_pairs={{8,0},{16,8},{24,16},{28,24},{20,28},{12,20},{4,12},{0,4},{9,1},{1... | collective-permute-start | bytes 1290248 | tf_op jit(solution)/shard_map/ppermute | solution.py:653
  66.6 20.4 %collective-permute-start.7 = (f32[840,128]{1,0:T(8,128)S(1)}, f32[840,128]{1,0:T(8,128)S(1)}, u32[]{:S(2)}, u32[]{:S(2)}) collective-permute-start(f32[840,128]{1,0:T(8,128)S(1)} %collective-permute-done.5), channel_id=1, source_target_pairs={{0,8},{8,16},{16,24},{24,28},{28,20},{20,12},{12,4},{4,0},{1,9},{9... | collective-permute-start | bytes 1290248 | tf_op jit(solution)/shard_map/ppermute | solution.py:650
  158.2 476.6 %reduce-scatter.3.cloned.1.call-start = ((), (), s32[]{:S(2)}) async-start(), calls=%async_computation.5 | async-start | bytes 5308416 | tf_op jit(solution)/shard_map/reduce_scatter | solution.py:996
  195.7 23.9 %collective-permute-start.23 = (f32[16,40,128]{2,1,0:T(8,128)S(1)}, f32[16,40,128]{2,1,0:T(8,128)S(1)}, u32[]{:S(2)}, u32[]{:S(2)}) collective-permute-start(f32[16,40,128]{2,1,0:T(8,128)S(1)} %bitcast.449), channel_id=1, source_target_pairs={{0,1},{1,0},{2,3},{3,2},{4,5},{5,4},{6,7},{7,6},{8,9},{9,8},{10,11... | collective-permute-start | bytes 983048 | tf_op jit(solution)/shard_map/ppermute | solution.py:559
  236.2 20.7 %collective-permute-start.29 = (f32[208,512]{1,0:T(8,128)S(1)}, f32[208,512]{1,0:T(8,128)S(1)}, u32[]{:S(2)}, u32[]{:S(2)}) collective-permute-start(f32[208,512]{1,0:T(8,128)S(1)} %collective-permute-done.21), channel_id=1, source_target_pairs={{0,8},{8,16},{16,24},{24,28},{28,20},{20,12},{12,4},{4,0},{1,9},{9... | collective-permute-start | bytes 1277960 | tf_op jit(solution)/shard_map/ppermute | solution.py:650
  237.6 32.7 %collective-permute-start.30 = (f32[208,512]{1,0:T(8,128)S(1)}, f32[208,512]{1,0:T(8,128)S(1)}, u32[]{:S(2)}, u32[]{:S(2)}) collective-permute-start(f32[208,512]{1,0:T(8,128)S(1)} %collective-permute-done.22), channel_id=1, source_target_pairs={{8,0},{16,8},{24,16},{28,24},{20,28},{12,20},{4,12},{0,4},{9,1},{1... | collective-permute-start | bytes 1277960 | tf_op jit(solution)/shard_map/ppermute | solution.py:653
  246.4 59.7 %collective-permute-start.35 = (f32[160,512]{1,0:T(8,128)}, f32[160,512]{1,0:T(8,128)S(1)}, u32[]{:S(2)}, u32[]{:S(2)}) collective-permute-start(f32[160,512]{1,0:T(8,128)} %get-tuple-element.311), channel_id=1, source_target_pairs={{0,3},{1,2},{2,1},{3,0},{4,7},{5,6},{6,5},{7,4},{8,11},{9,10},{10,... | collective-permute-start | bytes 983048 | tf_op jit(solution)/shard_map/ppermute | solution.py:559
  248.7 57.4 %collective-permute-start.36 = (f32[160,512]{1,0:T(8,128)S(1)}, f32[160,512]{1,0:T(8,128)S(1)}, u32[]{:S(2)}, u32[]{:S(2)}) collective-permute-start(f32[160,512]{1,0:T(8,128)S(1)} %get-tuple-element.310), channel_id=1, source_target_pairs={{0,2},{1,3},{2,0},{3,1},{4,6},{5,7},{6,4},{7,5},{8,10},{9,11},{10,... | collective-permute-start | bytes 983048 | tf_op jit(solution)/shard_map/ppermute | solution.py:559
  253.0 53.1 %collective-permute-start.37 = (f32[160,512]{1,0:T(8,128)S(1)}, f32[160,512]{1,0:T(8,128)S(1)}, u32[]{:S(2)}, u32[]{:S(2)}) collective-permute-start(f32[160,512]{1,0:T(8,128)S(1)} %get-tuple-element.309), channel_id=1, source_target_pairs={{0,1},{1,0},{2,3},{3,2},{4,5},{5,4},{6,7},{7,6},{8,9},{9,8},{10,11... | collective-permute-start | bytes 983048 | tf_op jit(solution)/shard_map/ppermute | solution.py:559
  256.9 25.7 %collective-permute-start.31 = (f32[208,512]{1,0:T(8,128)S(1)}, f32[208,512]{1,0:T(8,128)S(1)}, u32[]{:S(2)}, u32[]{:S(2)}) collective-permute-start(f32[208,512]{1,0:T(8,128)S(1)} %collective-permute-done.29), channel_id=1, source_target_pairs={{0,8},{8,16},{16,24},{24,28},{28,20},{20,12},{12,4},{4,0},{1,9},{9... | collective-permute-start | bytes 1277960 | tf_op jit(solution)/shard_map/ppermute | solution.py:650
  351.6 416.8 %reduce-scatter.5.cloned.1.call-start = ((), (), s32[]{:S(2)}) async-start(), calls=%async_computation.6 | async-start | bytes 10616832 | tf_op jit(solution)/shard_map/reduce_scatter | solution.py:1049
  404.4 25.6 %collective-permute-start.58 = (f32[2,160,512]{2,1,0:T(8,128)}, f32[2,160,512]{2,1,0:T(8,128)S(1)}, u32[]{:S(2)}, u32[]{:S(2)}) collective-permute-start(f32[2,160,512]{2,1,0:T(8,128)} %get-tuple-element.151), channel_id=1, source_target_pairs={{0,1},{1,0},{2,3},{3,2},{4,5},{5,4},{6,7},{7,6},{8,9},{9,8},{10,11... | collective-permute-start | bytes 1966088 | tf_op jit(solution)/shard_map/ppermute | solution.py:559
  408.5 21.4 %collective-permute-start.51 = (f32[288,512]{1,0:T(8,128)S(1)}, f32[288,512]{1,0:T(8,128)S(1)}, u32[]{:S(2)}, u32[]{:S(2)}) collective-permute-start(f32[288,512]{1,0:T(8,128)S(1)} %get-tuple-element.259), channel_id=1, source_target_pairs={{0,8},{8,16},{16,24},{24,28},{28,20},{20,12},{12,4},{4,0},{1,9},{9... | collective-permute-start | bytes 1769480 | tf_op jit(solution)/shard_map/ppermute | solution.py:683
  409.2 20.8 %collective-permute-start.52 = (f32[288,512]{1,0:T(8,128)S(1)}, f32[288,512]{1,0:T(8,128)S(1)}, u32[]{:S(2)}, u32[]{:S(2)}) collective-permute-start(f32[288,512]{1,0:T(8,128)S(1)} %get-tuple-element.258), channel_id=1, source_target_pairs={{8,0},{16,8},{24,16},{28,24},{20,28},{12,20},{4,12},{0,4},{9,1},{1... | collective-permute-start | bytes 1769480 | tf_op jit(solution)/shard_map/ppermute | solution.py:685
  452.9 25.0 %collective-permute-start.55 = (f32[288,512]{1,0:T(8,128)}, f32[288,512]{1,0:T(8,128)S(1)}, u32[]{:S(2)}, u32[]{:S(2)}) collective-permute-start(f32[288,512]{1,0:T(8,128)} %get-tuple-element.255), channel_id=1, source_target_pairs={{0,8},{8,16},{16,24},{24,28},{28,20},{20,12},{12,4},{4,0},{1,9},{9... | collective-permute-start | bytes 1769480 | tf_op jit(solution)/shard_map/ppermute | solution.py:683
  453.2 30.7 %collective-permute-start.56 = (f32[288,512]{1,0:T(8,128)}, f32[288,512]{1,0:T(8,128)S(1)}, u32[]{:S(2)}, u32[]{:S(2)}) collective-permute-start(f32[288,512]{1,0:T(8,128)} %get-tuple-element.254), channel_id=1, source_target_pairs={{8,0},{16,8},{24,16},{28,24},{20,28},{12,20},{4,12},{0,4},{9,1},{1... | collective-permute-start | bytes 1769480 | tf_op jit(solution)/shard_map/ppermute | solution.py:685
  596.7 22.4 %collective-permute-start.93 = (f32[8,3,16,512]{3,2,1,0:T(8,128)S(1)}, f32[8,3,16,512]{3,2,1,0:T(8,128)S(1)}, u32[]{:S(2)}, u32[]{:S(2)}) collective-permute-start(f32[8,3,16,512]{3,2,1,0:T(8,128)S(1)} %dynamic-slice_bitcast_fusion.1), channel_id=1, source_target_pairs={{0,2},{1,3},{2,0},{3,1},{4,6},{5,7},{6,4},{7,5},{8,10},{9,11},{10,... | collective-permute-start | bytes 2359304 | tf_op jit(solution)/shard_map/ppermute | solution.py:559
  636.1 38.2 %collective-permute-start.97 = (f32[256,512]{1,0:T(8,128)S(1)}, f32[256,512]{1,0:T(8,128)S(1)}, u32[]{:S(2)}, u32[]{:S(2)}) collective-permute-start(f32[256,512]{1,0:T(8,128)S(1)} %get-tuple-element.265), channel_id=1, source_target_pairs={{8,0},{16,8},{24,16},{28,24},{20,28},{12,20},{4,12},{0,4},{9,1},{1... | collective-permute-start | bytes 1572872 | tf_op jit(solution)/shard_map/ppermute | solution.py:685
  646.5 36.6 %collective-permute-start.86 = (f32[64,512]{1,0:T(8,128)S(1)}, f32[64,512]{1,0:T(8,128)S(1)}, u32[]{:S(2)}, u32[]{:S(2)}) collective-permute-start(f32[64,512]{1,0:T(8,128)S(1)} %get-tuple-element.320), channel_id=1, source_target_pairs={{8,0},{16,8},{24,16},{28,24},{20,28},{12,20},{4,12},{0,4},{9,1},{1... | collective-permute-start | bytes 393224 | tf_op jit(solution)/shard_map/ppermute | solution.py:685
  653.4 29.7 %collective-permute-start.83 = (f32[64,512]{1,0:T(8,128)S(1)}, f32[64,512]{1,0:T(8,128)S(1)}, u32[]{:S(2)}, u32[]{:S(2)}) collective-permute-start(f32[64,512]{1,0:T(8,128)S(1)} %bitcast_add_fusion.18), channel_id=1, source_target_pairs={{0,8},{8,16},{16,24},{24,28},{28,20},{20,12},{12,4},{4,0},{1,9},{9... | collective-permute-start | bytes 393224 | tf_op jit(solution)/shard_map/ppermute | solution.py:683
  656.4 45.9 %collective-permute-start.94 = (f32[256,512]{1,0:T(8,128)S(1)}, f32[256,512]{1,0:T(8,128)S(1)}, u32[]{:S(2)}, u32[]{:S(2)}) collective-permute-start(f32[256,512]{1,0:T(8,128)S(1)} %get-tuple-element.264), channel_id=1, source_target_pairs={{0,8},{8,16},{16,24},{24,28},{28,20},{20,12},{12,4},{4,0},{1,9},{9... | collective-permute-start | bytes 1572872 | tf_op jit(solution)/shard_map/ppermute | solution.py:683
  675.4 26.8 %collective-permute-start.98 = (f32[256,512]{1,0:T(8,128)S(1)}, f32[256,512]{1,0:T(8,128)S(1)}, u32[]{:S(2)}, u32[]{:S(2)}) collective-permute-start(f32[256,512]{1,0:T(8,128)S(1)} %bitcast_add_fusion.10), channel_id=1, source_target_pairs={{8,0},{16,8},{24,16},{28,24},{20,28},{12,20},{4,12},{0,4},{9,1},{1... | collective-permute-start | bytes 1572872 | tf_op jit(solution)/shard_map/ppermute | solution.py:685
  685.9 38.5 %collective-permute-start.107 = (f32[576,512]{1,0:T(8,128)}, f32[576,512]{1,0:T(8,128)S(1)}, u32[]{:S(2)}, u32[]{:S(2)}) collective-permute-start(f32[576,512]{1,0:T(8,128)} %maximum_multiply_fusion), channel_id=1, source_target_pairs={{0,2},{1,3},{2,0},{3,1},{4,6},{5,7},{6,4},{7,5},{8,10},{9,11},{10,... | collective-permute-start | bytes 3538952 | tf_op jit(solution)/shard_map/ppermute | solution.py:559
  724.4 25.1 %collective-permute-start.109 = (f32[576,512]{1,0:T(8,128)}, f32[576,512]{1,0:T(8,128)S(1)}, u32[]{:S(2)}, u32[]{:S(2)}) collective-permute-start(f32[576,512]{1,0:T(8,128)} %maximum_multiply_fusion), channel_id=1, source_target_pairs={{0,1},{1,0},{2,3},{3,2},{4,5},{5,4},{6,7},{7,6},{8,9},{9,8},{10,11... | collective-permute-start | bytes 3538952 | tf_op jit(solution)/shard_map/ppermute | solution.py:559
  724.9 24.6 %collective-permute-start.108 = (f32[576,512]{1,0:T(8,128)S(1)}, f32[576,512]{1,0:T(8,128)S(1)}, u32[]{:S(2)}, u32[]{:S(2)}) collective-permute-start(f32[576,512]{1,0:T(8,128)S(1)} %collective-permute-done.107), channel_id=1, source_target_pairs={{0,1},{1,0},{2,3},{3,2},{4,5},{5,4},{6,7},{7,6},{8,9},{9,8},{10,11... | collective-permute-start | bytes 3538952 | tf_op jit(solution)/shard_map/ppermute | solution.py:559
  770.9 27.9 %collective-permute-start.105 = (f32[576,512]{1,0:T(8,128)}, f32[576,512]{1,0:T(8,128)}, u32[]{:S(2)}, u32[]{:S(2)}) collective-permute-start(f32[576,512]{1,0:T(8,128)} %broadcast_multiply_fusion.one), channel_id=1, source_target_pairs={{0,2},{1,3},{2,0},{3,1},{4,6},{5,7},{6,4},{7,5},{8,10},{9,11},{10,... | collective-permute-start | bytes 3538952 | tf_op jit(solution)/shard_map/ppermute | solution.py:559
  773.2 31.4 %collective-permute-start.104 = (f32[576,512]{1,0:T(8,128)}, f32[576,512]{1,0:T(8,128)}, u32[]{:S(2)}, u32[]{:S(2)}) collective-permute-start(f32[576,512]{1,0:T(8,128)} %broadcast_multiply_fusion.one), channel_id=1, source_target_pairs={{0,1},{1,0},{2,3},{3,2},{4,5},{5,4},{6,7},{7,6},{8,9},{9,8},{10,11... | collective-permute-start | bytes 3538952 | tf_op jit(solution)/shard_map/ppermute | solution.py:559
  (163 other events, 1540.2 us)
Sparse Core Ops, SparseCore 0:
  12.5 161.5 all-gather.3
  176.8 106.1 all-gather.5
  285.8 80.2 all-gather.7
  369.6 119.4 reduce-scatter.2
  500.9 189.9 reduce-scatter.4

commit v4 on v3

--- a/solution.py
+++ b/solution.py
@@ -793,8 +793,6 @@
         ],
         axis=1,
     )
-    heads_full = lax.all_gather(heads_mine, "batch", axis=0, tiled=True)
-
     def message_runs(array):
         runs = array.reshape(groups, nrows, grain, mid)
         return lax.dynamic_index_in_dim(runs, row, 1, keepdims=True)
@@ -805,16 +803,6 @@
     run = grain if grain % 8 == 0 else part
     segment_pair_mine = message_pair(segment_message, contour_message).reshape(held // 2, mid)
     depth_pair_mine = message_pair(depth_message, normal_message).reshape(held // 2, mid)
-    segment_pair_w, depth_pair_w = [
-        regroup(
-            lax.all_gather(mine, "batch", axis=0, tiled=True).reshape(
-                nbatch * groups, 2, grain, mid
-            ),
-            run,
-        )
-        for mine in (segment_pair_mine, depth_pair_mine)
-    ]
-
     expand_norm_mine = lax.dynamic_index_in_dim(
         expand_norm.reshape(2, nrows, wide_part), row, 1, keepdims=False
     )
@@ -839,18 +827,6 @@
             "dilate": row_slice(dilate_weight, 1),
         }
     )
-    first_all, _ = ring.gather(first_mine, True)
-    reduce_full = from_narrow(first_all[:, first_spans["reduce"]]).reshape(nbatch * wide_part, mid)
-    params_all = first_all[:, first_spans["params"]]
-    dilate_full = first_all[:, first_spans["dilate"]].reshape(nbatch * held, part)
-
-    def all_params(pair, size):
-        return jnp.transpose(params_all[:, pair : pair + 2, :size], (1, 0, 2)).reshape(2, nbatch * size)
-
-    reduce_gain, reduce_bias = row_slice(all_params(0, mid_held), 1)
-    dilate_gain, dilate_bias = row_slice(all_params(2, mid_held), 1)
-    expand_gain, expand_bias = all_params(4, wide_part)
-
     spread_by_kernel = wide_part == 64 and part % 128 == 0
 
     def spread_wide(array):
@@ -868,6 +844,34 @@
             ]
         return jnp.concatenate(in_order(exchange_keyed(blocks), row), axis=0)
 
+    features, _ = lax.optimization_barrier((features, first_mine))
+    inputs = spread_wide(features.reshape(quarter, wide))
+    first_all, inputs = ring.gather(first_mine, True, inputs, 3)
+    first_all, heads_mine, segment_pair_mine, depth_pair_mine = lax.optimization_barrier(
+        (first_all, heads_mine, segment_pair_mine, depth_pair_mine)
+    )
+    heads_full = lax.all_gather(heads_mine, "batch", axis=0, tiled=True)
+    segment_pair_w, depth_pair_w = [
+        regroup(
+            lax.all_gather(mine, "batch", axis=0, tiled=True).reshape(
+                nbatch * groups, 2, grain, mid
+            ),
+            run,
+        )
+        for mine in (segment_pair_mine, depth_pair_mine)
+    ]
+
+    reduce_full = from_narrow(first_all[:, first_spans["reduce"]]).reshape(nbatch * wide_part, mid)
+    params_all = first_all[:, first_spans["params"]]
+    dilate_full = first_all[:, first_spans["dilate"]].reshape(nbatch * held, part)
+
+    def all_params(pair, size):
+        return jnp.transpose(params_all[:, pair : pair + 2, :size], (1, 0, 2)).reshape(2, nbatch * size)
+
+    reduce_gain, reduce_bias = row_slice(all_params(0, mid_held), 1)
+    dilate_gain, dilate_bias = row_slice(all_params(2, mid_held), 1)
+    expand_gain, expand_bias = all_params(4, wide_part)
+
     def exchange_wide(array):
         blocks = array.reshape(nrows, quarter, nbatch * wide_part)
         return exchange_keyed(
@@ -891,9 +895,6 @@
     def image_of(array):
         return array.reshape(height, breadth, array.shape[-1])
 
-    features, _ = lax.optimization_barrier((features, (heads_mine, segment_pair_mine, first_mine)))
-    inputs = spread_wide(features.reshape(quarter, wide))
-
     valid = depth_valid.astype(jnp.float32).reshape(quarter, 1)
     keep, give = single_call(
         split_product_kernel,
@@ -915,7 +916,6 @@
         here, gather_keyed(image_of(jax.nn.silu(normed_one))), dilate_full, 2
     )
     total_two = sum_batch(sums_of(pre_dilate, pre_dilate))
-    total_two, heads_full = lax.optimization_barrier((total_two, heads_full))
     hat_two, normed_two, inverse_two = norm_forward(
         pre_dilate, total_two, dilate_gain, dilate_bias, count
     )
@@ -933,11 +933,11 @@
         }
     )
     square_mine, inverse_two = lax.optimization_barrier((square_mine, inverse_two))
+    square_all, _ = ring.gather(square_mine, False)
+    square_all, heads_full = lax.optimization_barrier((square_all, heads_full))
     feats, mid_out, pairs = joined_conv(
         here, gather_keyed(image_of(jax.nn.silu(normed_two))), heads_full, 1, True
     )
-    square_all, feats = ring.gather(square_mine, False, feats, 2)
-    square_all, segment_pair_w = lax.optimization_barrier((square_all, segment_pair_w))
     depth_gate_w, segment_gate_w, expand_w = [
         square_all[:, square_spans[name]].reshape(mid, mid)
         for name in ("depth_gate", "segment_gate", "expand")
@@ -950,11 +950,10 @@
     )
     feats_image = image_of(feats)
 
-    segment_mine, segment_got = scatter_end(*note_forward(here, feats_image, 1, segment_pair_w))
     pairs_got = jnp.stack(exchange_keyed([pairs[key] for key in range(4)]))
-    block_cotangent, _ = lax.optimization_barrier((block_cotangent, feats))
+    block_cotangent, _ = lax.optimization_barrier((block_cotangent, inverse_two))
     cotangent = spread_wide(block_cotangent.reshape(quarter, wide))
-    pairs_got, segment_mine, cotangent = lax.optimization_barrier((pairs_got, segment_mine, cotangent))
+    pairs_got, cotangent = lax.optimization_barrier((pairs_got, cotangent))
     depth_cotangent = depth_cotangent.reshape(quarter, mid)
     both, one_map = (2 * quarter, mid), (quarter, mid)
     feat_pair, open_pair, d_depth_note = single_call(
@@ -964,6 +963,31 @@
         [both],
         8 * quarter * mid * mid,
     )
+
+    def lines(array):
+        return array.reshape(local_height, breadth, mid)
+
+    depth_pair_grad, d_depth_image = note_grad(here, feats, 0, gather_keyed(lines(d_depth_note)), run)
+    depth_pair_sums = lax.psum_scatter(
+        regroup(depth_pair_grad, grain).reshape(-1, mid), "batch", scatter_dimension=0, tiled=True
+    )
+    flat_mid_out = mid_out.reshape(pixels, mid)
+    pre_expand = product(flat_mid_out, expand_w, 1, 0)
+    hat_three, normed_three, inverse_three = norm_forward(
+        pre_expand, sum_batch(sums_of(pre_expand, pre_expand)), expand_gain, expand_bias, count
+    )
+    summed = normed_three + inputs
+    block_blocks = exchange_wide(jax.nn.silu(summed))
+    d_summed = cotangent * silu_grad(summed)
+    d_pre_expand, expand_sums = norm_backward(
+        d_summed, hat_three, inverse_three, expand_gain, count, False
+    )
+    segment_pair_w, block_blocks, _ = lax.optimization_barrier(
+        (segment_pair_w, block_blocks, (expand_sums, depth_pair_grad))
+    )
+    block_out = collect_wide(block_blocks)
+
+    segment_mine, segment_got = scatter_end(*note_forward(here, feats_image, 1, segment_pair_w))
 
     def segment_body(*refs):
         segment_kernel(classes, *refs)
@@ -986,38 +1010,13 @@
         8 * quarter * mid * mid,
     )
 
-    def lines(array):
-        return array.reshape(local_height, breadth, mid)
-
-    d_depth_blocks, d_segment_note = lax.optimization_barrier(
-        (gather_keyed(lines(d_depth_note)), d_segment_note)
-    )
-    depth_pair_grad, d_depth_image = note_grad(here, feats, 0, d_depth_blocks, run)
-    depth_pair_sums = lax.psum_scatter(
-        regroup(depth_pair_grad, grain).reshape(-1, mid), "batch", scatter_dimension=0, tiled=True
-    )
     segment_pair_grad, d_segment_image = note_grad(
         here, feats, 1, gather_keyed(lines(d_segment_note)), run
     )
-    flat_mid_out = mid_out.reshape(pixels, mid)
-    expand_input, _ = lax.optimization_barrier((flat_mid_out, d_segment_note))
-    pre_expand = product(expand_input, expand_w, 1, 0)
-    hat_three, normed_three, inverse_three = norm_forward(
-        pre_expand, sum_batch(sums_of(pre_expand, pre_expand)), expand_gain, expand_bias, count
-    )
-    summed = normed_three + inputs
-    block_blocks = exchange_wide(jax.nn.silu(summed))
-    d_summed = cotangent * silu_grad(summed)
-    d_pre_expand, expand_sums = norm_backward(
-        d_summed, hat_three, inverse_three, expand_gain, count, False
-    )
-
-    feats_late, depth_pair_w, _ = lax.optimization_barrier(
-        (feats_image, depth_pair_w, (segment_pair_grad, depth_pair_grad, expand_sums))
-    )
-    segment_pair_grad, _ = lax.optimization_barrier((segment_pair_grad, expand_sums))
     hops = Hops(ring, regroup(segment_pair_grad, grain).reshape(nbatch, held // 2, mid), True)
-    depth_mine, depth_got = scatter_end(*note_forward(here, feats_late, 0, depth_pair_w))
+    segment_back = note_back(d_segment_image, segment_pair_w)
+    depth_pair_w, segment_back = hops.step((depth_pair_w, segment_back))
+    depth_mine, depth_got = scatter_end(*note_forward(here, feats_image, 0, depth_pair_w))
     depth_back = note_back(hops.step(d_depth_image), depth_pair_w)
     depth_stream, direct_both, depth_gate_grad = single_call(
         depth_kernel,
@@ -1038,7 +1037,6 @@
         8 * quarter * mid * mid,
     )
     direct_got = jnp.stack(exchange_keyed([direct_both[key] for key in range(4)]))
-    segment_back = note_back(hops.step(d_segment_image), segment_pair_w)
     heads_grad, d_feats = heads_grad_of(
         here,
         hops.step(flat_mid_out),
@@ -1061,8 +1059,7 @@
     gate_terms = jnp.transpose(gate_terms.reshape(3, nbatch, nrows, gate_rows, mid), (2, 1, 0, 3, 4))
     gate_sums = scatter_rows(gate_terms, row).reshape(nbatch, 3 * gate_rows, mid)
 
-    d_feats, block_blocks = lax.optimization_barrier((hops.step(d_feats), block_blocks))
-    block_out = collect_wide(block_blocks)
+    d_feats = hops.step(d_feats)
     segment_pair_sums = hops.result()
     mine_terms, got_terms = scatter_end(
         *conv_back(here, d_feats, heads_full, 1, product(d_pre_expand, expand_w, 1, 1))
@@ -1099,7 +1096,12 @@
     square_grad, reduce_sums, depth_pair_sums, segment_pair_sums = lax.optimization_barrier(
         (square_grad, reduce_sums, depth_pair_sums, segment_pair_sums)
     )
-    square_sums = ring.scatter(square_grad, False)
+    square_hops = Hops(ring, square_grad, False)
+    square_hops.step()
+    square_hops.step()
+    heads_sums = square_hops.step(heads_sums)
+    square_hops.step()
+    square_sums = square_hops.result()
     reduce_out = ring.scatter(reduce_grad.reshape(nbatch, wide_part, mid), True)
     features_grad = collect_wide(exchange_wide(features_back))
 

time: 831 us -> 844 us (1.016)
  waiting for transfers between devices: 296 us -> 335 us
  starting transfers between devices: 170 us -> 132 us
  local copies, waits for them, and re-layouts: 71.5 us -> 80.3 us
    ppermute x7, waiting for transfers between devices: 58.2 us -> 15.4 us  [gather(): rising = lax.ppermute(rising, 'batch', self.up)]
    ppermute x7, waiting for transfers between devices: 34.1 us -> 74.4 us  [gather(): falling = lax.ppermute(falling, 'batch', self.down)]
    ppermute x18, starting transfers between devices: 49.3 us -> 23.2 us  [swap(): return lax.ppermute(block, 'batch', [(i, i ^ mask) for i in range(size)])]
    ppermute x7, starting transfers between devices: 24.1 us -> 3.94 us  [gather(): rising = lax.ppermute(rising, 'batch', self.up)]
    ppermute x10, waiting for transfers between devices: 43.2 us -> 60.7 us  [step(): self.falling = lax.ppermute(self.falling, 'batch', self.ring.down)]
    ppermute x18, waiting for transfers between devices: 19 us -> 30.3 us  [swap(): return lax.ppermute(block, 'batch', [(i, i ^ mask) for i in range(size)])]
  transfers between devices with their start and end apart: 115 -> 115, of which waited for: 50 -> 58; matrix products, arithmetic and copies ran while one was open for 15% -> 17% of each run, Pallas kernels for 21% -> 21%
where the time goes in v4:
time: 844 us; the launch traced here: 835 us
  waiting for transfers between devices  335 us (40%)
  Pallas kernels  184 us (22%)
  starting transfers between devices  132 us (16%)
  local copies, waits for them, and re-layouts  80.3 us (10%)
  other arithmetic  61.8 us (7%)
  between operations  31.4 us (4%)
  matrix products  10.8 us (1%)
    ppermute x57, waiting for transfers between devices, swap_rows(): return lax.ppermute(block, 'rows', [(i, i ^ mask) for i in range(size)])  113 us
    ppermute x7, waiting for transfers between devices, gather(): falling = lax.ppermute(falling, 'batch', self.down)  74.4 us
    ppermute x57, starting transfers between devices, swap_rows(): return lax.ppermute(block, 'rows', [(i, i ^ mask) for i in range(size)])  74.3 us
    ppermute x10, waiting for transfers between devices, step(): self.falling = lax.ppermute(self.falling, 'batch', self.ring.down)  60.7 us
    pallas_call x10, Pallas kernels, single_call(): kernel_call(body, (1,), [SCALAR] + [whole_spec(arg.shape) for arg in args...  44.4 us
    ppermute x11, waiting for transfers between devices, step(): self.rising = lax.ppermute(self.rising, 'batch', self.ring.up)  40.4 us
    ppermute x18, waiting for transfers between devices, swap(): return lax.ppermute(block, 'batch', [(i, i ^ mask) for i in range(size)])  30.3 us
    pallas_call x2, Pallas kernels, conv_back(): kernel_call(body, (9,), [SCALAR, whole_spec(image.shape), tap_rows(rows,...  25.3 us
  transfers between devices with their start and end apart: 115, of which 58 were waited for; matrix products, arithmetic and copies ran while one was open for 17% of the time, Pallas kernels for 21%

profile of v4, /device:TPU:1, one launch (start us, length us, event | category | flops | bytes accessed | tf_op | source)
XLA Modules:
  0.0 834.8 jit_solution(8916101389540814717)
XLA Ops:
  55.3 7.1 collective-permute-done.3
  75.7 7.1 collective-permute-done.9
  100.1 7.9 collective-permute-done.11
  135.0 10.1 %shard_map.384 = (f32[640,128]{1,0:T(8,128)}, f32[16,40,512]{2,1,0:T(8,128)}) custom-call(s32[1]{0:T(128)} %bitcast.row_ref.refs_0_, f32[16,40,128]{2,1,0:T(8,128)} %bitcast.450, f32[16,40,128]{2,1,0:T(8,128)} %copy-done.63, f32[16,40,128]{2,1,0:T(8,128)} %copy-done.60, f32[16,40,128]{2,1,0:T(8,128)} %copy-done.68, f32[4608,128]{1,0:T(8,128)} %bitcast.414), custom_call_target="tpu_custom_call" | custom-call | flops 2264924160 | bytes 12582912 | tf_op jit(solution)/shard_map/pallas_call | solution.py:431
  183.4 16.0 %collective-permute-done.25 = f32[208,512]{1,0:T(8,128)S(1)} collective-permute-done((f32[208,512]{1,0:T(8,128)S(1)}, f32[208,512]{1,0:T(8,128)S(1)}, u32[]{:S(2)}, u32[]{:S(2)}) %collective-permute-start.25) | collective-permute-done | bytes 426016 | tf_op jit(solution)/shard_map/ppermute | solution.py:653
  202.4 27.1 %collective-permute-done.27 = f32[208,512]{1,0:T(8,128)S(1)} collective-permute-done((f32[208,512]{1,0:T(8,128)S(1)}, f32[208,512]{1,0:T(8,128)S(1)}, u32[]{:S(2)}, u32[]{:S(2)}) %collective-permute-start.27) | collective-permute-done | bytes 426016 | tf_op jit(solution)/shard_map/ppermute | solution.py:653
  232.5 15.3 %collective-permute-done.29 = f32[208,512]{1,0:T(8,128)S(1)} collective-permute-done((f32[208,512]{1,0:T(8,128)S(1)}, f32[208,512]{1,0:T(8,128)S(1)}, u32[]{:S(2)}, u32[]{:S(2)}) %collective-permute-start.29) | collective-permute-done | bytes 426016 | tf_op jit(solution)/shard_map/ppermute | solution.py:653
  249.5 8.9 %collective-permute-done.30 = f32[208,512]{1,0:T(8,128)S(1)} collective-permute-done((f32[208,512]{1,0:T(8,128)S(1)}, f32[208,512]{1,0:T(8,128)S(1)}, u32[]{:S(2)}, u32[]{:S(2)}) %collective-permute-start.30) | collective-permute-done | bytes 426016 | tf_op jit(solution)/shard_map/ppermute | solution.py:653
  259.9 15.0 %shard_map.385 = (f32[640,512]{1,0:T(8,128)}, f32[16,40,512]{2,1,0:T(8,128)}, f32[4,320,128]{2,1,0:T(8,128)}) custom-call(s32[1]{0:T(128)} %bitcast.row_ref.refs_0_, f32[16,40,128]{2,1,0:T(8,128)} %bitcast.447, f32[16,40,128]{2,1,0:T(8,128)} %collective-permute-done.21.two, f32[16,40,128]{2,1,0:T(8,128)} %collective-permute-done.22.three, ...), custom_call_target="tpu_custom_call" | custom-call | flops 9059696640 | bytes 12582912 | tf_op jit(solution)/shard_map/pallas_call | solution.py:431
  293.5 8.0 collective-permute-done.47.three
  304.8 10.4 %shard_map.388 = (f32[72,2,16,512]{3,2,1,0:T(8,128)}, f32[16,40,512]{2,1,0:T(8,128)}) custom-call(s32[1]{0:T(128)} %bitcast.row_ref.refs_0_, f32[640,512]{1,0:T(8,128)} %get-tuple-element.117.input_ref, f32[4,40,512]{2,1,0:T(8,128)} %bitcast.531, f32[4,40,512]{2,1,0:T(8,128)} %copy-done.66, f32[4,40,512]{2,1,0:T(8,128)} %copy-done.64, f32[4,40,512]{2,1,0:T(8,128)} %copy-done.69), custom_call_target="tpu_custom_call" | custom-call | flops 4529848320 | bytes 12582912 | tf_op jit(solution)/shard_map/pallas_call | solution.py:540
  345.5 7.2 collective-permute-done.35.three
  352.7 10.4 %shard_map.390 = (f32[2,160,512]{2,1,0:T(8,128)}, f32[2,160,512]{2,1,0:T(8,128)}) custom-call(s32[1]{0:T(128)} %bitcast.row_ref.refs_0_, f32[16,40,512]{2,1,0:T(8,128)} %bitcast.533, f32[72,2,16,512]{3,2,1,0:T(8,128)} %bitcast.522), custom_call_target="tpu_custom_call" | custom-call | flops 4529848320 | bytes 12582912 | tf_op jit(solution)/shard_map/pallas_call | solution.py:504
  370.0 7.1 collective-permute-done.50.refs_2_
  385.1 7.0 collective-permute-done.52.three
  395.9 10.4 %shard_map.392 = (f32[72,2,16,512]{3,2,1,0:T(8,128)}, f32[16,40,512]{2,1,0:T(8,128)}) custom-call(s32[1]{0:T(128)} %bitcast.row_ref.refs_0_, f32[640,512]{1,0:T(8,128)} %get-tuple-element.117.input_ref, f32[4,40,512]{2,1,0:T(8,128)} %bitcast.528, f32[4,40,512]{2,1,0:T(8,128)} %copy-done.67, f32[4,40,512]{2,1,0:T(8,128)} %copy-done.65, f32[4,40,512]{2,1,0:T(8,128)} %copy-done.70), custom_call_target="tpu_custom_call" | custom-call | flops 4529848320 | bytes 12582912 | tf_op jit(solution)/shard_map/pallas_call | solution.py:540
  410.2 10.7 %shard_map.393 = f32[640,256]{1,0:T(8,128)} custom-call(f32[16,40,512]{2,1,0:T(8,128)} %get-tuple-element.133.note_ref, f32[72,2,16,512]{3,2,1,0:T(8,128)} %bitcast.523), custom_call_target="tpu_custom_call" | custom-call | flops 4529848320 | bytes 12582912 | tf_op jit(solution)/shard_map/pallas_call | solution.py:522
  423.9 10.4 %shard_map.394 = (f32[2,160,512]{2,1,0:T(8,128)}, f32[2,160,512]{2,1,0:T(8,128)}) custom-call(s32[1]{0:T(128)} %bitcast.row_ref.refs_0_, f32[16,40,512]{2,1,0:T(8,128)} %bitcast.534, f32[72,2,16,512]{3,2,1,0:T(8,128)} %bitcast.520), custom_call_target="tpu_custom_call" | custom-call | flops 4529848320 | bytes 12582912 | tf_op jit(solution)/shard_map/pallas_call | solution.py:504
  445.5 29.2 %collective-permute-done.59 = f32[288,512]{1,0:T(8,128)S(1)} collective-permute-done((f32[288,512]{1,0:T(8,128)S(1)}, f32[288,512]{1,0:T(8,128)S(1)}, u32[]{:S(2)}, u32[]{:S(2)}) %collective-permute-start.59) | collective-permute-done | bytes 589856 | tf_op jit(solution)/shard_map/ppermute | solution.py:685
  487.2 10.7 %shard_map.396 = f32[640,256]{1,0:T(8,128)} custom-call(f32[16,40,512]{2,1,0:T(8,128)} %get-tuple-element.148.note_ref, f32[72,2,16,512]{3,2,1,0:T(8,128)} %bitcast.521), custom_call_target="tpu_custom_call" | custom-call | flops 4529848320 | bytes 12582912 | tf_op jit(solution)/shard_map/pallas_call | solution.py:522
  498.8 17.0 %shard_map.397 = (f32[4608,512]{1,0:T(8,128)}, f32[16,40,512]{2,1,0:T(8,128)}) custom-call(s32[1]{0:T(128)} %bitcast.row_ref.refs_0_, f32[640,512]{1,0:T(8,128)} %bitcast.397, f32[16,40,256]{2,1,0:T(8,128)} %bitcast.536, f32[16,40,256]{2,1,0:T(8,128)} %bitcast.535, f32[4,8,40,128]{3,2,1,0:T(8,128)} %pad_maximum_fusion.9.direct_ref), custom_call_target="tpu_custom_call" | custom-call | flops 9059696640 | bytes 12582912 | tf_op jit(solution)/shard_map/pallas_call | solution.py:487
  520.1 17.1 %collective-permute-done.62 = f32[288,512]{1,0:T(8,128)} collective-permute-done((f32[288,512]{1,0:T(8,128)S(1)}, f32[288,512]{1,0:T(8,128)}, u32[]{:S(2)}, u32[]{:S(2)}) %collective-permute-start.62) | collective-permute-done | bytes 589856 | tf_op jit(solution)/shard_map/ppermute | solution.py:683
  537.2 15.5 %shard_map.398 = (f32[2,640,128]{2,1,0:T(8,128)}, f32[2,640,128]{2,1,0:T(8,128)}) custom-call(s32[1]{0:T(128)} %bitcast.row_ref.refs_0_, f32[16,40,512]{2,1,0:T(8,128)} %get-tuple-element.152.refs_1_, f32[4608,512]{1,0:T(8,128)} %all-gather.6.cloned.1.call-done.weight_ref.refs_2_, f32[640,512]{1,0:T(8,128)} %fusion.28.refs_3_), custom_call_target="tpu_custom_call" | custom-call | flops 9059696640 | bytes 12582912 | tf_op jit(solution)/shard_map/pallas_call | solution.py:452
  557.9 7.6 collective-permute-done.67
  579.5 9.8 %shard_map.399 = (f32[2,640,128]{2,1,0:T(8,128)}, f32[2,640,128]{2,1,0:T(8,128)}) custom-call(s32[1]{0:T(128)} %bitcast.row_ref.refs_0_, f32[16,40,128]{2,1,0:T(8,128)} %bitcast.443, f32[4608,128]{1,0:T(8,128)} %bitcast.415), custom_call_target="tpu_custom_call" | custom-call | flops 2264924160 | bytes 12582912 | tf_op jit(solution)/shard_map/pallas_call | solution.py:452
  626.3 8.8 %shard_map.402 = f32[4608,128]{1,0:T(8,128)} custom-call(f32[640,512]{1,0:T(8,128)} %bitcast.532, f32[16,40,128]{2,1,0:T(8,128)} %bitcast.444), custom_call_target="tpu_custom_call" | custom-call | flops 2264924160 | bytes 12582912 | tf_op jit(solution)/shard_map/pallas_call | solution.py:471
  678.3 18.8 %collective-permute-done.84 = f32[64,512]{1,0:T(8,128)S(1)} collective-permute-done((f32[64,512]{1,0:T(8,128)S(1)}, f32[64,512]{1,0:T(8,128)S(1)}, u32[]{:S(2)}, u32[]{:S(2)}) %collective-permute-start.84) | collective-permute-done | bytes 131104 | tf_op jit(solution)/shard_map/ppermute | solution.py:683
  697.1 13.0 %collective-permute-done.87 = f32[64,512]{1,0:T(8,128)S(1)} collective-permute-done((f32[64,512]{1,0:T(8,128)S(1)}, f32[64,512]{1,0:T(8,128)S(1)}, u32[]{:S(2)}, u32[]{:S(2)}) %collective-permute-start.87) | collective-permute-done | bytes 131104 | tf_op jit(solution)/shard_map/ppermute | solution.py:685
  727.8 7.3 collective-permute-done.81.four
  766.3 8.7 %collective-permute-done.100 = f32[256,512]{1,0:T(8,128)S(1)} collective-permute-done((f32[256,512]{1,0:T(8,128)S(1)}, f32[256,512]{1,0:T(8,128)S(1)}, u32[]{:S(2)}, u32[]{:S(2)}) %collective-permute-start.100) | collective-permute-done | bytes 524320 | tf_op jit(solution)/shard_map/ppermute | solution.py:685
  780.6 23.5 %collective-permute-done.101 = f32[264,512]{1,0:T(8,128)S(1)} collective-permute-done((f32[264,512]{1,0:T(8,128)S(1)}, f32[264,512]{1,0:T(8,128)S(1)}, u32[]{:S(2)}, u32[]{:S(2)}) %collective-permute-start.101) | collective-permute-done | bytes 540704 | tf_op jit(solution)/shard_map/ppermute | solution.py:559
  820.2 7.9 shard_map.403
  (571 shorter events, 412.3 us)
Async XLA Ops:
  7.2 252.0 %all-gather.6.cloned.1.call-start = ((), (), s32[]{:S(2)}) async-start(), calls=%async_computation.3 | async-start | bytes 10616832 | tf_op jit(solution)/shard_map/all_gather | solution.py:853
  12.9 38.1 %collective-permute-start.1 = (f32[840,128]{1,0:T(8,128)S(1)}, f32[840,128]{1,0:T(8,128)S(1)}, u32[]{:S(2)}, u32[]{:S(2)}) collective-permute-start(f32[840,128]{1,0:T(8,128)S(1)} %dynamic-slice_dynamic-update-slice_fusion), channel_id=1, source_target_pairs={{8,0},{16,8},{24,16},{28,24},{20,28},{12,20},{4,12},{0,4},{9,1},{1... | collective-permute-start | bytes 1290248 | tf_op jit(solution)/shard_map/ppermute | solution.py:653
  14.9 37.6 %collective-permute-start = (f32[840,128]{1,0:T(8,128)S(1)}, f32[840,128]{1,0:T(8,128)}, u32[]{:S(2)}, u32[]{:S(2)}) collective-permute-start(f32[840,128]{1,0:T(8,128)S(1)} %dynamic-slice_dynamic-update-slice_fusion), channel_id=1, source_target_pairs={{0,8},{8,16},{16,24},{24,28},{28,20},{20,12},{12,4},{4,0},{1,9},{9... | collective-permute-start | bytes 1290248 | tf_op jit(solution)/shard_map/ppermute | solution.py:650
  20.1 28.3 %collective-permute-start.6 = (f32[160,512]{1,0:T(8,128)}, f32[160,512]{1,0:T(8,128)}, u32[]{:S(2)}, u32[]{:S(2)}) collective-permute-start(f32[160,512]{1,0:T(8,128)} %get-tuple-element.304), channel_id=1, source_target_pairs={{0,1},{1,0},{2,3},{3,2},{4,5},{5,4},{6,7},{7,6},{8,9},{9,8},{10,11... | collective-permute-start | bytes 983048 | tf_op jit(solution)/shard_map/ppermute | solution.py:559
  21.1 27.3 %collective-permute-start.5 = (f32[160,512]{1,0:T(8,128)}, f32[160,512]{1,0:T(8,128)}, u32[]{:S(2)}, u32[]{:S(2)}) collective-permute-start(f32[160,512]{1,0:T(8,128)} %get-tuple-element.305), channel_id=1, source_target_pairs={{0,2},{1,3},{2,0},{3,1},{4,6},{5,7},{6,4},{7,5},{8,10},{9,11},{10,... | collective-permute-start | bytes 983048 | tf_op jit(solution)/shard_map/ppermute | solution.py:559
  22.7 25.7 %collective-permute-start.4 = (f32[160,512]{1,0:T(8,128)}, f32[160,512]{1,0:T(8,128)}, u32[]{:S(2)}, u32[]{:S(2)}) collective-permute-start(f32[160,512]{1,0:T(8,128)} %get-tuple-element.306), channel_id=1, source_target_pairs={{0,3},{1,2},{2,1},{3,0},{4,7},{5,6},{6,5},{7,4},{8,11},{9,10},{10,... | collective-permute-start | bytes 983048 | tf_op jit(solution)/shard_map/ppermute | solution.py:559
  83.7 260.1 %all-gather.4.cloned.1.call-start = ((), (), s32[]{:S(2)}) async-start(), calls=%async_computation.2 | async-start | bytes 5308416 | tf_op jit(solution)/shard_map/all_gather | solution.py:856
  84.4 336.4 %all-gather.8.cloned.1.call-start = ((), (), s32[]{:S(2)}) async-start(), calls=%async_computation.4 | async-start | bytes 5308416 | tf_op jit(solution)/shard_map/all_gather | solution.py:856
  117.2 546.1 %reduce-scatter.3.cloned.1.call-start = ((), (), s32[]{:S(2)}) async-start(), calls=%async_computation.5 | async-start | bytes 5308416 | tf_op jit(solution)/shard_map/reduce_scatter | solution.py:971
  166.5 92.7 %collective-permute-start.21 = (f32[16,40,128]{2,1,0:T(8,128)S(1)}, f32[16,40,128]{2,1,0:T(8,128)}, u32[]{:S(2)}, u32[]{:S(2)}) collective-permute-start(f32[16,40,128]{2,1,0:T(8,128)S(1)} %bitcast.446), channel_id=1, source_target_pairs={{0,1},{1,0},{2,3},{3,2},{4,5},{5,4},{6,7},{7,6},{8,9},{9,8},{10,11... | collective-permute-start | bytes 983048 | tf_op jit(solution)/shard_map/ppermute | solution.py:559
  169.7 29.6 %collective-permute-start.25 = (f32[208,512]{1,0:T(8,128)S(1)}, f32[208,512]{1,0:T(8,128)S(1)}, u32[]{:S(2)}, u32[]{:S(2)}) collective-permute-start(f32[208,512]{1,0:T(8,128)S(1)} %pad_maximum_fusion.13), channel_id=1, source_target_pairs={{8,0},{16,8},{24,16},{28,24},{20,28},{12,20},{4,12},{0,4},{9,1},{1... | collective-permute-start | bytes 1277960 | tf_op jit(solution)/shard_map/ppermute | solution.py:653
  171.1 28.3 %collective-permute-start.24 = (f32[208,512]{1,0:T(8,128)S(1)}, f32[208,512]{1,0:T(8,128)S(1)}, u32[]{:S(2)}, u32[]{:S(2)}) collective-permute-start(f32[208,512]{1,0:T(8,128)S(1)} %pad_maximum_fusion.13), channel_id=1, source_target_pairs={{0,8},{8,16},{16,24},{24,28},{28,20},{20,12},{12,4},{4,0},{1,9},{9... | collective-permute-start | bytes 1277960 | tf_op jit(solution)/shard_map/ppermute | solution.py:650
  173.7 85.4 %collective-permute-start.23 = (f32[16,40,128]{2,1,0:T(8,128)}, f32[16,40,128]{2,1,0:T(8,128)S(1)}, u32[]{:S(2)}, u32[]{:S(2)}) collective-permute-start(f32[16,40,128]{2,1,0:T(8,128)} %collective-permute-done.22.three), channel_id=1, source_target_pairs={{0,1},{1,0},{2,3},{3,2},{4,5},{5,4},{6,7},{7,6},{8,9},{9,8},{10,11... | collective-permute-start | bytes 983048 | tf_op jit(solution)/shard_map/ppermute | solution.py:559
  199.4 30.1 %collective-permute-start.27 = (f32[208,512]{1,0:T(8,128)S(1)}, f32[208,512]{1,0:T(8,128)S(1)}, u32[]{:S(2)}, u32[]{:S(2)}) collective-permute-start(f32[208,512]{1,0:T(8,128)S(1)} %collective-permute-done.25), channel_id=1, source_target_pairs={{8,0},{16,8},{24,16},{28,24},{20,28},{12,20},{4,12},{0,4},{9,1},{1... | collective-permute-start | bytes 1277960 | tf_op jit(solution)/shard_map/ppermute | solution.py:653
  199.4 30.1 %collective-permute-start.26 = (f32[208,512]{1,0:T(8,128)S(1)}, f32[208,512]{1,0:T(8,128)S(1)}, u32[]{:S(2)}, u32[]{:S(2)}) collective-permute-start(f32[208,512]{1,0:T(8,128)S(1)} %collective-permute-done.24), channel_id=1, source_target_pairs={{0,8},{8,16},{16,24},{24,28},{28,20},{20,12},{12,4},{4,0},{1,9},{9... | collective-permute-start | bytes 1277960 | tf_op jit(solution)/shard_map/ppermute | solution.py:650
  315.2 446.2 %reduce-scatter.5.cloned.1.call-start = ((), (), s32[]{:S(2)}) async-start(), calls=%async_computation.6 | async-start | bytes 10616832 | tf_op jit(solution)/shard_map/reduce_scatter | solution.py:1047
  442.1 32.6 %collective-permute-start.59 = (f32[288,512]{1,0:T(8,128)S(1)}, f32[288,512]{1,0:T(8,128)S(1)}, u32[]{:S(2)}, u32[]{:S(2)}) collective-permute-start(f32[288,512]{1,0:T(8,128)S(1)} %get-tuple-element.248), channel_id=1, source_target_pairs={{8,0},{16,8},{24,16},{28,24},{20,28},{12,20},{4,12},{0,4},{9,1},{1... | collective-permute-start | bytes 1769480 | tf_op jit(solution)/shard_map/ppermute | solution.py:685
  443.5 31.2 %collective-permute-start.58 = (f32[288,512]{1,0:T(8,128)S(1)}, f32[288,512]{1,0:T(8,128)S(1)}, u32[]{:S(2)}, u32[]{:S(2)}) collective-permute-start(f32[288,512]{1,0:T(8,128)S(1)} %get-tuple-element.249), channel_id=1, source_target_pairs={{0,8},{8,16},{16,24},{24,28},{28,20},{20,12},{12,4},{4,0},{1,9},{9... | collective-permute-start | bytes 1769480 | tf_op jit(solution)/shard_map/ppermute | solution.py:683
  444.4 33.3 %collective-permute-start.57 = (f32[160,512]{1,0:T(8,128)S(1)}, f32[160,512]{1,0:T(8,128)S(1)}, u32[]{:S(2)}, u32[]{:S(2)}) collective-permute-start(f32[160,512]{1,0:T(8,128)S(1)} %get-tuple-element.293), channel_id=1, source_target_pairs={{0,2},{1,3},{2,0},{3,1},{4,6},{5,7},{6,4},{7,5},{8,10},{9,11},{10,... | collective-permute-start | bytes 983048 | tf_op jit(solution)/shard_map/ppermute | solution.py:559
  476.2 22.6 %collective-permute-start.61 = (f32[288,512]{1,0:T(8,128)S(1)}, f32[288,512]{1,0:T(8,128)S(1)}, u32[]{:S(2)}, u32[]{:S(2)}) collective-permute-start(f32[288,512]{1,0:T(8,128)S(1)} %get-tuple-element.246), channel_id=1, source_target_pairs={{8,0},{16,8},{24,16},{28,24},{20,28},{12,20},{4,12},{0,4},{9,1},{1... | collective-permute-start | bytes 1769480 | tf_op jit(solution)/shard_map/ppermute | solution.py:685
  477.6 21.3 %collective-permute-start.60 = (f32[288,512]{1,0:T(8,128)S(1)}, f32[288,512]{1,0:T(8,128)S(1)}, u32[]{:S(2)}, u32[]{:S(2)}) collective-permute-start(f32[288,512]{1,0:T(8,128)S(1)} %get-tuple-element.247), channel_id=1, source_target_pairs={{0,8},{8,16},{16,24},{24,28},{28,20},{20,12},{12,4},{4,0},{1,9},{9... | collective-permute-start | bytes 1769480 | tf_op jit(solution)/shard_map/ppermute | solution.py:683
  619.4 29.0 %collective-permute-start.93 = (f32[8,3,16,512]{3,2,1,0:T(8,128)S(1)}, f32[8,3,16,512]{3,2,1,0:T(8,128)S(1)}, u32[]{:S(2)}, u32[]{:S(2)}) collective-permute-start(f32[8,3,16,512]{3,2,1,0:T(8,128)S(1)} %dynamic-slice_bitcast_fusion.1), channel_id=1, source_target_pairs={{0,2},{1,3},{2,0},{3,1},{4,6},{5,7},{6,4},{7,5},{8,10},{9,11},{10,... | collective-permute-start | bytes 2359304 | tf_op jit(solution)/shard_map/ppermute | solution.py:559
  664.6 52.2 %collective-permute-start.97 = (f32[256,512]{1,0:T(8,128)S(1)}, f32[256,512]{1,0:T(8,128)S(1)}, u32[]{:S(2)}, u32[]{:S(2)}) collective-permute-start(f32[256,512]{1,0:T(8,128)S(1)} %get-tuple-element.256), channel_id=1, source_target_pairs={{8,0},{16,8},{24,16},{28,24},{20,28},{12,20},{4,12},{0,4},{9,1},{1... | collective-permute-start | bytes 1572872 | tf_op jit(solution)/shard_map/ppermute | solution.py:685
  665.8 51.1 %collective-permute-start.94 = (f32[256,512]{1,0:T(8,128)S(1)}, f32[256,512]{1,0:T(8,128)S(1)}, u32[]{:S(2)}, u32[]{:S(2)}) collective-permute-start(f32[256,512]{1,0:T(8,128)S(1)} %get-tuple-element.257), channel_id=1, source_target_pairs={{0,8},{8,16},{16,24},{24,28},{28,20},{20,12},{12,4},{4,0},{1,9},{9... | collective-permute-start | bytes 1572872 | tf_op jit(solution)/shard_map/ppermute | solution.py:683
  671.8 25.4 %collective-permute-start.84 = (f32[64,512]{1,0:T(8,128)S(1)}, f32[64,512]{1,0:T(8,128)S(1)}, u32[]{:S(2)}, u32[]{:S(2)}) collective-permute-start(f32[64,512]{1,0:T(8,128)S(1)} %get-tuple-element.309), channel_id=1, source_target_pairs={{0,8},{8,16},{16,24},{24,28},{28,20},{20,12},{12,4},{4,0},{1,9},{9... | collective-permute-start | bytes 393224 | tf_op jit(solution)/shard_map/ppermute | solution.py:683
  672.6 37.5 %collective-permute-start.87 = (f32[64,512]{1,0:T(8,128)S(1)}, f32[64,512]{1,0:T(8,128)S(1)}, u32[]{:S(2)}, u32[]{:S(2)}) collective-permute-start(f32[64,512]{1,0:T(8,128)S(1)} %get-tuple-element.310), channel_id=1, source_target_pairs={{8,0},{16,8},{24,16},{28,24},{20,28},{12,20},{4,12},{0,4},{9,1},{1... | collective-permute-start | bytes 393224 | tf_op jit(solution)/shard_map/ppermute | solution.py:685
  676.9 67.6 %collective-permute-start.107 = (f32[576,512]{1,0:T(8,128)}, f32[576,512]{1,0:T(8,128)S(1)}, u32[]{:S(2)}, u32[]{:S(2)}) collective-permute-start(f32[576,512]{1,0:T(8,128)} %maximum_multiply_fusion), channel_id=1, source_target_pairs={{0,2},{1,3},{2,0},{3,1},{4,6},{5,7},{6,4},{7,5},{8,10},{9,11},{10,... | collective-permute-start | bytes 3538952 | tf_op jit(solution)/shard_map/ppermute | solution.py:559
  719.2 26.0 %collective-permute-start.98 = (f32[256,512]{1,0:T(8,128)}, f32[256,512]{1,0:T(8,128)}, u32[]{:S(2)}, u32[]{:S(2)}) collective-permute-start(f32[256,512]{1,0:T(8,128)} %get-tuple-element.254), channel_id=1, source_target_pairs={{8,0},{16,8},{24,16},{28,24},{20,28},{12,20},{4,12},{0,4},{9,1},{1... | collective-permute-start | bytes 1572872 | tf_op jit(solution)/shard_map/ppermute | solution.py:685
  720.6 24.6 %collective-permute-start.95 = (f32[256,512]{1,0:T(8,128)}, f32[256,512]{1,0:T(8,128)}, u32[]{:S(2)}, u32[]{:S(2)}) collective-permute-start(f32[256,512]{1,0:T(8,128)} %get-tuple-element.255), channel_id=1, source_target_pairs={{0,8},{8,16},{16,24},{24,28},{28,20},{20,12},{12,4},{4,0},{1,9},{9... | collective-permute-start | bytes 1572872 | tf_op jit(solution)/shard_map/ppermute | solution.py:683
  766.1 45.2 %collective-permute-start.105 = (f32[576,512]{1,0:T(8,128)}, f32[576,512]{1,0:T(8,128)}, u32[]{:S(2)}, u32[]{:S(2)}) collective-permute-start(f32[576,512]{1,0:T(8,128)} %broadcast_multiply_fusion.one), channel_id=1, source_target_pairs={{0,2},{1,3},{2,0},{3,1},{4,6},{5,7},{6,4},{7,5},{8,10},{9,11},{10,... | collective-permute-start | bytes 3538952 | tf_op jit(solution)/shard_map/ppermute | solution.py:559
  776.5 27.7 %collective-permute-start.101 = (f32[264,512]{1,0:T(8,128)S(1)}, f32[264,512]{1,0:T(8,128)S(1)}, u32[]{:S(2)}, u32[]{:S(2)}) collective-permute-start(f32[264,512]{1,0:T(8,128)S(1)} %fusion.5), channel_id=1, source_target_pairs={{0,2},{1,3},{2,0},{3,1},{4,6},{5,7},{6,4},{7,5},{8,10},{9,11},{10,... | collective-permute-start | bytes 1622024 | tf_op jit(solution)/shard_map/ppermute | solution.py:559
  778.3 33.5 %collective-permute-start.103 = (f32[264,512]{1,0:T(8,128)S(1)}, f32[264,512]{1,0:T(8,128)S(1)}, u32[]{:S(2)}, u32[]{:S(2)}) collective-permute-start(f32[264,512]{1,0:T(8,128)S(1)} %fusion.5), channel_id=1, source_target_pairs={{0,1},{1,0},{2,3},{3,2},{4,5},{5,4},{6,7},{7,6},{8,9},{9,8},{10,11... | collective-permute-start | bytes 1622024 | tf_op jit(solution)/shard_map/ppermute | solution.py:559
  (154 other events, 1281.2 us)
Sparse Core Ops, SparseCore 0:
  83.8 158.7 all-gather.5
  245.3 83.9 all-gather.3
  332.1 78.5 all-gather.7
  414.1 118.1 reduce-scatter.2
  535.8 183.7 reduce-scatter.4

commit v5 on v4

--- a/solution.py
+++ b/solution.py
@@ -411,8 +411,9 @@
     return pl.BlockSpec((rows, cols), lambda tap: (tap, 0))
 
 
-def tap_runs(weight_shape):
-    return pl.BlockSpec((weight_shape[0] // 9,) + weight_shape[1:], lambda tap: (tap, 0, 0, 0))
+def tap_runs(weight_shape, pair=0):
+    runs, _, grain, mid = weight_shape
+    return pl.BlockSpec((runs // 9, 2, grain, mid), lambda tap: (tap, pair, 0, 0))
 
 
 def joined_conv(row, blocks, weight, dilation, with_pairs=False):
@@ -507,7 +508,7 @@
         [
             SCALAR,
             pl.BlockSpec((height, breadth, depth), lambda tap: (0, 0, pair)),
-            tap_runs(weight.shape),
+            tap_runs(weight.shape, pair),
         ],
         [whole_spec(shape)] * 2,
         [struct(shape)] * 2,
@@ -516,13 +517,13 @@
     )(row, image, weight)
 
 
-def note_back(note, weight):
+def note_back(note, pair, weight):
     height, breadth, mid = note.shape
-    shape = (height * breadth, weight.shape[0] // 9 * weight.shape[1] * weight.shape[2])
+    shape = (height * breadth, weight.shape[0] // 9 * 2 * weight.shape[2])
     return kernel_call(
         note_back_kernel,
         (9,),
-        [whole_spec(note.shape), tap_runs(weight.shape)],
+        [whole_spec(note.shape), tap_runs(weight.shape, pair)],
         whole_spec(shape),
         struct(shape),
         [framed_scratch(note.shape, 1)],
@@ -694,6 +695,13 @@
         self.hop += 1
         self.done = self.hop == max(self.ups, self.downs)
         return later
+
+    def await_beside(self, array):
+        if not self.done:
+            self.rising, self.falling, array = lax.optimization_barrier(
+                (self.rising, self.falling, array)
+            )
+        return array
 
     def result(self):
         return self.sums if self.sums is not None else self.own(0) + self.rising + self.falling
@@ -801,8 +809,21 @@
         return jnp.concatenate([message_runs(first), message_runs(second)], axis=1)
 
     run = grain if grain % 8 == 0 else part
-    segment_pair_mine = message_pair(segment_message, contour_message).reshape(held // 2, mid)
-    depth_pair_mine = message_pair(depth_message, normal_message).reshape(held // 2, mid)
+    messages_mine = jnp.concatenate(
+        [
+            message_pair(depth_message, normal_message),
+            message_pair(segment_message, contour_message),
+        ],
+        axis=1,
+    ).reshape(held, mid)
+    heads_full = lax.all_gather(heads_mine, "batch", axis=0, tiled=True)
+    messages_full = regroup(
+        lax.all_gather(messages_mine, "batch", axis=0, tiled=True).reshape(
+            nbatch * groups, 4, grain, mid
+        ),
+        run,
+    )
+
     expand_norm_mine = lax.dynamic_index_in_dim(
         expand_norm.reshape(2, nrows, wide_part), row, 1, keepdims=False
     )
@@ -847,20 +868,6 @@
     features, _ = lax.optimization_barrier((features, first_mine))
     inputs = spread_wide(features.reshape(quarter, wide))
     first_all, inputs = ring.gather(first_mine, True, inputs, 3)
-    first_all, heads_mine, segment_pair_mine, depth_pair_mine = lax.optimization_barrier(
-        (first_all, heads_mine, segment_pair_mine, depth_pair_mine)
-    )
-    heads_full = lax.all_gather(heads_mine, "batch", axis=0, tiled=True)
-    segment_pair_w, depth_pair_w = [
-        regroup(
-            lax.all_gather(mine, "batch", axis=0, tiled=True).reshape(
-                nbatch * groups, 2, grain, mid
-            ),
-            run,
-        )
-        for mine in (segment_pair_mine, depth_pair_mine)
-    ]
-
     reduce_full = from_narrow(first_all[:, first_spans["reduce"]]).reshape(nbatch * wide_part, mid)
     params_all = first_all[:, first_spans["params"]]
     dilate_full = first_all[:, first_spans["dilate"]].reshape(nbatch * held, part)
@@ -916,6 +923,7 @@
         here, gather_keyed(image_of(jax.nn.silu(normed_one))), dilate_full, 2
     )
     total_two = sum_batch(sums_of(pre_dilate, pre_dilate))
+    total_two, heads_full = lax.optimization_barrier((total_two, heads_full))
     hat_two, normed_two, inverse_two = norm_forward(
         pre_dilate, total_two, dilate_gain, dilate_bias, count
     )
@@ -933,11 +941,10 @@
         }
     )
     square_mine, inverse_two = lax.optimization_barrier((square_mine, inverse_two))
-    square_all, _ = ring.gather(square_mine, False)
-    square_all, heads_full = lax.optimization_barrier((square_all, heads_full))
     feats, mid_out, pairs = joined_conv(
         here, gather_keyed(image_of(jax.nn.silu(normed_two))), heads_full, 1, True
     )
+    square_all, feats = ring.gather(square_mine, False, feats, 2)
     depth_gate_w, segment_gate_w, expand_w = [
         square_all[:, square_spans[name]].reshape(mid, mid)
         for name in ("depth_gate", "segment_gate", "expand")
@@ -951,7 +958,7 @@
     feats_image = image_of(feats)
 
     pairs_got = jnp.stack(exchange_keyed([pairs[key] for key in range(4)]))
-    block_cotangent, _ = lax.optimization_barrier((block_cotangent, inverse_two))
+    block_cotangent, _ = lax.optimization_barrier((block_cotangent, feats))
     cotangent = spread_wide(block_cotangent.reshape(quarter, wide))
     pairs_got, cotangent = lax.optimization_barrier((pairs_got, cotangent))
     depth_cotangent = depth_cotangent.reshape(quarter, mid)
@@ -982,12 +989,12 @@
     d_pre_expand, expand_sums = norm_backward(
         d_summed, hat_three, inverse_three, expand_gain, count, False
     )
-    segment_pair_w, block_blocks, _ = lax.optimization_barrier(
-        (segment_pair_w, block_blocks, (expand_sums, depth_pair_grad))
+    messages_full, block_blocks, _ = lax.optimization_barrier(
+        (messages_full, block_blocks, (expand_sums, depth_pair_grad))
     )
     block_out = collect_wide(block_blocks)
 
-    segment_mine, segment_got = scatter_end(*note_forward(here, feats_image, 1, segment_pair_w))
+    segment_mine, segment_got = scatter_end(*note_forward(here, feats_image, 1, messages_full))
 
     def segment_body(*refs):
         segment_kernel(classes, *refs)
@@ -1013,11 +1020,12 @@
     segment_pair_grad, d_segment_image = note_grad(
         here, feats, 1, gather_keyed(lines(d_segment_note)), run
     )
+    depth_mine, depth_got = scatter_end(*note_forward(here, feats_image, 0, messages_full))
     hops = Hops(ring, regroup(segment_pair_grad, grain).reshape(nbatch, held // 2, mid), True)
-    segment_back = note_back(d_segment_image, segment_pair_w)
-    depth_pair_w, segment_back = hops.step((depth_pair_w, segment_back))
-    depth_mine, depth_got = scatter_end(*note_forward(here, feats_image, 0, depth_pair_w))
-    depth_back = note_back(hops.step(d_depth_image), depth_pair_w)
+    d_depth_image, _ = lax.optimization_barrier((d_depth_image, segment_pair_grad))
+    depth_back = note_back(d_depth_image, 0, messages_full)
+    d_segment_image, depth_back = hops.step((d_segment_image, depth_back))
+    segment_back = note_back(d_segment_image, 1, messages_full)
     depth_stream, direct_both, depth_gate_grad = single_call(
         depth_kernel,
         (
@@ -1060,10 +1068,11 @@
     gate_sums = scatter_rows(gate_terms, row).reshape(nbatch, 3 * gate_rows, mid)
 
     d_feats = hops.step(d_feats)
-    segment_pair_sums = hops.result()
     mine_terms, got_terms = scatter_end(
         *conv_back(here, d_feats, heads_full, 1, product(d_pre_expand, expand_w, 1, 1))
     )
+    mine_terms, depth_pair_sums = hops.step((mine_terms, depth_pair_sums))
+    segment_pair_sums = hops.result()
     d_pre_dilate, dilate_sums = norm_backward(
         (mine_terms + got_terms) * silu_grad(normed_two), hat_two, inverse_two, dilate_gain, count, False
     )
@@ -1099,7 +1108,8 @@
     square_hops = Hops(ring, square_grad, False)
     square_hops.step()
     square_hops.step()
-    heads_sums = square_hops.step(heads_sums)
+    heads_sums = square_hops.await_beside(heads_sums)
+    square_hops.step()
     square_hops.step()
     square_sums = square_hops.result()
     reduce_out = ring.scatter(reduce_grad.reshape(nbatch, wide_part, mid), True)

time: 844 us -> 880 us (1.043)
  starting transfers between devices: 132 us -> 197 us
  local copies, waits for them, and re-layouts: 80.3 us -> 58 us
    ppermute x7, waiting for transfers between devices: 15.4 us -> 50.5 us  [gather(): rising = lax.ppermute(rising, 'batch', self.up)]
    ppermute x18, starting transfers between devices: 23.2 us -> 48.3 us  [swap(): return lax.ppermute(block, 'batch', [(i, i ^ mask) for i in range(size)])]
    ppermute x57, waiting for transfers between devices: 113 us -> 88.4 us  [swap_rows(): return lax.ppermute(block, 'rows', [(i, i ^ mask) for i in range(size)])]
    ppermute x57, starting transfers between devices: 74.3 us -> 97.1 us  [swap_rows(): return lax.ppermute(block, 'rows', [(i, i ^ mask) for i in range(size)])]
    ppermute x10, waiting for transfers between devices: 60.7 us -> 40.1 us  [step(): self.falling = lax.ppermute(self.falling, 'batch', self.ring.down)]
    ppermute x7, starting transfers between devices: 3.94 us -> 21.7 us  [gather(): rising = lax.ppermute(rising, 'batch', self.up)]
    ppermute x7, waiting for transfers between devices: 74.4 us -> 89.6 us  [gather(): falling = lax.ppermute(falling, 'batch', self.down)]
  transfers between devices with their start and end apart: 115 -> 114, of which waited for: 58 -> 49; matrix products, arithmetic and copies ran while one was open for 17% -> 13% of each run, Pallas kernels for 21% -> 20%
where the time goes in v5:
time: 880 us; the launch traced here: 868 us
  waiting for transfers between devices  332 us (38%)
  starting transfers between devices  197 us (22%)
  Pallas kernels  183 us (21%)
  local copies, waits for them, and re-layouts  58 us (7%)
  other arithmetic  56.6 us (6%)
  between operations  32 us (4%)
  matrix products  9.29 us (1%)
    ppermute x57, starting transfers between devices, swap_rows(): return lax.ppermute(block, 'rows', [(i, i ^ mask) for i in range(size)])  97.1 us
    ppermute x7, waiting for transfers between devices, gather(): falling = lax.ppermute(falling, 'batch', self.down)  89.6 us
    ppermute x57, waiting for transfers between devices, swap_rows(): return lax.ppermute(block, 'rows', [(i, i ^ mask) for i in range(size)])  88.4 us
    ppermute x7, waiting for transfers between devices, gather(): rising = lax.ppermute(rising, 'batch', self.up)  50.5 us
    ppermute x18, starting transfers between devices, swap(): return lax.ppermute(block, 'batch', [(i, i ^ mask) for i in range(size)])  48.3 us
    pallas_call x10, Pallas kernels, single_call(): kernel_call(body, (1,), [SCALAR] + [whole_spec(arg.shape) for arg in args...  44.9 us
    ppermute x10, waiting for transfers between devices, step(): self.falling = lax.ppermute(self.falling, 'batch', self.ring.down)  40.1 us
    ppermute x11, waiting for transfers between devices, step(): self.rising = lax.ppermute(self.rising, 'batch', self.ring.up)  33.4 us
  transfers between devices with their start and end apart: 114, of which 49 were waited for; matrix products, arithmetic and copies ran while one was open for 13% of the time, Pallas kernels for 20%

profile of v5, /device:TPU:1, one launch (start us, length us, event | category | flops | bytes accessed | tf_op | source)
XLA Modules:
  0.0 868.4 jit_solution(9579352375407524689)
XLA Ops:
  49.1 29.2 %collective-permute-done.3 = f32[840,128]{1,0:T(8,128)S(1)} collective-permute-done((f32[840,128]{1,0:T(8,128)S(1)}, f32[840,128]{1,0:T(8,128)S(1)}, u32[]{:S(2)}, u32[]{:S(2)}) %collective-permute-start.3) | collective-permute-done | bytes 430112 | tf_op jit(solution)/shard_map/ppermute | solution.py:654
  80.2 7.4 collective-permute-done.7
  88.2 18.4 %collective-permute-done.9 = f32[840,128]{1,0:T(8,128)S(1)} collective-permute-done((f32[840,128]{1,0:T(8,128)S(1)}, f32[840,128]{1,0:T(8,128)S(1)}, u32[]{:S(2)}, u32[]{:S(2)}) %collective-permute-start.9) | collective-permute-done | bytes 430112 | tf_op jit(solution)/shard_map/ppermute | solution.py:651
  113.1 8.0 collective-permute-start.10
  125.4 7.8 collective-permute-done.11
  134.4 11.2 %collective-permute-start.12 = (f32[3,128]{1,0:T(4,128)S(1)}, f32[3,128]{1,0:T(4,128)S(1)}, u32[]{:S(2)}, u32[]{:S(2)}) collective-permute-start(f32[3,128]{1,0:T(4,128)S(1)} %pad_maximum_fusion.18), channel_id=1, source_target_pairs={{0,4},{4,0},{8,12},{12,8},{16,20},{20,16},{24,28},{28,24},{1,5},{5... | collective-permute-start | bytes 4616 | tf_op jit(solution)/shard_map/ppermute | solution.py:610
  176.4 10.0 %shard_map.384 = (f32[640,128]{1,0:T(8,128)}, f32[16,40,512]{2,1,0:T(8,128)}) custom-call(s32[1]{0:T(128)} %bitcast.row_ref.refs_0_, f32[16,40,128]{2,1,0:T(8,128)} %bitcast.442, f32[16,40,128]{2,1,0:T(8,128)} %copy-done.72, f32[16,40,128]{2,1,0:T(8,128)} %copy-done.69, f32[16,40,128]{2,1,0:T(8,128)} %copy-done.76, f32[4608,128]{1,0:T(8,128)} %bitcast.408), custom_call_target="tpu_custom_call" | custom-call | flops 2264924160 | bytes 12582912 | tf_op jit(solution)/shard_map/pallas_call | solution.py:432
  208.4 9.8 %collective-permute-done.24 = f32[208,512]{1,0:T(8,128)S(1)} collective-permute-done((f32[208,512]{1,0:T(8,128)S(1)}, f32[208,512]{1,0:T(8,128)S(1)}, u32[]{:S(2)}, u32[]{:S(2)}) %collective-permute-start.24) | collective-permute-done | bytes 426016 | tf_op jit(solution)/shard_map/ppermute | solution.py:651
  219.7 14.9 %shard_map.385 = (f32[640,512]{1,0:T(8,128)}, f32[16,40,512]{2,1,0:T(8,128)}, f32[4,320,128]{2,1,0:T(8,128)}) custom-call(s32[1]{0:T(128)} %bitcast.row_ref.refs_0_, f32[16,40,128]{2,1,0:T(8,128)} %bitcast.439, f32[16,40,128]{2,1,0:T(8,128)} %copy-done.67, f32[16,40,128]{2,1,0:T(8,128)} %copy-done.64, f32[16,40,128]{2,1,0:T(8,128)} %copy-done.73, ...), custom_call_target="tpu_custom_call" | custom-call | flops 9059696640 | bytes 12582912 | tf_op jit(solution)/shard_map/pallas_call | solution.py:432
  247.0 10.6 %collective-permute-start.26 = (f32[208,512]{1,0:T(8,128)S(1)}, f32[208,512]{1,0:T(8,128)S(1)}, u32[]{:S(2)}, u32[]{:S(2)}) collective-permute-start(f32[208,512]{1,0:T(8,128)S(1)} %collective-permute-done.24), channel_id=1, source_target_pairs={{0,8},{8,16},{16,24},{24,28},{28,20},{20,12},{12,4},{4,0},{1,9},{9... | collective-permute-start | bytes 1277960 | tf_op jit(solution)/shard_map/ppermute | solution.py:651
  263.8 14.9 %collective-permute-done.26 = f32[208,512]{1,0:T(8,128)S(1)} collective-permute-done((f32[208,512]{1,0:T(8,128)S(1)}, f32[208,512]{1,0:T(8,128)S(1)}, u32[]{:S(2)}, u32[]{:S(2)}) %collective-permute-start.26) | collective-permute-done | bytes 426016 | tf_op jit(solution)/shard_map/ppermute | solution.py:651
  278.7 9.6 %collective-permute-start.28 = (f32[208,512]{1,0:T(8,128)S(1)}, f32[208,512]{1,0:T(8,128)S(1)}, u32[]{:S(2)}, u32[]{:S(2)}) collective-permute-start(f32[208,512]{1,0:T(8,128)S(1)} %collective-permute-done.26), channel_id=1, source_target_pairs={{0,8},{8,16},{16,24},{24,28},{28,20},{20,12},{12,4},{4,0},{1,9},{9... | collective-permute-start | bytes 1277960 | tf_op jit(solution)/shard_map/ppermute | solution.py:651
  290.1 30.1 %collective-permute-done.29 = f32[208,512]{1,0:T(8,128)S(1)} collective-permute-done((f32[208,512]{1,0:T(8,128)S(1)}, f32[208,512]{1,0:T(8,128)S(1)}, u32[]{:S(2)}, u32[]{:S(2)}) %collective-permute-start.29) | collective-permute-done | bytes 426016 | tf_op jit(solution)/shard_map/ppermute | solution.py:654
  320.3 28.5 %collective-permute-done.30 = f32[208,512]{1,0:T(8,128)S(1)} collective-permute-done((f32[208,512]{1,0:T(8,128)S(1)}, f32[208,512]{1,0:T(8,128)S(1)}, u32[]{:S(2)}, u32[]{:S(2)}) %collective-permute-start.30) | collective-permute-done | bytes 426016 | tf_op jit(solution)/shard_map/ppermute | solution.py:654
  368.8 10.4 %shard_map.388 = (f32[72,2,16,512]{3,2,1,0:T(8,128)}, f32[16,40,512]{2,1,0:T(8,128)}) custom-call(s32[1]{0:T(128)} %bitcast.row_ref.refs_0_, f32[640,512]{1,0:T(8,128)} %get-tuple-element.115.input_ref, f32[4,40,512]{2,1,0:T(8,128)} %bitcast.523, f32[4,40,512]{2,1,0:T(8,128)} %copy-done.75, f32[4,40,512]{2,1,0:T(8,128)} %copy-done.74, f32[4,40,512]{2,1,0:T(8,128)} %copy-done.77), custom_call_target="tpu_custom_call" | custom-call | flops 4529848320 | bytes 12582912 | tf_op jit(solution)/shard_map/pallas_call | solution.py:541
  418.4 10.5 %shard_map.391 = (f32[2,160,512]{2,1,0:T(8,128)}, f32[2,160,512]{2,1,0:T(8,128)}) custom-call(s32[1]{0:T(128)} %bitcast.row_ref.refs_0_, f32[16,40,512]{2,1,0:T(8,128)} %bitcast.525, f32[72,4,16,512]{3,2,1,0:T(8,128)} %bitcast.512), custom_call_target="tpu_custom_call" | custom-call | flops 4529848320 | bytes 12582912 | tf_op jit(solution)/shard_map/pallas_call | solution.py:505
  430.2 10.5 %shard_map.390 = (f32[2,160,512]{2,1,0:T(8,128)}, f32[2,160,512]{2,1,0:T(8,128)}) custom-call(s32[1]{0:T(128)} %bitcast.row_ref.refs_0_, f32[16,40,512]{2,1,0:T(8,128)} %bitcast.526, f32[72,4,16,512]{3,2,1,0:T(8,128)} %bitcast.513), custom_call_target="tpu_custom_call" | custom-call | flops 4529848320 | bytes 12582912 | tf_op jit(solution)/shard_map/pallas_call | solution.py:505
  481.5 10.4 %shard_map.394 = (f32[72,2,16,512]{3,2,1,0:T(8,128)}, f32[16,40,512]{2,1,0:T(8,128)}) custom-call(s32[1]{0:T(128)} %bitcast.row_ref.refs_0_, f32[640,512]{1,0:T(8,128)} %get-tuple-element.115.input_ref, f32[4,40,512]{2,1,0:T(8,128)} %bitcast.519, f32[4,40,512]{2,1,0:T(8,128)} %copy-done.66, f32[4,40,512]{2,1,0:T(8,128)} %copy-done.63, f32[4,40,512]{2,1,0:T(8,128)} %copy-done.68), custom_call_target="tpu_custom_call" | custom-call | flops 4529848320 | bytes 12582912 | tf_op jit(solution)/shard_map/pallas_call | solution.py:541
  498.6 10.7 %shard_map.395 = f32[640,256]{1,0:T(8,128)} custom-call(f32[16,40,512]{2,1,0:T(8,128)} %get-tuple-element.140.note_ref, f32[72,4,16,512]{3,2,1,0:T(8,128)} %bitcast.514), custom_call_target="tpu_custom_call" | custom-call | flops 4529848320 | bytes 12582912 | tf_op jit(solution)/shard_map/pallas_call | solution.py:523
  513.4 10.7 %shard_map.396 = f32[640,256]{1,0:T(8,128)} custom-call(f32[16,40,512]{2,1,0:T(8,128)} %get-tuple-element.147.note_ref, f32[72,4,16,512]{3,2,1,0:T(8,128)} %bitcast.515), custom_call_target="tpu_custom_call" | custom-call | flops 4529848320 | bytes 12582912 | tf_op jit(solution)/shard_map/pallas_call | solution.py:523
  525.9 16.8 %shard_map.397 = (f32[4608,512]{1,0:T(8,128)}, f32[16,40,512]{2,1,0:T(8,128)}) custom-call(s32[1]{0:T(128)} %bitcast.row_ref.refs_0_, f32[640,512]{1,0:T(8,128)} %bitcast.390, f32[16,40,256]{2,1,0:T(8,128)} %bitcast.527, f32[16,40,256]{2,1,0:T(8,128)} %bitcast.528, f32[4,8,40,128]{3,2,1,0:T(8,128)} %pad_maximum_fusion.10.direct_ref), custom_call_target="tpu_custom_call" | custom-call | flops 9059696640 | bytes 12582912 | tf_op jit(solution)/shard_map/pallas_call | solution.py:488
  549.2 18.9 %collective-permute-done.61 = f32[288,512]{1,0:T(8,128)} collective-permute-done((f32[288,512]{1,0:T(8,128)S(1)}, f32[288,512]{1,0:T(8,128)}, u32[]{:S(2)}, u32[]{:S(2)}) %collective-permute-start.61) | collective-permute-done | bytes 589856 | tf_op jit(solution)/shard_map/ppermute | solution.py:686
  568.1 14.9 %shard_map.398 = (f32[2,640,128]{2,1,0:T(8,128)}, f32[2,640,128]{2,1,0:T(8,128)}) custom-call(s32[1]{0:T(128)} %bitcast.row_ref.refs_0_, f32[16,40,512]{2,1,0:T(8,128)} %get-tuple-element.152.refs_1_, f32[4608,512]{1,0:T(8,128)} %all-gather.5.cloned.1.call-done.weight_ref.refs_2_, f32[640,512]{1,0:T(8,128)} %fusion.26.refs_3_), custom_call_target="tpu_custom_call" | custom-call | flops 9059696640 | bytes 12582912 | tf_op jit(solution)/shard_map/pallas_call | solution.py:453
  583.1 14.2 %collective-permute-start.66 = (f32[2,640,128]{2,1,0:T(8,128)}, f32[2,640,128]{2,1,0:T(8,128)S(1)}, u32[]{:S(2)}, u32[]{:S(2)}) collective-permute-start(f32[2,640,128]{2,1,0:T(8,128)} %get-tuple-element.154), channel_id=1, source_target_pairs={{0,1},{1,0},{2,3},{3,2},{4,5},{5,4},{6,7},{7,6},{8,9},{9,8},{10,11... | collective-permute-start | bytes 1966088 | tf_op jit(solution)/shard_map/ppermute | solution.py:560
  600.8 25.7 %collective-permute-done.65 = f32[288,512]{1,0:T(8,128)S(1)} collective-permute-done((f32[288,512]{1,0:T(8,128)}, f32[288,512]{1,0:T(8,128)S(1)}, u32[]{:S(2)}, u32[]{:S(2)}) %collective-permute-start.65) | collective-permute-done | bytes 589856 | tf_op jit(solution)/shard_map/ppermute | solution.py:684
  628.0 17.3 %collective-permute-start.68 = (f32[2,128]{1,0:T(2,128)S(1)}, f32[2,128]{1,0:T(2,128)S(1)}, u32[]{:S(2)}, u32[]{:S(2)}) collective-permute-start(f32[2,128]{1,0:T(2,128)S(1)} %pad_maximum_fusion.21), channel_id=1, source_target_pairs={{0,4},{4,0},{8,12},{12,8},{16,20},{20,16},{24,28},{28,24},{1,5},{5... | collective-permute-start | bytes 3080 | tf_op jit(solution)/shard_map/ppermute | solution.py:610
  656.1 9.8 %shard_map.399 = (f32[2,640,128]{2,1,0:T(8,128)}, f32[2,640,128]{2,1,0:T(8,128)}) custom-call(s32[1]{0:T(128)} %bitcast.row_ref.refs_0_, f32[16,40,128]{2,1,0:T(8,128)} %bitcast.435, f32[4608,128]{1,0:T(8,128)} %bitcast.409), custom_call_target="tpu_custom_call" | custom-call | flops 2264924160 | bytes 12582912 | tf_op jit(solution)/shard_map/pallas_call | solution.py:453
  687.2 12.1 %collective-permute-done.93 = f32[8,3,16,512]{3,2,1,0:T(8,128)S(1)} collective-permute-done((f32[8,3,16,512]{3,2,1,0:T(8,128)S(1)}, f32[8,3,16,512]{3,2,1,0:T(8,128)S(1)}, u32[]{:S(2)}, u32[]{:S(2)}) %collective-permute-start.93) | collective-permute-done | bytes 786464 | tf_op jit(solution)/shard_map/ppermute | solution.py:560
  704.7 8.8 %shard_map.402 = f32[4608,128]{1,0:T(8,128)} custom-call(f32[640,512]{1,0:T(8,128)} %bitcast.524, f32[16,40,128]{2,1,0:T(8,128)} %bitcast.436), custom_call_target="tpu_custom_call" | custom-call | flops 2264924160 | bytes 12582912 | tf_op jit(solution)/shard_map/pallas_call | solution.py:472
  757.1 7.3 collective-permute-done.81.four
  813.5 24.2 %collective-permute-done.101 = f32[264,512]{1,0:T(8,128)S(1)} collective-permute-done((f32[264,512]{1,0:T(8,128)S(1)}, f32[264,512]{1,0:T(8,128)S(1)}, u32[]{:S(2)}, u32[]{:S(2)}) %collective-permute-start.101) | collective-permute-done | bytes 540704 | tf_op jit(solution)/shard_map/ppermute | solution.py:560
  853.6 7.9 shard_map.403
  (580 shorter events, 385.1 us)
Async XLA Ops:
  7.2 190.3 %all-gather.5.cloned.1.call-start = ((), (), s32[]{:S(2)}) async-start(), calls=%async_computation.3 | async-start | bytes 10616832 | tf_op jit(solution)/shard_map/all_gather | solution.py:819
  12.4 398.8 %all-gather.3.cloned.1.call-start = ((), (), s32[]{:S(2)}) async-start(), calls=%async_computation.2 | async-start | bytes 10616832 | tf_op jit(solution)/shard_map/all_gather | solution.py:821
  15.9 610.6 %reduce-scatter.3.cloned.1.call-start = ((), (), s32[]{:S(2)}) async-start(), calls=%async_computation.4 | async-start | bytes 5308416 | tf_op jit(solution)/shard_map/reduce_scatter | solution.py:978
  20.1 27.3 %collective-permute-start.2 = (f32[840,128]{1,0:T(8,128)S(1)}, f32[840,128]{1,0:T(8,128)S(1)}, u32[]{:S(2)}, u32[]{:S(2)}) collective-permute-start(f32[840,128]{1,0:T(8,128)S(1)} %dynamic-slice_dynamic-update-slice_fusion), channel_id=1, source_target_pairs={{8,0},{16,8},{24,16},{28,24},{20,28},{12,20},{4,12},{0,4},{9,1},{1... | collective-permute-start | bytes 1290248 | tf_op jit(solution)/shard_map/ppermute | solution.py:654
  22.2 26.8 %collective-permute-start = (f32[840,128]{1,0:T(8,128)S(1)}, f32[840,128]{1,0:T(8,128)S(1)}, u32[]{:S(2)}, u32[]{:S(2)}) collective-permute-start(f32[840,128]{1,0:T(8,128)S(1)} %dynamic-slice_dynamic-update-slice_fusion), channel_id=1, source_target_pairs={{0,8},{8,16},{16,24},{24,28},{28,20},{20,12},{12,4},{4,0},{1,9},{9... | collective-permute-start | bytes 1290248 | tf_op jit(solution)/shard_map/ppermute | solution.py:651
  47.3 31.0 %collective-permute-start.3 = (f32[840,128]{1,0:T(8,128)S(1)}, f32[840,128]{1,0:T(8,128)S(1)}, u32[]{:S(2)}, u32[]{:S(2)}) collective-permute-start(f32[840,128]{1,0:T(8,128)S(1)} %collective-permute-done.2), channel_id=1, source_target_pairs={{8,0},{16,8},{24,16},{28,24},{20,28},{12,20},{4,12},{0,4},{9,1},{1... | collective-permute-start | bytes 1290248 | tf_op jit(solution)/shard_map/ppermute | solution.py:654
  48.9 29.4 %collective-permute-start.1 = (f32[840,128]{1,0:T(8,128)S(1)}, f32[840,128]{1,0:T(8,128)S(1)}, u32[]{:S(2)}, u32[]{:S(2)}) collective-permute-start(f32[840,128]{1,0:T(8,128)S(1)} %collective-permute-done), channel_id=1, source_target_pairs={{0,8},{8,16},{16,24},{24,28},{28,20},{20,12},{12,4},{4,0},{1,9},{9... | collective-permute-start | bytes 1290248 | tf_op jit(solution)/shard_map/ppermute | solution.py:651
  87.6 19.0 %collective-permute-start.9 = (f32[840,128]{1,0:T(8,128)S(1)}, f32[840,128]{1,0:T(8,128)S(1)}, u32[]{:S(2)}, u32[]{:S(2)}) collective-permute-start(f32[840,128]{1,0:T(8,128)S(1)} %collective-permute-done.7), channel_id=1, source_target_pairs={{0,8},{8,16},{16,24},{24,28},{28,20},{20,12},{12,4},{4,0},{1,9},{9... | collective-permute-start | bytes 1290248 | tf_op jit(solution)/shard_map/ppermute | solution.py:651
  203.2 31.4 %collective-permute-start.25 = (f32[208,512]{1,0:T(8,128)S(1)}, f32[208,512]{1,0:T(8,128)S(1)}, u32[]{:S(2)}, u32[]{:S(2)}) collective-permute-start(f32[208,512]{1,0:T(8,128)S(1)} %pad_maximum_fusion.12), channel_id=1, source_target_pairs={{8,0},{16,8},{24,16},{28,24},{20,28},{12,20},{4,12},{0,4},{9,1},{1... | collective-permute-start | bytes 1277960 | tf_op jit(solution)/shard_map/ppermute | solution.py:654
  247.0 31.7 %collective-permute-start.26 = (f32[208,512]{1,0:T(8,128)S(1)}, f32[208,512]{1,0:T(8,128)S(1)}, u32[]{:S(2)}, u32[]{:S(2)}) collective-permute-start(f32[208,512]{1,0:T(8,128)S(1)} %collective-permute-done.24), channel_id=1, source_target_pairs={{0,8},{8,16},{16,24},{24,28},{28,20},{20,12},{12,4},{4,0},{1,9},{9... | collective-permute-start | bytes 1277960 | tf_op jit(solution)/shard_map/ppermute | solution.py:651
  257.6 32.5 %collective-permute-start.27 = (f32[208,512]{1,0:T(8,128)S(1)}, f32[208,512]{1,0:T(8,128)S(1)}, u32[]{:S(2)}, u32[]{:S(2)}) collective-permute-start(f32[208,512]{1,0:T(8,128)S(1)} %collective-permute-done.25), channel_id=1, source_target_pairs={{8,0},{16,8},{24,16},{28,24},{20,28},{12,20},{4,12},{0,4},{9,1},{1... | collective-permute-start | bytes 1277960 | tf_op jit(solution)/shard_map/ppermute | solution.py:654
  278.7 41.6 %collective-permute-start.28 = (f32[208,512]{1,0:T(8,128)S(1)}, f32[208,512]{1,0:T(8,128)S(1)}, u32[]{:S(2)}, u32[]{:S(2)}) collective-permute-start(f32[208,512]{1,0:T(8,128)S(1)} %collective-permute-done.26), channel_id=1, source_target_pairs={{0,8},{8,16},{16,24},{24,28},{28,20},{20,12},{12,4},{4,0},{1,9},{9... | collective-permute-start | bytes 1277960 | tf_op jit(solution)/shard_map/ppermute | solution.py:651
  290.0 30.2 %collective-permute-start.29 = (f32[208,512]{1,0:T(8,128)S(1)}, f32[208,512]{1,0:T(8,128)S(1)}, u32[]{:S(2)}, u32[]{:S(2)}) collective-permute-start(f32[208,512]{1,0:T(8,128)S(1)} %collective-permute-done.27), channel_id=1, source_target_pairs={{8,0},{16,8},{24,16},{28,24},{20,28},{12,20},{4,12},{0,4},{9,1},{1... | collective-permute-start | bytes 1277960 | tf_op jit(solution)/shard_map/ppermute | solution.py:654
  320.2 28.6 %collective-permute-start.30 = (f32[208,512]{1,0:T(8,128)S(1)}, f32[208,512]{1,0:T(8,128)S(1)}, u32[]{:S(2)}, u32[]{:S(2)}) collective-permute-start(f32[208,512]{1,0:T(8,128)S(1)} %collective-permute-done.29), channel_id=1, source_target_pairs={{8,0},{16,8},{24,16},{28,24},{20,28},{12,20},{4,12},{0,4},{9,1},{1... | collective-permute-start | bytes 1277960 | tf_op jit(solution)/shard_map/ppermute | solution.py:654
  379.2 396.8 %reduce-scatter.5.cloned.1.call-start = ((), (), s32[]{:S(2)}) async-start(), calls=%async_computation.5 | async-start | bytes 10616832 | tf_op jit(solution)/shard_map/reduce_scatter | solution.py:1055
  460.9 19.1 %collective-permute-start.53 = (f32[4,40,512]{2,1,0:T(8,128)S(1)}, f32[4,40,512]{2,1,0:T(8,128)S(1)}, u32[]{:S(2)}, u32[]{:S(2)}) collective-permute-start(f32[4,40,512]{2,1,0:T(8,128)S(1)} %bitcast.520), channel_id=1, source_target_pairs={{0,1},{1,0},{2,3},{3,2},{4,5},{5,4},{6,7},{7,6},{8,9},{9,8},{10,11... | collective-permute-start | bytes 983048 | tf_op jit(solution)/shard_map/ppermute | solution.py:560
  544.7 23.4 %collective-permute-start.61 = (f32[288,512]{1,0:T(8,128)S(1)}, f32[288,512]{1,0:T(8,128)}, u32[]{:S(2)}, u32[]{:S(2)}) collective-permute-start(f32[288,512]{1,0:T(8,128)S(1)} %get-tuple-element.248), channel_id=1, source_target_pairs={{8,0},{16,8},{24,16},{28,24},{20,28},{12,20},{4,12},{0,4},{9,1},{1... | collective-permute-start | bytes 1769480 | tf_op jit(solution)/shard_map/ppermute | solution.py:686
  546.8 21.4 %collective-permute-start.60 = (f32[288,512]{1,0:T(8,128)S(1)}, f32[288,512]{1,0:T(8,128)S(1)}, u32[]{:S(2)}, u32[]{:S(2)}) collective-permute-start(f32[288,512]{1,0:T(8,128)S(1)} %get-tuple-element.249), channel_id=1, source_target_pairs={{0,8},{8,16},{16,24},{24,28},{28,20},{20,12},{12,4},{4,0},{1,9},{9... | collective-permute-start | bytes 1769480 | tf_op jit(solution)/shard_map/ppermute | solution.py:684
  599.2 27.3 %collective-permute-start.65 = (f32[288,512]{1,0:T(8,128)}, f32[288,512]{1,0:T(8,128)S(1)}, u32[]{:S(2)}, u32[]{:S(2)}) collective-permute-start(f32[288,512]{1,0:T(8,128)} %bitcast_add_fusion.3), channel_id=1, source_target_pairs={{0,8},{8,16},{16,24},{24,28},{28,20},{20,12},{12,4},{4,0},{1,9},{9... | collective-permute-start | bytes 1769480 | tf_op jit(solution)/shard_map/ppermute | solution.py:684
  600.7 25.8 %collective-permute-start.67 = (f32[640,128]{1,0:T(8,128)S(1)}, f32[640,128]{1,0:T(8,128)}, u32[]{:S(2)}, u32[]{:S(2)}) collective-permute-start(f32[640,128]{1,0:T(8,128)S(1)} %get-tuple-element.295), channel_id=1, source_target_pairs={{0,2},{1,3},{2,0},{3,1},{4,6},{5,7},{6,4},{7,5},{8,10},{9,11},{10,... | collective-permute-start | bytes 983048 | tf_op jit(solution)/shard_map/ppermute | solution.py:560
  628.0 18.7 %collective-permute-start.68 = (f32[2,128]{1,0:T(2,128)S(1)}, f32[2,128]{1,0:T(2,128)S(1)}, u32[]{:S(2)}, u32[]{:S(2)}) collective-permute-start(f32[2,128]{1,0:T(2,128)S(1)} %pad_maximum_fusion.21), channel_id=1, source_target_pairs={{0,4},{4,0},{8,12},{12,8},{16,20},{20,16},{24,28},{28,24},{1,5},{5... | collective-permute-start | bytes 3080 | tf_op jit(solution)/shard_map/ppermute | solution.py:610
  652.0 21.0 %collective-permute-start.92 = (f32[2,8,3,16,512]{4,3,2,1,0:T(8,128)}, f32[2,8,3,16,512]{4,3,2,1,0:T(8,128)}, u32[]{:S(2)}, u32[]{:S(2)}) collective-permute-start(f32[2,8,3,16,512]{4,3,2,1,0:T(8,128)} %dynamic-slice_bitcast_fusion), channel_id=1, source_target_pairs={{0,1},{1,0},{2,3},{3,2},{4,5},{5,4},{6,7},{7,6},{8,9},{9,8},{10,11... | collective-permute-start | bytes 4718600 | tf_op jit(solution)/shard_map/ppermute | solution.py:560
  675.6 23.7 %collective-permute-start.93 = (f32[8,3,16,512]{3,2,1,0:T(8,128)S(1)}, f32[8,3,16,512]{3,2,1,0:T(8,128)S(1)}, u32[]{:S(2)}, u32[]{:S(2)}) collective-permute-start(f32[8,3,16,512]{3,2,1,0:T(8,128)S(1)} %dynamic-slice_bitcast_fusion.1), channel_id=1, source_target_pairs={{0,2},{1,3},{2,0},{3,1},{4,6},{5,7},{6,4},{7,5},{8,10},{9,11},{10,... | collective-permute-start | bytes 2359304 | tf_op jit(solution)/shard_map/ppermute | solution.py:560
  729.4 42.0 %collective-permute-start.107 = (f32[576,512]{1,0:T(8,128)}, f32[576,512]{1,0:T(8,128)S(1)}, u32[]{:S(2)}, u32[]{:S(2)}) collective-permute-start(f32[576,512]{1,0:T(8,128)} %maximum_multiply_fusion), channel_id=1, source_target_pairs={{0,2},{1,3},{2,0},{3,1},{4,6},{5,7},{6,4},{7,5},{8,10},{9,11},{10,... | collective-permute-start | bytes 3538952 | tf_op jit(solution)/shard_map/ppermute | solution.py:560
  738.9 27.9 %collective-permute-start.97 = (f32[256,512]{1,0:T(8,128)}, f32[256,512]{1,0:T(8,128)S(1)}, u32[]{:S(2)}, u32[]{:S(2)}) collective-permute-start(f32[256,512]{1,0:T(8,128)} %get-tuple-element.256), channel_id=1, source_target_pairs={{8,0},{16,8},{24,16},{28,24},{20,28},{12,20},{4,12},{0,4},{9,1},{1... | collective-permute-start | bytes 1572872 | tf_op jit(solution)/shard_map/ppermute | solution.py:686
  743.8 20.6 %collective-permute-start.81 = (f32[160,512]{1,0:T(8,128)S(1)}, f32[160,512]{1,0:T(8,128)S(1)}, u32[]{:S(2)}, u32[]{:S(2)}) collective-permute-start(f32[160,512]{1,0:T(8,128)S(1)} %get-tuple-element.291), channel_id=1, source_target_pairs={{0,3},{1,2},{2,1},{3,0},{4,7},{5,6},{6,5},{7,4},{8,11},{9,10},{10,... | collective-permute-start | bytes 983048 | tf_op jit(solution)/shard_map/ppermute | solution.py:560
  746.6 26.1 %collective-permute-start.95 = (f32[256,512]{1,0:T(8,128)}, f32[256,512]{1,0:T(8,128)}, u32[]{:S(2)}, u32[]{:S(2)}) collective-permute-start(f32[256,512]{1,0:T(8,128)} %get-tuple-element.257), channel_id=1, source_target_pairs={{0,8},{8,16},{16,24},{24,28},{28,20},{20,12},{12,4},{4,0},{1,9},{9... | collective-permute-start | bytes 1572872 | tf_op jit(solution)/shard_map/ppermute | solution.py:684
  766.8 29.3 %collective-permute-start.109 = (f32[576,512]{1,0:T(8,128)}, f32[576,512]{1,0:T(8,128)}, u32[]{:S(2)}, u32[]{:S(2)}) collective-permute-start(f32[576,512]{1,0:T(8,128)} %maximum_multiply_fusion), channel_id=1, source_target_pairs={{0,1},{1,0},{2,3},{3,2},{4,5},{5,4},{6,7},{7,6},{8,9},{9,8},{10,11... | collective-permute-start | bytes 3538952 | tf_op jit(solution)/shard_map/ppermute | solution.py:560
  771.4 24.7 %collective-permute-start.108 = (f32[576,512]{1,0:T(8,128)S(1)}, f32[576,512]{1,0:T(8,128)}, u32[]{:S(2)}, u32[]{:S(2)}) collective-permute-start(f32[576,512]{1,0:T(8,128)S(1)} %collective-permute-done.107), channel_id=1, source_target_pairs={{0,1},{1,0},{2,3},{3,2},{4,5},{5,4},{6,7},{7,6},{8,9},{9,8},{10,11... | collective-permute-start | bytes 3538952 | tf_op jit(solution)/shard_map/ppermute | solution.py:560
  799.5 45.2 %collective-permute-start.105 = (f32[576,512]{1,0:T(8,128)}, f32[576,512]{1,0:T(8,128)}, u32[]{:S(2)}, u32[]{:S(2)}) collective-permute-start(f32[576,512]{1,0:T(8,128)} %broadcast_multiply_fusion.one), channel_id=1, source_target_pairs={{0,2},{1,3},{2,0},{3,1},{4,6},{5,7},{6,4},{7,5},{8,10},{9,11},{10,... | collective-permute-start | bytes 3538952 | tf_op jit(solution)/shard_map/ppermute | solution.py:560
  809.1 28.6 %collective-permute-start.101 = (f32[264,512]{1,0:T(8,128)S(1)}, f32[264,512]{1,0:T(8,128)S(1)}, u32[]{:S(2)}, u32[]{:S(2)}) collective-permute-start(f32[264,512]{1,0:T(8,128)S(1)} %fusion.5), channel_id=1, source_target_pairs={{0,2},{1,3},{2,0},{3,1},{4,6},{5,7},{6,4},{7,5},{8,10},{9,11},{10,... | collective-permute-start | bytes 1622024 | tf_op jit(solution)/shard_map/ppermute | solution.py:560
  811.6 33.6 %collective-permute-start.103 = (f32[264,512]{1,0:T(8,128)S(1)}, f32[264,512]{1,0:T(8,128)S(1)}, u32[]{:S(2)}, u32[]{:S(2)}) collective-permute-start(f32[264,512]{1,0:T(8,128)S(1)} %fusion.5), channel_id=1, source_target_pairs={{0,1},{1,0},{2,3},{3,2},{4,5},{5,4},{6,7},{7,6},{8,9},{9,8},{10,11... | collective-permute-start | bytes 1622024 | tf_op jit(solution)/shard_map/ppermute | solution.py:560
  (160 other events, 1552.0 us)
Sparse Core Ops, SparseCore 0:
  12.5 163.9 all-gather.4
  179.3 173.0 all-gather.2
  379.3 96.0 reduce-scatter.2
  542.9 183.8 reduce-scatter.4

commit v6 on v3

--- a/solution.py
+++ b/solution.py
@@ -126,15 +126,13 @@
         ref[:, pixels:] = jnp.broadcast_to(extra_ref[...], (2, 8, part))
 
 
-def conv_back_kernel(dilation, row_ref, image_ref, weight_ref, *rest):
-    extra_ref = rest[0] if len(rest) == 5 else None
-    keep_ref, give_ref, framed, total = rest[-4:]
+def conv_back_kernel(dilation, row_ref, image_ref, weight_ref, keep_ref, give_ref, framed, total):
     tap = pl.program_id(0)
 
     @pl.when(tap == 0)
     def _():
         frame(image_ref, framed, dilation)
-        total[...] = jnp.zeros_like(total) if extra_ref is None else extra_ref[...]
+        total[...] = jnp.zeros_like(total)
 
     moved = halves(shifted(framed, 8 - tap, image_ref.shape[0], dilation))
     total[...] += three_pass(moved, halves(weight_ref[...]), 1, 1)
@@ -143,6 +141,16 @@
     def _():
         part = keep_ref.shape[2]
         keep_and_give(row_ref[0], lambda j: total[:, at_lanes(j, part)], keep_ref, give_ref)
+
+
+def expand_back_kernel(
+    row_ref, left_ref, right_ref, keep_in_ref, give_in_ref, keep_ref, give_ref, total
+):
+    total[...] = three_pass(halves(left_ref[...]), halves(right_ref[...]), 1, 1)
+    part = keep_ref.shape[2]
+    keep_and_give(row_ref[0], lambda j: total[:, at_lanes(j, part)], keep_ref, give_ref)
+    keep_ref[...] += keep_in_ref[...]
+    give_ref[...] += give_in_ref[...]
 
 
 def conv_grad_kernel(dilation, input_ref, grad_ref, out_ref, framed, high, low):
@@ -214,9 +222,8 @@
     out_ref[...] += three_pass(moved, halves(source_rows(weight_ref[...])), 1, 1)
 
 
-def note_grad_kernel(
-    row_ref, input_ref, one, two, three, four, out_ref, image_ref, framed, high, low
-):
+def note_grad_kernel(row_ref, input_ref, one, two, three, four, *rest):
+    out_ref, image_ref, framed, high, low = rest[-5:]
     tap = pl.program_id(0)
 
     @pl.when(tap == 0)
@@ -439,7 +446,7 @@
     )(row, *blocks, weight)
 
 
-def conv_back(row, image, weight, dilation, extra=None):
+def conv_back(row, image, weight, dilation):
     height, breadth, _ = image.shape
     rows, cols = weight.shape[0] // 9, weight.shape[1]
     pixels = height * breadth
@@ -448,17 +455,15 @@
     def body(*refs):
         conv_back_kernel(dilation, *refs)
 
-    extras = [] if extra is None else [extra]
     return kernel_call(
         body,
         (9,),
-        [SCALAR, whole_spec(image.shape), tap_rows(rows, cols)]
-        + [whole_spec(array.shape) for array in extras],
+        [SCALAR, whole_spec(image.shape), tap_rows(rows, cols)],
         [whole_spec(shape)] * 2,
         [struct(shape)] * 2,
         [framed_scratch(image.shape, dilation), pltpu.VMEM((pixels, rows), jnp.float32)],
         2 * 9 * pixels * rows * cols,
-    )(row, image, weight, *extras)
+    )(row, image, weight)
 
 
 def conv_grad(flat_input, image_grad, dilation):
@@ -530,23 +535,34 @@
     )(note, weight)
 
 
-def note_grad(row, flat_input, pair, blocks, grain):
+def note_grad(row, flat_input, pair, blocks, grain, grads=None):
     pixels, depth = flat_input.shape
     depth = depth // 2
     lines, breadth, mid = blocks[0].shape
     image = (4 * lines, breadth, mid)
     runs = depth // 2 // grain
-    grad = (9 * runs, 2, grain, mid)
-    return kernel_call(
+    shape = (9 * runs, 4, grain, mid)
+    others = [] if grads is None else [grads]
+    return pl.pallas_call(
         note_grad_kernel,
-        (9,),
-        [SCALAR, pl.BlockSpec((pixels, depth), lambda tap: (0, pair))]
-        + [whole_spec(blocks[0].shape)] * 4,
-        [tap_runs(grad), whole_spec(image)],
-        [struct(grad), struct(image)],
-        [framed_scratch(image, 1)] + [pltpu.VMEM((depth, pixels), jnp.bfloat16)] * 2,
-        2 * 9 * pixels * depth * mid,
-    )(row, flat_input, *blocks)
+        grid=(9,),
+        in_specs=[SCALAR, pl.BlockSpec((pixels, depth), lambda tap: (0, pair))]
+        + [whole_spec(blocks[0].shape)] * 4
+        + [pl.BlockSpec(memory_space=pl.ANY)] * len(others),
+        out_specs=[
+            pl.BlockSpec((runs, 2, grain, mid), lambda tap: (tap, pair, 0, 0)),
+            whole_spec(image),
+        ],
+        out_shape=[struct(shape), struct(image)],
+        scratch_shapes=[framed_scratch(image, 1)] + [pltpu.VMEM((depth, pixels), jnp.bfloat16)] * 2,
+        input_output_aliases={6: 0} if others else {},
+        compiler_params=pltpu.CompilerParams(
+            dimension_semantics=("arbitrary",), vmem_limit_bytes=VMEM_LIMIT
+        ),
+        cost_estimate=pl.CostEstimate(
+            flops=6 * 9 * pixels * depth * mid, bytes_accessed=12 * 2**20, transcendentals=0
+        ),
+    )(row, flat_input, *blocks, *others)
 
 
 def silu_grad(values):
@@ -696,6 +712,8 @@
         return later
 
     def result(self):
+        while not self.done:
+            self.step()
         return self.sums if self.sums is not None else self.own(0) + self.rising + self.falling
 
 
@@ -992,33 +1010,16 @@
     d_depth_blocks, d_segment_note = lax.optimization_barrier(
         (gather_keyed(lines(d_depth_note)), d_segment_note)
     )
-    depth_pair_grad, d_depth_image = note_grad(here, feats, 0, d_depth_blocks, run)
-    depth_pair_sums = lax.psum_scatter(
-        regroup(depth_pair_grad, grain).reshape(-1, mid), "batch", scatter_dimension=0, tiled=True
-    )
-    segment_pair_grad, d_segment_image = note_grad(
-        here, feats, 1, gather_keyed(lines(d_segment_note)), run
-    )
-    flat_mid_out = mid_out.reshape(pixels, mid)
-    expand_input, _ = lax.optimization_barrier((flat_mid_out, d_segment_note))
-    pre_expand = product(expand_input, expand_w, 1, 0)
-    hat_three, normed_three, inverse_three = norm_forward(
-        pre_expand, sum_batch(sums_of(pre_expand, pre_expand)), expand_gain, expand_bias, count
-    )
-    summed = normed_three + inputs
-    block_blocks = exchange_wide(jax.nn.silu(summed))
-    d_summed = cotangent * silu_grad(summed)
-    d_pre_expand, expand_sums = norm_backward(
-        d_summed, hat_three, inverse_three, expand_gain, count, False
-    )
-
-    feats_late, depth_pair_w, _ = lax.optimization_barrier(
-        (feats_image, depth_pair_w, (segment_pair_grad, depth_pair_grad, expand_sums))
-    )
-    segment_pair_grad, _ = lax.optimization_barrier((segment_pair_grad, expand_sums))
-    hops = Hops(ring, regroup(segment_pair_grad, grain).reshape(nbatch, held // 2, mid), True)
-    depth_mine, depth_got = scatter_end(*note_forward(here, feats_late, 0, depth_pair_w))
-    depth_back = note_back(hops.step(d_depth_image), depth_pair_w)
+    message_grads, d_depth_image = note_grad(here, feats, 0, d_depth_blocks, run)
+    message_grads, d_segment_image = note_grad(
+        here, feats, 1, gather_keyed(lines(d_segment_note)), run, message_grads
+    )
+    message_sums = lax.psum_scatter(
+        regroup(message_grads, grain).reshape(-1, mid), "batch", scatter_dimension=0, tiled=True
+    )
+    segment_back = note_back(d_segment_image, segment_pair_w)
+    depth_mine, depth_got = scatter_end(*note_forward(here, feats_image, 0, depth_pair_w))
+    depth_back = note_back(d_depth_image, depth_pair_w)
     depth_stream, direct_both, depth_gate_grad = single_call(
         depth_kernel,
         (
@@ -1038,15 +1039,26 @@
         8 * quarter * mid * mid,
     )
     direct_got = jnp.stack(exchange_keyed([direct_both[key] for key in range(4)]))
-    segment_back = note_back(hops.step(d_segment_image), segment_pair_w)
+    flat_mid_out = mid_out.reshape(pixels, mid)
     heads_grad, d_feats = heads_grad_of(
         here,
-        hops.step(flat_mid_out),
+        flat_mid_out,
         image_of(depth_back),
         image_of(segment_back),
         direct_got.reshape(4, 2 * local_height, breadth, part),
     )
     heads_sums = lax.psum_scatter(heads_grad, "batch", scatter_dimension=0, tiled=True)
+
+    pre_expand = product(flat_mid_out, expand_w, 1, 0)
+    hat_three, normed_three, inverse_three = norm_forward(
+        pre_expand, sum_batch(sums_of(pre_expand, pre_expand)), expand_gain, expand_bias, count
+    )
+    summed = normed_three + inputs
+    block_blocks = exchange_wide(jax.nn.silu(summed))
+    d_summed = cotangent * silu_grad(summed)
+    d_pre_expand, expand_sums = norm_backward(
+        d_summed, hat_three, inverse_three, expand_gain, count, False
+    )
 
     expand_grad = product(flat_mid_out, d_pre_expand, 0, 0).reshape(nbatch, mid_held, mid)
 
@@ -1061,12 +1073,17 @@
     gate_terms = jnp.transpose(gate_terms.reshape(3, nbatch, nrows, gate_rows, mid), (2, 1, 0, 3, 4))
     gate_sums = scatter_rows(gate_terms, row).reshape(nbatch, 3 * gate_rows, mid)
 
-    d_feats, block_blocks = lax.optimization_barrier((hops.step(d_feats), block_blocks))
+    keep, give = conv_back(here, d_feats, heads_full, 1)
+    keep, give = single_call(
+        expand_back_kernel,
+        (here, d_pre_expand, expand_w, keep, give),
+        [(2, pixels, part)] * 2,
+        [(pixels, mid)],
+        2 * pixels * mid * mid,
+    )
+    mine_terms, got_terms = scatter_end(keep, give)
+    mine_terms, block_blocks = lax.optimization_barrier((mine_terms, block_blocks))
     block_out = collect_wide(block_blocks)
-    segment_pair_sums = hops.result()
-    mine_terms, got_terms = scatter_end(
-        *conv_back(here, d_feats, heads_full, 1, product(d_pre_expand, expand_w, 1, 1))
-    )
     d_pre_dilate, dilate_sums = norm_backward(
         (mine_terms + got_terms) * silu_grad(normed_two), hat_two, inverse_two, dilate_gain, count, False
     )
@@ -1075,6 +1092,7 @@
     d_pre_reduce, reduce_sums = norm_backward(
         (mine_terms + got_terms) * silu_grad(normed_one), hat_one, inverse_one, reduce_gain, count, False
     )
+    d_pre_reduce, message_sums = lax.optimization_barrier((d_pre_reduce, message_sums))
     reduce_grad, features_back = single_call(
         reduce_back_kernel,
         (here, *gather_keyed(d_pre_reduce), inputs, reduce_full, d_summed),
@@ -1093,30 +1111,25 @@
             ),
             expand_grad,
             gate_sums,
+            reduce_grad.reshape(nbatch, wide_part, mid),
         ],
         axis=1,
     )
-    square_grad, reduce_sums, depth_pair_sums, segment_pair_sums = lax.optimization_barrier(
-        (square_grad, reduce_sums, depth_pair_sums, segment_pair_sums)
-    )
-    square_sums = ring.scatter(square_grad, False)
-    reduce_out = ring.scatter(reduce_grad.reshape(nbatch, wide_part, mid), True)
-    features_grad = collect_wide(exchange_wide(features_back))
-
-    pair_sums = jnp.concatenate([depth_pair_sums, segment_pair_sums], axis=0) * factor
-    pairs_out = jnp.stack(gather_rows(pair_sums, row)).reshape(nrows, 2, groups, 2, grain, mid)
-    depth_pair_out, segment_pair_out = pairs_out[:, 0], pairs_out[:, 1]
-
-    def message_out(pair_got, index):
-        return jnp.transpose(pair_got[:, :, index], (1, 0, 2, 3)).reshape(held, mid)
-
-    segment_out, normal_out, depth_out, contour_out = single_call(
-        heads_out_kernel,
-        (here, *gather_keyed(heads_sums * factor), mix),
-        [(held, mid)] * 4,
-        [(held, mid)],
-        8 * held * mid * mid,
-    )
+    square_grad, reduce_sums = lax.optimization_barrier((square_grad, reduce_sums))
+    hops = Hops(ring, square_grad, False)
+    hops.step()
+    hops.step()
+    message_blocks = hops.step(gather_keyed(message_sums * factor))
+    features_blocks = hops.step(exchange_wide(features_back))
+    square_sums = hops.result()
+    features_grad = collect_wide(features_blocks)
+
+    messages_out = jnp.stack(in_order(message_blocks, row)).reshape(
+        nrows, groups, 4, grain, mid
+    )
+
+    def message_out(index):
+        return jnp.transpose(messages_out[:, :, index], (1, 0, 2, 3)).reshape(held, mid)
 
     expand_mine_sums = lax.dynamic_slice_in_dim(expand_sums, batch * wide_part, wide_part, 1)
     norm_sums = jnp.concatenate(
@@ -1127,7 +1140,17 @@
         axis=0,
     )
     small = jnp.concatenate([square_sums, jnp.pad(norm_sums, ((0, 2), (0, 0)))], axis=0) * factor
-    small_got = gather_rows(small, row)
+    small_blocks = gather_keyed(small)
+    heads_sums, small_blocks = lax.optimization_barrier((heads_sums, small_blocks))
+    small_got = in_order(small_blocks, row)
+    segment_out, normal_out, depth_out, contour_out = single_call(
+        heads_out_kernel,
+        (here, *gather_keyed(heads_sums * factor), mix),
+        [(held, mid)] * 4,
+        [(held, mid)],
+        8 * held * mid * mid,
+    )
+
     squares_got = jnp.stack([block[narrow : narrow + mid_held + 3 * gate_rows] for block in small_got])
     dilate_out = jnp.concatenate(
         [
@@ -1153,7 +1176,10 @@
         return lax.dynamic_slice_in_dim(full, batch * mid_held, mid_held, 1)
 
     expand_norm_out = jnp.concatenate([block[4:6, :wide_part] for block in norms_got], axis=1)
-    reduce_got = jnp.concatenate(gather_rows(reduce_out * factor, row), axis=0)
+    reduce_start = narrow + mid_held + 3 * gate_rows
+    reduce_got = jnp.concatenate(
+        [block[reduce_start : reduce_start + wide_part] for block in small_got], axis=0
+    )
 
     return (
         block_out,
@@ -1170,10 +1196,10 @@
         segment_out,
         normal_out,
         contour_out,
-        message_out(depth_pair_out, 0),
-        message_out(segment_pair_out, 0),
-        message_out(depth_pair_out, 1),
-        message_out(segment_pair_out, 1),
+        message_out(0),
+        message_out(2),
+        message_out(1),
+        message_out(3),
         gate_out(0),
         gate_out(1),
         gate_out(2)[:, :classes],

time: 831 us -> 829 us (level)
  other arithmetic: 57.1 us -> 41.7 us
  waiting for transfers between devices: 296 us -> 309 us
    ppermute x57 -> x54, starting transfers between devices: 77.9 us -> 110 us  [swap_rows(): return lax.ppermute(block, 'rows', [(i, i ^ mask) for i in range(size)])]
    ppermute x11 -> x3, waiting for transfers between devices: 32.7 us -> 7.78 us  [step(): self.rising = lax.ppermute(self.rising, 'batch', self.ring.up)]
    ppermute x7, waiting for transfers between devices: 34.1 us -> 57.2 us  [gather(): falling = lax.ppermute(falling, 'batch', self.down)]
    ppermute x7, waiting for transfers between devices: 58.2 us -> 39.1 us  [gather(): rising = lax.ppermute(rising, 'batch', self.up)]
    ppermute x18, starting transfers between devices: 49.3 us -> 34.1 us  [swap(): return lax.ppermute(block, 'batch', [(i, i ^ mask) for i in range(size)])]
    ppermute x10 -> x4, waiting for transfers between devices: 43.2 us -> 58.2 us  [step(): self.falling = lax.ppermute(self.falling, 'batch', self.ring.down)]
    ppermute x18, waiting for transfers between devices: 19 us -> 32.7 us  [swap(): return lax.ppermute(block, 'batch', [(i, i ^ mask) for i in range(size)])]
    ppermute x7, starting transfers between devices: 24.1 us -> 11.3 us  [gather(): rising = lax.ppermute(rising, 'batch', self.up)]
  transfers between devices with their start and end apart: 115 -> 98, of which waited for: 50 -> 52; matrix products, arithmetic and copies ran while one was open for 15% -> 13% of each run, Pallas kernels for 21% -> 22%
where the time goes in v6:
time: 829 us; the launch traced here: 818 us
  waiting for transfers between devices  309 us (37%)
  Pallas kernels  188 us (23%)
  starting transfers between devices  167 us (20%)
  local copies, waits for them, and re-layouts  71 us (9%)
  other arithmetic  41.7 us (5%)
  between operations  32 us (4%)
  matrix products  8.39 us (1%)
    ppermute x54, waiting for transfers between devices, swap_rows(): return lax.ppermute(block, 'rows', [(i, i ^ mask) for i in range(size)])  114 us
    ppermute x54, starting transfers between devices, swap_rows(): return lax.ppermute(block, 'rows', [(i, i ^ mask) for i in range(size)])  110 us
    ppermute x4, waiting for transfers between devices, step(): self.falling = lax.ppermute(self.falling, 'batch', self.ring.down)  58.2 us
    ppermute x7, waiting for transfers between devices, gather(): falling = lax.ppermute(falling, 'batch', self.down)  57.2 us
    pallas_call x11, Pallas kernels, single_call(): kernel_call(body, (1,), [SCALAR] + [whole_spec(arg.shape) for arg in args...  49 us
    ppermute x7, waiting for transfers between devices, gather(): rising = lax.ppermute(rising, 'batch', self.up)  39.1 us
    ppermute x18, starting transfers between devices, swap(): return lax.ppermute(block, 'batch', [(i, i ^ mask) for i in range(size)])  34.1 us
    ppermute x18, waiting for transfers between devices, swap(): return lax.ppermute(block, 'batch', [(i, i ^ mask) for i in range(size)])  32.7 us
  transfers between devices with their start and end apart: 98, of which 52 were waited for; matrix products, arithmetic and copies ran while one was open for 13% of the time, Pallas kernels for 22%

profile of v6, /device:TPU:1, one launch (start us, length us, event | category | flops | bytes accessed | tf_op | source)
XLA Modules:
  0.0 817.5 jit_solution(11847674827960677858)
XLA Ops:
  48.2 28.7 %collective-permute-done.6 = f32[840,128]{1,0:T(8,128)S(1)} collective-permute-done((f32[840,128]{1,0:T(8,128)S(1)}, f32[840,128]{1,0:T(8,128)S(1)}, u32[]{:S(2)}, u32[]{:S(2)}) %collective-permute-start.6) | collective-permute-done | bytes 430112 | tf_op jit(solution)/shard_map/ppermute | solution.py:669
  78.4 8.9 %collective-permute-done.7 = f32[840,128]{1,0:T(8,128)S(1)} collective-permute-done((f32[840,128]{1,0:T(8,128)S(1)}, f32[840,128]{1,0:T(8,128)S(1)}, u32[]{:S(2)}, u32[]{:S(2)}) %collective-permute-start.7) | collective-permute-done | bytes 430112 | tf_op jit(solution)/shard_map/ppermute | solution.py:666
  88.9 17.2 %collective-permute-done.9 = f32[840,128]{1,0:T(8,128)S(1)} collective-permute-done((f32[840,128]{1,0:T(8,128)S(1)}, f32[840,128]{1,0:T(8,128)S(1)}, u32[]{:S(2)}, u32[]{:S(2)}) %collective-permute-start.9) | collective-permute-done | bytes 430112 | tf_op jit(solution)/shard_map/ppermute | solution.py:666
  112.6 10.3 %collective-permute-start.10 = (f32[2,648,128]{2,1,0:T(8,128)}, f32[2,648,128]{2,1,0:T(8,128)S(1)}, u32[]{:S(2)}, u32[]{:S(2)}) collective-permute-start(f32[2,648,128]{2,1,0:T(8,128)} %get-tuple-element.108), channel_id=1, source_target_pairs={{0,1},{1,0},{2,3},{3,2},{4,5},{5,4},{6,7},{7,6},{8,9},{9,8},{10,11... | collective-permute-start | bytes 1990664 | tf_op jit(solution)/shard_map/ppermute | solution.py:575
  136.2 12.7 %collective-permute-start.12 = (f32[3,128]{1,0:T(4,128)S(1)}, f32[3,128]{1,0:T(4,128)S(1)}, u32[]{:S(2)}, u32[]{:S(2)}) collective-permute-start(f32[3,128]{1,0:T(4,128)S(1)} %pad_maximum_fusion.19), channel_id=1, source_target_pairs={{0,4},{4,0},{8,12},{12,8},{16,20},{20,16},{24,28},{28,24},{1,5},{5... | collective-permute-start | bytes 4616 | tf_op jit(solution)/shard_map/ppermute | solution.py:625
  176.7 10.0 %shard_map.384 = (f32[640,128]{1,0:T(8,128)}, f32[16,40,512]{2,1,0:T(8,128)}) custom-call(s32[1]{0:T(128)} %bitcast.row_ref.refs_0_, f32[16,40,128]{2,1,0:T(8,128)} %bitcast.389, f32[16,40,128]{2,1,0:T(8,128)} %copy-done.81, f32[16,40,128]{2,1,0:T(8,128)} %copy-done.70, f32[16,40,128]{2,1,0:T(8,128)} %copy-done.83, f32[4608,128]{1,0:T(8,128)} %bitcast.360), custom_call_target="tpu_custom_call" | custom-call | flops 2264924160 | bytes 12582912 | tf_op jit(solution)/shard_map/pallas_call | solution.py:438
  208.3 8.8 %collective-permute-done.24 = f32[208,512]{1,0:T(8,128)S(1)} collective-permute-done((f32[208,512]{1,0:T(8,128)S(1)}, f32[208,512]{1,0:T(8,128)S(1)}, u32[]{:S(2)}, u32[]{:S(2)}) %collective-permute-start.24) | collective-permute-done | bytes 426016 | tf_op jit(solution)/shard_map/ppermute | solution.py:666
  222.3 15.1 %shard_map.385 = (f32[640,512]{1,0:T(8,128)}, f32[16,40,512]{2,1,0:T(8,128)}, f32[4,320,128]{2,1,0:T(8,128)}) custom-call(s32[1]{0:T(128)} %bitcast.row_ref.refs_0_, f32[16,40,128]{2,1,0:T(8,128)} %bitcast.392, f32[16,40,128]{2,1,0:T(8,128)} %copy-done.74, f32[16,40,128]{2,1,0:T(8,128)} %copy-done.71, f32[16,40,128]{2,1,0:T(8,128)} %copy-done.80, ...), custom_call_target="tpu_custom_call" | custom-call | flops 9059696640 | bytes 12582912 | tf_op jit(solution)/shard_map/pallas_call | solution.py:438
  273.1 10.6 %collective-permute-done.29 = f32[208,512]{1,0:T(8,128)S(1)} collective-permute-done((f32[208,512]{1,0:T(8,128)S(1)}, f32[208,512]{1,0:T(8,128)S(1)}, u32[]{:S(2)}, u32[]{:S(2)}) %collective-permute-start.29) | collective-permute-done | bytes 426016 | tf_op jit(solution)/shard_map/ppermute | solution.py:669
  285.7 8.5 %collective-permute-done.30 = f32[208,512]{1,0:T(8,128)S(1)} collective-permute-done((f32[208,512]{1,0:T(8,128)S(1)}, f32[208,512]{1,0:T(8,128)S(1)}, u32[]{:S(2)}, u32[]{:S(2)}) %collective-permute-start.30) | collective-permute-done | bytes 426016 | tf_op jit(solution)/shard_map/ppermute | solution.py:669
  295.0 10.5 %shard_map.386 = (f32[2,160,512]{2,1,0:T(8,128)}, f32[2,160,512]{2,1,0:T(8,128)}) custom-call(s32[1]{0:T(128)} %bitcast.row_ref.refs_0_, f32[16,40,512]{2,1,0:T(8,128)} %bitcast.470, f32[72,2,16,512]{3,2,1,0:T(8,128)} %bitcast.457), custom_call_target="tpu_custom_call" | custom-call | flops 4529848320 | bytes 12582912 | tf_op jit(solution)/shard_map/pallas_call | solution.py:509
  352.3 11.0 %shard_map.390 = (f32[72,4,16,512]{3,2,1,0:T(8,128)}, f32[16,40,512]{2,1,0:T(8,128)}) custom-call(s32[1]{0:T(128)} %bitcast.row_ref.refs_0_, f32[640,512]{1,0:T(8,128)} %get-tuple-element.119.input_ref, f32[4,40,512]{2,1,0:T(8,128)} %bitcast.465, f32[4,40,512]{2,1,0:T(8,128)} %copy-done.69, f32[4,40,512]{2,1,0:T(8,128)} %copy-done.68, f32[4,40,512]{2,1,0:T(8,128)} %copy-done.72), custom_call_target="tpu_custom_call" | custom-call | flops 4529848320 | bytes 12582912 | tf_op jit(solution)/shard_map/pallas_call | solution.py:546
  364.1 10.8 %shard_map.392 = (f32[72,4,16,512]{3,2,1,0:T(8,128)}, f32[16,40,512]{2,1,0:T(8,128)}) custom-call(s32[1]{0:T(128)} %bitcast.row_ref.refs_0_, f32[640,512]{1,0:T(8,128)} %get-tuple-element.119.input_ref, f32[4,40,512]{2,1,0:T(8,128)} %bitcast.468, f32[4,40,512]{2,1,0:T(8,128)} %copy-done.79, ...), custom_call_target="tpu_custom_call", output_to_operand_aliasing={{0}: (6, {})} | custom-call | flops 4529848320 | bytes 12582912 | tf_op jit(solution)/shard_map/pallas_call | solution.py:546
  375.2 10.6 %shard_map.394 = (f32[2,160,512]{2,1,0:T(8,128)}, f32[2,160,512]{2,1,0:T(8,128)}) custom-call(s32[1]{0:T(128)} %bitcast.row_ref.refs_0_, f32[16,40,512]{2,1,0:T(8,128)} %bitcast.471, f32[72,2,16,512]{3,2,1,0:T(8,128)} %bitcast.459), custom_call_target="tpu_custom_call" | custom-call | flops 4529848320 | bytes 12582912 | tf_op jit(solution)/shard_map/pallas_call | solution.py:509
  391.2 8.1 collective-permute-done.52.got_ref
  417.7 10.7 %shard_map.391 = f32[640,256]{1,0:T(8,128)} custom-call(f32[16,40,512]{2,1,0:T(8,128)} %get-tuple-element.135.note_ref, f32[72,2,16,512]{3,2,1,0:T(8,128)} %bitcast.460), custom_call_target="tpu_custom_call" | custom-call | flops 4529848320 | bytes 12582912 | tf_op jit(solution)/shard_map/pallas_call | solution.py:527
  428.4 10.7 %shard_map.393 = f32[640,256]{1,0:T(8,128)} custom-call(f32[16,40,512]{2,1,0:T(8,128)} %get-tuple-element.138.note_ref, f32[72,2,16,512]{3,2,1,0:T(8,128)} %bitcast.458), custom_call_target="tpu_custom_call" | custom-call | flops 4529848320 | bytes 12582912 | tf_op jit(solution)/shard_map/pallas_call | solution.py:527
  439.1 16.6 %shard_map.396 = (f32[4608,512]{1,0:T(8,128)}, f32[16,40,512]{2,1,0:T(8,128)}) custom-call(s32[1]{0:T(128)} %bitcast.row_ref.refs_0_, f32[640,512]{1,0:T(8,128)} %bitcast.347, f32[16,40,256]{2,1,0:T(8,128)} %bitcast.472, f32[16,40,256]{2,1,0:T(8,128)} %bitcast.473, f32[4,8,40,128]{3,2,1,0:T(8,128)} %pad_maximum_fusion.9.direct_ref), custom_call_target="tpu_custom_call" | custom-call | flops 9059696640 | bytes 12582912 | tf_op jit(solution)/shard_map/pallas_call | solution.py:492
  483.6 14.8 %shard_map.397 = (f32[2,640,128]{2,1,0:T(8,128)}, f32[2,640,128]{2,1,0:T(8,128)}) custom-call(s32[1]{0:T(128)} %bitcast.row_ref.refs_0_, f32[16,40,512]{2,1,0:T(8,128)} %get-tuple-element.143.refs_1_, f32[4608,512]{1,0:T(8,128)} %all-gather.4.cloned.1.call-done.weight_ref.refs_2_), custom_call_target="tpu_custom_call" | custom-call | flops 9059696640 | bytes 12582912 | tf_op jit(solution)/shard_map/pallas_call | solution.py:458
  542.8 9.9 %shard_map.401 = (f32[2,640,128]{2,1,0:T(8,128)}, f32[2,640,128]{2,1,0:T(8,128)}) custom-call(s32[1]{0:T(128)} %bitcast.row_ref.refs_0_, f32[16,40,128]{2,1,0:T(8,128)} %bitcast.385, f32[4608,128]{1,0:T(8,128)} %bitcast.361), custom_call_target="tpu_custom_call" | custom-call | flops 2264924160 | bytes 12582912 | tf_op jit(solution)/shard_map/pallas_call | solution.py:458
  560.6 8.1 collective-permute-done.67
  585.7 8.8 %shard_map.400 = f32[4608,128]{1,0:T(8,128)} custom-call(f32[640,512]{1,0:T(8,128)} %bitcast.469, f32[16,40,128]{2,1,0:T(8,128)} %bitcast.386), custom_call_target="tpu_custom_call" | custom-call | flops 2264924160 | bytes 12582912 | tf_op jit(solution)/shard_map/pallas_call | solution.py:476
  619.3 21.8 %collective-permute-done.77 = f32[320,512]{1,0:T(8,128)S(1)} collective-permute-done((f32[320,512]{1,0:T(8,128)S(1)}, f32[320,512]{1,0:T(8,128)S(1)}, u32[]{:S(2)}, u32[]{:S(2)}) %collective-permute-start.77) | collective-permute-done | bytes 655392 | tf_op jit(solution)/shard_map/ppermute | solution.py:701
  648.7 11.7 %collective-permute-done.78 = f32[320,512]{1,0:T(8,128)S(1)} collective-permute-done((f32[320,512]{1,0:T(8,128)S(1)}, f32[320,512]{1,0:T(8,128)S(1)}, u32[]{:S(2)}, u32[]{:S(2)}) %collective-permute-start.78) | collective-permute-done | bytes 655392 | tf_op jit(solution)/shard_map/ppermute | solution.py:701
  665.8 12.9 %collective-permute-done.79 = f32[320,512]{1,0:T(8,128)S(1)} collective-permute-done((f32[320,512]{1,0:T(8,128)S(1)}, f32[320,512]{1,0:T(8,128)S(1)}, u32[]{:S(2)}, u32[]{:S(2)}) %collective-permute-start.79) | collective-permute-done | bytes 655392 | tf_op jit(solution)/shard_map/ppermute | solution.py:701
  682.2 11.7 %collective-permute-start.86 = (f32[160,512]{1,0:T(8,128)}, f32[160,512]{1,0:T(8,128)}, u32[]{:S(2)}, u32[]{:S(2)}) collective-permute-start(f32[160,512]{1,0:T(8,128)} %get-tuple-element.295), channel_id=1, source_target_pairs={{0,3},{1,2},{2,1},{3,0},{4,7},{5,6},{6,5},{7,4},{8,11},{9,10},{10,... | collective-permute-start | bytes 983048 | tf_op jit(solution)/shard_map/ppermute | solution.py:575
  693.9 8.3 %collective-permute-start.85 = (f32[160,512]{1,0:T(8,128)S(1)}, f32[160,512]{1,0:T(8,128)}, u32[]{:S(2)}, u32[]{:S(2)}) collective-permute-start(f32[160,512]{1,0:T(8,128)S(1)} %get-tuple-element.296), channel_id=1, source_target_pairs={{0,2},{1,3},{2,0},{3,1},{4,6},{5,7},{6,4},{7,5},{8,10},{9,11},{10,... | collective-permute-start | bytes 983048 | tf_op jit(solution)/shard_map/ppermute | solution.py:575
  704.3 10.0 %collective-permute-done.85.three = f32[160,512]{1,0:T(8,128)} collective-permute-done((f32[160,512]{1,0:T(8,128)S(1)}, f32[160,512]{1,0:T(8,128)}, u32[]{:S(2)}, u32[]{:S(2)}) %collective-permute-start.85) | collective-permute-done | bytes 327712 | tf_op jit(solution)/shard_map/ppermute | solution.py:575
  714.3 11.9 %collective-permute-done.83 = f32[320,512]{1,0:T(8,128)} collective-permute-done((f32[320,512]{1,0:T(8,128)S(1)}, f32[320,512]{1,0:T(8,128)}, u32[]{:S(2)}, u32[]{:S(2)}) %collective-permute-start.83) | collective-permute-done | bytes 655392 | tf_op jit(solution)/shard_map/ppermute | solution.py:701
  730.8 11.7 %collective-permute-start.87 = (f32[328,512]{1,0:T(8,128)S(1)}, f32[328,512]{1,0:T(8,128)}, u32[]{:S(2)}, u32[]{:S(2)}) collective-permute-start(f32[328,512]{1,0:T(8,128)S(1)} %fusion.4), channel_id=1, source_target_pairs={{0,1},{1,0},{2,3},{3,2},{4,5},{5,4},{6,7},{7,6},{8,9},{9,8},{10,11... | collective-permute-start | bytes 2015240 | tf_op jit(solution)/shard_map/ppermute | solution.py:575
  768.4 24.4 %collective-permute-done.91.three = f32[576,512]{1,0:T(8,128)} collective-permute-done((f32[576,512]{1,0:T(8,128)S(1)}, f32[576,512]{1,0:T(8,128)}, u32[]{:S(2)}, u32[]{:S(2)}) %collective-permute-start.91) | collective-permute-done | bytes 1179680 | tf_op jit(solution)/shard_map/ppermute | solution.py:575
  802.7 7.9 shard_map.404
  (557 shorter events, 392.0 us)
Async XLA Ops:
  7.2 190.7 %all-gather.4.cloned.1.call-start = ((), (), s32[]{:S(2)}) async-start(), calls=%async_computation.2 | async-start | bytes 10616832 | tf_op jit(solution)/shard_map/all_gather | solution.py:814
  12.4 282.6 %all-gather.6.cloned.1.call-start = ((), (), s32[]{:S(2)}) async-start(), calls=%async_computation.3 | async-start | bytes 5308416 | tf_op jit(solution)/shard_map/all_gather | solution.py:828
  14.5 360.7 %all-gather.8.cloned.1.call-start = ((), (), s32[]{:S(2)}) async-start(), calls=%async_computation.4 | async-start | bytes 5308416 | tf_op jit(solution)/shard_map/all_gather | solution.py:828
  18.7 27.7 %collective-permute-start.4 = (f32[840,128]{1,0:T(8,128)S(1)}, f32[840,128]{1,0:T(8,128)S(1)}, u32[]{:S(2)}, u32[]{:S(2)}) collective-permute-start(f32[840,128]{1,0:T(8,128)S(1)} %dynamic-slice_dynamic-update-slice_fusion), channel_id=1, source_target_pairs={{8,0},{16,8},{24,16},{28,24},{20,28},{12,20},{4,12},{0,4},{9,1},{1... | collective-permute-start | bytes 1290248 | tf_op jit(solution)/shard_map/ppermute | solution.py:669
  20.8 27.2 %collective-permute-start.3 = (f32[840,128]{1,0:T(8,128)S(1)}, f32[840,128]{1,0:T(8,128)S(1)}, u32[]{:S(2)}, u32[]{:S(2)}) collective-permute-start(f32[840,128]{1,0:T(8,128)S(1)} %dynamic-slice_dynamic-update-slice_fusion), channel_id=1, source_target_pairs={{0,8},{8,16},{16,24},{24,28},{28,20},{20,12},{12,4},{4,0},{1,9},{9... | collective-permute-start | bytes 1290248 | tf_op jit(solution)/shard_map/ppermute | solution.py:666
  46.4 30.5 %collective-permute-start.6 = (f32[840,128]{1,0:T(8,128)S(1)}, f32[840,128]{1,0:T(8,128)S(1)}, u32[]{:S(2)}, u32[]{:S(2)}) collective-permute-start(f32[840,128]{1,0:T(8,128)S(1)} %collective-permute-done.4), channel_id=1, source_target_pairs={{8,0},{16,8},{24,16},{28,24},{20,28},{12,20},{4,12},{0,4},{9,1},{1... | collective-permute-start | bytes 1290248 | tf_op jit(solution)/shard_map/ppermute | solution.py:669
  48.0 28.9 %collective-permute-start.5 = (f32[840,128]{1,0:T(8,128)S(1)}, f32[840,128]{1,0:T(8,128)S(1)}, u32[]{:S(2)}, u32[]{:S(2)}) collective-permute-start(f32[840,128]{1,0:T(8,128)S(1)} %collective-permute-done.3), channel_id=1, source_target_pairs={{0,8},{8,16},{16,24},{24,28},{28,20},{20,12},{12,4},{4,0},{1,9},{9... | collective-permute-start | bytes 1290248 | tf_op jit(solution)/shard_map/ppermute | solution.py:666
  87.3 18.8 %collective-permute-start.9 = (f32[840,128]{1,0:T(8,128)S(1)}, f32[840,128]{1,0:T(8,128)S(1)}, u32[]{:S(2)}, u32[]{:S(2)}) collective-permute-start(f32[840,128]{1,0:T(8,128)S(1)} %collective-permute-done.7), channel_id=1, source_target_pairs={{0,8},{8,16},{16,24},{24,28},{28,20},{20,12},{12,4},{4,0},{1,9},{9... | collective-permute-start | bytes 1290248 | tf_op jit(solution)/shard_map/ppermute | solution.py:666
  164.9 416.5 %reduce-scatter.3.cloned.1.call-start = ((), (), s32[]{:S(2)}) async-start(), calls=%async_computation.5 | async-start | bytes 10616832 | tf_op jit(solution)/shard_map/reduce_scatter | solution.py:1017
  200.6 20.2 %collective-permute-start.21 = (f32[16,40,128]{2,1,0:T(8,128)S(1)}, f32[16,40,128]{2,1,0:T(8,128)S(1)}, u32[]{:S(2)}, u32[]{:S(2)}) collective-permute-start(f32[16,40,128]{2,1,0:T(8,128)S(1)} %bitcast.391), channel_id=1, source_target_pairs={{0,1},{1,0},{2,3},{3,2},{4,5},{5,4},{6,7},{7,6},{8,9},{9,8},{10,11... | collective-permute-start | bytes 983048 | tf_op jit(solution)/shard_map/ppermute | solution.py:575
  237.4 20.7 %collective-permute-start.26 = (f32[208,512]{1,0:T(8,128)S(1)}, f32[208,512]{1,0:T(8,128)S(1)}, u32[]{:S(2)}, u32[]{:S(2)}) collective-permute-start(f32[208,512]{1,0:T(8,128)S(1)} %collective-permute-done.24), channel_id=1, source_target_pairs={{0,8},{8,16},{16,24},{24,28},{28,20},{20,12},{12,4},{4,0},{1,9},{9... | collective-permute-start | bytes 1277960 | tf_op jit(solution)/shard_map/ppermute | solution.py:666
  238.7 32.8 %collective-permute-start.27 = (f32[208,512]{1,0:T(8,128)S(1)}, f32[208,512]{1,0:T(8,128)S(1)}, u32[]{:S(2)}, u32[]{:S(2)}) collective-permute-start(f32[208,512]{1,0:T(8,128)S(1)} %collective-permute-done.25), channel_id=1, source_target_pairs={{8,0},{16,8},{24,16},{28,24},{20,28},{12,20},{4,12},{0,4},{9,1},{1... | collective-permute-start | bytes 1277960 | tf_op jit(solution)/shard_map/ppermute | solution.py:669
  247.6 59.7 %collective-permute-start.40 = (f32[160,512]{1,0:T(8,128)}, f32[160,512]{1,0:T(8,128)S(1)}, u32[]{:S(2)}, u32[]{:S(2)}) collective-permute-start(f32[160,512]{1,0:T(8,128)} %get-tuple-element.309), channel_id=1, source_target_pairs={{0,1},{1,0},{2,3},{3,2},{4,5},{5,4},{6,7},{7,6},{8,9},{9,8},{10,11... | collective-permute-start | bytes 983048 | tf_op jit(solution)/shard_map/ppermute | solution.py:575
  251.0 56.3 %collective-permute-start.39 = (f32[160,512]{1,0:T(8,128)S(1)}, f32[160,512]{1,0:T(8,128)S(1)}, u32[]{:S(2)}, u32[]{:S(2)}) collective-permute-start(f32[160,512]{1,0:T(8,128)S(1)} %get-tuple-element.310), channel_id=1, source_target_pairs={{0,2},{1,3},{2,0},{3,1},{4,6},{5,7},{6,4},{7,5},{8,10},{9,11},{10,... | collective-permute-start | bytes 983048 | tf_op jit(solution)/shard_map/ppermute | solution.py:575
  251.8 55.5 %collective-permute-start.38 = (f32[160,512]{1,0:T(8,128)S(1)}, f32[160,512]{1,0:T(8,128)S(1)}, u32[]{:S(2)}, u32[]{:S(2)}) collective-permute-start(f32[160,512]{1,0:T(8,128)S(1)} %get-tuple-element.311), channel_id=1, source_target_pairs={{0,3},{1,2},{2,1},{3,0},{4,7},{5,6},{6,5},{7,4},{8,11},{9,10},{10,... | collective-permute-start | bytes 983048 | tf_op jit(solution)/shard_map/ppermute | solution.py:575
  258.0 26.0 %collective-permute-start.28 = (f32[208,512]{1,0:T(8,128)S(1)}, f32[208,512]{1,0:T(8,128)S(1)}, u32[]{:S(2)}, u32[]{:S(2)}) collective-permute-start(f32[208,512]{1,0:T(8,128)S(1)} %collective-permute-done.26), channel_id=1, source_target_pairs={{0,8},{8,16},{16,24},{24,28},{28,20},{20,12},{12,4},{4,0},{1,9},{9... | collective-permute-start | bytes 1277960 | tf_op jit(solution)/shard_map/ppermute | solution.py:666
  321.7 20.2 %collective-permute-start.44 = (f32[4,40,512]{2,1,0:T(8,128)}, f32[4,40,512]{2,1,0:T(8,128)S(1)}, u32[]{:S(2)}, u32[]{:S(2)}) collective-permute-start(f32[4,40,512]{2,1,0:T(8,128)} %bitcast.464), channel_id=1, source_target_pairs={{0,1},{1,0},{2,3},{3,2},{4,5},{5,4},{6,7},{7,6},{8,9},{9,8},{10,11... | collective-permute-start | bytes 983048 | tf_op jit(solution)/shard_map/ppermute | solution.py:575
  343.2 20.1 %collective-permute-start.48 = (f32[4,40,512]{2,1,0:T(8,128)}, f32[4,40,512]{2,1,0:T(8,128)S(1)}, u32[]{:S(2)}, u32[]{:S(2)}) collective-permute-start(f32[4,40,512]{2,1,0:T(8,128)} %bitcast.467), channel_id=1, source_target_pairs={{0,1},{1,0},{2,3},{3,2},{4,5},{5,4},{6,7},{7,6},{8,9},{9,8},{10,11... | collective-permute-start | bytes 983048 | tf_op jit(solution)/shard_map/ppermute | solution.py:575
  374.9 385.9 %reduce-scatter.5.cloned.1.call-start = ((), (), s32[]{:S(2)}) async-start(), calls=%async_computation.6 | async-start | bytes 10616832 | tf_op jit(solution)/shard_map/reduce_scatter | solution.py:1050
  511.8 20.9 %collective-permute-start.60 = (f32[640,128]{1,0:T(8,128)S(1)}, f32[640,128]{1,0:T(8,128)S(1)}, u32[]{:S(2)}, u32[]{:S(2)}) collective-permute-start(f32[640,128]{1,0:T(8,128)S(1)} %get-tuple-element.299), channel_id=1, source_target_pairs={{0,2},{1,3},{2,0},{3,1},{4,6},{5,7},{6,4},{7,5},{8,10},{9,11},{10,... | collective-permute-start | bytes 983048 | tf_op jit(solution)/shard_map/ppermute | solution.py:575
  577.5 29.0 %collective-permute-start.65 = (f32[8,3,16,512]{3,2,1,0:T(8,128)}, f32[8,3,16,512]{3,2,1,0:T(8,128)S(1)}, u32[]{:S(2)}, u32[]{:S(2)}) collective-permute-start(f32[8,3,16,512]{3,2,1,0:T(8,128)} %dynamic-slice_bitcast_fusion.1), channel_id=1, source_target_pairs={{0,2},{1,3},{2,0},{3,1},{4,6},{5,7},{6,4},{7,5},{8,10},{9,11},{10,... | collective-permute-start | bytes 2359304 | tf_op jit(solution)/shard_map/ppermute | solution.py:575
  615.9 25.2 %collective-permute-start.77 = (f32[320,512]{1,0:T(8,128)S(1)}, f32[320,512]{1,0:T(8,128)S(1)}, u32[]{:S(2)}, u32[]{:S(2)}) collective-permute-start(f32[320,512]{1,0:T(8,128)S(1)} %get-tuple-element.258), channel_id=1, source_target_pairs={{8,0},{16,8},{24,16},{28,24},{20,28},{12,20},{4,12},{0,4},{9,1},{1... | collective-permute-start | bytes 1966088 | tf_op jit(solution)/shard_map/ppermute | solution.py:701
  616.9 26.0 %collective-permute-start.74 = (f32[320,512]{1,0:T(8,128)S(1)}, f32[320,512]{1,0:T(8,128)S(1)}, u32[]{:S(2)}, u32[]{:S(2)}) collective-permute-start(f32[320,512]{1,0:T(8,128)S(1)} %get-tuple-element.259), channel_id=1, source_target_pairs={{0,8},{8,16},{16,24},{24,28},{28,20},{20,12},{12,4},{4,0},{1,9},{9... | collective-permute-start | bytes 1966088 | tf_op jit(solution)/shard_map/ppermute | solution.py:699
  618.1 30.5 %collective-permute-start.81 = (f32[576,512]{1,0:T(8,128)S(1)}, f32[576,512]{1,0:T(8,128)S(1)}, u32[]{:S(2)}, u32[]{:S(2)}) collective-permute-start(f32[576,512]{1,0:T(8,128)S(1)} %broadcast_multiply_fusion.1), channel_id=1, source_target_pairs={{0,2},{1,3},{2,0},{3,1},{4,6},{5,7},{6,4},{7,5},{8,10},{9,11},{10,... | collective-permute-start | bytes 3538952 | tf_op jit(solution)/shard_map/ppermute | solution.py:575
  643.6 20.3 %collective-permute-start.75 = (f32[320,512]{1,0:T(8,128)S(1)}, f32[320,512]{1,0:T(8,128)S(1)}, u32[]{:S(2)}, u32[]{:S(2)}) collective-permute-start(f32[320,512]{1,0:T(8,128)S(1)} %get-tuple-element.257), channel_id=1, source_target_pairs={{0,8},{8,16},{16,24},{24,28},{28,20},{20,12},{12,4},{4,0},{1,9},{9... | collective-permute-start | bytes 1966088 | tf_op jit(solution)/shard_map/ppermute | solution.py:699
  645.0 20.8 %collective-permute-start.80 = (f32[576,512]{1,0:T(8,128)S(1)}, f32[576,512]{1,0:T(8,128)S(1)}, u32[]{:S(2)}, u32[]{:S(2)}) collective-permute-start(f32[576,512]{1,0:T(8,128)S(1)} %broadcast_multiply_fusion.1), channel_id=1, source_target_pairs={{0,1},{1,0},{2,3},{3,2},{4,5},{5,4},{6,7},{7,6},{8,9},{9,8},{10,11... | collective-permute-start | bytes 3538952 | tf_op jit(solution)/shard_map/ppermute | solution.py:575
  681.1 45.1 %collective-permute-start.83 = (f32[320,512]{1,0:T(8,128)S(1)}, f32[320,512]{1,0:T(8,128)}, u32[]{:S(2)}, u32[]{:S(2)}) collective-permute-start(f32[320,512]{1,0:T(8,128)S(1)} %bitcast_add_fusion.3), channel_id=1, source_target_pairs={{8,0},{16,8},{24,16},{28,24},{20,28},{12,20},{4,12},{0,4},{9,1},{1... | collective-permute-start | bytes 1966088 | tf_op jit(solution)/shard_map/ppermute | solution.py:701
  682.2 22.1 %collective-permute-start.86 = (f32[160,512]{1,0:T(8,128)}, f32[160,512]{1,0:T(8,128)}, u32[]{:S(2)}, u32[]{:S(2)}) collective-permute-start(f32[160,512]{1,0:T(8,128)} %get-tuple-element.295), channel_id=1, source_target_pairs={{0,3},{1,2},{2,1},{3,0},{4,7},{5,6},{6,5},{7,4},{8,11},{9,10},{10,... | collective-permute-start | bytes 983048 | tf_op jit(solution)/shard_map/ppermute | solution.py:575
  693.9 20.4 %collective-permute-start.85 = (f32[160,512]{1,0:T(8,128)S(1)}, f32[160,512]{1,0:T(8,128)}, u32[]{:S(2)}, u32[]{:S(2)}) collective-permute-start(f32[160,512]{1,0:T(8,128)S(1)} %get-tuple-element.296), channel_id=1, source_target_pairs={{0,2},{1,3},{2,0},{3,1},{4,6},{5,7},{6,4},{7,5},{8,10},{9,11},{10,... | collective-permute-start | bytes 983048 | tf_op jit(solution)/shard_map/ppermute | solution.py:575
  730.8 30.0 %collective-permute-start.87 = (f32[328,512]{1,0:T(8,128)S(1)}, f32[328,512]{1,0:T(8,128)}, u32[]{:S(2)}, u32[]{:S(2)}) collective-permute-start(f32[328,512]{1,0:T(8,128)S(1)} %fusion.4), channel_id=1, source_target_pairs={{0,1},{1,0},{2,3},{3,2},{4,5},{5,4},{6,7},{7,6},{8,9},{9,8},{10,11... | collective-permute-start | bytes 2015240 | tf_op jit(solution)/shard_map/ppermute | solution.py:575
  765.1 27.8 %collective-permute-start.91 = (f32[576,512]{1,0:T(8,128)S(1)}, f32[576,512]{1,0:T(8,128)}, u32[]{:S(2)}, u32[]{:S(2)}) collective-permute-start(f32[576,512]{1,0:T(8,128)S(1)} %broadcast_multiply_fusion.one), channel_id=1, source_target_pairs={{0,2},{1,3},{2,0},{3,1},{4,6},{5,7},{6,4},{7,5},{8,10},{9,11},{10,... | collective-permute-start | bytes 3538952 | tf_op jit(solution)/shard_map/ppermute | solution.py:575
  765.1 37.5 %collective-permute-start.90 = (f32[576,512]{1,0:T(8,128)S(1)}, f32[576,512]{1,0:T(8,128)}, u32[]{:S(2)}, u32[]{:S(2)}) collective-permute-start(f32[576,512]{1,0:T(8,128)S(1)} %broadcast_multiply_fusion.one), channel_id=1, source_target_pairs={{0,1},{1,0},{2,3},{3,2},{4,5},{5,4},{6,7},{7,6},{8,9},{9,8},{10,11... | collective-permute-start | bytes 3538952 | tf_op jit(solution)/shard_map/ppermute | solution.py:575
  (151 other events, 2302.3 us)
Sparse Core Ops, SparseCore 0:
  12.5 162.9 all-gather.3
  178.2 105.9 all-gather.5
  287.0 80.6 all-gather.7
  375.1 164.0 reduce-scatter.2
  542.6 197.1 reduce-scatter.4

commit v7 on v6

--- a/solution.py
+++ b/solution.py
@@ -1141,7 +1141,6 @@
     )
     small = jnp.concatenate([square_sums, jnp.pad(norm_sums, ((0, 2), (0, 0)))], axis=0) * factor
     small_blocks = gather_keyed(small)
-    heads_sums, small_blocks = lax.optimization_barrier((heads_sums, small_blocks))
     small_got = in_order(small_blocks, row)
     segment_out, normal_out, depth_out, contour_out = single_call(
         heads_out_kernel,

time: 829 us -> 831 us (level)
  starting transfers between devices: 167 us -> 140 us
  waiting for transfers between devices: 309 us -> 334 us
    reduce_scatter x1, waiting for transfers between devices: 0.01 us -> 76.9 us  [shards(): lax.psum_scatter(heads_grad, 'batch', scatter_dimension=0, tiled=True)]
    ppermute x54, starting transfers between devices: 110 us -> 82.9 us  [swap_rows(): return lax.ppermute(block, 'rows', [(i, i ^ mask) for i in range(size)])]
    ppermute x4, waiting for transfers between devices: 58.2 us -> 33.3 us  [step(): self.falling = lax.ppermute(self.falling, 'batch', self.ring.down)]
    ppermute x54, waiting for transfers between devices: 114 us -> 92 us  [swap_rows(): return lax.ppermute(block, 'rows', [(i, i ^ mask) for i in range(size)])]
  transfers between devices with their start and end apart: 98 -> 98, of which waited for: 52 -> 52; matrix products, arithmetic and copies ran while one was open for 13% -> 12% of each run, Pallas kernels for 22% -> 23%
where the time goes in v7:
time: 831 us; the launch traced here: 819 us
  waiting for transfers between devices  334 us (40%)
  Pallas kernels  188 us (23%)
  starting transfers between devices  140 us (17%)
  local copies, waits for them, and re-layouts  67 us (8%)
  other arithmetic  49.7 us (6%)
  between operations  31.8 us (4%)
  matrix products  8.4 us (1%)
    ppermute x54, waiting for transfers between devices, swap_rows(): return lax.ppermute(block, 'rows', [(i, i ^ mask) for i in range(size)])  92 us
    ppermute x54, starting transfers between devices, swap_rows(): return lax.ppermute(block, 'rows', [(i, i ^ mask) for i in range(size)])  82.9 us
    reduce_scatter x1, waiting for transfers between devices, shards(): lax.psum_scatter(heads_grad, 'batch', scatter_dimension=0, tiled=True)  76.9 us
    ppermute x7, waiting for transfers between devices, gather(): falling = lax.ppermute(falling, 'batch', self.down)  57.1 us
    pallas_call x11, Pallas kernels, single_call(): kernel_call(body, (1,), [SCALAR] + [whole_spec(arg.shape) for arg in args...  48.9 us
    ppermute x7, waiting for transfers between devices, gather(): rising = lax.ppermute(rising, 'batch', self.up)  39.1 us
    ppermute x18, starting transfers between devices, swap(): return lax.ppermute(block, 'batch', [(i, i ^ mask) for i in range(size)])  34.5 us
    ppermute x4, waiting for transfers between devices, step(): self.falling = lax.ppermute(self.falling, 'batch', self.ring.down)  33.3 us
  transfers between devices with their start and end apart: 98, of which 52 were waited for; matrix products, arithmetic and copies ran while one was open for 12% of the time, Pallas kernels for 23%

profile of v7, /device:TPU:1, one launch (start us, length us, event | category | flops | bytes accessed | tf_op | source)
XLA Modules:
  0.0 819.4 jit_solution(11178744001811302292)
XLA Ops:
  48.2 28.7 %collective-permute-done.6 = f32[840,128]{1,0:T(8,128)S(1)} collective-permute-done((f32[840,128]{1,0:T(8,128)S(1)}, f32[840,128]{1,0:T(8,128)S(1)}, u32[]{:S(2)}, u32[]{:S(2)}) %collective-permute-start.6) | collective-permute-done | bytes 430112 | tf_op jit(solution)/shard_map/ppermute | solution.py:669
  78.4 8.9 %collective-permute-done.7 = f32[840,128]{1,0:T(8,128)S(1)} collective-permute-done((f32[840,128]{1,0:T(8,128)S(1)}, f32[840,128]{1,0:T(8,128)S(1)}, u32[]{:S(2)}, u32[]{:S(2)}) %collective-permute-start.7) | collective-permute-done | bytes 430112 | tf_op jit(solution)/shard_map/ppermute | solution.py:666
  89.0 17.2 %collective-permute-done.9 = f32[840,128]{1,0:T(8,128)S(1)} collective-permute-done((f32[840,128]{1,0:T(8,128)S(1)}, f32[840,128]{1,0:T(8,128)S(1)}, u32[]{:S(2)}, u32[]{:S(2)}) %collective-permute-start.9) | collective-permute-done | bytes 430112 | tf_op jit(solution)/shard_map/ppermute | solution.py:666
  112.7 10.2 %collective-permute-start.10 = (f32[2,648,128]{2,1,0:T(8,128)}, f32[2,648,128]{2,1,0:T(8,128)S(1)}, u32[]{:S(2)}, u32[]{:S(2)}) collective-permute-start(f32[2,648,128]{2,1,0:T(8,128)} %get-tuple-element.103), channel_id=1, source_target_pairs={{0,1},{1,0},{2,3},{3,2},{4,5},{5,4},{6,7},{7,6},{8,9},{9,8},{10,11... | collective-permute-start | bytes 1990664 | tf_op jit(solution)/shard_map/ppermute | solution.py:575
  127.4 7.7 collective-permute-done.11
  136.2 12.6 %collective-permute-start.12 = (f32[3,128]{1,0:T(4,128)S(1)}, f32[3,128]{1,0:T(4,128)S(1)}, u32[]{:S(2)}, u32[]{:S(2)}) collective-permute-start(f32[3,128]{1,0:T(4,128)S(1)} %pad_maximum_fusion.19), channel_id=1, source_target_pairs={{0,4},{4,0},{8,12},{12,8},{16,20},{20,16},{24,28},{28,24},{1,5},{5... | collective-permute-start | bytes 4616 | tf_op jit(solution)/shard_map/ppermute | solution.py:625
  176.7 10.0 %shard_map.384 = (f32[640,128]{1,0:T(8,128)}, f32[16,40,512]{2,1,0:T(8,128)}) custom-call(s32[1]{0:T(128)} %bitcast.row_ref.refs_0_, f32[16,40,128]{2,1,0:T(8,128)} %bitcast.389, f32[16,40,128]{2,1,0:T(8,128)} %copy-done.73, f32[16,40,128]{2,1,0:T(8,128)} %copy-done.62, f32[16,40,128]{2,1,0:T(8,128)} %copy-done.75, f32[4608,128]{1,0:T(8,128)} %bitcast.360), custom_call_target="tpu_custom_call" | custom-call | flops 2264924160 | bytes 12582912 | tf_op jit(solution)/shard_map/pallas_call | solution.py:438
  208.3 8.8 %collective-permute-done.24 = f32[208,512]{1,0:T(8,128)S(1)} collective-permute-done((f32[208,512]{1,0:T(8,128)S(1)}, f32[208,512]{1,0:T(8,128)S(1)}, u32[]{:S(2)}, u32[]{:S(2)}) %collective-permute-start.24) | collective-permute-done | bytes 426016 | tf_op jit(solution)/shard_map/ppermute | solution.py:666
  222.3 15.1 %shard_map.385 = (f32[640,512]{1,0:T(8,128)}, f32[16,40,512]{2,1,0:T(8,128)}, f32[4,320,128]{2,1,0:T(8,128)}) custom-call(s32[1]{0:T(128)} %bitcast.row_ref.refs_0_, f32[16,40,128]{2,1,0:T(8,128)} %bitcast.392, f32[16,40,128]{2,1,0:T(8,128)} %copy-done.66, f32[16,40,128]{2,1,0:T(8,128)} %copy-done.63, f32[16,40,128]{2,1,0:T(8,128)} %copy-done.72, ...), custom_call_target="tpu_custom_call" | custom-call | flops 9059696640 | bytes 12582912 | tf_op jit(solution)/shard_map/pallas_call | solution.py:438
  258.1 6.2 collective-permute-start.28
  264.2 7.3 collective-permute-done.27
  273.1 10.6 %collective-permute-done.29 = f32[208,512]{1,0:T(8,128)S(1)} collective-permute-done((f32[208,512]{1,0:T(8,128)S(1)}, f32[208,512]{1,0:T(8,128)S(1)}, u32[]{:S(2)}, u32[]{:S(2)}) %collective-permute-start.29) | collective-permute-done | bytes 426016 | tf_op jit(solution)/shard_map/ppermute | solution.py:669
  285.6 8.5 %collective-permute-done.30 = f32[208,512]{1,0:T(8,128)S(1)} collective-permute-done((f32[208,512]{1,0:T(8,128)S(1)}, f32[208,512]{1,0:T(8,128)S(1)}, u32[]{:S(2)}, u32[]{:S(2)}) %collective-permute-start.30) | collective-permute-done | bytes 426016 | tf_op jit(solution)/shard_map/ppermute | solution.py:669
  294.9 10.5 %shard_map.386 = (f32[2,160,512]{2,1,0:T(8,128)}, f32[2,160,512]{2,1,0:T(8,128)}) custom-call(s32[1]{0:T(128)} %bitcast.row_ref.refs_0_, f32[16,40,512]{2,1,0:T(8,128)} %bitcast.470, f32[72,2,16,512]{3,2,1,0:T(8,128)} %bitcast.457), custom_call_target="tpu_custom_call" | custom-call | flops 4529848320 | bytes 12582912 | tf_op jit(solution)/shard_map/pallas_call | solution.py:509
  344.1 6.6 collective-permute-done.49.three
  352.2 11.0 %shard_map.390 = (f32[72,4,16,512]{3,2,1,0:T(8,128)}, f32[16,40,512]{2,1,0:T(8,128)}) custom-call(s32[1]{0:T(128)} %bitcast.row_ref.refs_0_, f32[640,512]{1,0:T(8,128)} %get-tuple-element.114.input_ref, f32[4,40,512]{2,1,0:T(8,128)} %bitcast.465, f32[4,40,512]{2,1,0:T(8,128)} %copy-done.61, f32[4,40,512]{2,1,0:T(8,128)} %copy-done.60, f32[4,40,512]{2,1,0:T(8,128)} %copy-done.64), custom_call_target="tpu_custom_call" | custom-call | flops 4529848320 | bytes 12582912 | tf_op jit(solution)/shard_map/pallas_call | solution.py:546
  364.0 10.9 %shard_map.392 = (f32[72,4,16,512]{3,2,1,0:T(8,128)}, f32[16,40,512]{2,1,0:T(8,128)}) custom-call(s32[1]{0:T(128)} %bitcast.row_ref.refs_0_, f32[640,512]{1,0:T(8,128)} %get-tuple-element.114.input_ref, f32[4,40,512]{2,1,0:T(8,128)} %bitcast.468, f32[4,40,512]{2,1,0:T(8,128)} %copy-done.71, ...), custom_call_target="tpu_custom_call", output_to_operand_aliasing={{0}: (6, {})} | custom-call | flops 4529848320 | bytes 12582912 | tf_op jit(solution)/shard_map/pallas_call | solution.py:546
  375.1 10.6 %shard_map.394 = (f32[2,160,512]{2,1,0:T(8,128)}, f32[2,160,512]{2,1,0:T(8,128)}) custom-call(s32[1]{0:T(128)} %bitcast.row_ref.refs_0_, f32[16,40,512]{2,1,0:T(8,128)} %bitcast.471, f32[72,2,16,512]{3,2,1,0:T(8,128)} %bitcast.459), custom_call_target="tpu_custom_call" | custom-call | flops 4529848320 | bytes 12582912 | tf_op jit(solution)/shard_map/pallas_call | solution.py:509
  391.1 8.0 collective-permute-done.52.got_ref
  417.6 10.7 %shard_map.391 = f32[640,256]{1,0:T(8,128)} custom-call(f32[16,40,512]{2,1,0:T(8,128)} %get-tuple-element.130.note_ref, f32[72,2,16,512]{3,2,1,0:T(8,128)} %bitcast.460), custom_call_target="tpu_custom_call" | custom-call | flops 4529848320 | bytes 12582912 | tf_op jit(solution)/shard_map/pallas_call | solution.py:527
  428.3 10.7 %shard_map.393 = f32[640,256]{1,0:T(8,128)} custom-call(f32[16,40,512]{2,1,0:T(8,128)} %get-tuple-element.133.note_ref, f32[72,2,16,512]{3,2,1,0:T(8,128)} %bitcast.458), custom_call_target="tpu_custom_call" | custom-call | flops 4529848320 | bytes 12582912 | tf_op jit(solution)/shard_map/pallas_call | solution.py:527
  439.1 16.6 %shard_map.396 = (f32[4608,512]{1,0:T(8,128)}, f32[16,40,512]{2,1,0:T(8,128)}) custom-call(s32[1]{0:T(128)} %bitcast.row_ref.refs_0_, f32[640,512]{1,0:T(8,128)} %bitcast.347, f32[16,40,256]{2,1,0:T(8,128)} %bitcast.472, f32[16,40,256]{2,1,0:T(8,128)} %bitcast.473, f32[4,8,40,128]{3,2,1,0:T(8,128)} %pad_maximum_fusion.9.direct_ref), custom_call_target="tpu_custom_call" | custom-call | flops 9059696640 | bytes 12582912 | tf_op jit(solution)/shard_map/pallas_call | solution.py:492
  483.8 14.8 %shard_map.397 = (f32[2,640,128]{2,1,0:T(8,128)}, f32[2,640,128]{2,1,0:T(8,128)}) custom-call(s32[1]{0:T(128)} %bitcast.row_ref.refs_0_, f32[16,40,512]{2,1,0:T(8,128)} %get-tuple-element.138.refs_1_, f32[4608,512]{1,0:T(8,128)} %all-gather.4.cloned.1.call-done.weight_ref.refs_2_), custom_call_target="tpu_custom_call" | custom-call | flops 9059696640 | bytes 12582912 | tf_op jit(solution)/shard_map/pallas_call | solution.py:458
  512.7 7.2 collective-permute-done.59.four
  525.7 7.0 collective-permute-done.60
  542.8 9.9 %shard_map.401 = (f32[2,640,128]{2,1,0:T(8,128)}, f32[2,640,128]{2,1,0:T(8,128)}) custom-call(s32[1]{0:T(128)} %bitcast.row_ref.refs_0_, f32[16,40,128]{2,1,0:T(8,128)} %bitcast.385, f32[4608,128]{1,0:T(8,128)} %bitcast.361), custom_call_target="tpu_custom_call" | custom-call | flops 2264924160 | bytes 12582912 | tf_op jit(solution)/shard_map/pallas_call | solution.py:458
  560.5 8.1 collective-permute-done.67
  585.7 8.8 %shard_map.400 = f32[4608,128]{1,0:T(8,128)} custom-call(f32[640,512]{1,0:T(8,128)} %bitcast.469, f32[16,40,128]{2,1,0:T(8,128)} %bitcast.386), custom_call_target="tpu_custom_call" | custom-call | flops 2264924160 | bytes 12582912 | tf_op jit(solution)/shard_map/pallas_call | solution.py:476
  619.3 21.9 %collective-permute-done.77 = f32[320,512]{1,0:T(8,128)S(1)} collective-permute-done((f32[320,512]{1,0:T(8,128)S(1)}, f32[320,512]{1,0:T(8,128)S(1)}, u32[]{:S(2)}, u32[]{:S(2)}) %collective-permute-start.77) | collective-permute-done | bytes 655392 | tf_op jit(solution)/shard_map/ppermute | solution.py:701
  649.8 76.9 %reduce-scatter.5.cloned.1.call-done = f32[576,512]{1,0:T(8,128)} async-done(((f32[4608,512]{1,0:T(8,128)}), f32[576,512]{1,0:T(8,128)}) %reduce-scatter.5.cloned.1.call-update) | async-done | bytes 1179664 | tf_op jit(solution)/shard_map/reduce_scatter | solution.py:1050
  736.4 11.4 %collective-permute-done.79 = f32[320,512]{1,0:T(8,128)S(1)} collective-permute-done((f32[320,512]{1,0:T(8,128)S(1)}, f32[320,512]{1,0:T(8,128)S(1)}, u32[]{:S(2)}, u32[]{:S(2)}) %collective-permute-start.79) | collective-permute-done | bytes 655392 | tf_op jit(solution)/shard_map/ppermute | solution.py:701
  776.3 7.9 shard_map.404
  (541 shorter events, 366.5 us)
Async XLA Ops:
  7.2 190.7 %all-gather.4.cloned.1.call-start = ((), (), s32[]{:S(2)}) async-start(), calls=%async_computation.2 | async-start | bytes 10616832 | tf_op jit(solution)/shard_map/all_gather | solution.py:814
  12.4 282.5 %all-gather.6.cloned.1.call-start = ((), (), s32[]{:S(2)}) async-start(), calls=%async_computation.3 | async-start | bytes 5308416 | tf_op jit(solution)/shard_map/all_gather | solution.py:828
  14.5 360.6 %all-gather.8.cloned.1.call-start = ((), (), s32[]{:S(2)}) async-start(), calls=%async_computation.4 | async-start | bytes 5308416 | tf_op jit(solution)/shard_map/all_gather | solution.py:828
  18.7 27.7 %collective-permute-start.4 = (f32[840,128]{1,0:T(8,128)S(1)}, f32[840,128]{1,0:T(8,128)S(1)}, u32[]{:S(2)}, u32[]{:S(2)}) collective-permute-start(f32[840,128]{1,0:T(8,128)S(1)} %dynamic-slice_dynamic-update-slice_fusion), channel_id=1, source_target_pairs={{8,0},{16,8},{24,16},{28,24},{20,28},{12,20},{4,12},{0,4},{9,1},{1... | collective-permute-start | bytes 1290248 | tf_op jit(solution)/shard_map/ppermute | solution.py:669
  20.8 27.2 %collective-permute-start.3 = (f32[840,128]{1,0:T(8,128)S(1)}, f32[840,128]{1,0:T(8,128)S(1)}, u32[]{:S(2)}, u32[]{:S(2)}) collective-permute-start(f32[840,128]{1,0:T(8,128)S(1)} %dynamic-slice_dynamic-update-slice_fusion), channel_id=1, source_target_pairs={{0,8},{8,16},{16,24},{24,28},{28,20},{20,12},{12,4},{4,0},{1,9},{9... | collective-permute-start | bytes 1290248 | tf_op jit(solution)/shard_map/ppermute | solution.py:666
  46.4 30.5 %collective-permute-start.6 = (f32[840,128]{1,0:T(8,128)S(1)}, f32[840,128]{1,0:T(8,128)S(1)}, u32[]{:S(2)}, u32[]{:S(2)}) collective-permute-start(f32[840,128]{1,0:T(8,128)S(1)} %collective-permute-done.4), channel_id=1, source_target_pairs={{8,0},{16,8},{24,16},{28,24},{20,28},{12,20},{4,12},{0,4},{9,1},{1... | collective-permute-start | bytes 1290248 | tf_op jit(solution)/shard_map/ppermute | solution.py:669
  48.0 28.9 %collective-permute-start.5 = (f32[840,128]{1,0:T(8,128)S(1)}, f32[840,128]{1,0:T(8,128)S(1)}, u32[]{:S(2)}, u32[]{:S(2)}) collective-permute-start(f32[840,128]{1,0:T(8,128)S(1)} %collective-permute-done.3), channel_id=1, source_target_pairs={{0,8},{8,16},{16,24},{24,28},{28,20},{20,12},{12,4},{4,0},{1,9},{9... | collective-permute-start | bytes 1290248 | tf_op jit(solution)/shard_map/ppermute | solution.py:666
  164.8 416.5 %reduce-scatter.3.cloned.1.call-start = ((), (), s32[]{:S(2)}) async-start(), calls=%async_computation.5 | async-start | bytes 10616832 | tf_op jit(solution)/shard_map/reduce_scatter | solution.py:1017
  200.6 20.2 %collective-permute-start.21 = (f32[16,40,128]{2,1,0:T(8,128)S(1)}, f32[16,40,128]{2,1,0:T(8,128)S(1)}, u32[]{:S(2)}, u32[]{:S(2)}) collective-permute-start(f32[16,40,128]{2,1,0:T(8,128)S(1)} %bitcast.391), channel_id=1, source_target_pairs={{0,1},{1,0},{2,3},{3,2},{4,5},{5,4},{6,7},{7,6},{8,9},{9,8},{10,11... | collective-permute-start | bytes 983048 | tf_op jit(solution)/shard_map/ppermute | solution.py:575
  237.4 20.7 %collective-permute-start.26 = (f32[208,512]{1,0:T(8,128)S(1)}, f32[208,512]{1,0:T(8,128)S(1)}, u32[]{:S(2)}, u32[]{:S(2)}) collective-permute-start(f32[208,512]{1,0:T(8,128)S(1)} %collective-permute-done.24), channel_id=1, source_target_pairs={{0,8},{8,16},{16,24},{24,28},{28,20},{20,12},{12,4},{4,0},{1,9},{9... | collective-permute-start | bytes 1277960 | tf_op jit(solution)/shard_map/ppermute | solution.py:666
  238.7 32.7 %collective-permute-start.27 = (f32[208,512]{1,0:T(8,128)S(1)}, f32[208,512]{1,0:T(8,128)S(1)}, u32[]{:S(2)}, u32[]{:S(2)}) collective-permute-start(f32[208,512]{1,0:T(8,128)S(1)} %collective-permute-done.25), channel_id=1, source_target_pairs={{8,0},{16,8},{24,16},{28,24},{20,28},{12,20},{4,12},{0,4},{9,1},{1... | collective-permute-start | bytes 1277960 | tf_op jit(solution)/shard_map/ppermute | solution.py:669
  247.6 59.6 %collective-permute-start.40 = (f32[160,512]{1,0:T(8,128)}, f32[160,512]{1,0:T(8,128)S(1)}, u32[]{:S(2)}, u32[]{:S(2)}) collective-permute-start(f32[160,512]{1,0:T(8,128)} %get-tuple-element.299), channel_id=1, source_target_pairs={{0,1},{1,0},{2,3},{3,2},{4,5},{5,4},{6,7},{7,6},{8,9},{9,8},{10,11... | collective-permute-start | bytes 983048 | tf_op jit(solution)/shard_map/ppermute | solution.py:575
  250.9 56.3 %collective-permute-start.39 = (f32[160,512]{1,0:T(8,128)S(1)}, f32[160,512]{1,0:T(8,128)S(1)}, u32[]{:S(2)}, u32[]{:S(2)}) collective-permute-start(f32[160,512]{1,0:T(8,128)S(1)} %get-tuple-element.300), channel_id=1, source_target_pairs={{0,2},{1,3},{2,0},{3,1},{4,6},{5,7},{6,4},{7,5},{8,10},{9,11},{10,... | collective-permute-start | bytes 983048 | tf_op jit(solution)/shard_map/ppermute | solution.py:575
  251.8 55.5 %collective-permute-start.38 = (f32[160,512]{1,0:T(8,128)S(1)}, f32[160,512]{1,0:T(8,128)S(1)}, u32[]{:S(2)}, u32[]{:S(2)}) collective-permute-start(f32[160,512]{1,0:T(8,128)S(1)} %get-tuple-element.301), channel_id=1, source_target_pairs={{0,3},{1,2},{2,1},{3,0},{4,7},{5,6},{6,5},{7,4},{8,11},{9,10},{10,... | collective-permute-start | bytes 983048 | tf_op jit(solution)/shard_map/ppermute | solution.py:575
  258.1 26.0 %collective-permute-start.28 = (f32[208,512]{1,0:T(8,128)S(1)}, f32[208,512]{1,0:T(8,128)S(1)}, u32[]{:S(2)}, u32[]{:S(2)}) collective-permute-start(f32[208,512]{1,0:T(8,128)S(1)} %collective-permute-done.26), channel_id=1, source_target_pairs={{0,8},{8,16},{16,24},{24,28},{28,20},{20,12},{12,4},{4,0},{1,9},{9... | collective-permute-start | bytes 1277960 | tf_op jit(solution)/shard_map/ppermute | solution.py:666
  321.5 20.2 %collective-permute-start.44 = (f32[4,40,512]{2,1,0:T(8,128)}, f32[4,40,512]{2,1,0:T(8,128)S(1)}, u32[]{:S(2)}, u32[]{:S(2)}) collective-permute-start(f32[4,40,512]{2,1,0:T(8,128)} %bitcast.464), channel_id=1, source_target_pairs={{0,1},{1,0},{2,3},{3,2},{4,5},{5,4},{6,7},{7,6},{8,9},{9,8},{10,11... | collective-permute-start | bytes 983048 | tf_op jit(solution)/shard_map/ppermute | solution.py:575
  343.0 20.1 %collective-permute-start.48 = (f32[4,40,512]{2,1,0:T(8,128)}, f32[4,40,512]{2,1,0:T(8,128)S(1)}, u32[]{:S(2)}, u32[]{:S(2)}) collective-permute-start(f32[4,40,512]{2,1,0:T(8,128)} %bitcast.467), channel_id=1, source_target_pairs={{0,1},{1,0},{2,3},{3,2},{4,5},{5,4},{6,7},{7,6},{8,9},{9,8},{10,11... | collective-permute-start | bytes 983048 | tf_op jit(solution)/shard_map/ppermute | solution.py:575
  374.9 351.9 %reduce-scatter.5.cloned.1.call-start = ((), (), s32[]{:S(2)}) async-start(), calls=%async_computation.6 | async-start | bytes 10616832 | tf_op jit(solution)/shard_map/reduce_scatter | solution.py:1050
  511.8 20.9 %collective-permute-start.60 = (f32[640,128]{1,0:T(8,128)S(1)}, f32[640,128]{1,0:T(8,128)S(1)}, u32[]{:S(2)}, u32[]{:S(2)}) collective-permute-start(f32[640,128]{1,0:T(8,128)S(1)} %get-tuple-element.289), channel_id=1, source_target_pairs={{0,2},{1,3},{2,0},{3,1},{4,6},{5,7},{6,4},{7,5},{8,10},{9,11},{10,... | collective-permute-start | bytes 983048 | tf_op jit(solution)/shard_map/ppermute | solution.py:575
  577.7 29.0 %collective-permute-start.65 = (f32[8,3,16,512]{3,2,1,0:T(8,128)}, f32[8,3,16,512]{3,2,1,0:T(8,128)S(1)}, u32[]{:S(2)}, u32[]{:S(2)}) collective-permute-start(f32[8,3,16,512]{3,2,1,0:T(8,128)} %dynamic-slice_bitcast_fusion.1), channel_id=1, source_target_pairs={{0,2},{1,3},{2,0},{3,1},{4,6},{5,7},{6,4},{7,5},{8,10},{9,11},{10,... | collective-permute-start | bytes 2359304 | tf_op jit(solution)/shard_map/ppermute | solution.py:575
  616.1 25.1 %collective-permute-start.77 = (f32[320,512]{1,0:T(8,128)S(1)}, f32[320,512]{1,0:T(8,128)S(1)}, u32[]{:S(2)}, u32[]{:S(2)}) collective-permute-start(f32[320,512]{1,0:T(8,128)S(1)} %get-tuple-element.248), channel_id=1, source_target_pairs={{8,0},{16,8},{24,16},{28,24},{20,28},{12,20},{4,12},{0,4},{9,1},{1... | collective-permute-start | bytes 1966088 | tf_op jit(solution)/shard_map/ppermute | solution.py:701
  617.0 26.1 %collective-permute-start.74 = (f32[320,512]{1,0:T(8,128)S(1)}, f32[320,512]{1,0:T(8,128)S(1)}, u32[]{:S(2)}, u32[]{:S(2)}) collective-permute-start(f32[320,512]{1,0:T(8,128)S(1)} %get-tuple-element.249), channel_id=1, source_target_pairs={{0,8},{8,16},{16,24},{24,28},{28,20},{20,12},{12,4},{4,0},{1,9},{9... | collective-permute-start | bytes 1966088 | tf_op jit(solution)/shard_map/ppermute | solution.py:699
  618.2 31.6 %collective-permute-start.81 = (f32[576,512]{1,0:T(8,128)S(1)}, f32[576,512]{1,0:T(8,128)S(1)}, u32[]{:S(2)}, u32[]{:S(2)}) collective-permute-start(f32[576,512]{1,0:T(8,128)S(1)} %broadcast_multiply_fusion.1), channel_id=1, source_target_pairs={{0,2},{1,3},{2,0},{3,1},{4,6},{5,7},{6,4},{7,5},{8,10},{9,11},{10,... | collective-permute-start | bytes 3538952 | tf_op jit(solution)/shard_map/ppermute | solution.py:575
  644.5 85.9 %collective-permute-start.78 = (f32[320,512]{1,0:T(8,128)}, f32[320,512]{1,0:T(8,128)}, u32[]{:S(2)}, u32[]{:S(2)}) collective-permute-start(f32[320,512]{1,0:T(8,128)} %get-tuple-element.246), channel_id=1, source_target_pairs={{8,0},{16,8},{24,16},{28,24},{20,28},{12,20},{4,12},{0,4},{9,1},{1... | collective-permute-start | bytes 1966088 | tf_op jit(solution)/shard_map/ppermute | solution.py:701
  644.9 85.5 %collective-permute-start.75 = (f32[320,512]{1,0:T(8,128)}, f32[320,512]{1,0:T(8,128)}, u32[]{:S(2)}, u32[]{:S(2)}) collective-permute-start(f32[320,512]{1,0:T(8,128)} %get-tuple-element.247), channel_id=1, source_target_pairs={{0,8},{8,16},{16,24},{24,28},{28,20},{20,12},{12,4},{4,0},{1,9},{9... | collective-permute-start | bytes 1966088 | tf_op jit(solution)/shard_map/ppermute | solution.py:699
  646.2 88.6 %collective-permute-start.80 = (f32[576,512]{1,0:T(8,128)S(1)}, f32[576,512]{1,0:T(8,128)S(1)}, u32[]{:S(2)}, u32[]{:S(2)}) collective-permute-start(f32[576,512]{1,0:T(8,128)S(1)} %broadcast_multiply_fusion.1), channel_id=1, source_target_pairs={{0,1},{1,0},{2,3},{3,2},{4,5},{5,4},{6,7},{7,6},{8,9},{9,8},{10,11... | collective-permute-start | bytes 3538952 | tf_op jit(solution)/shard_map/ppermute | solution.py:575
  649.8 86.6 %collective-permute-start.82 = (f32[576,512]{1,0:T(8,128)S(1)}, f32[576,512]{1,0:T(8,128)}, u32[]{:S(2)}, u32[]{:S(2)}) collective-permute-start(f32[576,512]{1,0:T(8,128)S(1)} %collective-permute-done.81), channel_id=1, source_target_pairs={{0,1},{1,0},{2,3},{3,2},{4,5},{5,4},{6,7},{7,6},{8,9},{9,8},{10,11... | collective-permute-start | bytes 3538952 | tf_op jit(solution)/shard_map/ppermute | solution.py:575
  729.2 27.2 %collective-permute-start.91 = (f32[576,512]{1,0:T(8,128)}, f32[576,512]{1,0:T(8,128)}, u32[]{:S(2)}, u32[]{:S(2)}) collective-permute-start(f32[576,512]{1,0:T(8,128)} %broadcast_multiply_fusion.one), channel_id=1, source_target_pairs={{0,2},{1,3},{2,0},{3,1},{4,6},{5,7},{6,4},{7,5},{8,10},{9,11},{10,... | collective-permute-start | bytes 3538952 | tf_op jit(solution)/shard_map/ppermute | solution.py:575
  734.8 30.8 %collective-permute-start.86 = (f32[160,512]{1,0:T(8,128)S(1)}, f32[160,512]{1,0:T(8,128)S(1)}, u32[]{:S(2)}, u32[]{:S(2)}) collective-permute-start(f32[160,512]{1,0:T(8,128)S(1)} %get-tuple-element.285), channel_id=1, source_target_pairs={{0,3},{1,2},{2,1},{3,0},{4,7},{5,6},{6,5},{7,4},{8,11},{9,10},{10,... | collective-permute-start | bytes 983048 | tf_op jit(solution)/shard_map/ppermute | solution.py:575
  751.0 19.4 %collective-permute-start.83 = (f32[320,512]{1,0:T(8,128)}, f32[320,512]{1,0:T(8,128)}, u32[]{:S(2)}, u32[]{:S(2)}) collective-permute-start(f32[320,512]{1,0:T(8,128)} %bitcast_add_fusion.3), channel_id=1, source_target_pairs={{8,0},{16,8},{24,16},{28,24},{20,28},{12,20},{4,12},{0,4},{9,1},{1... | collective-permute-start | bytes 1966088 | tf_op jit(solution)/shard_map/ppermute | solution.py:701
  751.3 24.9 %collective-permute-start.90 = (f32[576,512]{1,0:T(8,128)}, f32[576,512]{1,0:T(8,128)}, u32[]{:S(2)}, u32[]{:S(2)}) collective-permute-start(f32[576,512]{1,0:T(8,128)} %broadcast_multiply_fusion.one), channel_id=1, source_target_pairs={{0,1},{1,0},{2,3},{3,2},{4,5},{5,4},{6,7},{7,6},{8,9},{9,8},{10,11... | collective-permute-start | bytes 3538952 | tf_op jit(solution)/shard_map/ppermute | solution.py:575
  756.4 19.8 %collective-permute-start.92 = (f32[576,512]{1,0:T(8,128)}, f32[576,512]{1,0:T(8,128)}, u32[]{:S(2)}, u32[]{:S(2)}) collective-permute-start(f32[576,512]{1,0:T(8,128)} %collective-permute-done.91.three), channel_id=1, source_target_pairs={{0,1},{1,0},{2,3},{3,2},{4,5},{5,4},{6,7},{7,6},{8,9},{9,8},{10,11... | collective-permute-start | bytes 3538952 | tf_op jit(solution)/shard_map/ppermute | solution.py:575
  (143 other events, 2156.5 us)
Sparse Core Ops, SparseCore 0:
  12.5 162.9 all-gather.3
  178.2 106.0 all-gather.5
  287.1 80.5 all-gather.7
  375.0 164.0 reduce-scatter.2
  542.6 184.1 reduce-scatter.4
